TPU v7x, 128 devices: a whole 4x4x4 slice. The times are simulated.
128 devices in a mesh: pts: 128 (over x, y, z, core).
Axes of the slice: x: 4, y: 4, z: 4, core: 2. Of those that a mesh axis runs over, the one named last changes fastest.
Arguments:
- points: bfloat16 [49152, 128], P('pts'), may hold values from -5 to 5
- noise_var: float32 [49152], P('pts'), may hold values from 0.5 to 4
- right_side: float32 [49152, 32], P('pts'), may hold values from -8 to 8
Outputs:
- solution_field: float32 [49152, 32], P('pts')
- residual: float32 [49152, 32], P('pts')
All inputs are finite; a program needn't handle non-finite values.
Results may differ from a plain program's by a relative error of at most 0.0075.
Values may be sent and summed in bfloat16 or wider, within the bound.
No kernel may reach another device: no remote copies, remote signals or barrier semaphores. Data moves between devices by JAX's collectives and lax.ppermute only.
A program may use at most 128 MiB of HBM per device.

v0:
```python
import math

import jax
import jax.numpy as jnp
from jax import lax
from jax.sharding import PartitionSpec as P

ITERS = 2


def kernel_tile(left, left_sq, right, width):
    right_sq = jnp.sum(jnp.square(right.astype(jnp.float32)), axis=1)
    cross = lax.dot_general(
        left, right, (((1,), (1,)), ((), ())), preferred_element_type=jnp.float32
    )
    dist = left_sq[:, None] + right_sq[None, :] - 2.0 * cross
    return jnp.exp(-dist / width).astype(jnp.bfloat16)


def as_blocks(piece, rows):
    shards = piece.shape[0] // rows
    pieces = math.gcd(shards, 8)
    return piece.reshape(pieces, piece.shape[0] // pieces, piece.shape[1])


def column_sums(values):
    return lax.psum(values, "pts")


def per_device(points, noise_var, right_side):
    rows = points.shape[0]
    feats = points.shape[1]
    width = float(feats)
    columns = right_side.shape[1]
    left_sq = jnp.sum(jnp.square(points.astype(jnp.float32)), axis=1)
    empty = jnp.zeros((rows, columns), jnp.float32)
    solution_field = jnp.zeros_like(right_side)
    residual = right_side
    direction = right_side
    norm_now = column_sums(jnp.sum(residual * residual, axis=0))
    for step_count in range(ITERS):
        total = empty

        def step(acc, item):
            tile = kernel_tile(points, left_sq, item[0], width)
            return (acc + jnp.dot(tile, item[1], preferred_element_type=jnp.float32), None)

        total, unused = lax.scan(
            step,
            total,
            (
                as_blocks(lax.all_gather(points, "pts", axis=0, tiled=True), rows),
                as_blocks(
                    lax.all_gather(direction.astype(jnp.bfloat16), "pts", axis=0, tiled=True), rows
                ),
            ),
        )
        image = total + noise_var[:, None] * direction
        alpha = norm_now / lax.psum(jnp.sum(direction * image, axis=0), "pts")
        solution_field = solution_field + alpha * direction
        residual = residual - alpha * image
        norm_next = column_sums(jnp.sum(residual * residual, axis=0))
        direction = residual + norm_next / norm_now * direction
        norm_now = norm_next
    return (solution_field, residual)


def solution(mesh):
    return jax.shard_map(
        per_device,
        mesh=mesh,
        in_specs=(P("pts", None), P("pts"), P("pts", None)),
        out_specs=(P("pts", None), P("pts", None)),
        check_vma=False,
    )
```

profile of v0, /device:TPU:1, one launch (start us, length us, event | category | flops | bytes accessed | tf_op | source)
XLA Modules:
  0.0 543.5 jit_solution(13235806180449488108)
XLA Ops:
  7.2 0.0 copy-start.1
  7.2 0.0 all-gather.6.cloned.1.call-start
  7.2 1.4 convert_element_type.22
  8.6 0.0 all-gather.6.cloned.1.call-update
  8.7 0.0 all-gather.4.cloned.1.call-start
  8.7 0.7 all-gather.4.cloned.1.call-update
  9.4 0.0 all-gather.8.cloned.1.call-start
  9.5 1.0 multiply_reduce_fusion.2
  10.5 70.7 %all-gather.6.cloned.1.call-done = bf16[49152,32]{0,1:T(8,128)(2,1)} async-done(((bf16[384,32]{0,1:T(8,128)(2,1)}), bf16[49152,32]{0,1:T(8,128)(2,1)}) %all-gather.6.cloned.1.call-update) | async-done | bytes 3145744 | tf_op jit(solution)/shard_map/all_gather | solution.py:54
  81.2 10.6 %copy.5 = bf16[49152,32]{1,0:T(8,128)(2,1)} copy(bf16[49152,32]{0,1:T(8,128)(2,1)} %all-gather.6.cloned.1.call-done) | data formatting | bytes 6291456 | tf_op jit(solution)/shard_map/all_gather | solution.py:54
  91.8 63.3 %all-gather.4.cloned.1.call-done = bf16[49152,128]{1,0:T(8,128)(2,1)} async-done(((bf16[384,128]{1,0:T(8,128)(2,1)}), bf16[49152,128]{1,0:T(8,128)(2,1)}) %all-gather.4.cloned.1.call-update) | async-done | bytes 12582928 | tf_op jit(solution)/shard_map/all_gather | solution.py:52
  155.1 0.0 copy-done.1
  155.1 0.0 copy-start
  155.1 0.0 copy-start.2
  155.1 57.6 %while.22 = (s32[]{:T(128)}, f32[384,32]{0,1:T(8,128)S(1)}, f32[384]{0:T(512)S(1)}, bf16[8,6144,128]{2,1,0:T(8,128)(2,1)}, bf16[384,128]{1,0:T(8,128)(2,1)S(1)},...) while((s32[]{:T(128)}, f32[384,32]{0,1:T(8,128)S(1)}, f32[384]{0:T(512)S(1)}, ...), condition=%wide.region_5.6_spmd.clone, body=%wide.region_3.5_spmd.clone.sunk | while | flops 771508224 | bytes 4967011 | solution.py:48
  155.1 2.3 multiply_reduce_fusion.9
  157.5 4.9 fusion.54
  162.4 2.3 multiply_reduce_fusion.9
  164.7 4.9 fusion.54
  169.6 2.3 multiply_reduce_fusion.9
  171.9 4.9 fusion.54
  176.8 2.3 multiply_reduce_fusion.9
  179.1 4.9 fusion.54
  184.0 2.3 multiply_reduce_fusion.9
  186.3 4.9 fusion.54
  191.2 2.3 multiply_reduce_fusion.9
  193.5 4.9 fusion.54
  198.4 2.3 multiply_reduce_fusion.9
  200.7 4.9 fusion.54
  205.6 2.3 multiply_reduce_fusion.9
  207.9 4.9 fusion.54
  212.8 0.0 copy-done
  212.8 0.0 copy-done.2
  212.8 0.1 multiply_reduce_fusion.5
  212.9 64.5 %all-reduce = (f32[32]{0:T(128)S(1)}, f32[32]{0:T(128)S(1)}) all-reduce(f32[32]{0:T(128)S(1)} %get-tuple-element.117, f32[32]{0:T(128)S(1)} %get-tuple-element.116), channel_id=1, replica_groups=mesh['pts'=128] {'pts'}, use_global_device_ids=true, to_apply=%region_1.0 | all-reduce | flops 64 | bytes 512 | tf_op jit(solution)/shard_map/psum | solution.py:27
  277.4 0.2 multiply_reduce_fusion.4
  277.6 64.0 %psum.30 = f32[32]{0:T(128)S(1)} all-reduce(f32[32]{0:T(128)S(1)} %multiply_reduce_fusion.4), channel_id=1, replica_groups=mesh['pts'=128] {'pts'}, use_global_device_ids=true, to_apply=%region_9.10 | all-reduce | flops 32 | bytes 256 | tf_op jit(solution)/shard_map/psum | solution.py:27
  341.6 0.7 fusion.40
  342.3 0.0 all-gather.8.cloned.1.call-update
  342.4 63.1 %all-gather.8.cloned.1.call-done = bf16[49152,32]{0,1:T(8,128)(2,1)} async-done(((bf16[384,32]{0,1:T(8,128)(2,1)}), bf16[49152,32]{0,1:T(8,128)(2,1)}) %all-gather.8.cloned.1.call-update) | async-done | bytes 3145744 | tf_op jit(solution)/shard_map/all_gather | solution.py:54
  405.4 10.6 %copy.7 = bf16[49152,32]{1,0:T(8,128)(2,1)} copy(bf16[49152,32]{0,1:T(8,128)(2,1)} %all-gather.8.cloned.1.call-done) | data formatting | bytes 6291456
  416.0 57.6 %while.23 = (s32[]{:T(128)}, f32[384,32]{0,1:T(8,128)S(1)}, f32[384]{0:T(512)S(1)}, bf16[8,6144,128]{2,1,0:T(8,128)(2,1)}, bf16[384,128]{1,0:T(8,128)(2,1)S(1)},...) while((s32[]{:T(128)}, f32[384,32]{0,1:T(8,128)S(1)}, f32[384]{0:T(512)S(1)}, ...), condition=%wide.region_12.13_spmd.clone, body=%wide.region_10.12_spmd.clone.sunk | while | flops 771508224 | bytes 4967011 | solution.py:48
  416.0 2.3 multiply_reduce_fusion.10
  418.3 4.9 fusion.58
  423.2 2.3 multiply_reduce_fusion.10
  425.5 4.9 fusion.58
  430.4 2.3 multiply_reduce_fusion.10
  432.7 4.9 fusion.58
  437.6 2.3 multiply_reduce_fusion.10
  439.9 4.9 fusion.58
  444.8 2.3 multiply_reduce_fusion.10
  447.1 4.9 fusion.58
  452.0 2.3 multiply_reduce_fusion.10
  454.3 4.9 fusion.58
  459.2 2.3 multiply_reduce_fusion.10
  461.5 4.9 fusion.58
  466.4 2.3 multiply_reduce_fusion.10
  468.7 4.9 fusion.58
  473.6 0.2 multiply_reduce_fusion.3
  473.8 62.4 %psum.31 = f32[32]{0:T(128)S(1)} all-reduce(f32[32]{0:T(128)S(1)} %multiply_reduce_fusion.3), channel_id=1, replica_groups=mesh['pts'=128] {'pts'}, use_global_device_ids=true, to_apply=%region_14.15 | all-reduce | flops 32 | bytes 256 | tf_op jit(solution)/shard_map/psum | solution.py:59
  536.3 0.7 multiply_subtract_fusion
  (5 shorter events, 0.0 us)
Async XLA Ops:
  7.2 148.0 %copy-start.1 = (bf16[384,128]{1,0:T(8,128)(2,1)S(1)}, bf16[384,128]{1,0:T(8,128)(2,1)}, u32[]{:S(2)}) copy-start(bf16[384,128]{1,0:T(8,128)(2,1)} %param.7) | copy-start | bytes 294916
  7.2 74.0 %all-gather.6.cloned.1.call-start = ((), (), s32[]{:S(2)}) async-start(), calls=%async_computation.1 | async-start | bytes 3170304 | tf_op jit(solution)/shard_map/all_gather | solution.py:54
  8.7 146.5 %all-gather.4.cloned.1.call-start = ((), (), s32[]{:S(2)}) async-start(), calls=%async_computation | async-start | bytes 12681216 | tf_op jit(solution)/shard_map/all_gather | solution.py:52
  9.4 396.0 %all-gather.8.cloned.1.call-start = ((), (), s32[]{:S(2)}) async-start(), calls=%async_computation.2 | async-start | bytes 3170304 | tf_op jit(solution)/shard_map/all_gather | solution.py:54
  155.1 57.6 %copy-start = (f32[384,32]{0,1:T(8,128)S(1)}, f32[384,32]{0,1:T(8,128)}, u32[]{:S(2)}) copy-start(f32[384,32]{0,1:T(8,128)} %param.9) | copy-start | bytes 147460
  155.1 57.6 %copy-start.2 = (f32[384]{0:T(512)S(1)}, f32[384]{0:T(512)}, u32[]{:S(2)}) copy-start(f32[384]{0:T(512)} %param.8) | copy-start | bytes 4612
Sparse Core Ops, SparseCore 0:
  11.4 69.7 all-gather.5
  84.2 70.8 all-gather.3
  342.5 62.9 all-gather.7
where the time goes:
time: 545 us; the launch traced here: 544 us
  waiting for transfers between devices  198 us (36%)
  blocking collectives  191 us (35%)
  matrix products  78.3 us (14%)
  other arithmetic  41.1 us (8%)
  local copies, waits for them, and re-layouts  21.2 us (4%)
  between operations  13.8 us (3%)
    all_gather x2, waiting for transfers between devices, per_device(): lax.all_gather(direction.astype(jnp.bfloat16), 'pts', axis=0, tiled=True)  134 us
    psum x2, blocking collectives, column_sums(): return lax.psum(values, 'pts')  129 us
    dot_general x16, matrix products, step(): jnp.dot(tile, item[1], preferred_element_type=jnp.float32)  78.3 us
    all_gather x1, waiting for transfers between devices, per_device(): lax.all_gather(points, 'pts', axis=0, tiled=True)  63.3 us
    psum x1, blocking collectives, per_device(): alpha = norm_now / lax.psum(jnp.sum(direction * image, axis=0), 'pts')  62.4 us
    reduce_sum x16, other arithmetic, kernel_tile(): right_sq = jnp.sum(jnp.square(right.astype(jnp.float32)), axis=1)  36.7 us
  transfers between devices with their start and end apart: 3, of which 3 were waited for; matrix products, arithmetic and copies ran while one was open for 2% of the time, Pallas kernels for 0%

commit v1 on v0

v1 whole, which is shorter than its diff:
```python
import functools
import math

import jax
import jax.numpy as jnp
from jax import lax
from jax.experimental import pallas as pl
from jax.experimental.pallas import tpu as pltpu
from jax.sharding import PartitionSpec as P

DEVICES = 128
NEAR_MASKS = (2, 8)
SIDE_MASKS = (6, 24)
LINE_MASKS = (32, 64)
CORE_MASK = 1
NEAR = 1 << len(NEAR_MASKS)
SIDE = 1 << len(SIDE_MASKS)
EVEN_LINES = (0, 1, 3, 2)
ODD_LINES = (0, 1, 2, 3)
TURNS = 4
CHIPS = SIDE * TURNS
PAIR = 2
UNROLL = 2
LANES = 128
CHUNK = 512
UNIT = 256
SPLITS = 3
LIMIT = 6 * 1024 * 1024
SMALL = 8 * 1024 * 1024
INSIDE = pl.BlockSpec(memory_space=pltpu.VMEM)


def scale_of(feats):
    return 2.0 / feats * math.log2(math.e)


def reach(masks, k):
    mask = 0
    for bit, step in enumerate(masks):
        if (k >> bit) & 1:
            mask ^= step
    return mask


def chip_groups():
    groups, seen = [], set()
    for base in range(DEVICES):
        if base not in seen:
            group = [base ^ reach(SIDE_MASKS + LINE_MASKS, k) for k in range(CHIPS)]
            groups.append(group)
            seen.update(group)
    return groups


def place_in_group(index):
    place = 0
    for bit, mask in enumerate(SIDE_MASKS + LINE_MASKS):
        place += lax.rem(lax.div(index, 1 << (mask.bit_length() - 1)), 2) << bit
    return place


def partner(value, even, odd=None):
    odd = even if odd is None else odd
    pairs = [(k, k ^ (odd if k & CORE_MASK else even)) for k in range(DEVICES)]
    return lax.ppermute(value, "pts", pairs)


def exchange(items, masks):
    return [items[0]] + [partner(items[k], reach(masks, k)) for k in range(1, len(items))]


def line_masks(turn):
    return reach(LINE_MASKS, EVEN_LINES[turn]), reach(SIDE_MASKS, ODD_LINES[turn])


def share(copies):
    return lax.all_to_all(copies, "pts", 0, 0, axis_index_groups=chip_groups())


def small_call(body, shapes, *args):
    return pl.pallas_call(
        body,
        in_specs=[INSIDE] * len(args),
        out_specs=[INSIDE] * len(shapes),
        out_shape=[jax.ShapeDtypeStruct(*shape) for shape in shapes],
        compiler_params=pltpu.CompilerParams(vmem_limit_bytes=SMALL),
    )(*args)


def half_norms(scale, block):
    ones = jnp.ones((8, block.shape[1]), jnp.bfloat16)
    dims = (((1,), (1,)), ((), ()))
    square = jnp.square(block.astype(jnp.float32))
    high = square.astype(jnp.bfloat16)
    low = (square - high.astype(jnp.float32)).astype(jnp.bfloat16)
    total = lax.dot_general(ones, high, dims, preferred_element_type=jnp.float32)
    total += lax.dot_general(ones, low, dims, preferred_element_type=jnp.float32)
    return total * (-0.5 * scale)


def first_product(scale, rows, turn, *refs):
    far_refs = refs[:2]
    near_ref, half_ref = refs[2:4]
    kern_ref, sum_ref, far_ref = refs[-3:]
    sum_ref[...] = jnp.zeros_like(sum_ref) if turn == 0 else refs[4][...]
    cols = sum_ref.shape[0]
    width = near_ref.shape[1]
    chunks = width // UNIT
    tall = rows + cols * (rows // near_ref.shape[0])
    for k, ref in enumerate(far_refs):
        far_ref[pl.ds(k * SIDE, SIDE)] = ref[...]
        for j in range(SIDE):
            sum_ref[:, width:] += ref[j, pl.ds(tall, cols), :].astype(jnp.float32)

    @pl.loop(0, far_ref.shape[0] // (PAIR * UNROLL))
    def _(step):
        units, far, vec, far_half, here = [], [], [], [], []
        for u in range(UNROLL):
            first = PAIR * (UNROLL * step + u)
            block = jnp.concatenate([far_ref[first + k, :rows, :] for k in range(PAIR)], axis=0)
            pieces = [
                far_ref[first + k, pl.ds(at, cols), :]
                for k in range(PAIR)
                for at in range(rows, tall, cols)
            ]
            block_f = block.astype(jnp.float32)
            far.append(block)
            vec.append(jnp.concatenate(pieces, axis=1))
            far_half.append(jnp.sum(block_f * block_f, axis=1, keepdims=True) * (-0.5 * scale))
            here.append(pl.ds(pl.multiple_of(first * rows, PAIR * rows), PAIR * rows))
            units += [(u, pl.ds(c * UNIT, UNIT)) for c in range(chunks)]
        cross, tile = {}, {}
        for c in range(len(units) + 2):
            if c < len(units):
                u, part = units[c]
                cross[c] = jnp.dot(far[u], near_ref[:, part], preferred_element_type=jnp.float32)
            if 0 <= c - 1 < len(units):
                u, part = units[c - 1]
                tile[c - 1] = jnp.exp2(
                    cross.pop(c - 1) * scale + far_half[u] + half_ref[0:1, part]
                ).astype(jnp.bfloat16)
                kern_ref[here[u], part] = tile[c - 1]
            if 0 <= c - 2 < len(units):
                u, part = units[c - 2]
                sum_ref[:, part] += jnp.dot(
                    vec[u], tile.pop(c - 2), preferred_element_type=jnp.float32
                )


def split_product(rows, sum_ref, *outs):
    for k, ref in enumerate(outs):
        ref[:, :rows] = sum_ref[:, pl.ds(k * rows, rows)]
        ref[:, rows:] = sum_ref[:, pl.ds(len(outs) * rows, LANES)]


def second_product(rows, core, *refs):
    kerns = refs[:TURNS]
    blocks_ref = refs[TURNS]
    vec_ref, total_ref = refs[-2:]
    index = lax.axis_index("pts")
    place = place_in_group(index)
    odd = lax.rem(index, 2)
    for n in range(TURNS):
        for side in range(SIDE):
            even_slot = side + SIDE * EVEN_LINES[n]
            odd_slot = SIDE * side + ODD_LINES[n]
            slot = jnp.bitwise_xor(place, jnp.where(odd == core, even_slot, odd_slot))
            vec_ref[n, :, pl.ds(side * rows, rows)] = blocks_ref[slot, :, pl.ds(0, rows)]
    half = pl.ds(core * SIDE * rows, SIDE * rows)
    for c in range(total_ref.shape[1] // CHUNK):
        part = pl.ds(c * CHUNK, CHUNK)
        value = jnp.zeros((total_ref.shape[0], CHUNK), jnp.float32)
        if core == 1:
            value = refs[TURNS + 1][:, part]
        for n, ref in enumerate(kerns):
            value += jnp.dot(vec_ref[n], ref[half, part], preferred_element_type=jnp.float32)
        total_ref[:, part] = value
    if core == 0:
        refs[-3][...] = total_ref[...]
    else:
        other_ref = refs[TURNS + 2]
        lanes = jnp.zeros((total_ref.shape[0], LANES), jnp.float32)
        for k in range(CHIPS):
            lanes += blocks_ref[k, :, rows:].astype(jnp.float32)
            lanes += other_ref[k, :, rows:].astype(jnp.float32)
        for k, ref in enumerate(refs[TURNS + 3 : TURNS + 3 + NEAR]):
            ref[:, :rows] = total_ref[:, pl.ds(k * rows, rows)]
            ref[:, rows:] = lanes


def run_first(turn, far, near, half, last, rows, cols):
    feats, width = near.shape
    inputs = list(far) + [near, half] + ([last] if turn > 0 else [])
    count = 2 * SIDE * rows
    return pl.pallas_call(
        functools.partial(first_product, scale_of(feats), rows, turn),
        in_specs=[INSIDE] * len(inputs),
        out_specs=[INSIDE, INSIDE],
        out_shape=[
            pltpu.VMEM((count, width), jnp.bfloat16),
            jax.ShapeDtypeStruct((cols, width + LANES), jnp.float32),
        ],
        scratch_shapes=[pltpu.VMEM((2 * SIDE,) + far[0].shape[1:], jnp.bfloat16)],
        compiler_params=pltpu.CompilerParams(vmem_limit_bytes=LIMIT),
        cost_estimate=pl.CostEstimate(
            flops=2 * count * width * 2 * feats,
            bytes_accessed=2 * count * width,
            transcendentals=count * width,
        ),
    )(*inputs)


def run_second(core, kerns, blocks, rows, *others):
    width = kerns[0].shape[1]
    cols = blocks.shape[1]
    kerns = [pltpu.with_memory_space_constraint(kern, pltpu.VMEM) for kern in kerns]
    inputs = kerns + [blocks] + list(others)
    if core == 0:
        outs = [jax.ShapeDtypeStruct((cols, width), jnp.float32)]
    else:
        outs = [jax.ShapeDtypeStruct((cols, rows + LANES), jnp.float32)] * NEAR
    return pl.pallas_call(
        functools.partial(second_product, rows, core),
        in_specs=[INSIDE] * len(inputs),
        out_specs=[INSIDE] * len(outs),
        out_shape=outs,
        scratch_shapes=[
            pltpu.VMEM((TURNS, cols, SIDE * rows), jnp.bfloat16),
            pltpu.VMEM((cols, width), jnp.float32),
        ],
        compiler_params=pltpu.CompilerParams(vmem_limit_bytes=LIMIT),
        cost_estimate=pl.CostEstimate(
            flops=2 * TURNS * SIDE * rows * width * 8 * cols,
            bytes_accessed=2 * TURNS * SIDE * rows * width,
            transcendentals=0,
        ),
    )(*inputs)


def spread_lanes(items, shape):
    lane = lax.broadcasted_iota(jnp.int32, shape, 1)
    lanes = jnp.zeros(shape, jnp.float32)
    for k, rest in enumerate(items):
        for j in range(SPLITS):
            piece = rest.astype(jnp.bfloat16).astype(jnp.float32)
            lanes = jnp.where(lane == SPLITS * k + j, piece, lanes)
            rest = rest - piece
    return lanes.astype(jnp.bfloat16)


def collect_lanes(lanes, count):
    lane = lax.broadcasted_iota(jnp.int32, lanes.shape, 1)
    items = []
    for k in range(count):
        inside = (lane >= SPLITS * k) & (lane < SPLITS * (k + 1))
        items.append(jnp.sum(jnp.where(inside, lanes, 0.0), axis=1, keepdims=True))
    return items


def row_sum(value):
    return jnp.sum(value, axis=1, keepdims=True)


def pack(points_ref, rhs_ref, noise_ref, out_ref, keep_ref, noisy_ref, sems):
    rows, feats = points_ref.shape
    cols = rhs_ref.shape[0]
    first = pltpu.make_async_copy(points_ref, out_ref.at[pl.ds(0, rows), :], sems.at[0])
    second = pltpu.make_async_copy(rhs_ref, keep_ref, sems.at[1])
    first.start()
    second.start()
    second.wait()
    for k in range(rows // feats):
        part = keep_ref[:, pl.ds(k * feats, feats)]
        out_ref[pl.ds(rows + k * cols, cols), :] = part.astype(jnp.bfloat16)
    rhs = keep_ref[...]
    noisy = noise_ref[...] * rhs
    noisy_ref[...] = noisy
    lanes = spread_lanes((row_sum(rhs * rhs), row_sum(rhs * noisy)), (cols, LANES))
    out_ref[pl.ds(rows + cols * (rows // feats), cols), :] = lanes
    first.wait()


def run_pack(points, rhs, noise):
    rows, feats = points.shape
    cols = rhs.shape[0]
    tall = rows + cols * (rows // feats) + cols
    place = pl.BlockSpec(memory_space=pl.ANY)
    return pl.pallas_call(
        pack,
        in_specs=[place, place, INSIDE],
        out_specs=[INSIDE] * 3,
        out_shape=[
            jax.ShapeDtypeStruct((tall, feats), points.dtype),
            jax.ShapeDtypeStruct(rhs.shape, rhs.dtype),
            jax.ShapeDtypeStruct(rhs.shape, rhs.dtype),
        ],
        scratch_shapes=[pltpu.SemaphoreType.DMA((2,))],
        compiler_params=pltpu.CompilerParams(vmem_limit_bytes=SMALL),
    )(points, rhs, noise)


def run_bundle(side, near):
    place = pl.BlockSpec(memory_space=pl.ANY)
    return pl.pallas_call(
        bundle,
        in_specs=[INSIDE] * len(side) + [place] * len(near),
        out_specs=INSIDE,
        out_shape=jax.ShapeDtypeStruct((len(side),) + side[0].shape, side[0].dtype),
        compiler_params=pltpu.CompilerParams(vmem_limit_bytes=SMALL),
    )(*side, *near)


def bundle(*refs):
    for k, ref in enumerate(refs[:SIDE]):
        refs[-1][k] = ref[...]


def prepare(scale, *refs):
    near_ref, half_ref = refs[NEAR:]
    rows = refs[0].shape[0]
    for k, ref in enumerate(refs[:NEAR]):
        block = ref[...]
        part = pl.ds(k * rows, rows)
        near_ref[:, part] = block.astype(jnp.float32).T.astype(jnp.bfloat16)
        half_ref[:, part] = half_norms(scale, block)


def middle(*refs):
    noisy_ref, rhs_ref, image_ref, rest_ref, known_ref, copies_ref = refs[NEAR:]
    rhs = rhs_ref[...]
    rows = rhs.shape[1]
    total = refs[0][...]
    for ref in refs[1:NEAR]:
        total += ref[...]
    norm, noisy_norm = collect_lanes(total[:, rows:], 2)
    shift = 1.0 + noisy_norm / norm
    image = total[:, :rows] + noisy_ref[...]
    rest = image - shift * rhs
    image_ref[...] = image
    rest_ref[...] = rest
    lane = lax.broadcasted_iota(jnp.int32, known_ref.shape, 1)
    known_ref[...] = jnp.where(lane == 0, norm, shift)
    lanes = spread_lanes((row_sum(rhs * rest), row_sum(rest * rest)), known_ref.shape)
    packed = jnp.concatenate([rest.astype(jnp.bfloat16), lanes], axis=1)
    for k in range(copies_ref.shape[0]):
        copies_ref[k] = packed


def closing(*refs):
    noise_ref, rhs_ref, image_ref, rest_ref, known_ref = refs[NEAR : NEAR + 5]
    field_ref, residual_ref, direction_ref, image_dir_ref, norm_ref, curve_ref = refs[NEAR + 5 :]
    rhs = rhs_ref[...]
    image = image_ref[...]
    rows = rhs.shape[1]
    total = refs[0][...]
    for ref in refs[1:NEAR]:
        total += ref[...]
    rest_image = total[:, :rows] + noise_ref[...] * rest_ref[...]
    cross, square = collect_lanes(total[:, rows:], 2)
    norm, shift = known_ref[:, 0:1], known_ref[:, 1:2]
    extra = cross / norm
    alpha = 1.0 / (shift + extra)
    norm_next = alpha * alpha * jnp.maximum(square - extra * cross, 0.0)
    beta = norm_next / norm
    residual = rhs - alpha * image
    direction = residual + beta * rhs
    image_dir = (alpha * extra + beta) * image - alpha * rest_image
    curve_two = row_sum(direction * image_dir)
    field_ref[...] = alpha * rhs
    residual_ref[...] = residual
    direction_ref[...] = direction
    image_dir_ref[...] = image_dir
    norm_ref[...] = jnp.broadcast_to(norm_next, norm_ref.shape)
    curve_ref[...] = jnp.broadcast_to(curve_two, norm_ref.shape).T


def finish(curve_ref, norm_ref, field_ref, residual_ref, direction_ref, image_dir_ref, *outs):
    cols = curve_ref.shape[1]
    curve = jnp.sum(curve_ref[...], axis=0, keepdims=True)
    curve = jnp.concatenate([curve, jnp.ones((1, LANES - cols), jnp.float32)], axis=1)
    curve = jnp.broadcast_to(curve, (LANES, LANES)).T[:cols, 0:1]
    alpha = norm_ref[:, 0:1] / curve
    outs[0][...] = field_ref[...] + alpha * direction_ref[...]
    outs[1][...] = residual_ref[...] - alpha * image_dir_ref[...]


def per_device(points, noise_var, right_side):
    rows, feats = points.shape
    noise = noise_var[None, :]
    packed, rhs, noisy = run_pack(points, right_side.T, noise)
    cols = rhs.shape[0]
    field_shape = ((cols, rows), jnp.float32)
    lanes_shape = ((cols, LANES), jnp.float32)
    side = [packed]
    for k in range(1, SIDE):
        side.append(partner(packed, reach(SIDE_MASKS, k), reach(LINE_MASKS, k)))
    near = exchange([points] * NEAR, NEAR_MASKS)
    own = run_bundle(side, near)
    first, second = [partner(own, *line_masks(turn)) for turn in (1, 2)]
    near, half = small_call(
        functools.partial(prepare, scale_of(feats)),
        [((feats, NEAR * rows), points.dtype), ((8, NEAR * rows), jnp.float32)],
        *near,
    )

    kerns = []
    kern, total = run_first(0, (own, partner(own, CORE_MASK)), near, half, None, rows, cols)
    kerns.append(kern)
    first, second, total = lax.optimization_barrier((first, second, total))
    third = partner(second, *line_masks(1))
    across = [partner(item, CORE_MASK) for item in (first, second)]
    kern, total = run_first(1, (first, across[0]), near, half, total, rows, cols)
    kerns.append(kern)
    kern, total = run_first(2, (second, across[1]), near, half, total, rows, cols)
    kerns.append(kern)
    third, total = lax.optimization_barrier((third, total))
    kern, total = run_first(3, (third, partner(third, CORE_MASK)), near, half, total, rows, cols)
    kerns.append(kern)
    wide_shape = ((cols, rows + LANES), jnp.float32)
    parts = small_call(functools.partial(split_product, rows), [wide_shape] * NEAR, total)
    image, rest, known, copies = small_call(
        middle,
        [field_shape, field_shape, lanes_shape, ((CHIPS, cols, rows + LANES), jnp.bfloat16)],
        *exchange(parts, NEAR_MASKS),
        noisy,
        rhs,
    )
    copies = share(copies)
    other = partner(copies, CORE_MASK)
    half_total = run_second(0, kerns, copies, rows)[0]
    parts = run_second(1, kerns, other, rows, half_total, copies)
    field, residual, direction, image_dir, norm_next, curve = small_call(
        closing,
        [field_shape] * 4 + [lanes_shape, ((DEVICES, cols), jnp.float32)],
        *exchange(parts, NEAR_MASKS),
        noise,
        rhs,
        image,
        rest,
        known,
    )
    curve = lax.all_to_all(curve[:, None, :], "pts", 0, 0).reshape(DEVICES, cols)
    field, residual = small_call(
        finish, [field_shape] * 2, curve, norm_next, field, residual, direction, image_dir
    )
    return (field.T, residual.T)


def solution(mesh):
    return jax.shard_map(
        per_device,
        mesh=mesh,
        in_specs=(P("pts", None), P("pts"), P("pts", None)),
        out_specs=(P("pts", None), P("pts", None)),
        check_vma=False,
    )
```

time: 545 us -> 103 us (0.19)
  waiting for transfers between devices: 198 us -> 15.6 us
  blocking collectives: 191 us -> 29.6 us
  matrix products: 78.3 us -> 0 us
  other arithmetic: 41.1 us -> 0 us
  Pallas kernels: 0 us -> 27.9 us
  starting transfers between devices: 0.12 us -> 26.8 us
  local copies, waits for them, and re-layouts: 21.2 us -> 2.37 us
  between operations: 13.8 us -> 0.73 us
    all_gather x3 -> x0, waiting for transfers between devices: 197 us -> none  [the longest x2 134 us: per_device(): lax.all_gather(direction.astype(jnp.bfloat16), 'pts', axis=0, tiled=True)]
    psum x3 -> x0, blocking collectives: 191 us -> none  [the longest x2 129 us: column_sums(): return lax.psum(values, 'pts')]
    dot_general x16 -> x0, matrix products: 78.3 us -> none  [step(): jnp.dot(tile, item[1], preferred_element_type=jnp.float32)]
    reduce_sum x20 -> x0, other arithmetic: 38.2 us -> none  [the longest x16 36.7 us: kernel_tile(): right_sq = jnp.sum(jnp.square(right.astype(jnp.float32)), axis=1)]
    all_to_all x0 -> x2, blocking collectives: none -> 29.6 us  [the longest x1 15 us: share(): return lax.all_to_all(copies, 'pts', 0, 0, axis_index_groups=chip_groups())]
    pallas_call x0 -> x13, Pallas kernels: none -> 27.9 us  [the longest x4 19.1 us: run_first(): pl.pallas_call(functools.partial(first_product, scale_of(feats), rows, tu...]
    ppermute x0 -> x20, starting transfers between devices: none -> 26.8 us  [partner(): return lax.ppermute(value, 'pts', pairs)]
    ppermute x0 -> x20, waiting for transfers between devices: none -> 15.6 us  [partner(): return lax.ppermute(value, 'pts', pairs)]
  transfers between devices with their start and end apart: 3 -> 20, of which waited for: 3 -> 13; matrix products, arithmetic and copies ran while one was open for 2% -> 1% of each run, Pallas kernels for 0% -> 18%
where the time goes in v1:
time: 103 us
  blocking collectives  29.6 us (29%)
  Pallas kernels  27.9 us (27%)
  starting transfers between devices  26.8 us (26%)
  waiting for transfers between devices  15.6 us (15%)
  local copies, waits for them, and re-layouts  2.37 us (2%)
    ppermute x20, starting transfers between devices, partner(): return lax.ppermute(value, 'pts', pairs)  26.8 us
    pallas_call x4, Pallas kernels, run_first(): pl.pallas_call(functools.partial(first_product, scale_of(feats), rows, tu...  19.1 us
    ppermute x20, waiting for transfers between devices, partner(): return lax.ppermute(value, 'pts', pairs)  15.6 us
    all_to_all x1, blocking collectives, share(): return lax.all_to_all(copies, 'pts', 0, 0, axis_index_groups=chip_groups())  15 us
    all_to_all x1, blocking collectives, per_device(): lax.all_to_all(curve[:, None, :], 'pts', 0, 0).reshape(DEVICES, cols)  14.7 us
    pallas_call x2, Pallas kernels, run_second(): pl.pallas_call(functools.partial(second_product, rows, core), in_specs=[I...  6.63 us
  transfers between devices with their start and end apart: 20, of which 13 were waited for; matrix products, arithmetic and copies ran while one was open for 1% of the time, Pallas kernels for 18%

profile of v1, /device:TPU:1, one launch (start us, length us, event | category | flops | bytes accessed | tf_op | source)
XLA Modules:
  0.0 103.0 jit_solution(16958991724090384116)
XLA Ops:
  0.6 3.6 %collective-permute-start.5 = (bf16[384,128]{1,0:T(8,128)(2,1)}, bf16[384,128]{1,0:T(8,128)(2,1)S(1)}, u32[]{:S(2)}, u32[]{:S(2)}) collective-permute-start(bf16[384,128]{1,0:T(8,128)(2,1)} %refs_0_.1), channel_id=1, source_target_pairs={{0,10},{1,11},{2,8},{3,9},{4,14},{5,15},{6,12},{7,13},{8,2},{9,3},... | collective-permute-start | bytes 294920 | tf_op jit(solution)/shard_map/ppermute | solution.py:65
  4.2 0.7 broadcast_in_dim.6.noise_ref.refs_4_
  4.9 0.0 copy-start
  4.9 0.9 copy-done
  5.8 0.0 copy-start.1
  5.8 0.8 copy-done.1
  6.6 0.3 shard_map.50
  6.8 2.6 %collective-permute-start.2 = (bf16[512,128]{1,0:T(8,128)(2,1)S(1)}, bf16[512,128]{1,0:T(8,128)(2,1)S(1)}, u32[]{:S(2)}, u32[]{:S(2)}) collective-permute-start(bf16[512,128]{1,0:T(8,128)(2,1)S(1)} %get-tuple-element.40.refs_0_), channel_id=1, source_target_pairs={{0,30},{1,97},{2,28},{3,99},{4,26},{5,101},{6,24},{7,103},{8,22},{... | collective-permute-start | bytes 393224 | tf_op jit(solution)/shard_map/ppermute | solution.py:65
  9.4 0.5 collective-permute-start.1
  9.9 0.3 collective-permute-start
  10.2 0.2 collective-permute-start.4
  10.3 0.0 collective-permute-done.5.refs_7_.refs_3_
  10.4 0.1 collective-permute-start.3
  10.5 3.2 %collective-permute-done.4.refs_6_.refs_2_ = bf16[384,128]{1,0:T(8,128)(2,1)S(1)} collective-permute-done((bf16[384,128]{1,0:T(8,128)(2,1)S(1)}, bf16[384,128]{1,0:T(8,128)(2,1)S(1)}, u32[]{:S(2)}, u32[]{:S(2)}) %collective-permute-start.4) | collective-permute-done | bytes 98336 | tf_op jit(solution)/shard_map/ppermute | solution.py:65
  13.6 0.5 collective-permute-done.3.refs_5_.refs_1_
  14.1 0.0 collective-permute-done.2.refs_3_
  14.1 0.9 collective-permute-done.1.refs_2_
  15.0 0.0 collective-permute-done.refs_1_
  15.1 4.3 %collective-permute-start.6 = (bf16[4,512,128]{2,1,0:T(8,128)(2,1)S(1)}, bf16[4,512,128]{2,1,0:T(8,128)(2,1)S(1)}, u32[]{:S(2)}, u32[]{:S(2)}) collective-permute-start(bf16[4,512,128]{2,1,0:T(8,128)(2,1)S(1)} %shard_map.51.refs_0_), channel_id=1, source_target_pairs={{0,1},{1,0},{2,3},{3,2},{4,5},{5,4},{6,7},{7,6},{8,9},{9,8},{10,11... | collective-permute-start | bytes 1572872 | tf_op jit(solution)/shard_map/ppermute | solution.py:65
  19.4 1.9 %collective-permute-start.8 = (bf16[4,512,128]{2,1,0:T(8,128)(2,1)S(1)}, bf16[4,512,128]{2,1,0:T(8,128)(2,1)S(1)}, u32[]{:S(2)}, u32[]{:S(2)}) collective-permute-start(bf16[4,512,128]{2,1,0:T(8,128)(2,1)S(1)} %shard_map.51.refs_0_), channel_id=1, source_target_pairs={{0,96},{1,25},{2,98},{3,27},{4,100},{5,29},{6,102},{7,31},{8,104},... | collective-permute-start | bytes 1572872 | tf_op jit(solution)/shard_map/ppermute | solution.py:65
  21.3 1.5 %collective-permute-start.7 = (bf16[4,512,128]{2,1,0:T(8,128)(2,1)S(1)}, bf16[4,512,128]{2,1,0:T(8,128)(2,1)S(1)}, u32[]{:S(2)}, u32[]{:S(2)}) collective-permute-start(bf16[4,512,128]{2,1,0:T(8,128)(2,1)S(1)} %shard_map.51.refs_0_), channel_id=1, source_target_pairs={{0,32},{1,7},{2,34},{3,5},{4,36},{5,3},{6,38},{7,1},{8,40},{9,15},... | collective-permute-start | bytes 1572872 | tf_op jit(solution)/shard_map/ppermute | solution.py:65
  22.8 0.4 shard_map.52
  23.2 0.0 collective-permute-done.6.refs_1_
  23.2 4.8 %shard_map.53 = (bf16[3072,1536]{1,0:T(8,128)(2,1)S(1)}, f32[32,1664]{1,0:T(8,128)S(1)}) custom-call(bf16[4,512,128]{2,1,0:T(8,128)(2,1)S(1)} %shard_map.51.refs_0_, bf16[4,512,128]{2,1,0:T(8,128)(2,1)S(1)} %collective-permute-done.6.refs_1_, bf16[128,1536]{1,0:T(8,128)(2,1)S(1)} %get-tuple-element.41.refs_2_, f32[8,1536]{1,0:T(8,128)S(1)} %get-tuple-element.42.refs_3_), custom_call_target="tpu_custom_call" | custom-call | flops 2415919104 | bytes 9437184 | tf_op jit(solution)/shard_map/pallas_call | solution.py:195
  27.9 1.0 collective-permute-done.8.refs_0_
  28.9 1.6 %collective-permute-done.7.refs_0_ = bf16[4,512,128]{2,1,0:T(8,128)(2,1)S(1)} collective-permute-done((bf16[4,512,128]{2,1,0:T(8,128)(2,1)S(1)}, bf16[4,512,128]{2,1,0:T(8,128)(2,1)S(1)}, u32[]{:S(2)}, u32[]{:S(2)}) %collective-permute-start.7) | collective-permute-done | bytes 524320 | tf_op jit(solution)/shard_map/ppermute | solution.py:65
  30.5 0.9 collective-permute-start.9
  31.4 0.0 collective-permute-start.10
  31.4 1.4 %collective-permute-start.11 = (bf16[4,512,128]{2,1,0:T(8,128)(2,1)S(1)}, bf16[4,512,128]{2,1,0:T(8,128)(2,1)S(1)}, u32[]{:S(2)}, u32[]{:S(2)}) collective-permute-start(bf16[4,512,128]{2,1,0:T(8,128)(2,1)S(1)} %collective-permute-done.8.refs_0_), channel_id=1, source_target_pairs={{0,32},{1,7},{2,34},{3,5},{4,36},{5,3},{6,38},{7,1},{8,40},{9,15},... | collective-permute-start | bytes 1572872 | tf_op jit(solution)/shard_map/ppermute | solution.py:65
  32.8 0.1 collective-permute-done.9.refs_1_
  32.9 4.8 %shard_map.54 = (bf16[3072,1536]{1,0:T(8,128)(2,1)S(1)}, f32[32,1664]{1,0:T(8,128)S(1)}) custom-call(bf16[4,512,128]{2,1,0:T(8,128)(2,1)S(1)} %collective-permute-done.7.refs_0_, bf16[4,512,128]{2,1,0:T(8,128)(2,1)S(1)} %collective-permute-done.9.refs_1_, bf16[128,1536]{1,0:T(8,128)(2,1)S(1)} %get-tuple-element.41.refs_2_, ...), custom_call_target="tpu_custom_call" | custom-call | flops 2415919104 | bytes 9437184 | tf_op jit(solution)/shard_map/pallas_call | solution.py:195
  37.7 0.0 collective-permute-done.10.refs_1_
  37.7 4.8 %shard_map.55 = (bf16[3072,1536]{1,0:T(8,128)(2,1)S(1)}, f32[32,1664]{1,0:T(8,128)S(1)}) custom-call(bf16[4,512,128]{2,1,0:T(8,128)(2,1)S(1)} %collective-permute-done.8.refs_0_, bf16[4,512,128]{2,1,0:T(8,128)(2,1)S(1)} %collective-permute-done.10.refs_1_, bf16[128,1536]{1,0:T(8,128)(2,1)S(1)} %get-tuple-element.41.refs_2_, ...), custom_call_target="tpu_custom_call" | custom-call | flops 2415919104 | bytes 9437184 | tf_op jit(solution)/shard_map/pallas_call | solution.py:195
  42.5 0.0 collective-permute-done.11.refs_0_
  42.5 0.6 collective-permute-start.12
  43.2 1.5 %collective-permute-done.12.refs_1_ = bf16[4,512,128]{2,1,0:T(8,128)(2,1)S(1)} collective-permute-done((bf16[4,512,128]{2,1,0:T(8,128)(2,1)S(1)}, bf16[4,512,128]{2,1,0:T(8,128)(2,1)S(1)}, u32[]{:S(2)}, u32[]{:S(2)}) %collective-permute-start.12) | collective-permute-done | bytes 524320 | tf_op jit(solution)/shard_map/ppermute | solution.py:65
  44.7 4.8 %shard_map.56 = (bf16[3072,1536]{1,0:T(8,128)(2,1)S(1)}, f32[32,1664]{1,0:T(8,128)S(1)}) custom-call(bf16[4,512,128]{2,1,0:T(8,128)(2,1)S(1)} %collective-permute-done.11.refs_0_, bf16[4,512,128]{2,1,0:T(8,128)(2,1)S(1)} %collective-permute-done.12.refs_1_, bf16[128,1536]{1,0:T(8,128)(2,1)S(1)} %get-tuple-element.41.refs_2_, ...), custom_call_target="tpu_custom_call" | custom-call | flops 2415919104 | bytes 9437184 | tf_op jit(solution)/shard_map/pallas_call | solution.py:195
  49.5 0.1 collective-permute-start.13
  49.6 1.7 %collective-permute-start.14 = (f32[32,512]{1,0:T(8,128)S(1)}, f32[32,512]{1,0:T(8,128)S(1)}, u32[]{:S(2)}, u32[]{:S(2)}) collective-permute-start(f32[32,512]{1,0:T(8,128)S(1)} %get-tuple-element.58), channel_id=1, source_target_pairs={{0,8},{1,9},{2,10},{3,11},{4,12},{5,13},{6,14},{7,15},{8,0},{9,1},... | collective-permute-start | bytes 196616 | tf_op jit(solution)/shard_map/ppermute | solution.py:65
  51.3 1.1 %collective-permute-start.15 = (f32[32,512]{1,0:T(8,128)S(1)}, f32[32,512]{1,0:T(8,128)S(1)}, u32[]{:S(2)}, u32[]{:S(2)}) collective-permute-start(f32[32,512]{1,0:T(8,128)S(1)} %get-tuple-element.59), channel_id=1, source_target_pairs={{0,10},{1,11},{2,8},{3,9},{4,14},{5,15},{6,12},{7,13},{8,2},{9,3},... | collective-permute-start | bytes 196616 | tf_op jit(solution)/shard_map/ppermute | solution.py:65
  52.4 0.3 collective-permute-done.13.refs_1_
  52.7 0.7 collective-permute-done.14.refs_2_
  53.3 2.8 %collective-permute-done.15.refs_3_ = f32[32,512]{1,0:T(8,128)S(1)} collective-permute-done((f32[32,512]{1,0:T(8,128)S(1)}, f32[32,512]{1,0:T(8,128)S(1)}, u32[]{:S(2)}, u32[]{:S(2)}) %collective-permute-start.15) | collective-permute-done | bytes 65568 | tf_op jit(solution)/shard_map/ppermute | solution.py:65
  56.2 0.2 shard_map.58
  56.4 15.0 %all_to_all.10.refs_4_.refs_6_ = bf16[16,32,512]{2,1,0:T(8,128)(2,1)S(1)} all-to-all(bf16[16,32,512]{2,1,0:T(8,128)(2,1)S(1)} %get-tuple-element.62), channel_id=1, replica_groups={{0,6,24,30,32,38,56,62,64,70,88,94,96,102,120,126},{1,7,25,31,33,39,57,..., dimensions={0} | all-to-all | bytes 1048576 | tf_op jit(solution)/shard_map/all_to_all | solution.py:77
  71.4 3.4 %collective-permute-start.16 = (bf16[16,32,512]{2,1,0:T(8,128)(2,1)S(1)}, bf16[16,32,512]{2,1,0:T(8,128)(2,1)S(1)}, u32[]{:S(2)}, u32[]{:S(2)}) collective-permute-start(bf16[16,32,512]{2,1,0:T(8,128)(2,1)S(1)} %all_to_all.10.refs_4_.refs_6_), channel_id=1, source_target_pairs={{0,1},{1,0},{2,3},{3,2},{4,5},{5,4},{6,7},{7,6},{8,9},{9,8},{10,11... | collective-permute-start | bytes 1572872 | tf_op jit(solution)/shard_map/ppermute | solution.py:65
  74.8 3.3 %shard_map.59.refs_5_ = f32[32,1536]{1,0:T(8,128)S(1)} custom-call(bf16[3072,1536]{1,0:T(8,128)(2,1)S(1)} %get-tuple-element.43.refs_0_, bf16[3072,1536]{1,0:T(8,128)(2,1)S(1)} %get-tuple-element.47.refs_1_, bf16[3072,1536]{1,0:T(8,128)(2,1)S(1)} %get-tuple-element.50.refs_2_, bf16[3072,1536]{1,0:T(8,128)(2,1)S(1)} %get-tuple-element.54.refs_3_, ...), custom_call_target="tpu_custom_call" | custom-call | flops 4831838208 | bytes 18874368 | tf_op jit(solution)/shard_map/pallas_call | solution.py:222
  78.1 0.0 collective-permute-done.16.refs_4_
  78.1 3.3 %shard_map.60 = (f32[32,512]{1,0:T(8,128)S(1)}, f32[32,512]{1,0:T(8,128)S(1)}, f32[32,512]{1,0:T(8,128)S(1)}, f32[32,512]{1,0:T(8,128)S(1)}) custom-call(bf16[3072,1536]{1,0:T(8,128)(2,1)S(1)} %get-tuple-element.43.refs_0_, bf16[3072,1536]{1,0:T(8,128)(2,1)S(1)} %get-tuple-element.47.refs_1_, bf16[3072,1536]{1,0:T(8,128)(2,1)S(1)} %get-tuple-element.50.refs_2_, ...), custom_call_target="tpu_custom_call" | custom-call | flops 4831838208 | bytes 18874368 | tf_op jit(solution)/shard_map/pallas_call | solution.py:222
  81.4 0.0 collective-permute-start.17
  81.4 0.1 collective-permute-start.18
  81.5 2.6 %collective-permute-start.19 = (f32[32,512]{1,0:T(8,128)S(1)}, f32[32,512]{1,0:T(8,128)S(1)}, u32[]{:S(2)}, u32[]{:S(2)}) collective-permute-start(f32[32,512]{1,0:T(8,128)S(1)} %get-tuple-element.66), channel_id=1, source_target_pairs={{0,10},{1,11},{2,8},{3,9},{4,14},{5,15},{6,12},{7,13},{8,2},{9,3},... | collective-permute-start | bytes 196616 | tf_op jit(solution)/shard_map/ppermute | solution.py:65
  84.1 1.1 %collective-permute-done.17.refs_1_ = f32[32,512]{1,0:T(8,128)S(1)} collective-permute-done((f32[32,512]{1,0:T(8,128)S(1)}, f32[32,512]{1,0:T(8,128)S(1)}, u32[]{:S(2)}, u32[]{:S(2)}) %collective-permute-start.17) | collective-permute-done | bytes 65568 | tf_op jit(solution)/shard_map/ppermute | solution.py:65
  85.1 0.1 collective-permute-done.18.refs_2_
  85.2 1.9 %collective-permute-done.19.refs_3_ = f32[32,512]{1,0:T(8,128)S(1)} collective-permute-done((f32[32,512]{1,0:T(8,128)S(1)}, f32[32,512]{1,0:T(8,128)S(1)}, u32[]{:S(2)}, u32[]{:S(2)}) %collective-permute-start.19) | collective-permute-done | bytes 65568 | tf_op jit(solution)/shard_map/ppermute | solution.py:65
  87.1 0.4 shard_map.61
  87.5 14.7 %all_to_all.11 = f32[128,1,32]{2,1,0:T(1,128)S(1)} all-to-all(f32[128,1,32]{2,1,0:T(1,128)S(1)} %bitcast.8), channel_id=1, replica_groups=mesh['pts'=128] {'pts'}, dimensions={0} | all-to-all | bytes 32768 | tf_op jit(solution)/shard_map/all_to_all | solution.py:442
  102.2 0.8 shard_map.62
  (2 shorter events, 0.1 us)
Async XLA Ops:
  0.6 9.7 %collective-permute-start.5 = (bf16[384,128]{1,0:T(8,128)(2,1)}, bf16[384,128]{1,0:T(8,128)(2,1)S(1)}, u32[]{:S(2)}, u32[]{:S(2)}) collective-permute-start(bf16[384,128]{1,0:T(8,128)(2,1)} %refs_0_.1), channel_id=1, source_target_pairs={{0,10},{1,11},{2,8},{3,9},{4,14},{5,15},{6,12},{7,13},{8,2},{9,3},... | collective-permute-start | bytes 294920 | tf_op jit(solution)/shard_map/ppermute | solution.py:65
  4.9 0.9 copy-start
  5.8 0.8 copy-start.1
  6.8 7.3 %collective-permute-start.2 = (bf16[512,128]{1,0:T(8,128)(2,1)S(1)}, bf16[512,128]{1,0:T(8,128)(2,1)S(1)}, u32[]{:S(2)}, u32[]{:S(2)}) collective-permute-start(bf16[512,128]{1,0:T(8,128)(2,1)S(1)} %get-tuple-element.40.refs_0_), channel_id=1, source_target_pairs={{0,30},{1,97},{2,28},{3,99},{4,26},{5,101},{6,24},{7,103},{8,22},{... | collective-permute-start | bytes 393224 | tf_op jit(solution)/shard_map/ppermute | solution.py:65
  9.4 5.6 %collective-permute-start.1 = (bf16[512,128]{1,0:T(8,128)(2,1)S(1)}, bf16[512,128]{1,0:T(8,128)(2,1)S(1)}, u32[]{:S(2)}, u32[]{:S(2)}) collective-permute-start(bf16[512,128]{1,0:T(8,128)(2,1)S(1)} %get-tuple-element.40.refs_0_), channel_id=1, source_target_pairs={{0,24},{1,65},{2,26},{3,67},{4,28},{5,69},{6,30},{7,71},{8,16},{9,... | collective-permute-start | bytes 393224 | tf_op jit(solution)/shard_map/ppermute | solution.py:65
  9.9 5.1 %collective-permute-start = (bf16[512,128]{1,0:T(8,128)(2,1)S(1)}, bf16[512,128]{1,0:T(8,128)(2,1)S(1)}, u32[]{:S(2)}, u32[]{:S(2)}) collective-permute-start(bf16[512,128]{1,0:T(8,128)(2,1)S(1)} %get-tuple-element.40.refs_0_), channel_id=1, source_target_pairs={{0,6},{1,33},{2,4},{3,35},{4,2},{5,37},{6,0},{7,39},{8,14},{9,41},... | collective-permute-start | bytes 393224 | tf_op jit(solution)/shard_map/ppermute | solution.py:65
  10.2 3.5 %collective-permute-start.4 = (bf16[384,128]{1,0:T(8,128)(2,1)S(1)}, bf16[384,128]{1,0:T(8,128)(2,1)S(1)}, u32[]{:S(2)}, u32[]{:S(2)}) collective-permute-start(bf16[384,128]{1,0:T(8,128)(2,1)S(1)} %copy-done), channel_id=1, source_target_pairs={{0,8},{1,9},{2,10},{3,11},{4,12},{5,13},{6,14},{7,15},{8,0},{9,1},... | collective-permute-start | bytes 294920 | tf_op jit(solution)/shard_map/ppermute | solution.py:65
  10.4 3.8 %collective-permute-start.3 = (bf16[384,128]{1,0:T(8,128)(2,1)S(1)}, bf16[384,128]{1,0:T(8,128)(2,1)S(1)}, u32[]{:S(2)}, u32[]{:S(2)}) collective-permute-start(bf16[384,128]{1,0:T(8,128)(2,1)S(1)} %copy-done), channel_id=1, source_target_pairs={{0,2},{1,3},{2,0},{3,1},{4,6},{5,7},{6,4},{7,5},{8,10},{9,11},{10,... | collective-permute-start | bytes 294920 | tf_op jit(solution)/shard_map/ppermute | solution.py:65
  15.1 8.1 %collective-permute-start.6 = (bf16[4,512,128]{2,1,0:T(8,128)(2,1)S(1)}, bf16[4,512,128]{2,1,0:T(8,128)(2,1)S(1)}, u32[]{:S(2)}, u32[]{:S(2)}) collective-permute-start(bf16[4,512,128]{2,1,0:T(8,128)(2,1)S(1)} %shard_map.51.refs_0_), channel_id=1, source_target_pairs={{0,1},{1,0},{2,3},{3,2},{4,5},{5,4},{6,7},{7,6},{8,9},{9,8},{10,11... | collective-permute-start | bytes 1572872 | tf_op jit(solution)/shard_map/ppermute | solution.py:65
  19.4 9.5 %collective-permute-start.8 = (bf16[4,512,128]{2,1,0:T(8,128)(2,1)S(1)}, bf16[4,512,128]{2,1,0:T(8,128)(2,1)S(1)}, u32[]{:S(2)}, u32[]{:S(2)}) collective-permute-start(bf16[4,512,128]{2,1,0:T(8,128)(2,1)S(1)} %shard_map.51.refs_0_), channel_id=1, source_target_pairs={{0,96},{1,25},{2,98},{3,27},{4,100},{5,29},{6,102},{7,31},{8,104},... | collective-permute-start | bytes 1572872 | tf_op jit(solution)/shard_map/ppermute | solution.py:65
  21.3 9.2 %collective-permute-start.7 = (bf16[4,512,128]{2,1,0:T(8,128)(2,1)S(1)}, bf16[4,512,128]{2,1,0:T(8,128)(2,1)S(1)}, u32[]{:S(2)}, u32[]{:S(2)}) collective-permute-start(bf16[4,512,128]{2,1,0:T(8,128)(2,1)S(1)} %shard_map.51.refs_0_), channel_id=1, source_target_pairs={{0,32},{1,7},{2,34},{3,5},{4,36},{5,3},{6,38},{7,1},{8,40},{9,15},... | collective-permute-start | bytes 1572872 | tf_op jit(solution)/shard_map/ppermute | solution.py:65
  30.5 2.4 %collective-permute-start.9 = (bf16[4,512,128]{2,1,0:T(8,128)(2,1)S(1)}, bf16[4,512,128]{2,1,0:T(8,128)(2,1)S(1)}, u32[]{:S(2)}, u32[]{:S(2)}) collective-permute-start(bf16[4,512,128]{2,1,0:T(8,128)(2,1)S(1)} %collective-permute-done.7.refs_0_), channel_id=1, source_target_pairs={{0,1},{1,0},{2,3},{3,2},{4,5},{5,4},{6,7},{7,6},{8,9},{9,8},{10,11... | collective-permute-start | bytes 1572872 | tf_op jit(solution)/shard_map/ppermute | solution.py:65
  31.4 6.3 %collective-permute-start.10 = (bf16[4,512,128]{2,1,0:T(8,128)(2,1)S(1)}, bf16[4,512,128]{2,1,0:T(8,128)(2,1)S(1)}, u32[]{:S(2)}, u32[]{:S(2)}) collective-permute-start(bf16[4,512,128]{2,1,0:T(8,128)(2,1)S(1)} %collective-permute-done.8.refs_0_), channel_id=1, source_target_pairs={{0,1},{1,0},{2,3},{3,2},{4,5},{5,4},{6,7},{7,6},{8,9},{9,8},{10,11... | collective-permute-start | bytes 1572872 | tf_op jit(solution)/shard_map/ppermute | solution.py:65
  31.4 11.1 %collective-permute-start.11 = (bf16[4,512,128]{2,1,0:T(8,128)(2,1)S(1)}, bf16[4,512,128]{2,1,0:T(8,128)(2,1)S(1)}, u32[]{:S(2)}, u32[]{:S(2)}) collective-permute-start(bf16[4,512,128]{2,1,0:T(8,128)(2,1)S(1)} %collective-permute-done.8.refs_0_), channel_id=1, source_target_pairs={{0,32},{1,7},{2,34},{3,5},{4,36},{5,3},{6,38},{7,1},{8,40},{9,15},... | collective-permute-start | bytes 1572872 | tf_op jit(solution)/shard_map/ppermute | solution.py:65
  42.5 2.2 %collective-permute-start.12 = (bf16[4,512,128]{2,1,0:T(8,128)(2,1)S(1)}, bf16[4,512,128]{2,1,0:T(8,128)(2,1)S(1)}, u32[]{:S(2)}, u32[]{:S(2)}) collective-permute-start(bf16[4,512,128]{2,1,0:T(8,128)(2,1)S(1)} %collective-permute-done.11.refs_0_), channel_id=1, source_target_pairs={{0,1},{1,0},{2,3},{3,2},{4,5},{5,4},{6,7},{7,6},{8,9},{9,8},{10,11... | collective-permute-start | bytes 1572872 | tf_op jit(solution)/shard_map/ppermute | solution.py:65
  49.5 3.2 %collective-permute-start.13 = (f32[32,512]{1,0:T(8,128)S(1)}, f32[32,512]{1,0:T(8,128)S(1)}, u32[]{:S(2)}, u32[]{:S(2)}) collective-permute-start(f32[32,512]{1,0:T(8,128)S(1)} %get-tuple-element.57), channel_id=1, source_target_pairs={{0,2},{1,3},{2,0},{3,1},{4,6},{5,7},{6,4},{7,5},{8,10},{9,11},{10,... | collective-permute-start | bytes 196616 | tf_op jit(solution)/shard_map/ppermute | solution.py:65
  49.6 3.8 %collective-permute-start.14 = (f32[32,512]{1,0:T(8,128)S(1)}, f32[32,512]{1,0:T(8,128)S(1)}, u32[]{:S(2)}, u32[]{:S(2)}) collective-permute-start(f32[32,512]{1,0:T(8,128)S(1)} %get-tuple-element.58), channel_id=1, source_target_pairs={{0,8},{1,9},{2,10},{3,11},{4,12},{5,13},{6,14},{7,15},{8,0},{9,1},... | collective-permute-start | bytes 196616 | tf_op jit(solution)/shard_map/ppermute | solution.py:65
  51.3 4.9 %collective-permute-start.15 = (f32[32,512]{1,0:T(8,128)S(1)}, f32[32,512]{1,0:T(8,128)S(1)}, u32[]{:S(2)}, u32[]{:S(2)}) collective-permute-start(f32[32,512]{1,0:T(8,128)S(1)} %get-tuple-element.59), channel_id=1, source_target_pairs={{0,10},{1,11},{2,8},{3,9},{4,14},{5,15},{6,12},{7,13},{8,2},{9,3},... | collective-permute-start | bytes 196616 | tf_op jit(solution)/shard_map/ppermute | solution.py:65
  71.4 6.7 %collective-permute-start.16 = (bf16[16,32,512]{2,1,0:T(8,128)(2,1)S(1)}, bf16[16,32,512]{2,1,0:T(8,128)(2,1)S(1)}, u32[]{:S(2)}, u32[]{:S(2)}) collective-permute-start(bf16[16,32,512]{2,1,0:T(8,128)(2,1)S(1)} %all_to_all.10.refs_4_.refs_6_), channel_id=1, source_target_pairs={{0,1},{1,0},{2,3},{3,2},{4,5},{5,4},{6,7},{7,6},{8,9},{9,8},{10,11... | collective-permute-start | bytes 1572872 | tf_op jit(solution)/shard_map/ppermute | solution.py:65
  81.4 3.7 %collective-permute-start.17 = (f32[32,512]{1,0:T(8,128)S(1)}, f32[32,512]{1,0:T(8,128)S(1)}, u32[]{:S(2)}, u32[]{:S(2)}) collective-permute-start(f32[32,512]{1,0:T(8,128)S(1)} %get-tuple-element.64), channel_id=1, source_target_pairs={{0,2},{1,3},{2,0},{3,1},{4,6},{5,7},{6,4},{7,5},{8,10},{9,11},{10,... | collective-permute-start | bytes 196616 | tf_op jit(solution)/shard_map/ppermute | solution.py:65
  81.4 3.8 %collective-permute-start.18 = (f32[32,512]{1,0:T(8,128)S(1)}, f32[32,512]{1,0:T(8,128)S(1)}, u32[]{:S(2)}, u32[]{:S(2)}) collective-permute-start(f32[32,512]{1,0:T(8,128)S(1)} %get-tuple-element.65), channel_id=1, source_target_pairs={{0,8},{1,9},{2,10},{3,11},{4,12},{5,13},{6,14},{7,15},{8,0},{9,1},... | collective-permute-start | bytes 196616 | tf_op jit(solution)/shard_map/ppermute | solution.py:65
  81.5 5.6 %collective-permute-start.19 = (f32[32,512]{1,0:T(8,128)S(1)}, f32[32,512]{1,0:T(8,128)S(1)}, u32[]{:S(2)}, u32[]{:S(2)}) collective-permute-start(f32[32,512]{1,0:T(8,128)S(1)} %get-tuple-element.66), channel_id=1, source_target_pairs={{0,10},{1,11},{2,8},{3,9},{4,14},{5,15},{6,12},{7,13},{8,2},{9,3},... | collective-permute-start | bytes 196616 | tf_op jit(solution)/shard_map/ppermute | solution.py:65

commit v2 on v1

--- a/solution.py
+++ b/solution.py
@@ -98,11 +98,11 @@
     return total * (-0.5 * scale)
 
 
-def first_product(scale, rows, turn, *refs):
-    far_refs = refs[:2]
-    near_ref, half_ref = refs[2:4]
-    kern_ref, sum_ref, far_ref = refs[-3:]
-    sum_ref[...] = jnp.zeros_like(sum_ref) if turn == 0 else refs[4][...]
+def first_product(scale, rows, count, opening, ending, *refs):
+    far_refs = refs[:count]
+    near_ref, half_ref = refs[count : count + 2]
+    kern_ref, sum_ref, far_ref = refs[count + 2 + (0 if opening else 1) :][:1] + refs[-2:]
+    sum_ref[...] = jnp.zeros_like(sum_ref) if opening else refs[count + 2][...]
     cols = sum_ref.shape[0]
     width = near_ref.shape[1]
     chunks = width // UNIT
@@ -146,14 +146,13 @@
                     vec[u], tile.pop(c - 2), preferred_element_type=jnp.float32
                 )
 
-
-def split_product(rows, sum_ref, *outs):
-    for k, ref in enumerate(outs):
-        ref[:, :rows] = sum_ref[:, pl.ds(k * rows, rows)]
-        ref[:, rows:] = sum_ref[:, pl.ds(len(outs) * rows, LANES)]
-
-
-def second_product(rows, core, *refs):
+    if ending:
+        for k, ref in enumerate(refs[-2 - NEAR : -2]):
+            ref[:, :rows] = sum_ref[:, pl.ds(k * rows, rows)]
+            ref[:, rows:] = sum_ref[:, width:]
+
+
+def second_product(rows, core, starts, *refs):
     kerns = refs[:TURNS]
     blocks_ref = refs[TURNS]
     vec_ref, total_ref = refs[-2:]
@@ -166,14 +165,14 @@
             odd_slot = SIDE * side + ODD_LINES[n]
             slot = jnp.bitwise_xor(place, jnp.where(odd == core, even_slot, odd_slot))
             vec_ref[n, :, pl.ds(side * rows, rows)] = blocks_ref[slot, :, pl.ds(0, rows)]
-    half = pl.ds(core * SIDE * rows, SIDE * rows)
     for c in range(total_ref.shape[1] // CHUNK):
         part = pl.ds(c * CHUNK, CHUNK)
         value = jnp.zeros((total_ref.shape[0], CHUNK), jnp.float32)
         if core == 1:
             value = refs[TURNS + 1][:, part]
         for n, ref in enumerate(kerns):
-            value += jnp.dot(vec_ref[n], ref[half, part], preferred_element_type=jnp.float32)
+            tile = ref[pl.ds(starts[n], SIDE * rows), part]
+            value += jnp.dot(vec_ref[n], tile, preferred_element_type=jnp.float32)
         total_ref[:, part] = value
     if core == 0:
         refs[-3][...] = total_ref[...]
@@ -188,39 +187,45 @@
             ref[:, rows:] = lanes
 
 
-def run_first(turn, far, near, half, last, rows, cols):
+def run_first(far, near, half, last, rows, cols, ending=False):
     feats, width = near.shape
-    inputs = list(far) + [near, half] + ([last] if turn > 0 else [])
-    count = 2 * SIDE * rows
+    opening = last is None
+    inputs = list(far) + [near, half] + ([] if opening else [last])
+    count = len(far) * SIDE * rows
+    running = (cols, width + LANES)
+    if ending:
+        outs = [jax.ShapeDtypeStruct((cols, rows + LANES), jnp.float32)] * NEAR
+        scratch = [pltpu.VMEM(running, jnp.float32)]
+    else:
+        outs = [jax.ShapeDtypeStruct(running, jnp.float32)]
+        scratch = []
     return pl.pallas_call(
-        functools.partial(first_product, scale_of(feats), rows, turn),
+        functools.partial(first_product, scale_of(feats), rows, len(far), opening, ending),
         in_specs=[INSIDE] * len(inputs),
-        out_specs=[INSIDE, INSIDE],
-        out_shape=[
-            pltpu.VMEM((count, width), jnp.bfloat16),
-            jax.ShapeDtypeStruct((cols, width + LANES), jnp.float32),
-        ],
-        scratch_shapes=[pltpu.VMEM((2 * SIDE,) + far[0].shape[1:], jnp.bfloat16)],
+        out_specs=[INSIDE] * (1 + len(outs)),
+        out_shape=[pltpu.VMEM((count, width), jnp.bfloat16)] + outs,
+        scratch_shapes=scratch + [pltpu.VMEM((len(far) * SIDE,) + far[0].shape[1:], jnp.bfloat16)],
         compiler_params=pltpu.CompilerParams(vmem_limit_bytes=LIMIT),
         cost_estimate=pl.CostEstimate(
-            flops=2 * count * width * 2 * feats,
+            flops=4 * count * width * feats,
             bytes_accessed=2 * count * width,
             transcendentals=count * width,
         ),
     )(*inputs)
 
 
-def run_second(core, kerns, blocks, rows, *others):
-    width = kerns[0].shape[1]
+def run_second(core, pieces, blocks, rows, *others):
+    width = pieces[0][0].shape[1]
     cols = blocks.shape[1]
-    kerns = [pltpu.with_memory_space_constraint(kern, pltpu.VMEM) for kern in kerns]
+    starts = [start for _, start in pieces]
+    kerns = [pltpu.with_memory_space_constraint(kern, pltpu.VMEM) for kern, _ in pieces]
     inputs = kerns + [blocks] + list(others)
     if core == 0:
         outs = [jax.ShapeDtypeStruct((cols, width), jnp.float32)]
     else:
         outs = [jax.ShapeDtypeStruct((cols, rows + LANES), jnp.float32)] * NEAR
     return pl.pallas_call(
-        functools.partial(second_product, rows, core),
+        functools.partial(second_product, rows, core, starts),
         in_specs=[INSIDE] * len(inputs),
         out_specs=[INSIDE] * len(outs),
         out_shape=outs,
@@ -280,11 +285,15 @@
     first.wait()
 
 
+def outside(value):
+    return pltpu.with_memory_space_constraint(value, pltpu.HBM)
+
+
 def run_pack(points, rhs, noise):
     rows, feats = points.shape
     cols = rhs.shape[0]
     tall = rows + cols * (rows // feats) + cols
-    place = pl.BlockSpec(memory_space=pl.ANY)
+    place = pl.BlockSpec(memory_space=pltpu.HBM)
     return pl.pallas_call(
         pack,
         in_specs=[place, place, INSIDE],
@@ -296,7 +305,7 @@
         ],
         scratch_shapes=[pltpu.SemaphoreType.DMA((2,))],
         compiler_params=pltpu.CompilerParams(vmem_limit_bytes=SMALL),
-    )(points, rhs, noise)
+    )(outside(points), outside(rhs), noise)
 
 
 def run_bundle(side, near):
@@ -317,9 +326,9 @@
 
 def prepare(scale, *refs):
     near_ref, half_ref = refs[NEAR:]
-    rows = refs[0].shape[0]
+    rows = refs[1].shape[0]
     for k, ref in enumerate(refs[:NEAR]):
-        block = ref[...]
+        block = ref[:rows, :]
         part = pl.ds(k * rows, rows)
         near_ref[:, part] = block.astype(jnp.float32).T.astype(jnp.bfloat16)
         half_ref[:, part] = half_norms(scale, block)
@@ -395,29 +404,35 @@
     for k in range(1, SIDE):
         side.append(partner(packed, reach(SIDE_MASKS, k), reach(LINE_MASKS, k)))
     near = exchange([points] * NEAR, NEAR_MASKS)
-    own = run_bundle(side, near)
+    own = run_bundle(side, near[1:])
+    own_across = partner(own, CORE_MASK)
     first, second = [partner(own, *line_masks(turn)) for turn in (1, 2)]
     near, half = small_call(
         functools.partial(prepare, scale_of(feats)),
         [((feats, NEAR * rows), points.dtype), ((8, NEAR * rows), jnp.float32)],
-        *near,
+        packed,
+        *near[1:],
     )
 
-    kerns = []
-    kern, total = run_first(0, (own, partner(own, CORE_MASK)), near, half, None, rows, cols)
-    kerns.append(kern)
+    def first_call(far, last, ending=False):
+        return run_first(far, near, half, last, rows, cols, ending)
+
+    across = own_across
+    half_a, total = first_call([own], None)
+    half_b, total = first_call([across], total)
     first, second, total = lax.optimization_barrier((first, second, total))
     third = partner(second, *line_masks(1))
     across = [partner(item, CORE_MASK) for item in (first, second)]
-    kern, total = run_first(1, (first, across[0]), near, half, total, rows, cols)
-    kerns.append(kern)
-    kern, total = run_first(2, (second, across[1]), near, half, total, rows, cols)
-    kerns.append(kern)
+    pair_a, total = first_call([first, across[0]], total)
+    pair_b, total = first_call([second, across[1]], total)
     third, total = lax.optimization_barrier((third, total))
-    kern, total = run_first(3, (third, partner(third, CORE_MASK)), near, half, total, rows, cols)
-    kerns.append(kern)
-    wide_shape = ((cols, rows + LANES), jnp.float32)
-    parts = small_call(functools.partial(split_product, rows), [wide_shape] * NEAR, total)
+    across = partner(third, CORE_MASK)
+    half_c, total = first_call([third], total)
+    half_d, *parts = first_call([across], total, True)
+    skip = SIDE * rows
+    own_pieces = [(half_a, 0), (pair_a, 0), (pair_b, 0), (half_c, 0)]
+    other_pieces = [(half_b, 0), (pair_a, skip), (pair_b, skip), (half_d, 0)]
+
     image, rest, known, copies = small_call(
         middle,
         [field_shape, field_shape, lanes_shape, ((CHIPS, cols, rows + LANES), jnp.bfloat16)],
@@ -427,8 +442,8 @@
     )
     copies = share(copies)
     other = partner(copies, CORE_MASK)
-    half_total = run_second(0, kerns, copies, rows)[0]
-    parts = run_second(1, kerns, other, rows, half_total, copies)
+    half_total = run_second(0, own_pieces, copies, rows)[0]
+    parts = run_second(1, other_pieces, other, rows, half_total, copies)
     field, residual, direction, image_dir, norm_next, curve = small_call(
         closing,
         [field_shape] * 4 + [lanes_shape, ((DEVICES, cols), jnp.float32)],

time: 103 us -> 101 us (0.981)
  waiting for transfers between devices: 15.6 us -> 11.6 us
  blocking collectives: 29.6 us -> 31.3 us
  local copies, waits for them, and re-layouts: 2.37 us -> 0.68 us
  starting transfers between devices: 26.8 us -> 28.2 us
    ppermute x20, waiting for transfers between devices: 15.6 us -> 11.6 us  [partner(): return lax.ppermute(value, 'pts', pairs)]
    unnamed x4 -> x0, local copies, waits for them, and re-layouts: 1.69 us -> none
    all_to_all x1, blocking collectives: 15 us -> 16.6 us  [share(): return lax.all_to_all(copies, 'pts', 0, 0, axis_index_groups=chip_groups())]
    ppermute x20, starting transfers between devices: 26.8 us -> 28.2 us  [partner(): return lax.ppermute(value, 'pts', pairs)]
    pallas_call x6 -> x8, Pallas kernels: 25.7 us -> 25.7 us  [the longest x6 19 us: run_first(): pl.pallas_call(functools.partial(first_product, scale_of(feats), rows, le...]
  transfers between devices with their start and end apart: 20 -> 20, of which waited for: 13 -> 9; matrix products, arithmetic and copies ran while one was open for 1% -> 1% of each run, Pallas kernels for 18% -> 21%
where the time goes in v2:
time: 101 us
  blocking collectives  31.3 us (31%)
  Pallas kernels  28.5 us (28%)
  starting transfers between devices  28.2 us (28%)
  waiting for transfers between devices  11.6 us (11%)
    ppermute x20, starting transfers between devices, partner(): return lax.ppermute(value, 'pts', pairs)  28.2 us
    pallas_call x6, Pallas kernels, run_first(): pl.pallas_call(functools.partial(first_product, scale_of(feats), rows, le...  19 us
    all_to_all x1, blocking collectives, share(): return lax.all_to_all(copies, 'pts', 0, 0, axis_index_groups=chip_groups())  16.6 us
    all_to_all x1, blocking collectives, per_device(): lax.all_to_all(curve[:, None, :], 'pts', 0, 0).reshape(DEVICES, cols)  14.7 us
    ppermute x20, waiting for transfers between devices, partner(): return lax.ppermute(value, 'pts', pairs)  11.6 us
    pallas_call x2, Pallas kernels, run_second(): pl.pallas_call(functools.partial(second_product, rows, core, starts), in_...  6.63 us
  transfers between devices with their start and end apart: 20, of which 9 were waited for; matrix products, arithmetic and copies ran while one was open for 1% of the time, Pallas kernels for 21%

profile of v2, /device:TPU:1, one launch (start us, length us, event | category | flops | bytes accessed | tf_op | source)
XLA Modules:
  0.0 101.0 jit_solution(5740019986756289710)
XLA Ops:
  0.6 2.5 %collective-permute-start.3 = (bf16[384,128]{1,0:T(8,128)(2,1)}, bf16[384,128]{1,0:T(8,128)(2,1)S(1)}, u32[]{:S(2)}, u32[]{:S(2)}) collective-permute-start(bf16[384,128]{1,0:T(8,128)(2,1)} %points_ref.1), channel_id=1, source_target_pairs={{0,2},{1,3},{2,0},{3,1},{4,6},{5,7},{6,4},{7,5},{8,10},{9,11},{10,... | collective-permute-start | bytes 294920 | tf_op jit(solution)/shard_map/ppermute | solution.py:65
  3.2 0.7 broadcast_in_dim.6.noise_ref.refs_4_
  3.9 1.0 shard_map.50
  4.8 2.6 %collective-permute-start.2 = (bf16[512,128]{1,0:T(8,128)(2,1)S(1)}, bf16[512,128]{1,0:T(8,128)(2,1)S(1)}, u32[]{:S(2)}, u32[]{:S(2)}) collective-permute-start(bf16[512,128]{1,0:T(8,128)(2,1)S(1)} %get-tuple-element.43.refs_0_), channel_id=1, source_target_pairs={{0,30},{1,97},{2,28},{3,99},{4,26},{5,101},{6,24},{7,103},{8,22},{... | collective-permute-start | bytes 393224 | tf_op jit(solution)/shard_map/ppermute | solution.py:65
  7.4 0.5 collective-permute-start.1
  7.9 0.3 collective-permute-start
  8.2 1.0 %collective-permute-start.5 = (bf16[384,128]{1,0:T(8,128)(2,1)}, bf16[384,128]{1,0:T(8,128)(2,1)S(1)}, u32[]{:S(2)}, u32[]{:S(2)}) collective-permute-start(bf16[384,128]{1,0:T(8,128)(2,1)} %points_ref.1), channel_id=1, source_target_pairs={{0,10},{1,11},{2,8},{3,9},{4,14},{5,15},{6,12},{7,13},{8,2},{9,3},... | collective-permute-start | bytes 294920 | tf_op jit(solution)/shard_map/ppermute | solution.py:65
  9.2 0.0 collective-permute-done.3.refs_4_.refs_1_
  9.2 0.3 collective-permute-start.4
  9.5 3.6 %collective-permute-done.5.refs_6_.refs_3_ = bf16[384,128]{1,0:T(8,128)(2,1)S(1)} collective-permute-done((bf16[384,128]{1,0:T(8,128)(2,1)}, bf16[384,128]{1,0:T(8,128)(2,1)S(1)}, u32[]{:S(2)}, u32[]{:S(2)}) %collective-permute-start.5) | collective-permute-done | bytes 98336 | tf_op jit(solution)/shard_map/ppermute | solution.py:65
  13.0 0.1 collective-permute-done.4.refs_5_.refs_2_
  13.2 0.0 collective-permute-done.2.refs_3_
  13.2 0.0 collective-permute-done.1.refs_2_
  13.2 0.0 collective-permute-done.refs_1_
  13.2 4.7 %collective-permute-start.6 = (bf16[4,512,128]{2,1,0:T(8,128)(2,1)S(1)}, bf16[4,512,128]{2,1,0:T(8,128)(2,1)S(1)}, u32[]{:S(2)}, u32[]{:S(2)}) collective-permute-start(bf16[4,512,128]{2,1,0:T(8,128)(2,1)S(1)} %shard_map.51.refs_0_), channel_id=1, source_target_pairs={{0,1},{1,0},{2,3},{3,2},{4,5},{5,4},{6,7},{7,6},{8,9},{9,8},{10,11... | collective-permute-start | bytes 1572872 | tf_op jit(solution)/shard_map/ppermute | solution.py:65
  18.0 2.4 %collective-permute-start.8 = (bf16[4,512,128]{2,1,0:T(8,128)(2,1)S(1)}, bf16[4,512,128]{2,1,0:T(8,128)(2,1)S(1)}, u32[]{:S(2)}, u32[]{:S(2)}) collective-permute-start(bf16[4,512,128]{2,1,0:T(8,128)(2,1)S(1)} %shard_map.51.refs_0_), channel_id=1, source_target_pairs={{0,96},{1,25},{2,98},{3,27},{4,100},{5,29},{6,102},{7,31},{8,104},... | collective-permute-start | bytes 1572872 | tf_op jit(solution)/shard_map/ppermute | solution.py:65
  20.4 2.2 %collective-permute-start.7 = (bf16[4,512,128]{2,1,0:T(8,128)(2,1)S(1)}, bf16[4,512,128]{2,1,0:T(8,128)(2,1)S(1)}, u32[]{:S(2)}, u32[]{:S(2)}) collective-permute-start(bf16[4,512,128]{2,1,0:T(8,128)(2,1)S(1)} %shard_map.51.refs_0_), channel_id=1, source_target_pairs={{0,32},{1,7},{2,34},{3,5},{4,36},{5,3},{6,38},{7,1},{8,40},{9,15},... | collective-permute-start | bytes 1572872 | tf_op jit(solution)/shard_map/ppermute | solution.py:65
  22.6 0.4 shard_map.52
  23.0 2.4 %shard_map.53 = (bf16[1536,1536]{1,0:T(8,128)(2,1)S(1)}, f32[32,1664]{1,0:T(8,128)S(1)}) custom-call(bf16[4,512,128]{2,1,0:T(8,128)(2,1)S(1)} %shard_map.51.refs_0_, bf16[128,1536]{1,0:T(8,128)(2,1)S(1)} %get-tuple-element.44.refs_1_.refs_2_, f32[8,1536]{1,0:T(8,128)S(1)} %get-tuple-element.45.refs_2_.refs_3_), custom_call_target="tpu_custom_call" | custom-call | flops 1207959552 | bytes 4718592 | tf_op jit(solution)/shard_map/pallas_call | solution.py:202
  25.4 0.0 collective-permute-done.6.refs_0_
  25.4 2.4 %shard_map.54 = (bf16[1536,1536]{1,0:T(8,128)(2,1)S(1)}, f32[32,1664]{1,0:T(8,128)S(1)}) custom-call(bf16[4,512,128]{2,1,0:T(8,128)(2,1)S(1)} %collective-permute-done.6.refs_0_, bf16[128,1536]{1,0:T(8,128)(2,1)S(1)} %get-tuple-element.44.refs_1_.refs_2_, f32[8,1536]{1,0:T(8,128)S(1)} %get-tuple-element.45.refs_2_.refs_3_, ...), custom_call_target="tpu_custom_call" | custom-call | flops 1207959552 | bytes 4718592 | tf_op jit(solution)/shard_map/pallas_call | solution.py:202
  27.7 0.0 collective-permute-done.8.refs_0_
  27.8 1.9 %collective-permute-done.7.refs_0_ = bf16[4,512,128]{2,1,0:T(8,128)(2,1)S(1)} collective-permute-done((bf16[4,512,128]{2,1,0:T(8,128)(2,1)S(1)}, bf16[4,512,128]{2,1,0:T(8,128)(2,1)S(1)}, u32[]{:S(2)}, u32[]{:S(2)}) %collective-permute-start.7) | collective-permute-done | bytes 524320 | tf_op jit(solution)/shard_map/ppermute | solution.py:65
  29.6 0.4 collective-permute-start.9
  30.0 0.1 collective-permute-start.10
  30.1 2.2 %collective-permute-start.11 = (bf16[4,512,128]{2,1,0:T(8,128)(2,1)S(1)}, bf16[4,512,128]{2,1,0:T(8,128)(2,1)S(1)}, u32[]{:S(2)}, u32[]{:S(2)}) collective-permute-start(bf16[4,512,128]{2,1,0:T(8,128)(2,1)S(1)} %collective-permute-done.8.refs_0_), channel_id=1, source_target_pairs={{0,32},{1,7},{2,34},{3,5},{4,36},{5,3},{6,38},{7,1},{8,40},{9,15},... | collective-permute-start | bytes 1572872 | tf_op jit(solution)/shard_map/ppermute | solution.py:65
  32.4 0.0 collective-permute-done.9.refs_1_
  32.4 4.8 %shard_map.55 = (bf16[3072,1536]{1,0:T(8,128)(2,1)S(1)}, f32[32,1664]{1,0:T(8,128)S(1)}) custom-call(bf16[4,512,128]{2,1,0:T(8,128)(2,1)S(1)} %collective-permute-done.7.refs_0_, bf16[4,512,128]{2,1,0:T(8,128)(2,1)S(1)} %collective-permute-done.9.refs_1_, bf16[128,1536]{1,0:T(8,128)(2,1)S(1)} %get-tuple-element.44.refs_1_.refs_2_, ...), custom_call_target="tpu_custom_call" | custom-call | flops 2415919104 | bytes 9437184 | tf_op jit(solution)/shard_map/pallas_call | solution.py:202
  37.2 0.0 collective-permute-done.10.refs_1_
  37.2 4.8 %shard_map.56 = (bf16[3072,1536]{1,0:T(8,128)(2,1)S(1)}, f32[32,1664]{1,0:T(8,128)S(1)}) custom-call(bf16[4,512,128]{2,1,0:T(8,128)(2,1)S(1)} %collective-permute-done.8.refs_0_, bf16[4,512,128]{2,1,0:T(8,128)(2,1)S(1)} %collective-permute-done.10.refs_1_, bf16[128,1536]{1,0:T(8,128)(2,1)S(1)} %get-tuple-element.44.refs_1_.refs_2_, ...), custom_call_target="tpu_custom_call" | custom-call | flops 2415919104 | bytes 9437184 | tf_op jit(solution)/shard_map/pallas_call | solution.py:202
  42.0 0.0 collective-permute-done.11.refs_0_
  42.0 0.1 collective-permute-start.12
  42.1 2.4 %shard_map.57 = (bf16[1536,1536]{1,0:T(8,128)(2,1)S(1)}, f32[32,1664]{1,0:T(8,128)S(1)}) custom-call(bf16[4,512,128]{2,1,0:T(8,128)(2,1)S(1)} %collective-permute-done.11.refs_0_, bf16[128,1536]{1,0:T(8,128)(2,1)S(1)} %get-tuple-element.44.refs_1_.refs_2_, f32[8,1536]{1,0:T(8,128)S(1)} %get-tuple-element.45.refs_2_.refs_3_, ...), custom_call_target="tpu_custom_call" | custom-call | flops 1207959552 | bytes 4718592 | tf_op jit(solution)/shard_map/pallas_call | solution.py:202
  44.4 0.0 collective-permute-done.12.refs_0_
  44.4 2.4 %shard_map.58 = (bf16[1536,1536]{1,0:T(8,128)(2,1)S(1)}, f32[32,512]{1,0:T(8,128)S(1)}, f32[32,512]{1,0:T(8,128)S(1)}, f32[32,512]{1,0:T(8,128)S(1)}, f32[32,512]{1,0:T(8,128)S(1)}) custom-call(bf16[4,512,128]{2,1,0:T(8,128)(2,1)S(1)} %collective-permute-done.12.refs_0_, bf16[128,1536]{1,0:T(8,128)(2,1)S(1)} %get-tuple-element.44.refs_1_.refs_2_, ...), custom_call_target="tpu_custom_call" | custom-call | flops 1207959552 | bytes 4718592 | tf_op jit(solution)/shard_map/pallas_call | solution.py:202
  46.8 0.6 collective-permute-start.13
  47.4 0.7 collective-permute-start.14
  48.1 1.4 %collective-permute-start.15 = (f32[32,512]{1,0:T(8,128)S(1)}, f32[32,512]{1,0:T(8,128)S(1)}, u32[]{:S(2)}, u32[]{:S(2)}) collective-permute-start(f32[32,512]{1,0:T(8,128)S(1)} %get-tuple-element.63), channel_id=1, source_target_pairs={{0,10},{1,11},{2,8},{3,9},{4,14},{5,15},{6,12},{7,13},{8,2},{9,3},... | collective-permute-start | bytes 196616 | tf_op jit(solution)/shard_map/ppermute | solution.py:65
  49.5 0.5 collective-permute-done.13.refs_1_
  50.0 0.8 collective-permute-done.14.refs_2_
  50.8 1.7 %collective-permute-done.15.refs_3_ = f32[32,512]{1,0:T(8,128)S(1)} collective-permute-done((f32[32,512]{1,0:T(8,128)S(1)}, f32[32,512]{1,0:T(8,128)S(1)}, u32[]{:S(2)}, u32[]{:S(2)}) %collective-permute-start.15) | collective-permute-done | bytes 65568 | tf_op jit(solution)/shard_map/ppermute | solution.py:65
  52.5 0.2 shard_map.59
  52.7 16.6 %all_to_all.10.refs_4_.refs_6_ = bf16[16,32,512]{2,1,0:T(8,128)(2,1)S(1)} all-to-all(bf16[16,32,512]{2,1,0:T(8,128)(2,1)S(1)} %get-tuple-element.66), channel_id=1, replica_groups={{0,6,24,30,32,38,56,62,64,70,88,94,96,102,120,126},{1,7,25,31,33,39,57,..., dimensions={0} | all-to-all | bytes 1048576 | tf_op jit(solution)/shard_map/all_to_all | solution.py:77
  69.4 3.4 %collective-permute-start.16 = (bf16[16,32,512]{2,1,0:T(8,128)(2,1)S(1)}, bf16[16,32,512]{2,1,0:T(8,128)(2,1)S(1)}, u32[]{:S(2)}, u32[]{:S(2)}) collective-permute-start(bf16[16,32,512]{2,1,0:T(8,128)(2,1)S(1)} %all_to_all.10.refs_4_.refs_6_), channel_id=1, source_target_pairs={{0,1},{1,0},{2,3},{3,2},{4,5},{5,4},{6,7},{7,6},{8,9},{9,8},{10,11... | collective-permute-start | bytes 1572872 | tf_op jit(solution)/shard_map/ppermute | solution.py:65
  72.8 3.3 %shard_map.60.refs_5_ = f32[32,1536]{1,0:T(8,128)S(1)} custom-call(bf16[1536,1536]{1,0:T(8,128)(2,1)S(1)} %get-tuple-element.67.refs_0_, bf16[3072,1536]{1,0:T(8,128)(2,1)S(1)} %get-tuple-element.51.refs_1_, bf16[3072,1536]{1,0:T(8,128)(2,1)S(1)} %get-tuple-element.54.refs_2_, bf16[1536,1536]{1,0:T(8,128)(2,1)S(1)} %get-tuple-element.68.refs_3_, ...), custom_call_target="tpu_custom_call" | custom-call | flops 4831838208 | bytes 18874368 | tf_op jit(solution)/shard_map/pallas_call | solution.py:227
  76.1 0.0 collective-permute-done.16.refs_4_
  76.1 3.3 %shard_map.61 = (f32[32,512]{1,0:T(8,128)S(1)}, f32[32,512]{1,0:T(8,128)S(1)}, f32[32,512]{1,0:T(8,128)S(1)}, f32[32,512]{1,0:T(8,128)S(1)}) custom-call(bf16[1536,1536]{1,0:T(8,128)(2,1)S(1)} %get-tuple-element.47.refs_0_, bf16[3072,1536]{1,0:T(8,128)(2,1)S(1)} %get-tuple-element.51.refs_1_, bf16[3072,1536]{1,0:T(8,128)(2,1)S(1)} %get-tuple-element.54.refs_2_, ...), custom_call_target="tpu_custom_call" | custom-call | flops 4831838208 | bytes 18874368 | tf_op jit(solution)/shard_map/pallas_call | solution.py:227
  79.4 0.0 collective-permute-start.17
  79.4 0.1 collective-permute-start.18
  79.5 2.6 %collective-permute-start.19 = (f32[32,512]{1,0:T(8,128)S(1)}, f32[32,512]{1,0:T(8,128)S(1)}, u32[]{:S(2)}, u32[]{:S(2)}) collective-permute-start(f32[32,512]{1,0:T(8,128)S(1)} %get-tuple-element.72), channel_id=1, source_target_pairs={{0,10},{1,11},{2,8},{3,9},{4,14},{5,15},{6,12},{7,13},{8,2},{9,3},... | collective-permute-start | bytes 196616 | tf_op jit(solution)/shard_map/ppermute | solution.py:65
  82.1 1.1 %collective-permute-done.17.refs_1_ = f32[32,512]{1,0:T(8,128)S(1)} collective-permute-done((f32[32,512]{1,0:T(8,128)S(1)}, f32[32,512]{1,0:T(8,128)S(1)}, u32[]{:S(2)}, u32[]{:S(2)}) %collective-permute-start.17) | collective-permute-done | bytes 65568 | tf_op jit(solution)/shard_map/ppermute | solution.py:65
  83.2 0.1 collective-permute-done.18.refs_2_
  83.2 1.9 %collective-permute-done.19.refs_3_ = f32[32,512]{1,0:T(8,128)S(1)} collective-permute-done((f32[32,512]{1,0:T(8,128)S(1)}, f32[32,512]{1,0:T(8,128)S(1)}, u32[]{:S(2)}, u32[]{:S(2)}) %collective-permute-start.19) | collective-permute-done | bytes 65568 | tf_op jit(solution)/shard_map/ppermute | solution.py:65
  85.1 0.4 shard_map.62
  85.6 14.7 %all_to_all.11 = f32[128,1,32]{2,1,0:T(1,128)S(1)} all-to-all(f32[128,1,32]{2,1,0:T(1,128)S(1)} %bitcast.8), channel_id=1, replica_groups=mesh['pts'=128] {'pts'}, dimensions={0} | all-to-all | bytes 32768 | tf_op jit(solution)/shard_map/all_to_all | solution.py:457
  100.2 0.8 shard_map.63
  (1 shorter events, 0.0 us)
Async XLA Ops:
  0.6 8.6 %collective-permute-start.3 = (bf16[384,128]{1,0:T(8,128)(2,1)}, bf16[384,128]{1,0:T(8,128)(2,1)S(1)}, u32[]{:S(2)}, u32[]{:S(2)}) collective-permute-start(bf16[384,128]{1,0:T(8,128)(2,1)} %points_ref.1), channel_id=1, source_target_pairs={{0,2},{1,3},{2,0},{3,1},{4,6},{5,7},{6,4},{7,5},{8,10},{9,11},{10,... | collective-permute-start | bytes 294920 | tf_op jit(solution)/shard_map/ppermute | solution.py:65
  4.8 8.3 %collective-permute-start.2 = (bf16[512,128]{1,0:T(8,128)(2,1)S(1)}, bf16[512,128]{1,0:T(8,128)(2,1)S(1)}, u32[]{:S(2)}, u32[]{:S(2)}) collective-permute-start(bf16[512,128]{1,0:T(8,128)(2,1)S(1)} %get-tuple-element.43.refs_0_), channel_id=1, source_target_pairs={{0,30},{1,97},{2,28},{3,99},{4,26},{5,101},{6,24},{7,103},{8,22},{... | collective-permute-start | bytes 393224 | tf_op jit(solution)/shard_map/ppermute | solution.py:65
  7.4 5.8 %collective-permute-start.1 = (bf16[512,128]{1,0:T(8,128)(2,1)S(1)}, bf16[512,128]{1,0:T(8,128)(2,1)S(1)}, u32[]{:S(2)}, u32[]{:S(2)}) collective-permute-start(bf16[512,128]{1,0:T(8,128)(2,1)S(1)} %get-tuple-element.43.refs_0_), channel_id=1, source_target_pairs={{0,24},{1,65},{2,26},{3,67},{4,28},{5,69},{6,30},{7,71},{8,16},{9,... | collective-permute-start | bytes 393224 | tf_op jit(solution)/shard_map/ppermute | solution.py:65
  7.9 5.3 %collective-permute-start = (bf16[512,128]{1,0:T(8,128)(2,1)S(1)}, bf16[512,128]{1,0:T(8,128)(2,1)S(1)}, u32[]{:S(2)}, u32[]{:S(2)}) collective-permute-start(bf16[512,128]{1,0:T(8,128)(2,1)S(1)} %get-tuple-element.43.refs_0_), channel_id=1, source_target_pairs={{0,6},{1,33},{2,4},{3,35},{4,2},{5,37},{6,0},{7,39},{8,14},{9,41},... | collective-permute-start | bytes 393224 | tf_op jit(solution)/shard_map/ppermute | solution.py:65
  8.2 4.9 %collective-permute-start.5 = (bf16[384,128]{1,0:T(8,128)(2,1)}, bf16[384,128]{1,0:T(8,128)(2,1)S(1)}, u32[]{:S(2)}, u32[]{:S(2)}) collective-permute-start(bf16[384,128]{1,0:T(8,128)(2,1)} %points_ref.1), channel_id=1, source_target_pairs={{0,10},{1,11},{2,8},{3,9},{4,14},{5,15},{6,12},{7,13},{8,2},{9,3},... | collective-permute-start | bytes 294920 | tf_op jit(solution)/shard_map/ppermute | solution.py:65
  9.2 4.0 %collective-permute-start.4 = (bf16[384,128]{1,0:T(8,128)(2,1)}, bf16[384,128]{1,0:T(8,128)(2,1)S(1)}, u32[]{:S(2)}, u32[]{:S(2)}) collective-permute-start(bf16[384,128]{1,0:T(8,128)(2,1)} %points_ref.1), channel_id=1, source_target_pairs={{0,8},{1,9},{2,10},{3,11},{4,12},{5,13},{6,14},{7,15},{8,0},{9,1},... | collective-permute-start | bytes 294920 | tf_op jit(solution)/shard_map/ppermute | solution.py:65
  13.2 12.1 %collective-permute-start.6 = (bf16[4,512,128]{2,1,0:T(8,128)(2,1)S(1)}, bf16[4,512,128]{2,1,0:T(8,128)(2,1)S(1)}, u32[]{:S(2)}, u32[]{:S(2)}) collective-permute-start(bf16[4,512,128]{2,1,0:T(8,128)(2,1)S(1)} %shard_map.51.refs_0_), channel_id=1, source_target_pairs={{0,1},{1,0},{2,3},{3,2},{4,5},{5,4},{6,7},{7,6},{8,9},{9,8},{10,11... | collective-permute-start | bytes 1572872 | tf_op jit(solution)/shard_map/ppermute | solution.py:65
  18.0 9.8 %collective-permute-start.8 = (bf16[4,512,128]{2,1,0:T(8,128)(2,1)S(1)}, bf16[4,512,128]{2,1,0:T(8,128)(2,1)S(1)}, u32[]{:S(2)}, u32[]{:S(2)}) collective-permute-start(bf16[4,512,128]{2,1,0:T(8,128)(2,1)S(1)} %shard_map.51.refs_0_), channel_id=1, source_target_pairs={{0,96},{1,25},{2,98},{3,27},{4,100},{5,29},{6,102},{7,31},{8,104},... | collective-permute-start | bytes 1572872 | tf_op jit(solution)/shard_map/ppermute | solution.py:65
  20.4 9.2 %collective-permute-start.7 = (bf16[4,512,128]{2,1,0:T(8,128)(2,1)S(1)}, bf16[4,512,128]{2,1,0:T(8,128)(2,1)S(1)}, u32[]{:S(2)}, u32[]{:S(2)}) collective-permute-start(bf16[4,512,128]{2,1,0:T(8,128)(2,1)S(1)} %shard_map.51.refs_0_), channel_id=1, source_target_pairs={{0,32},{1,7},{2,34},{3,5},{4,36},{5,3},{6,38},{7,1},{8,40},{9,15},... | collective-permute-start | bytes 1572872 | tf_op jit(solution)/shard_map/ppermute | solution.py:65
  29.6 2.8 %collective-permute-start.9 = (bf16[4,512,128]{2,1,0:T(8,128)(2,1)S(1)}, bf16[4,512,128]{2,1,0:T(8,128)(2,1)S(1)}, u32[]{:S(2)}, u32[]{:S(2)}) collective-permute-start(bf16[4,512,128]{2,1,0:T(8,128)(2,1)S(1)} %collective-permute-done.7.refs_0_), channel_id=1, source_target_pairs={{0,1},{1,0},{2,3},{3,2},{4,5},{5,4},{6,7},{7,6},{8,9},{9,8},{10,11... | collective-permute-start | bytes 1572872 | tf_op jit(solution)/shard_map/ppermute | solution.py:65
  30.0 7.2 %collective-permute-start.10 = (bf16[4,512,128]{2,1,0:T(8,128)(2,1)S(1)}, bf16[4,512,128]{2,1,0:T(8,128)(2,1)S(1)}, u32[]{:S(2)}, u32[]{:S(2)}) collective-permute-start(bf16[4,512,128]{2,1,0:T(8,128)(2,1)S(1)} %collective-permute-done.8.refs_0_), channel_id=1, source_target_pairs={{0,1},{1,0},{2,3},{3,2},{4,5},{5,4},{6,7},{7,6},{8,9},{9,8},{10,11... | collective-permute-start | bytes 1572872 | tf_op jit(solution)/shard_map/ppermute | solution.py:65
  30.1 11.8 %collective-permute-start.11 = (bf16[4,512,128]{2,1,0:T(8,128)(2,1)S(1)}, bf16[4,512,128]{2,1,0:T(8,128)(2,1)S(1)}, u32[]{:S(2)}, u32[]{:S(2)}) collective-permute-start(bf16[4,512,128]{2,1,0:T(8,128)(2,1)S(1)} %collective-permute-done.8.refs_0_), channel_id=1, source_target_pairs={{0,32},{1,7},{2,34},{3,5},{4,36},{5,3},{6,38},{7,1},{8,40},{9,15},... | collective-permute-start | bytes 1572872 | tf_op jit(solution)/shard_map/ppermute | solution.py:65
  42.0 2.5 %collective-permute-start.12 = (bf16[4,512,128]{2,1,0:T(8,128)(2,1)S(1)}, bf16[4,512,128]{2,1,0:T(8,128)(2,1)S(1)}, u32[]{:S(2)}, u32[]{:S(2)}) collective-permute-start(bf16[4,512,128]{2,1,0:T(8,128)(2,1)S(1)} %collective-permute-done.11.refs_0_), channel_id=1, source_target_pairs={{0,1},{1,0},{2,3},{3,2},{4,5},{5,4},{6,7},{7,6},{8,9},{9,8},{10,11... | collective-permute-start | bytes 1572872 | tf_op jit(solution)/shard_map/ppermute | solution.py:65
  46.8 3.2 %collective-permute-start.13 = (f32[32,512]{1,0:T(8,128)S(1)}, f32[32,512]{1,0:T(8,128)S(1)}, u32[]{:S(2)}, u32[]{:S(2)}) collective-permute-start(f32[32,512]{1,0:T(8,128)S(1)} %get-tuple-element.61), channel_id=1, source_target_pairs={{0,2},{1,3},{2,0},{3,1},{4,6},{5,7},{6,4},{7,5},{8,10},{9,11},{10,... | collective-permute-start | bytes 196616 | tf_op jit(solution)/shard_map/ppermute | solution.py:65
  47.4 3.4 %collective-permute-start.14 = (f32[32,512]{1,0:T(8,128)S(1)}, f32[32,512]{1,0:T(8,128)S(1)}, u32[]{:S(2)}, u32[]{:S(2)}) collective-permute-start(f32[32,512]{1,0:T(8,128)S(1)} %get-tuple-element.62), channel_id=1, source_target_pairs={{0,8},{1,9},{2,10},{3,11},{4,12},{5,13},{6,14},{7,15},{8,0},{9,1},... | collective-permute-start | bytes 196616 | tf_op jit(solution)/shard_map/ppermute | solution.py:65
  48.1 4.4 %collective-permute-start.15 = (f32[32,512]{1,0:T(8,128)S(1)}, f32[32,512]{1,0:T(8,128)S(1)}, u32[]{:S(2)}, u32[]{:S(2)}) collective-permute-start(f32[32,512]{1,0:T(8,128)S(1)} %get-tuple-element.63), channel_id=1, source_target_pairs={{0,10},{1,11},{2,8},{3,9},{4,14},{5,15},{6,12},{7,13},{8,2},{9,3},... | collective-permute-start | bytes 196616 | tf_op jit(solution)/shard_map/ppermute | solution.py:65
  69.4 6.7 %collective-permute-start.16 = (bf16[16,32,512]{2,1,0:T(8,128)(2,1)S(1)}, bf16[16,32,512]{2,1,0:T(8,128)(2,1)S(1)}, u32[]{:S(2)}, u32[]{:S(2)}) collective-permute-start(bf16[16,32,512]{2,1,0:T(8,128)(2,1)S(1)} %all_to_all.10.refs_4_.refs_6_), channel_id=1, source_target_pairs={{0,1},{1,0},{2,3},{3,2},{4,5},{5,4},{6,7},{7,6},{8,9},{9,8},{10,11... | collective-permute-start | bytes 1572872 | tf_op jit(solution)/shard_map/ppermute | solution.py:65
  79.4 3.7 %collective-permute-start.17 = (f32[32,512]{1,0:T(8,128)S(1)}, f32[32,512]{1,0:T(8,128)S(1)}, u32[]{:S(2)}, u32[]{:S(2)}) collective-permute-start(f32[32,512]{1,0:T(8,128)S(1)} %get-tuple-element.70), channel_id=1, source_target_pairs={{0,2},{1,3},{2,0},{3,1},{4,6},{5,7},{6,4},{7,5},{8,10},{9,11},{10,... | collective-permute-start | bytes 196616 | tf_op jit(solution)/shard_map/ppermute | solution.py:65
  79.4 3.8 %collective-permute-start.18 = (f32[32,512]{1,0:T(8,128)S(1)}, f32[32,512]{1,0:T(8,128)S(1)}, u32[]{:S(2)}, u32[]{:S(2)}) collective-permute-start(f32[32,512]{1,0:T(8,128)S(1)} %get-tuple-element.71), channel_id=1, source_target_pairs={{0,8},{1,9},{2,10},{3,11},{4,12},{5,13},{6,14},{7,15},{8,0},{9,1},... | collective-permute-start | bytes 196616 | tf_op jit(solution)/shard_map/ppermute | solution.py:65
  79.5 5.6 %collective-permute-start.19 = (f32[32,512]{1,0:T(8,128)S(1)}, f32[32,512]{1,0:T(8,128)S(1)}, u32[]{:S(2)}, u32[]{:S(2)}) collective-permute-start(f32[32,512]{1,0:T(8,128)S(1)} %get-tuple-element.72), channel_id=1, source_target_pairs={{0,10},{1,11},{2,8},{3,9},{4,14},{5,15},{6,12},{7,13},{8,2},{9,3},... | collective-permute-start | bytes 196616 | tf_op jit(solution)/shard_map/ppermute | solution.py:65

commit v3 on v2

--- a/solution.py
+++ b/solution.py
@@ -9,7 +9,7 @@
 from jax.sharding import PartitionSpec as P
 
 DEVICES = 128
-NEAR_MASKS = (2, 8)
+NEAR_MASKS = (10, 2)
 SIDE_MASKS = (6, 24)
 LINE_MASKS = (32, 64)
 CORE_MASK = 1
@@ -266,19 +266,24 @@
     return jnp.sum(value, axis=1, keepdims=True)
 
 
-def pack(points_ref, rhs_ref, noise_ref, out_ref, keep_ref, noisy_ref, sems):
+def pack(points_ref, rhs_ref, noise_ref, out_ref, keep_ref, noisy_ref, row_ref, line_ref, sems):
     rows, feats = points_ref.shape
     cols = rhs_ref.shape[0]
     first = pltpu.make_async_copy(points_ref, out_ref.at[pl.ds(0, rows), :], sems.at[0])
     second = pltpu.make_async_copy(rhs_ref, keep_ref, sems.at[1])
+    third = pltpu.make_async_copy(noise_ref, line_ref, sems.at[2])
+    second.start()
+    third.start()
     first.start()
-    second.start()
     second.wait()
     for k in range(rows // feats):
         part = keep_ref[:, pl.ds(k * feats, feats)]
         out_ref[pl.ds(rows + k * cols, cols), :] = part.astype(jnp.bfloat16)
     rhs = keep_ref[...]
-    noisy = noise_ref[...] * rhs
+    third.wait()
+    noise = line_ref[...].reshape(1, rows)
+    row_ref[...] = noise
+    noisy = noise * rhs
     noisy_ref[...] = noisy
     lanes = spread_lanes((row_sum(rhs * rhs), row_sum(rhs * noisy)), (cols, LANES))
     out_ref[pl.ds(rows + cols * (rows // feats), cols), :] = lanes
@@ -296,16 +301,17 @@
     place = pl.BlockSpec(memory_space=pltpu.HBM)
     return pl.pallas_call(
         pack,
-        in_specs=[place, place, INSIDE],
-        out_specs=[INSIDE] * 3,
+        in_specs=[place] * 3,
+        out_specs=[INSIDE] * 4,
         out_shape=[
             jax.ShapeDtypeStruct((tall, feats), points.dtype),
             jax.ShapeDtypeStruct(rhs.shape, rhs.dtype),
             jax.ShapeDtypeStruct(rhs.shape, rhs.dtype),
+            jax.ShapeDtypeStruct((1, rows), noise.dtype),
         ],
-        scratch_shapes=[pltpu.SemaphoreType.DMA((2,))],
+        scratch_shapes=[pltpu.VMEM((rows,), noise.dtype), pltpu.SemaphoreType.DMA((3,))],
         compiler_params=pltpu.CompilerParams(vmem_limit_bytes=SMALL),
-    )(outside(points), outside(rhs), noise)
+    )(outside(points), outside(rhs), outside(noise))
 
 
 def run_bundle(side, near):
@@ -395,8 +401,7 @@
 
 def per_device(points, noise_var, right_side):
     rows, feats = points.shape
-    noise = noise_var[None, :]
-    packed, rhs, noisy = run_pack(points, right_side.T, noise)
+    packed, rhs, noisy, noise = run_pack(points, right_side.T, noise_var)
     cols = rhs.shape[0]
     field_shape = ((cols, rows), jnp.float32)
     lanes_shape = ((cols, LANES), jnp.float32)

time: 101 us -> 99.3 us (0.983)
  starting transfers between devices: 28.2 us -> 26.5 us
  waiting for transfers between devices: 11.6 us -> 13 us
    ppermute x20, starting transfers between devices: 28.2 us -> 26.5 us  [partner(): return lax.ppermute(value, 'pts', pairs)]
    ppermute x20, waiting for transfers between devices: 11.6 us -> 13 us  [partner(): return lax.ppermute(value, 'pts', pairs)]
  transfers between devices with their start and end apart: 20 -> 20, of which waited for: 9 -> 9; matrix products, arithmetic and copies ran while one was open for 1% -> 0% of each run, Pallas kernels for 21% -> 22%
where the time goes in v3:
time: 99.3 us; the launch traced here: 99.1 us
  blocking collectives  30.4 us (31%)
  Pallas kernels  28.5 us (29%)
  starting transfers between devices  26.5 us (27%)
  waiting for transfers between devices  13 us (13%)
    ppermute x20, starting transfers between devices, partner(): return lax.ppermute(value, 'pts', pairs)  26.5 us
    pallas_call x6, Pallas kernels, run_first(): pl.pallas_call(functools.partial(first_product, scale_of(feats), rows, le...  19 us
    all_to_all x1, blocking collectives, share(): return lax.all_to_all(copies, 'pts', 0, 0, axis_index_groups=chip_groups())  15.9 us
    all_to_all x1, blocking collectives, per_device(): lax.all_to_all(curve[:, None, :], 'pts', 0, 0).reshape(DEVICES, cols)  14.5 us
    ppermute x20, waiting for transfers between devices, partner(): return lax.ppermute(value, 'pts', pairs)  13 us
    pallas_call x2, Pallas kernels, run_second(): pl.pallas_call(functools.partial(second_product, rows, core, starts), in_...  6.63 us
  transfers between devices with their start and end apart: 20, of which 9 were waited for; matrix products, arithmetic and copies ran while one was open for 0% of the time, Pallas kernels for 22%

profile of v3, /device:TPU:1, one launch (start us, length us, event | category | flops | bytes accessed | tf_op | source)
XLA Modules:
  0.0 99.1 jit_solution(15303395034164424956)
XLA Ops:
  0.6 3.6 %collective-permute-start.3 = (bf16[384,128]{1,0:T(8,128)(2,1)}, bf16[384,128]{1,0:T(8,128)(2,1)S(1)}, u32[]{:S(2)}, u32[]{:S(2)}) collective-permute-start(bf16[384,128]{1,0:T(8,128)(2,1)} %points_ref.1), channel_id=1, source_target_pairs={{0,10},{1,11},{2,8},{3,9},{4,14},{5,15},{6,12},{7,13},{8,2},{9,3},... | collective-permute-start | bytes 294920 | tf_op jit(solution)/shard_map/ppermute | solution.py:65
  4.2 1.0 %shard_map.50 = (bf16[512,128]{1,0:T(8,128)(2,1)S(1)}, f32[32,384]{1,0:T(8,128)S(1)}, f32[32,384]{1,0:T(8,128)S(1)}, f32[1,384]{1,0:T(1,128)S(1)}) custom-call(bf16[384,128]{1,0:T(8,128)(2,1)} %points_ref.1, f32[32,384]{1,0:T(8,128)} %bitcast.9, f32[384]{0:T(512)} %noise_ref.1), custom_call_target="tpu_custom_call" | custom-call | tf_op jit(solution)/shard_map/pallas_call | solution.py:302
  5.2 2.6 %collective-permute-start.2 = (bf16[512,128]{1,0:T(8,128)(2,1)S(1)}, bf16[512,128]{1,0:T(8,128)(2,1)S(1)}, u32[]{:S(2)}, u32[]{:S(2)}) collective-permute-start(bf16[512,128]{1,0:T(8,128)(2,1)S(1)} %get-tuple-element.44.refs_0_), channel_id=1, source_target_pairs={{0,30},{1,97},{2,28},{3,99},{4,26},{5,101},{6,24},{7,103},{8,22},{... | collective-permute-start | bytes 393224 | tf_op jit(solution)/shard_map/ppermute | solution.py:65
  7.8 0.5 collective-permute-start.1
  8.3 0.3 collective-permute-start
  8.5 0.2 collective-permute-start.5
  8.7 0.0 collective-permute-done.3.refs_4_.refs_1_
  8.7 0.1 collective-permute-start.4
  8.8 3.7 %collective-permute-done.5.refs_6_.refs_3_ = bf16[384,128]{1,0:T(8,128)(2,1)S(1)} collective-permute-done((bf16[384,128]{1,0:T(8,128)(2,1)}, bf16[384,128]{1,0:T(8,128)(2,1)S(1)}, u32[]{:S(2)}, u32[]{:S(2)}) %collective-permute-start.5) | collective-permute-done | bytes 98336 | tf_op jit(solution)/shard_map/ppermute | solution.py:65
  12.5 0.2 collective-permute-done.4.refs_5_.refs_2_
  12.7 0.0 collective-permute-done.2.refs_3_
  12.7 0.7 collective-permute-done.1.refs_2_
  13.4 0.0 collective-permute-done.refs_1_
  13.4 4.3 %collective-permute-start.6 = (bf16[4,512,128]{2,1,0:T(8,128)(2,1)S(1)}, bf16[4,512,128]{2,1,0:T(8,128)(2,1)S(1)}, u32[]{:S(2)}, u32[]{:S(2)}) collective-permute-start(bf16[4,512,128]{2,1,0:T(8,128)(2,1)S(1)} %shard_map.51.refs_0_), channel_id=1, source_target_pairs={{0,1},{1,0},{2,3},{3,2},{4,5},{5,4},{6,7},{7,6},{8,9},{9,8},{10,11... | collective-permute-start | bytes 1572872 | tf_op jit(solution)/shard_map/ppermute | solution.py:65
  17.7 1.9 %collective-permute-start.8 = (bf16[4,512,128]{2,1,0:T(8,128)(2,1)S(1)}, bf16[4,512,128]{2,1,0:T(8,128)(2,1)S(1)}, u32[]{:S(2)}, u32[]{:S(2)}) collective-permute-start(bf16[4,512,128]{2,1,0:T(8,128)(2,1)S(1)} %shard_map.51.refs_0_), channel_id=1, source_target_pairs={{0,96},{1,25},{2,98},{3,27},{4,100},{5,29},{6,102},{7,31},{8,104},... | collective-permute-start | bytes 1572872 | tf_op jit(solution)/shard_map/ppermute | solution.py:65
  19.6 1.7 %collective-permute-start.7 = (bf16[4,512,128]{2,1,0:T(8,128)(2,1)S(1)}, bf16[4,512,128]{2,1,0:T(8,128)(2,1)S(1)}, u32[]{:S(2)}, u32[]{:S(2)}) collective-permute-start(bf16[4,512,128]{2,1,0:T(8,128)(2,1)S(1)} %shard_map.51.refs_0_), channel_id=1, source_target_pairs={{0,32},{1,7},{2,34},{3,5},{4,36},{5,3},{6,38},{7,1},{8,40},{9,15},... | collective-permute-start | bytes 1572872 | tf_op jit(solution)/shard_map/ppermute | solution.py:65
  21.3 0.4 shard_map.52
  21.7 2.4 %shard_map.53 = (bf16[1536,1536]{1,0:T(8,128)(2,1)S(1)}, f32[32,1664]{1,0:T(8,128)S(1)}) custom-call(bf16[4,512,128]{2,1,0:T(8,128)(2,1)S(1)} %shard_map.51.refs_0_, bf16[128,1536]{1,0:T(8,128)(2,1)S(1)} %get-tuple-element.45.refs_1_.refs_2_, f32[8,1536]{1,0:T(8,128)S(1)} %get-tuple-element.46.refs_2_.refs_3_), custom_call_target="tpu_custom_call" | custom-call | flops 1207959552 | bytes 4718592 | tf_op jit(solution)/shard_map/pallas_call | solution.py:202
  24.1 0.0 collective-permute-done.6.refs_0_
  24.1 2.4 %shard_map.54 = (bf16[1536,1536]{1,0:T(8,128)(2,1)S(1)}, f32[32,1664]{1,0:T(8,128)S(1)}) custom-call(bf16[4,512,128]{2,1,0:T(8,128)(2,1)S(1)} %collective-permute-done.6.refs_0_, bf16[128,1536]{1,0:T(8,128)(2,1)S(1)} %get-tuple-element.45.refs_1_.refs_2_, f32[8,1536]{1,0:T(8,128)S(1)} %get-tuple-element.46.refs_2_.refs_3_, ...), custom_call_target="tpu_custom_call" | custom-call | flops 1207959552 | bytes 4718592 | tf_op jit(solution)/shard_map/pallas_call | solution.py:202
  26.4 0.8 collective-permute-done.8.refs_0_
  27.3 1.6 %collective-permute-done.7.refs_0_ = bf16[4,512,128]{2,1,0:T(8,128)(2,1)S(1)} collective-permute-done((bf16[4,512,128]{2,1,0:T(8,128)(2,1)S(1)}, bf16[4,512,128]{2,1,0:T(8,128)(2,1)S(1)}, u32[]{:S(2)}, u32[]{:S(2)}) %collective-permute-start.7) | collective-permute-done | bytes 524320 | tf_op jit(solution)/shard_map/ppermute | solution.py:65
  28.9 0.9 collective-permute-start.9
  29.8 0.0 collective-permute-start.10
  29.8 1.6 %collective-permute-start.11 = (bf16[4,512,128]{2,1,0:T(8,128)(2,1)S(1)}, bf16[4,512,128]{2,1,0:T(8,128)(2,1)S(1)}, u32[]{:S(2)}, u32[]{:S(2)}) collective-permute-start(bf16[4,512,128]{2,1,0:T(8,128)(2,1)S(1)} %collective-permute-done.8.refs_0_), channel_id=1, source_target_pairs={{0,32},{1,7},{2,34},{3,5},{4,36},{5,3},{6,38},{7,1},{8,40},{9,15},... | collective-permute-start | bytes 1572872 | tf_op jit(solution)/shard_map/ppermute | solution.py:65
  31.4 0.0 collective-permute-done.9.refs_1_
  31.4 4.8 %shard_map.55 = (bf16[3072,1536]{1,0:T(8,128)(2,1)S(1)}, f32[32,1664]{1,0:T(8,128)S(1)}) custom-call(bf16[4,512,128]{2,1,0:T(8,128)(2,1)S(1)} %collective-permute-done.7.refs_0_, bf16[4,512,128]{2,1,0:T(8,128)(2,1)S(1)} %collective-permute-done.9.refs_1_, bf16[128,1536]{1,0:T(8,128)(2,1)S(1)} %get-tuple-element.45.refs_1_.refs_2_, ...), custom_call_target="tpu_custom_call" | custom-call | flops 2415919104 | bytes 9437184 | tf_op jit(solution)/shard_map/pallas_call | solution.py:202
  36.2 0.0 collective-permute-done.10.refs_1_
  36.2 4.8 %shard_map.56 = (bf16[3072,1536]{1,0:T(8,128)(2,1)S(1)}, f32[32,1664]{1,0:T(8,128)S(1)}) custom-call(bf16[4,512,128]{2,1,0:T(8,128)(2,1)S(1)} %collective-permute-done.8.refs_0_, bf16[4,512,128]{2,1,0:T(8,128)(2,1)S(1)} %collective-permute-done.10.refs_1_, bf16[128,1536]{1,0:T(8,128)(2,1)S(1)} %get-tuple-element.45.refs_1_.refs_2_, ...), custom_call_target="tpu_custom_call" | custom-call | flops 2415919104 | bytes 9437184 | tf_op jit(solution)/shard_map/pallas_call | solution.py:202
  41.0 0.0 collective-permute-done.11.refs_0_
  41.0 0.3 collective-permute-start.12
  41.3 2.4 %shard_map.57 = (bf16[1536,1536]{1,0:T(8,128)(2,1)S(1)}, f32[32,1664]{1,0:T(8,128)S(1)}) custom-call(bf16[4,512,128]{2,1,0:T(8,128)(2,1)S(1)} %collective-permute-done.11.refs_0_, bf16[128,1536]{1,0:T(8,128)(2,1)S(1)} %get-tuple-element.45.refs_1_.refs_2_, f32[8,1536]{1,0:T(8,128)S(1)} %get-tuple-element.46.refs_2_.refs_3_, ...), custom_call_target="tpu_custom_call" | custom-call | flops 1207959552 | bytes 4718592 | tf_op jit(solution)/shard_map/pallas_call | solution.py:202
  43.7 0.0 collective-permute-done.12.refs_0_
  43.7 2.4 %shard_map.58 = (bf16[1536,1536]{1,0:T(8,128)(2,1)S(1)}, f32[32,512]{1,0:T(8,128)S(1)}, f32[32,512]{1,0:T(8,128)S(1)}, f32[32,512]{1,0:T(8,128)S(1)}, f32[32,512]{1,0:T(8,128)S(1)}) custom-call(bf16[4,512,128]{2,1,0:T(8,128)(2,1)S(1)} %collective-permute-done.12.refs_0_, bf16[128,1536]{1,0:T(8,128)(2,1)S(1)} %get-tuple-element.45.refs_1_.refs_2_, ...), custom_call_target="tpu_custom_call" | custom-call | flops 1207959552 | bytes 4718592 | tf_op jit(solution)/shard_map/pallas_call | solution.py:202
  46.1 0.9 collective-permute-start.13
  47.0 1.8 %collective-permute-start.14 = (f32[32,512]{1,0:T(8,128)S(1)}, f32[32,512]{1,0:T(8,128)S(1)}, u32[]{:S(2)}, u32[]{:S(2)}) collective-permute-start(f32[32,512]{1,0:T(8,128)S(1)} %get-tuple-element.63), channel_id=1, source_target_pairs={{0,2},{1,3},{2,0},{3,1},{4,6},{5,7},{6,4},{7,5},{8,10},{9,11},{10,... | collective-permute-start | bytes 196616 | tf_op jit(solution)/shard_map/ppermute | solution.py:65
  48.8 0.0 collective-permute-start.15
  48.8 1.4 %collective-permute-done.13.refs_1_ = f32[32,512]{1,0:T(8,128)S(1)} collective-permute-done((f32[32,512]{1,0:T(8,128)S(1)}, f32[32,512]{1,0:T(8,128)S(1)}, u32[]{:S(2)}, u32[]{:S(2)}) %collective-permute-start.13) | collective-permute-done | bytes 65568 | tf_op jit(solution)/shard_map/ppermute | solution.py:65
  50.2 2.3 %collective-permute-done.14.refs_2_ = f32[32,512]{1,0:T(8,128)S(1)} collective-permute-done((f32[32,512]{1,0:T(8,128)S(1)}, f32[32,512]{1,0:T(8,128)S(1)}, u32[]{:S(2)}, u32[]{:S(2)}) %collective-permute-start.14) | collective-permute-done | bytes 65568 | tf_op jit(solution)/shard_map/ppermute | solution.py:65
  52.5 0.0 collective-permute-done.15.refs_3_
  52.5 0.2 shard_map.59
  52.7 15.9 %all_to_all.10.refs_4_.refs_6_ = bf16[16,32,512]{2,1,0:T(8,128)(2,1)S(1)} all-to-all(bf16[16,32,512]{2,1,0:T(8,128)(2,1)S(1)} %get-tuple-element.67), channel_id=1, replica_groups={{0,6,24,30,32,38,56,62,64,70,88,94,96,102,120,126},{1,7,25,31,33,39,57,..., dimensions={0} | all-to-all | bytes 1048576 | tf_op jit(solution)/shard_map/all_to_all | solution.py:77
  68.6 3.2 %collective-permute-start.16 = (bf16[16,32,512]{2,1,0:T(8,128)(2,1)S(1)}, bf16[16,32,512]{2,1,0:T(8,128)(2,1)S(1)}, u32[]{:S(2)}, u32[]{:S(2)}) collective-permute-start(bf16[16,32,512]{2,1,0:T(8,128)(2,1)S(1)} %all_to_all.10.refs_4_.refs_6_), channel_id=1, source_target_pairs={{0,1},{1,0},{2,3},{3,2},{4,5},{5,4},{6,7},{7,6},{8,9},{9,8},{10,11... | collective-permute-start | bytes 1572872 | tf_op jit(solution)/shard_map/ppermute | solution.py:65
  71.8 3.3 %shard_map.60.refs_5_ = f32[32,1536]{1,0:T(8,128)S(1)} custom-call(bf16[1536,1536]{1,0:T(8,128)(2,1)S(1)} %get-tuple-element.68.refs_0_, bf16[3072,1536]{1,0:T(8,128)(2,1)S(1)} %get-tuple-element.52.refs_1_, bf16[3072,1536]{1,0:T(8,128)(2,1)S(1)} %get-tuple-element.55.refs_2_, bf16[1536,1536]{1,0:T(8,128)(2,1)S(1)} %get-tuple-element.69.refs_3_, ...), custom_call_target="tpu_custom_call" | custom-call | flops 4831838208 | bytes 18874368 | tf_op jit(solution)/shard_map/pallas_call | solution.py:227
  75.1 0.0 collective-permute-done.16.refs_4_
  75.1 3.3 %shard_map.61 = (f32[32,512]{1,0:T(8,128)S(1)}, f32[32,512]{1,0:T(8,128)S(1)}, f32[32,512]{1,0:T(8,128)S(1)}, f32[32,512]{1,0:T(8,128)S(1)}) custom-call(bf16[1536,1536]{1,0:T(8,128)(2,1)S(1)} %get-tuple-element.48.refs_0_, bf16[3072,1536]{1,0:T(8,128)(2,1)S(1)} %get-tuple-element.52.refs_1_, bf16[3072,1536]{1,0:T(8,128)(2,1)S(1)} %get-tuple-element.55.refs_2_, ...), custom_call_target="tpu_custom_call" | custom-call | flops 4831838208 | bytes 18874368 | tf_op jit(solution)/shard_map/pallas_call | solution.py:227
  78.4 0.0 collective-permute-start.17
  78.4 0.1 collective-permute-start.18
  78.5 2.6 %collective-permute-start.19 = (f32[32,512]{1,0:T(8,128)S(1)}, f32[32,512]{1,0:T(8,128)S(1)}, u32[]{:S(2)}, u32[]{:S(2)}) collective-permute-start(f32[32,512]{1,0:T(8,128)S(1)} %get-tuple-element.73), channel_id=1, source_target_pairs={{0,8},{1,9},{2,10},{3,11},{4,12},{5,13},{6,14},{7,15},{8,0},{9,1},... | collective-permute-start | bytes 196616 | tf_op jit(solution)/shard_map/ppermute | solution.py:65
  81.1 2.0 %collective-permute-done.17.refs_1_ = f32[32,512]{1,0:T(8,128)S(1)} collective-permute-done((f32[32,512]{1,0:T(8,128)S(1)}, f32[32,512]{1,0:T(8,128)S(1)}, u32[]{:S(2)}, u32[]{:S(2)}) %collective-permute-start.17) | collective-permute-done | bytes 65568 | tf_op jit(solution)/shard_map/ppermute | solution.py:65
  83.1 0.3 collective-permute-done.18.refs_2_
  83.4 0.0 collective-permute-done.19.refs_3_
  83.4 0.4 shard_map.62
  83.8 14.5 %all_to_all.11 = f32[128,1,32]{2,1,0:T(1,128)S(1)} all-to-all(f32[128,1,32]{2,1,0:T(1,128)S(1)} %bitcast.8), channel_id=1, replica_groups=mesh['pts'=128] {'pts'}, dimensions={0} | all-to-all | bytes 32768 | tf_op jit(solution)/shard_map/all_to_all | solution.py:462
  98.3 0.8 shard_map.63
  (1 shorter events, 0.0 us)
Async XLA Ops:
  0.6 8.1 %collective-permute-start.3 = (bf16[384,128]{1,0:T(8,128)(2,1)}, bf16[384,128]{1,0:T(8,128)(2,1)S(1)}, u32[]{:S(2)}, u32[]{:S(2)}) collective-permute-start(bf16[384,128]{1,0:T(8,128)(2,1)} %points_ref.1), channel_id=1, source_target_pairs={{0,10},{1,11},{2,8},{3,9},{4,14},{5,15},{6,12},{7,13},{8,2},{9,3},... | collective-permute-start | bytes 294920 | tf_op jit(solution)/shard_map/ppermute | solution.py:65
  5.2 7.5 %collective-permute-start.2 = (bf16[512,128]{1,0:T(8,128)(2,1)S(1)}, bf16[512,128]{1,0:T(8,128)(2,1)S(1)}, u32[]{:S(2)}, u32[]{:S(2)}) collective-permute-start(bf16[512,128]{1,0:T(8,128)(2,1)S(1)} %get-tuple-element.44.refs_0_), channel_id=1, source_target_pairs={{0,30},{1,97},{2,28},{3,99},{4,26},{5,101},{6,24},{7,103},{8,22},{... | collective-permute-start | bytes 393224 | tf_op jit(solution)/shard_map/ppermute | solution.py:65
  7.8 5.6 %collective-permute-start.1 = (bf16[512,128]{1,0:T(8,128)(2,1)S(1)}, bf16[512,128]{1,0:T(8,128)(2,1)S(1)}, u32[]{:S(2)}, u32[]{:S(2)}) collective-permute-start(bf16[512,128]{1,0:T(8,128)(2,1)S(1)} %get-tuple-element.44.refs_0_), channel_id=1, source_target_pairs={{0,24},{1,65},{2,26},{3,67},{4,28},{5,69},{6,30},{7,71},{8,16},{9,... | collective-permute-start | bytes 393224 | tf_op jit(solution)/shard_map/ppermute | solution.py:65
  8.3 5.1 %collective-permute-start = (bf16[512,128]{1,0:T(8,128)(2,1)S(1)}, bf16[512,128]{1,0:T(8,128)(2,1)S(1)}, u32[]{:S(2)}, u32[]{:S(2)}) collective-permute-start(bf16[512,128]{1,0:T(8,128)(2,1)S(1)} %get-tuple-element.44.refs_0_), channel_id=1, source_target_pairs={{0,6},{1,33},{2,4},{3,35},{4,2},{5,37},{6,0},{7,39},{8,14},{9,41},... | collective-permute-start | bytes 393224 | tf_op jit(solution)/shard_map/ppermute | solution.py:65
  8.5 4.0 %collective-permute-start.5 = (bf16[384,128]{1,0:T(8,128)(2,1)}, bf16[384,128]{1,0:T(8,128)(2,1)S(1)}, u32[]{:S(2)}, u32[]{:S(2)}) collective-permute-start(bf16[384,128]{1,0:T(8,128)(2,1)} %points_ref.1), channel_id=1, source_target_pairs={{0,8},{1,9},{2,10},{3,11},{4,12},{5,13},{6,14},{7,15},{8,0},{9,1},... | collective-permute-start | bytes 294920 | tf_op jit(solution)/shard_map/ppermute | solution.py:65
  8.7 4.0 %collective-permute-start.4 = (bf16[384,128]{1,0:T(8,128)(2,1)}, bf16[384,128]{1,0:T(8,128)(2,1)S(1)}, u32[]{:S(2)}, u32[]{:S(2)}) collective-permute-start(bf16[384,128]{1,0:T(8,128)(2,1)} %points_ref.1), channel_id=1, source_target_pairs={{0,2},{1,3},{2,0},{3,1},{4,6},{5,7},{6,4},{7,5},{8,10},{9,11},{10,... | collective-permute-start | bytes 294920 | tf_op jit(solution)/shard_map/ppermute | solution.py:65
  13.4 10.7 %collective-permute-start.6 = (bf16[4,512,128]{2,1,0:T(8,128)(2,1)S(1)}, bf16[4,512,128]{2,1,0:T(8,128)(2,1)S(1)}, u32[]{:S(2)}, u32[]{:S(2)}) collective-permute-start(bf16[4,512,128]{2,1,0:T(8,128)(2,1)S(1)} %shard_map.51.refs_0_), channel_id=1, source_target_pairs={{0,1},{1,0},{2,3},{3,2},{4,5},{5,4},{6,7},{7,6},{8,9},{9,8},{10,11... | collective-permute-start | bytes 1572872 | tf_op jit(solution)/shard_map/ppermute | solution.py:65
  17.7 9.5 %collective-permute-start.8 = (bf16[4,512,128]{2,1,0:T(8,128)(2,1)S(1)}, bf16[4,512,128]{2,1,0:T(8,128)(2,1)S(1)}, u32[]{:S(2)}, u32[]{:S(2)}) collective-permute-start(bf16[4,512,128]{2,1,0:T(8,128)(2,1)S(1)} %shard_map.51.refs_0_), channel_id=1, source_target_pairs={{0,96},{1,25},{2,98},{3,27},{4,100},{5,29},{6,102},{7,31},{8,104},... | collective-permute-start | bytes 1572872 | tf_op jit(solution)/shard_map/ppermute | solution.py:65
  19.6 9.2 %collective-permute-start.7 = (bf16[4,512,128]{2,1,0:T(8,128)(2,1)S(1)}, bf16[4,512,128]{2,1,0:T(8,128)(2,1)S(1)}, u32[]{:S(2)}, u32[]{:S(2)}) collective-permute-start(bf16[4,512,128]{2,1,0:T(8,128)(2,1)S(1)} %shard_map.51.refs_0_), channel_id=1, source_target_pairs={{0,32},{1,7},{2,34},{3,5},{4,36},{5,3},{6,38},{7,1},{8,40},{9,15},... | collective-permute-start | bytes 1572872 | tf_op jit(solution)/shard_map/ppermute | solution.py:65
  28.9 2.5 %collective-permute-start.9 = (bf16[4,512,128]{2,1,0:T(8,128)(2,1)S(1)}, bf16[4,512,128]{2,1,0:T(8,128)(2,1)S(1)}, u32[]{:S(2)}, u32[]{:S(2)}) collective-permute-start(bf16[4,512,128]{2,1,0:T(8,128)(2,1)S(1)} %collective-permute-done.7.refs_0_), channel_id=1, source_target_pairs={{0,1},{1,0},{2,3},{3,2},{4,5},{5,4},{6,7},{7,6},{8,9},{9,8},{10,11... | collective-permute-start | bytes 1572872 | tf_op jit(solution)/shard_map/ppermute | solution.py:65
  29.8 6.4 %collective-permute-start.10 = (bf16[4,512,128]{2,1,0:T(8,128)(2,1)S(1)}, bf16[4,512,128]{2,1,0:T(8,128)(2,1)S(1)}, u32[]{:S(2)}, u32[]{:S(2)}) collective-permute-start(bf16[4,512,128]{2,1,0:T(8,128)(2,1)S(1)} %collective-permute-done.8.refs_0_), channel_id=1, source_target_pairs={{0,1},{1,0},{2,3},{3,2},{4,5},{5,4},{6,7},{7,6},{8,9},{9,8},{10,11... | collective-permute-start | bytes 1572872 | tf_op jit(solution)/shard_map/ppermute | solution.py:65
  29.8 11.2 %collective-permute-start.11 = (bf16[4,512,128]{2,1,0:T(8,128)(2,1)S(1)}, bf16[4,512,128]{2,1,0:T(8,128)(2,1)S(1)}, u32[]{:S(2)}, u32[]{:S(2)}) collective-permute-start(bf16[4,512,128]{2,1,0:T(8,128)(2,1)S(1)} %collective-permute-done.8.refs_0_), channel_id=1, source_target_pairs={{0,32},{1,7},{2,34},{3,5},{4,36},{5,3},{6,38},{7,1},{8,40},{9,15},... | collective-permute-start | bytes 1572872 | tf_op jit(solution)/shard_map/ppermute | solution.py:65
  41.0 2.7 %collective-permute-start.12 = (bf16[4,512,128]{2,1,0:T(8,128)(2,1)S(1)}, bf16[4,512,128]{2,1,0:T(8,128)(2,1)S(1)}, u32[]{:S(2)}, u32[]{:S(2)}) collective-permute-start(bf16[4,512,128]{2,1,0:T(8,128)(2,1)S(1)} %collective-permute-done.11.refs_0_), channel_id=1, source_target_pairs={{0,1},{1,0},{2,3},{3,2},{4,5},{5,4},{6,7},{7,6},{8,9},{9,8},{10,11... | collective-permute-start | bytes 1572872 | tf_op jit(solution)/shard_map/ppermute | solution.py:65
  46.1 4.1 %collective-permute-start.13 = (f32[32,512]{1,0:T(8,128)S(1)}, f32[32,512]{1,0:T(8,128)S(1)}, u32[]{:S(2)}, u32[]{:S(2)}) collective-permute-start(f32[32,512]{1,0:T(8,128)S(1)} %get-tuple-element.62), channel_id=1, source_target_pairs={{0,10},{1,11},{2,8},{3,9},{4,14},{5,15},{6,12},{7,13},{8,2},{9,3},... | collective-permute-start | bytes 196616 | tf_op jit(solution)/shard_map/ppermute | solution.py:65
  47.0 5.4 %collective-permute-start.14 = (f32[32,512]{1,0:T(8,128)S(1)}, f32[32,512]{1,0:T(8,128)S(1)}, u32[]{:S(2)}, u32[]{:S(2)}) collective-permute-start(f32[32,512]{1,0:T(8,128)S(1)} %get-tuple-element.63), channel_id=1, source_target_pairs={{0,2},{1,3},{2,0},{3,1},{4,6},{5,7},{6,4},{7,5},{8,10},{9,11},{10,... | collective-permute-start | bytes 196616 | tf_op jit(solution)/shard_map/ppermute | solution.py:65
  48.8 3.7 %collective-permute-start.15 = (f32[32,512]{1,0:T(8,128)S(1)}, f32[32,512]{1,0:T(8,128)S(1)}, u32[]{:S(2)}, u32[]{:S(2)}) collective-permute-start(f32[32,512]{1,0:T(8,128)S(1)} %get-tuple-element.64), channel_id=1, source_target_pairs={{0,8},{1,9},{2,10},{3,11},{4,12},{5,13},{6,14},{7,15},{8,0},{9,1},... | collective-permute-start | bytes 196616 | tf_op jit(solution)/shard_map/ppermute | solution.py:65
  68.6 6.5 %collective-permute-start.16 = (bf16[16,32,512]{2,1,0:T(8,128)(2,1)S(1)}, bf16[16,32,512]{2,1,0:T(8,128)(2,1)S(1)}, u32[]{:S(2)}, u32[]{:S(2)}) collective-permute-start(bf16[16,32,512]{2,1,0:T(8,128)(2,1)S(1)} %all_to_all.10.refs_4_.refs_6_), channel_id=1, source_target_pairs={{0,1},{1,0},{2,3},{3,2},{4,5},{5,4},{6,7},{7,6},{8,9},{9,8},{10,11... | collective-permute-start | bytes 1572872 | tf_op jit(solution)/shard_map/ppermute | solution.py:65
  78.4 4.7 %collective-permute-start.17 = (f32[32,512]{1,0:T(8,128)S(1)}, f32[32,512]{1,0:T(8,128)S(1)}, u32[]{:S(2)}, u32[]{:S(2)}) collective-permute-start(f32[32,512]{1,0:T(8,128)S(1)} %get-tuple-element.71), channel_id=1, source_target_pairs={{0,10},{1,11},{2,8},{3,9},{4,14},{5,15},{6,12},{7,13},{8,2},{9,3},... | collective-permute-start | bytes 196616 | tf_op jit(solution)/shard_map/ppermute | solution.py:65
  78.4 5.0 %collective-permute-start.18 = (f32[32,512]{1,0:T(8,128)S(1)}, f32[32,512]{1,0:T(8,128)S(1)}, u32[]{:S(2)}, u32[]{:S(2)}) collective-permute-start(f32[32,512]{1,0:T(8,128)S(1)} %get-tuple-element.72), channel_id=1, source_target_pairs={{0,2},{1,3},{2,0},{3,1},{4,6},{5,7},{6,4},{7,5},{8,10},{9,11},{10,... | collective-permute-start | bytes 196616 | tf_op jit(solution)/shard_map/ppermute | solution.py:65
  78.5 4.9 %collective-permute-start.19 = (f32[32,512]{1,0:T(8,128)S(1)}, f32[32,512]{1,0:T(8,128)S(1)}, u32[]{:S(2)}, u32[]{:S(2)}) collective-permute-start(f32[32,512]{1,0:T(8,128)S(1)} %get-tuple-element.73), channel_id=1, source_target_pairs={{0,8},{1,9},{2,10},{3,11},{4,12},{5,13},{6,14},{7,15},{8,0},{9,1},... | collective-permute-start | bytes 196616 | tf_op jit(solution)/shard_map/ppermute | solution.py:65

commit v4 on v3

--- a/solution.py
+++ b/solution.py
@@ -156,6 +156,7 @@
     kerns = refs[:TURNS]
     blocks_ref = refs[TURNS]
     vec_ref, total_ref = refs[-2:]
+    cols = total_ref.shape[0]
     index = lax.axis_index("pts")
     place = place_in_group(index)
     odd = lax.rem(index, 2)
@@ -164,15 +165,18 @@
             even_slot = side + SIDE * EVEN_LINES[n]
             odd_slot = SIDE * side + ODD_LINES[n]
             slot = jnp.bitwise_xor(place, jnp.where(odd == core, even_slot, odd_slot))
-            vec_ref[n, :, pl.ds(side * rows, rows)] = blocks_ref[slot, :, pl.ds(0, rows)]
+            part = pl.ds(side * rows, rows)
+            vec_ref[n, :cols, part] = blocks_ref[slot, :, pl.ds(0, rows)]
+            vec_ref[n, cols:, part] = blocks_ref[slot, :, pl.ds(rows, rows)]
     for c in range(total_ref.shape[1] // CHUNK):
         part = pl.ds(c * CHUNK, CHUNK)
-        value = jnp.zeros((total_ref.shape[0], CHUNK), jnp.float32)
-        if core == 1:
-            value = refs[TURNS + 1][:, part]
+        value = jnp.zeros((2 * cols, CHUNK), jnp.float32)
         for n, ref in enumerate(kerns):
             tile = ref[pl.ds(starts[n], SIDE * rows), part]
             value += jnp.dot(vec_ref[n], tile, preferred_element_type=jnp.float32)
+        value = value[:cols] + value[cols:]
+        if core == 1:
+            value += refs[TURNS + 1][:, part]
         total_ref[:, part] = value
     if core == 0:
         refs[-3][...] = total_ref[...]
@@ -180,8 +184,8 @@
         other_ref = refs[TURNS + 2]
         lanes = jnp.zeros((total_ref.shape[0], LANES), jnp.float32)
         for k in range(CHIPS):
-            lanes += blocks_ref[k, :, rows:].astype(jnp.float32)
-            lanes += other_ref[k, :, rows:].astype(jnp.float32)
+            lanes += blocks_ref[k, :, 2 * rows :].astype(jnp.float32)
+            lanes += other_ref[k, :, 2 * rows :].astype(jnp.float32)
         for k, ref in enumerate(refs[TURNS + 3 : TURNS + 3 + NEAR]):
             ref[:, :rows] = total_ref[:, pl.ds(k * rows, rows)]
             ref[:, rows:] = lanes
@@ -230,7 +234,7 @@
         out_specs=[INSIDE] * len(outs),
         out_shape=outs,
         scratch_shapes=[
-            pltpu.VMEM((TURNS, cols, SIDE * rows), jnp.bfloat16),
+            pltpu.VMEM((TURNS, 2 * cols, SIDE * rows), jnp.bfloat16),
             pltpu.VMEM((cols, width), jnp.float32),
         ],
         compiler_params=pltpu.CompilerParams(vmem_limit_bytes=LIMIT),
@@ -356,7 +360,9 @@
     lane = lax.broadcasted_iota(jnp.int32, known_ref.shape, 1)
     known_ref[...] = jnp.where(lane == 0, norm, shift)
     lanes = spread_lanes((row_sum(rhs * rest), row_sum(rest * rest)), known_ref.shape)
-    packed = jnp.concatenate([rest.astype(jnp.bfloat16), lanes], axis=1)
+    high = rest.astype(jnp.bfloat16)
+    low = (rest - high.astype(jnp.float32)).astype(jnp.bfloat16)
+    packed = jnp.concatenate([high, low, lanes], axis=1)
     for k in range(copies_ref.shape[0]):
         copies_ref[k] = packed
 
@@ -440,7 +446,7 @@
 
     image, rest, known, copies = small_call(
         middle,
-        [field_shape, field_shape, lanes_shape, ((CHIPS, cols, rows + LANES), jnp.bfloat16)],
+        [field_shape, field_shape, lanes_shape, ((CHIPS, cols, 2 * rows + LANES), jnp.bfloat16)],
         *exchange(parts, NEAR_MASKS),
         noisy,
         rhs,

time: 99.3 us -> 104 us (1.047)
  blocking collectives: 30.4 us -> 34.9 us
    all_to_all x1, blocking collectives: 15.9 us -> 20.5 us  [share(): return lax.all_to_all(copies, 'pts', 0, 0, axis_index_groups=chip_groups())]
  transfers between devices with their start and end apart: 20 -> 20, of which waited for: 9 -> 9; matrix products, arithmetic and copies ran while one was open for 0% -> 0% of each run, Pallas kernels for 22% -> 21%
where the time goes in v4:
time: 104 us; the launch traced here: 103 us
  blocking collectives  34.9 us (34%)
  Pallas kernels  28.6 us (28%)
  starting transfers between devices  26.3 us (25%)
  waiting for transfers between devices  13 us (12%)
    ppermute x20, starting transfers between devices, partner(): return lax.ppermute(value, 'pts', pairs)  26.3 us
    all_to_all x1, blocking collectives, share(): return lax.all_to_all(copies, 'pts', 0, 0, axis_index_groups=chip_groups())  20.5 us
    pallas_call x6, Pallas kernels, run_first(): pl.pallas_call(functools.partial(first_product, scale_of(feats), rows, le...  19 us
    all_to_all x1, blocking collectives, per_device(): lax.all_to_all(curve[:, None, :], 'pts', 0, 0).reshape(DEVICES, cols)  14.4 us
    ppermute x20, waiting for transfers between devices, partner(): return lax.ppermute(value, 'pts', pairs)  13 us
    pallas_call x2, Pallas kernels, run_second(): pl.pallas_call(functools.partial(second_product, rows, core, starts), in_...  6.7 us
  transfers between devices with their start and end apart: 20, of which 9 were waited for; matrix products, arithmetic and copies ran while one was open for 0% of the time, Pallas kernels for 21%

profile of v4, /device:TPU:1, one launch (start us, length us, event | category | flops | bytes accessed | tf_op | source)
XLA Modules:
  0.0 103.5 jit_solution(7755460913907713726)
XLA Ops:
  0.6 3.6 %collective-permute-start.3 = (bf16[384,128]{1,0:T(8,128)(2,1)}, bf16[384,128]{1,0:T(8,128)(2,1)S(1)}, u32[]{:S(2)}, u32[]{:S(2)}) collective-permute-start(bf16[384,128]{1,0:T(8,128)(2,1)} %points_ref.1), channel_id=1, source_target_pairs={{0,10},{1,11},{2,8},{3,9},{4,14},{5,15},{6,12},{7,13},{8,2},{9,3},... | collective-permute-start | bytes 294920 | tf_op jit(solution)/shard_map/ppermute | solution.py:65
  4.2 1.0 shard_map.50
  5.2 2.6 %collective-permute-start.2 = (bf16[512,128]{1,0:T(8,128)(2,1)S(1)}, bf16[512,128]{1,0:T(8,128)(2,1)S(1)}, u32[]{:S(2)}, u32[]{:S(2)}) collective-permute-start(bf16[512,128]{1,0:T(8,128)(2,1)S(1)} %get-tuple-element.44.refs_0_), channel_id=1, source_target_pairs={{0,30},{1,97},{2,28},{3,99},{4,26},{5,101},{6,24},{7,103},{8,22},{... | collective-permute-start | bytes 393224 | tf_op jit(solution)/shard_map/ppermute | solution.py:65
  7.8 0.5 collective-permute-start.1
  8.3 0.3 collective-permute-start
  8.5 0.2 collective-permute-start.5
  8.7 0.0 collective-permute-done.3.refs_4_.refs_1_
  8.7 0.1 collective-permute-start.4
  8.8 3.7 %collective-permute-done.5.refs_6_.refs_3_ = bf16[384,128]{1,0:T(8,128)(2,1)S(1)} collective-permute-done((bf16[384,128]{1,0:T(8,128)(2,1)}, bf16[384,128]{1,0:T(8,128)(2,1)S(1)}, u32[]{:S(2)}, u32[]{:S(2)}) %collective-permute-start.5) | collective-permute-done | bytes 98336 | tf_op jit(solution)/shard_map/ppermute | solution.py:65
  12.5 0.2 collective-permute-done.4.refs_5_.refs_2_
  12.7 0.0 collective-permute-done.2.refs_3_
  12.7 0.7 collective-permute-done.1.refs_2_
  13.4 0.0 collective-permute-done.refs_1_
  13.4 4.3 %collective-permute-start.6 = (bf16[4,512,128]{2,1,0:T(8,128)(2,1)S(1)}, bf16[4,512,128]{2,1,0:T(8,128)(2,1)S(1)}, u32[]{:S(2)}, u32[]{:S(2)}) collective-permute-start(bf16[4,512,128]{2,1,0:T(8,128)(2,1)S(1)} %shard_map.51.refs_0_), channel_id=1, source_target_pairs={{0,1},{1,0},{2,3},{3,2},{4,5},{5,4},{6,7},{7,6},{8,9},{9,8},{10,11... | collective-permute-start | bytes 1572872 | tf_op jit(solution)/shard_map/ppermute | solution.py:65
  17.7 1.9 %collective-permute-start.8 = (bf16[4,512,128]{2,1,0:T(8,128)(2,1)S(1)}, bf16[4,512,128]{2,1,0:T(8,128)(2,1)S(1)}, u32[]{:S(2)}, u32[]{:S(2)}) collective-permute-start(bf16[4,512,128]{2,1,0:T(8,128)(2,1)S(1)} %shard_map.51.refs_0_), channel_id=1, source_target_pairs={{0,96},{1,25},{2,98},{3,27},{4,100},{5,29},{6,102},{7,31},{8,104},... | collective-permute-start | bytes 1572872 | tf_op jit(solution)/shard_map/ppermute | solution.py:65
  19.6 1.7 %collective-permute-start.7 = (bf16[4,512,128]{2,1,0:T(8,128)(2,1)S(1)}, bf16[4,512,128]{2,1,0:T(8,128)(2,1)S(1)}, u32[]{:S(2)}, u32[]{:S(2)}) collective-permute-start(bf16[4,512,128]{2,1,0:T(8,128)(2,1)S(1)} %shard_map.51.refs_0_), channel_id=1, source_target_pairs={{0,32},{1,7},{2,34},{3,5},{4,36},{5,3},{6,38},{7,1},{8,40},{9,15},... | collective-permute-start | bytes 1572872 | tf_op jit(solution)/shard_map/ppermute | solution.py:65
  21.3 0.4 shard_map.52
  21.7 2.4 %shard_map.53 = (bf16[1536,1536]{1,0:T(8,128)(2,1)S(1)}, f32[32,1664]{1,0:T(8,128)S(1)}) custom-call(bf16[4,512,128]{2,1,0:T(8,128)(2,1)S(1)} %shard_map.51.refs_0_, bf16[128,1536]{1,0:T(8,128)(2,1)S(1)} %get-tuple-element.45.refs_1_.refs_2_, f32[8,1536]{1,0:T(8,128)S(1)} %get-tuple-element.46.refs_2_.refs_3_), custom_call_target="tpu_custom_call" | custom-call | flops 1207959552 | bytes 4718592 | tf_op jit(solution)/shard_map/pallas_call | solution.py:206
  24.1 0.0 collective-permute-done.6.refs_0_
  24.1 2.4 %shard_map.54 = (bf16[1536,1536]{1,0:T(8,128)(2,1)S(1)}, f32[32,1664]{1,0:T(8,128)S(1)}) custom-call(bf16[4,512,128]{2,1,0:T(8,128)(2,1)S(1)} %collective-permute-done.6.refs_0_, bf16[128,1536]{1,0:T(8,128)(2,1)S(1)} %get-tuple-element.45.refs_1_.refs_2_, f32[8,1536]{1,0:T(8,128)S(1)} %get-tuple-element.46.refs_2_.refs_3_, ...), custom_call_target="tpu_custom_call" | custom-call | flops 1207959552 | bytes 4718592 | tf_op jit(solution)/shard_map/pallas_call | solution.py:206
  26.5 0.8 collective-permute-done.8.refs_0_
  27.3 1.6 %collective-permute-done.7.refs_0_ = bf16[4,512,128]{2,1,0:T(8,128)(2,1)S(1)} collective-permute-done((bf16[4,512,128]{2,1,0:T(8,128)(2,1)S(1)}, bf16[4,512,128]{2,1,0:T(8,128)(2,1)S(1)}, u32[]{:S(2)}, u32[]{:S(2)}) %collective-permute-start.7) | collective-permute-done | bytes 524320 | tf_op jit(solution)/shard_map/ppermute | solution.py:65
  28.9 0.9 collective-permute-start.9
  29.8 0.0 collective-permute-start.10
  29.8 1.6 %collective-permute-start.11 = (bf16[4,512,128]{2,1,0:T(8,128)(2,1)S(1)}, bf16[4,512,128]{2,1,0:T(8,128)(2,1)S(1)}, u32[]{:S(2)}, u32[]{:S(2)}) collective-permute-start(bf16[4,512,128]{2,1,0:T(8,128)(2,1)S(1)} %collective-permute-done.8.refs_0_), channel_id=1, source_target_pairs={{0,32},{1,7},{2,34},{3,5},{4,36},{5,3},{6,38},{7,1},{8,40},{9,15},... | collective-permute-start | bytes 1572872 | tf_op jit(solution)/shard_map/ppermute | solution.py:65
  31.4 0.0 collective-permute-done.9.refs_1_
  31.4 4.8 %shard_map.55 = (bf16[3072,1536]{1,0:T(8,128)(2,1)S(1)}, f32[32,1664]{1,0:T(8,128)S(1)}) custom-call(bf16[4,512,128]{2,1,0:T(8,128)(2,1)S(1)} %collective-permute-done.7.refs_0_, bf16[4,512,128]{2,1,0:T(8,128)(2,1)S(1)} %collective-permute-done.9.refs_1_, bf16[128,1536]{1,0:T(8,128)(2,1)S(1)} %get-tuple-element.45.refs_1_.refs_2_, ...), custom_call_target="tpu_custom_call" | custom-call | flops 2415919104 | bytes 9437184 | tf_op jit(solution)/shard_map/pallas_call | solution.py:206
  36.2 0.0 collective-permute-done.10.refs_1_
  36.2 4.8 %shard_map.56 = (bf16[3072,1536]{1,0:T(8,128)(2,1)S(1)}, f32[32,1664]{1,0:T(8,128)S(1)}) custom-call(bf16[4,512,128]{2,1,0:T(8,128)(2,1)S(1)} %collective-permute-done.8.refs_0_, bf16[4,512,128]{2,1,0:T(8,128)(2,1)S(1)} %collective-permute-done.10.refs_1_, bf16[128,1536]{1,0:T(8,128)(2,1)S(1)} %get-tuple-element.45.refs_1_.refs_2_, ...), custom_call_target="tpu_custom_call" | custom-call | flops 2415919104 | bytes 9437184 | tf_op jit(solution)/shard_map/pallas_call | solution.py:206
  41.0 0.0 collective-permute-done.11.refs_0_
  41.0 0.3 collective-permute-start.12
  41.3 2.4 %shard_map.57 = (bf16[1536,1536]{1,0:T(8,128)(2,1)S(1)}, f32[32,1664]{1,0:T(8,128)S(1)}) custom-call(bf16[4,512,128]{2,1,0:T(8,128)(2,1)S(1)} %collective-permute-done.11.refs_0_, bf16[128,1536]{1,0:T(8,128)(2,1)S(1)} %get-tuple-element.45.refs_1_.refs_2_, f32[8,1536]{1,0:T(8,128)S(1)} %get-tuple-element.46.refs_2_.refs_3_, ...), custom_call_target="tpu_custom_call" | custom-call | flops 1207959552 | bytes 4718592 | tf_op jit(solution)/shard_map/pallas_call | solution.py:206
  43.7 0.0 collective-permute-done.12.refs_0_
  43.7 2.4 %shard_map.58 = (bf16[1536,1536]{1,0:T(8,128)(2,1)S(1)}, f32[32,512]{1,0:T(8,128)S(1)}, f32[32,512]{1,0:T(8,128)S(1)}, f32[32,512]{1,0:T(8,128)S(1)}, f32[32,512]{1,0:T(8,128)S(1)}) custom-call(bf16[4,512,128]{2,1,0:T(8,128)(2,1)S(1)} %collective-permute-done.12.refs_0_, bf16[128,1536]{1,0:T(8,128)(2,1)S(1)} %get-tuple-element.45.refs_1_.refs_2_, ...), custom_call_target="tpu_custom_call" | custom-call | flops 1207959552 | bytes 4718592 | tf_op jit(solution)/shard_map/pallas_call | solution.py:206
  46.1 0.9 collective-permute-start.13
  47.0 1.8 %collective-permute-start.14 = (f32[32,512]{1,0:T(8,128)S(1)}, f32[32,512]{1,0:T(8,128)S(1)}, u32[]{:S(2)}, u32[]{:S(2)}) collective-permute-start(f32[32,512]{1,0:T(8,128)S(1)} %get-tuple-element.63), channel_id=1, source_target_pairs={{0,2},{1,3},{2,0},{3,1},{4,6},{5,7},{6,4},{7,5},{8,10},{9,11},{10,... | collective-permute-start | bytes 196616 | tf_op jit(solution)/shard_map/ppermute | solution.py:65
  48.8 0.0 collective-permute-start.15
  48.8 1.4 %collective-permute-done.13.refs_1_ = f32[32,512]{1,0:T(8,128)S(1)} collective-permute-done((f32[32,512]{1,0:T(8,128)S(1)}, f32[32,512]{1,0:T(8,128)S(1)}, u32[]{:S(2)}, u32[]{:S(2)}) %collective-permute-start.13) | collective-permute-done | bytes 65568 | tf_op jit(solution)/shard_map/ppermute | solution.py:65
  50.2 2.3 %collective-permute-done.14.refs_2_ = f32[32,512]{1,0:T(8,128)S(1)} collective-permute-done((f32[32,512]{1,0:T(8,128)S(1)}, f32[32,512]{1,0:T(8,128)S(1)}, u32[]{:S(2)}, u32[]{:S(2)}) %collective-permute-start.14) | collective-permute-done | bytes 65568 | tf_op jit(solution)/shard_map/ppermute | solution.py:65
  52.5 0.0 collective-permute-done.15.refs_3_
  52.5 0.2 shard_map.59
  52.7 20.5 %all_to_all.10.refs_4_.refs_6_ = bf16[16,32,896]{2,1,0:T(8,128)(2,1)S(1)} all-to-all(bf16[16,32,896]{2,1,0:T(8,128)(2,1)S(1)} %get-tuple-element.67), channel_id=1, replica_groups={{0,6,24,30,32,38,56,62,64,70,88,94,96,102,120,126},{1,7,25,31,33,39,57,..., dimensions={0} | all-to-all | bytes 1835008 | tf_op jit(solution)/shard_map/all_to_all | solution.py:77
  73.2 3.0 %collective-permute-start.16 = (bf16[16,32,896]{2,1,0:T(8,128)(2,1)S(1)}, bf16[16,32,896]{2,1,0:T(8,128)(2,1)S(1)}, u32[]{:S(2)}, u32[]{:S(2)}) collective-permute-start(bf16[16,32,896]{2,1,0:T(8,128)(2,1)S(1)} %all_to_all.10.refs_4_.refs_6_), channel_id=1, source_target_pairs={{0,1},{1,0},{2,3},{3,2},{4,5},{5,4},{6,7},{7,6},{8,9},{9,8},{10,11... | collective-permute-start | bytes 2752520 | tf_op jit(solution)/shard_map/ppermute | solution.py:65
  76.2 3.3 %shard_map.60.refs_5_ = f32[32,1536]{1,0:T(8,128)S(1)} custom-call(bf16[1536,1536]{1,0:T(8,128)(2,1)S(1)} %get-tuple-element.68.refs_0_, bf16[3072,1536]{1,0:T(8,128)(2,1)S(1)} %get-tuple-element.52.refs_1_, bf16[3072,1536]{1,0:T(8,128)(2,1)S(1)} %get-tuple-element.55.refs_2_, bf16[1536,1536]{1,0:T(8,128)(2,1)S(1)} %get-tuple-element.69.refs_3_, ...), custom_call_target="tpu_custom_call" | custom-call | flops 4831838208 | bytes 18874368 | tf_op jit(solution)/shard_map/pallas_call | solution.py:231
  79.5 0.0 collective-permute-done.16.refs_4_
  79.5 3.4 %shard_map.61 = (f32[32,512]{1,0:T(8,128)S(1)}, f32[32,512]{1,0:T(8,128)S(1)}, f32[32,512]{1,0:T(8,128)S(1)}, f32[32,512]{1,0:T(8,128)S(1)}) custom-call(bf16[1536,1536]{1,0:T(8,128)(2,1)S(1)} %get-tuple-element.48.refs_0_, bf16[3072,1536]{1,0:T(8,128)(2,1)S(1)} %get-tuple-element.52.refs_1_, bf16[3072,1536]{1,0:T(8,128)(2,1)S(1)} %get-tuple-element.55.refs_2_, ...), custom_call_target="tpu_custom_call" | custom-call | flops 4831838208 | bytes 18874368 | tf_op jit(solution)/shard_map/pallas_call | solution.py:231
  82.9 0.0 collective-permute-start.17
  82.9 0.1 collective-permute-start.18
  83.0 2.6 %collective-permute-start.19 = (f32[32,512]{1,0:T(8,128)S(1)}, f32[32,512]{1,0:T(8,128)S(1)}, u32[]{:S(2)}, u32[]{:S(2)}) collective-permute-start(f32[32,512]{1,0:T(8,128)S(1)} %get-tuple-element.73), channel_id=1, source_target_pairs={{0,8},{1,9},{2,10},{3,11},{4,12},{5,13},{6,14},{7,15},{8,0},{9,1},... | collective-permute-start | bytes 196616 | tf_op jit(solution)/shard_map/ppermute | solution.py:65
  85.5 2.0 %collective-permute-done.17.refs_1_ = f32[32,512]{1,0:T(8,128)S(1)} collective-permute-done((f32[32,512]{1,0:T(8,128)S(1)}, f32[32,512]{1,0:T(8,128)S(1)}, u32[]{:S(2)}, u32[]{:S(2)}) %collective-permute-start.17) | collective-permute-done | bytes 65568 | tf_op jit(solution)/shard_map/ppermute | solution.py:65
  87.5 0.3 collective-permute-done.18.refs_2_
  87.9 0.0 collective-permute-done.19.refs_3_
  87.9 0.4 shard_map.62
  88.3 14.4 %all_to_all.11 = f32[128,1,32]{2,1,0:T(1,128)S(1)} all-to-all(f32[128,1,32]{2,1,0:T(1,128)S(1)} %bitcast.8), channel_id=1, replica_groups=mesh['pts'=128] {'pts'}, dimensions={0} | all-to-all | bytes 32768 | tf_op jit(solution)/shard_map/all_to_all | solution.py:468
  102.7 0.8 shard_map.63
  (1 shorter events, 0.0 us)
Async XLA Ops:
  0.6 8.1 %collective-permute-start.3 = (bf16[384,128]{1,0:T(8,128)(2,1)}, bf16[384,128]{1,0:T(8,128)(2,1)S(1)}, u32[]{:S(2)}, u32[]{:S(2)}) collective-permute-start(bf16[384,128]{1,0:T(8,128)(2,1)} %points_ref.1), channel_id=1, source_target_pairs={{0,10},{1,11},{2,8},{3,9},{4,14},{5,15},{6,12},{7,13},{8,2},{9,3},... | collective-permute-start | bytes 294920 | tf_op jit(solution)/shard_map/ppermute | solution.py:65
  5.2 7.5 %collective-permute-start.2 = (bf16[512,128]{1,0:T(8,128)(2,1)S(1)}, bf16[512,128]{1,0:T(8,128)(2,1)S(1)}, u32[]{:S(2)}, u32[]{:S(2)}) collective-permute-start(bf16[512,128]{1,0:T(8,128)(2,1)S(1)} %get-tuple-element.44.refs_0_), channel_id=1, source_target_pairs={{0,30},{1,97},{2,28},{3,99},{4,26},{5,101},{6,24},{7,103},{8,22},{... | collective-permute-start | bytes 393224 | tf_op jit(solution)/shard_map/ppermute | solution.py:65
  7.8 5.6 %collective-permute-start.1 = (bf16[512,128]{1,0:T(8,128)(2,1)S(1)}, bf16[512,128]{1,0:T(8,128)(2,1)S(1)}, u32[]{:S(2)}, u32[]{:S(2)}) collective-permute-start(bf16[512,128]{1,0:T(8,128)(2,1)S(1)} %get-tuple-element.44.refs_0_), channel_id=1, source_target_pairs={{0,24},{1,65},{2,26},{3,67},{4,28},{5,69},{6,30},{7,71},{8,16},{9,... | collective-permute-start | bytes 393224 | tf_op jit(solution)/shard_map/ppermute | solution.py:65
  8.3 5.1 %collective-permute-start = (bf16[512,128]{1,0:T(8,128)(2,1)S(1)}, bf16[512,128]{1,0:T(8,128)(2,1)S(1)}, u32[]{:S(2)}, u32[]{:S(2)}) collective-permute-start(bf16[512,128]{1,0:T(8,128)(2,1)S(1)} %get-tuple-element.44.refs_0_), channel_id=1, source_target_pairs={{0,6},{1,33},{2,4},{3,35},{4,2},{5,37},{6,0},{7,39},{8,14},{9,41},... | collective-permute-start | bytes 393224 | tf_op jit(solution)/shard_map/ppermute | solution.py:65
  8.5 4.0 %collective-permute-start.5 = (bf16[384,128]{1,0:T(8,128)(2,1)}, bf16[384,128]{1,0:T(8,128)(2,1)S(1)}, u32[]{:S(2)}, u32[]{:S(2)}) collective-permute-start(bf16[384,128]{1,0:T(8,128)(2,1)} %points_ref.1), channel_id=1, source_target_pairs={{0,8},{1,9},{2,10},{3,11},{4,12},{5,13},{6,14},{7,15},{8,0},{9,1},... | collective-permute-start | bytes 294920 | tf_op jit(solution)/shard_map/ppermute | solution.py:65
  8.7 4.0 %collective-permute-start.4 = (bf16[384,128]{1,0:T(8,128)(2,1)}, bf16[384,128]{1,0:T(8,128)(2,1)S(1)}, u32[]{:S(2)}, u32[]{:S(2)}) collective-permute-start(bf16[384,128]{1,0:T(8,128)(2,1)} %points_ref.1), channel_id=1, source_target_pairs={{0,2},{1,3},{2,0},{3,1},{4,6},{5,7},{6,4},{7,5},{8,10},{9,11},{10,... | collective-permute-start | bytes 294920 | tf_op jit(solution)/shard_map/ppermute | solution.py:65
  13.4 10.7 %collective-permute-start.6 = (bf16[4,512,128]{2,1,0:T(8,128)(2,1)S(1)}, bf16[4,512,128]{2,1,0:T(8,128)(2,1)S(1)}, u32[]{:S(2)}, u32[]{:S(2)}) collective-permute-start(bf16[4,512,128]{2,1,0:T(8,128)(2,1)S(1)} %shard_map.51.refs_0_), channel_id=1, source_target_pairs={{0,1},{1,0},{2,3},{3,2},{4,5},{5,4},{6,7},{7,6},{8,9},{9,8},{10,11... | collective-permute-start | bytes 1572872 | tf_op jit(solution)/shard_map/ppermute | solution.py:65
  17.7 9.5 %collective-permute-start.8 = (bf16[4,512,128]{2,1,0:T(8,128)(2,1)S(1)}, bf16[4,512,128]{2,1,0:T(8,128)(2,1)S(1)}, u32[]{:S(2)}, u32[]{:S(2)}) collective-permute-start(bf16[4,512,128]{2,1,0:T(8,128)(2,1)S(1)} %shard_map.51.refs_0_), channel_id=1, source_target_pairs={{0,96},{1,25},{2,98},{3,27},{4,100},{5,29},{6,102},{7,31},{8,104},... | collective-permute-start | bytes 1572872 | tf_op jit(solution)/shard_map/ppermute | solution.py:65
  19.6 9.2 %collective-permute-start.7 = (bf16[4,512,128]{2,1,0:T(8,128)(2,1)S(1)}, bf16[4,512,128]{2,1,0:T(8,128)(2,1)S(1)}, u32[]{:S(2)}, u32[]{:S(2)}) collective-permute-start(bf16[4,512,128]{2,1,0:T(8,128)(2,1)S(1)} %shard_map.51.refs_0_), channel_id=1, source_target_pairs={{0,32},{1,7},{2,34},{3,5},{4,36},{5,3},{6,38},{7,1},{8,40},{9,15},... | collective-permute-start | bytes 1572872 | tf_op jit(solution)/shard_map/ppermute | solution.py:65
  28.9 2.5 %collective-permute-start.9 = (bf16[4,512,128]{2,1,0:T(8,128)(2,1)S(1)}, bf16[4,512,128]{2,1,0:T(8,128)(2,1)S(1)}, u32[]{:S(2)}, u32[]{:S(2)}) collective-permute-start(bf16[4,512,128]{2,1,0:T(8,128)(2,1)S(1)} %collective-permute-done.7.refs_0_), channel_id=1, source_target_pairs={{0,1},{1,0},{2,3},{3,2},{4,5},{5,4},{6,7},{7,6},{8,9},{9,8},{10,11... | collective-permute-start | bytes 1572872 | tf_op jit(solution)/shard_map/ppermute | solution.py:65
  29.8 6.4 %collective-permute-start.10 = (bf16[4,512,128]{2,1,0:T(8,128)(2,1)S(1)}, bf16[4,512,128]{2,1,0:T(8,128)(2,1)S(1)}, u32[]{:S(2)}, u32[]{:S(2)}) collective-permute-start(bf16[4,512,128]{2,1,0:T(8,128)(2,1)S(1)} %collective-permute-done.8.refs_0_), channel_id=1, source_target_pairs={{0,1},{1,0},{2,3},{3,2},{4,5},{5,4},{6,7},{7,6},{8,9},{9,8},{10,11... | collective-permute-start | bytes 1572872 | tf_op jit(solution)/shard_map/ppermute | solution.py:65
  29.8 11.2 %collective-permute-start.11 = (bf16[4,512,128]{2,1,0:T(8,128)(2,1)S(1)}, bf16[4,512,128]{2,1,0:T(8,128)(2,1)S(1)}, u32[]{:S(2)}, u32[]{:S(2)}) collective-permute-start(bf16[4,512,128]{2,1,0:T(8,128)(2,1)S(1)} %collective-permute-done.8.refs_0_), channel_id=1, source_target_pairs={{0,32},{1,7},{2,34},{3,5},{4,36},{5,3},{6,38},{7,1},{8,40},{9,15},... | collective-permute-start | bytes 1572872 | tf_op jit(solution)/shard_map/ppermute | solution.py:65
  41.0 2.7 %collective-permute-start.12 = (bf16[4,512,128]{2,1,0:T(8,128)(2,1)S(1)}, bf16[4,512,128]{2,1,0:T(8,128)(2,1)S(1)}, u32[]{:S(2)}, u32[]{:S(2)}) collective-permute-start(bf16[4,512,128]{2,1,0:T(8,128)(2,1)S(1)} %collective-permute-done.11.refs_0_), channel_id=1, source_target_pairs={{0,1},{1,0},{2,3},{3,2},{4,5},{5,4},{6,7},{7,6},{8,9},{9,8},{10,11... | collective-permute-start | bytes 1572872 | tf_op jit(solution)/shard_map/ppermute | solution.py:65
  46.1 4.1 %collective-permute-start.13 = (f32[32,512]{1,0:T(8,128)S(1)}, f32[32,512]{1,0:T(8,128)S(1)}, u32[]{:S(2)}, u32[]{:S(2)}) collective-permute-start(f32[32,512]{1,0:T(8,128)S(1)} %get-tuple-element.62), channel_id=1, source_target_pairs={{0,10},{1,11},{2,8},{3,9},{4,14},{5,15},{6,12},{7,13},{8,2},{9,3},... | collective-permute-start | bytes 196616 | tf_op jit(solution)/shard_map/ppermute | solution.py:65
  47.0 5.4 %collective-permute-start.14 = (f32[32,512]{1,0:T(8,128)S(1)}, f32[32,512]{1,0:T(8,128)S(1)}, u32[]{:S(2)}, u32[]{:S(2)}) collective-permute-start(f32[32,512]{1,0:T(8,128)S(1)} %get-tuple-element.63), channel_id=1, source_target_pairs={{0,2},{1,3},{2,0},{3,1},{4,6},{5,7},{6,4},{7,5},{8,10},{9,11},{10,... | collective-permute-start | bytes 196616 | tf_op jit(solution)/shard_map/ppermute | solution.py:65
  48.8 3.7 %collective-permute-start.15 = (f32[32,512]{1,0:T(8,128)S(1)}, f32[32,512]{1,0:T(8,128)S(1)}, u32[]{:S(2)}, u32[]{:S(2)}) collective-permute-start(f32[32,512]{1,0:T(8,128)S(1)} %get-tuple-element.64), channel_id=1, source_target_pairs={{0,8},{1,9},{2,10},{3,11},{4,12},{5,13},{6,14},{7,15},{8,0},{9,1},... | collective-permute-start | bytes 196616 | tf_op jit(solution)/shard_map/ppermute | solution.py:65
  73.2 6.3 %collective-permute-start.16 = (bf16[16,32,896]{2,1,0:T(8,128)(2,1)S(1)}, bf16[16,32,896]{2,1,0:T(8,128)(2,1)S(1)}, u32[]{:S(2)}, u32[]{:S(2)}) collective-permute-start(bf16[16,32,896]{2,1,0:T(8,128)(2,1)S(1)} %all_to_all.10.refs_4_.refs_6_), channel_id=1, source_target_pairs={{0,1},{1,0},{2,3},{3,2},{4,5},{5,4},{6,7},{7,6},{8,9},{9,8},{10,11... | collective-permute-start | bytes 2752520 | tf_op jit(solution)/shard_map/ppermute | solution.py:65
  82.9 4.7 %collective-permute-start.17 = (f32[32,512]{1,0:T(8,128)S(1)}, f32[32,512]{1,0:T(8,128)S(1)}, u32[]{:S(2)}, u32[]{:S(2)}) collective-permute-start(f32[32,512]{1,0:T(8,128)S(1)} %get-tuple-element.71), channel_id=1, source_target_pairs={{0,10},{1,11},{2,8},{3,9},{4,14},{5,15},{6,12},{7,13},{8,2},{9,3},... | collective-permute-start | bytes 196616 | tf_op jit(solution)/shard_map/ppermute | solution.py:65
  82.9 5.0 %collective-permute-start.18 = (f32[32,512]{1,0:T(8,128)S(1)}, f32[32,512]{1,0:T(8,128)S(1)}, u32[]{:S(2)}, u32[]{:S(2)}) collective-permute-start(f32[32,512]{1,0:T(8,128)S(1)} %get-tuple-element.72), channel_id=1, source_target_pairs={{0,2},{1,3},{2,0},{3,1},{4,6},{5,7},{6,4},{7,5},{8,10},{9,11},{10,... | collective-permute-start | bytes 196616 | tf_op jit(solution)/shard_map/ppermute | solution.py:65
  83.0 4.9 %collective-permute-start.19 = (f32[32,512]{1,0:T(8,128)S(1)}, f32[32,512]{1,0:T(8,128)S(1)}, u32[]{:S(2)}, u32[]{:S(2)}) collective-permute-start(f32[32,512]{1,0:T(8,128)S(1)} %get-tuple-element.73), channel_id=1, source_target_pairs={{0,8},{1,9},{2,10},{3,11},{4,12},{5,13},{6,14},{7,15},{8,0},{9,1},... | collective-permute-start | bytes 196616 | tf_op jit(solution)/shard_map/ppermute | solution.py:65

commit v5 on v4

--- a/solution.py
+++ b/solution.py
@@ -17,8 +17,6 @@
 SIDE = 1 << len(SIDE_MASKS)
 EVEN_LINES = (0, 1, 3, 2)
 ODD_LINES = (0, 1, 2, 3)
-TURNS = 4
-CHIPS = SIDE * TURNS
 PAIR = 2
 UNROLL = 2
 LANES = 128
@@ -42,23 +40,6 @@
     return mask
 
 
-def chip_groups():
-    groups, seen = [], set()
-    for base in range(DEVICES):
-        if base not in seen:
-            group = [base ^ reach(SIDE_MASKS + LINE_MASKS, k) for k in range(CHIPS)]
-            groups.append(group)
-            seen.update(group)
-    return groups
-
-
-def place_in_group(index):
-    place = 0
-    for bit, mask in enumerate(SIDE_MASKS + LINE_MASKS):
-        place += lax.rem(lax.div(index, 1 << (mask.bit_length() - 1)), 2) << bit
-    return place
-
-
 def partner(value, even, odd=None):
     odd = even if odd is None else odd
     pairs = [(k, k ^ (odd if k & CORE_MASK else even)) for k in range(DEVICES)]
@@ -71,10 +52,6 @@
 
 def line_masks(turn):
     return reach(LINE_MASKS, EVEN_LINES[turn]), reach(SIDE_MASKS, ODD_LINES[turn])
-
-
-def share(copies):
-    return lax.all_to_all(copies, "pts", 0, 0, axis_index_groups=chip_groups())
 
 
 def small_call(body, shapes, *args):
@@ -147,48 +124,43 @@
                 )
 
     if ending:
-        for k, ref in enumerate(refs[-2 - NEAR : -2]):
-            ref[:, :rows] = sum_ref[:, pl.ds(k * rows, rows)]
-            ref[:, rows:] = sum_ref[:, width:]
-
-
-def second_product(rows, core, starts, *refs):
-    kerns = refs[:TURNS]
-    blocks_ref = refs[TURNS]
-    vec_ref, total_ref = refs[-2:]
-    cols = total_ref.shape[0]
-    index = lax.axis_index("pts")
-    place = place_in_group(index)
-    odd = lax.rem(index, 2)
-    for n in range(TURNS):
+        write_parts(rows, width, sum_ref, refs[-2 - NEAR : -2])
+
+
+def write_parts(rows, width, sum_ref, outs):
+    for k, ref in enumerate(outs):
+        ref[:, :rows] = sum_ref[:, pl.ds(k * rows, rows)]
+        ref[:, rows:] = sum_ref[:, width:]
+
+
+def second_product(rows, starts, ending, *refs):
+    count = len(starts)
+    blocks, pieces = refs[:count], refs[count : 2 * count]
+    vec_ref = refs[-1]
+    sum_ref = refs[-2]
+    cols = sum_ref.shape[0]
+    width = pieces[0].shape[1]
+    last_ref = None if len(refs) == 2 * count + 2 else refs[2 * count]
+    lanes = jnp.zeros((cols, LANES), jnp.float32) if last_ref is None else last_ref[:, width:]
+    for n, ref in enumerate(blocks):
         for side in range(SIDE):
-            even_slot = side + SIDE * EVEN_LINES[n]
-            odd_slot = SIDE * side + ODD_LINES[n]
-            slot = jnp.bitwise_xor(place, jnp.where(odd == core, even_slot, odd_slot))
             part = pl.ds(side * rows, rows)
-            vec_ref[n, :cols, part] = blocks_ref[slot, :, pl.ds(0, rows)]
-            vec_ref[n, cols:, part] = blocks_ref[slot, :, pl.ds(rows, rows)]
-    for c in range(total_ref.shape[1] // CHUNK):
+            vec_ref[n, :cols, part] = ref[side, :, pl.ds(0, rows)]
+            vec_ref[n, cols:, part] = ref[side, :, pl.ds(rows, rows)]
+            lanes += ref[side, :, 2 * rows :].astype(jnp.float32)
+    sum_ref[:, width:] = lanes
+    for c in range(width // CHUNK):
         part = pl.ds(c * CHUNK, CHUNK)
         value = jnp.zeros((2 * cols, CHUNK), jnp.float32)
-        for n, ref in enumerate(kerns):
+        for n, ref in enumerate(pieces):
             tile = ref[pl.ds(starts[n], SIDE * rows), part]
             value += jnp.dot(vec_ref[n], tile, preferred_element_type=jnp.float32)
         value = value[:cols] + value[cols:]
-        if core == 1:
-            value += refs[TURNS + 1][:, part]
-        total_ref[:, part] = value
-    if core == 0:
-        refs[-3][...] = total_ref[...]
-    else:
-        other_ref = refs[TURNS + 2]
-        lanes = jnp.zeros((total_ref.shape[0], LANES), jnp.float32)
-        for k in range(CHIPS):
-            lanes += blocks_ref[k, :, 2 * rows :].astype(jnp.float32)
-            lanes += other_ref[k, :, 2 * rows :].astype(jnp.float32)
-        for k, ref in enumerate(refs[TURNS + 3 : TURNS + 3 + NEAR]):
-            ref[:, :rows] = total_ref[:, pl.ds(k * rows, rows)]
-            ref[:, rows:] = lanes
+        if last_ref is not None:
+            value += last_ref[:, part]
+        sum_ref[:, part] = value
+    if ending:
+        write_parts(rows, width, sum_ref, refs[-2 - NEAR : -2])
 
 
 def run_first(far, near, half, last, rows, cols, ending=False):
@@ -218,29 +190,30 @@
     )(*inputs)
 
 
-def run_second(core, pieces, blocks, rows, *others):
+def run_second(blocks, pieces, last, rows, ending=False):
     width = pieces[0][0].shape[1]
-    cols = blocks.shape[1]
+    cols = blocks[0].shape[1]
     starts = [start for _, start in pieces]
     kerns = [pltpu.with_memory_space_constraint(kern, pltpu.VMEM) for kern, _ in pieces]
-    inputs = kerns + [blocks] + list(others)
-    if core == 0:
-        outs = [jax.ShapeDtypeStruct((cols, width), jnp.float32)]
+    inputs = list(blocks) + kerns + ([] if last is None else [last])
+    running = (cols, width + LANES)
+    if ending:
+        outs = [jax.ShapeDtypeStruct((cols, rows + LANES), jnp.float32)] * NEAR
+        scratch = [pltpu.VMEM(running, jnp.float32)]
     else:
-        outs = [jax.ShapeDtypeStruct((cols, rows + LANES), jnp.float32)] * NEAR
+        outs = [jax.ShapeDtypeStruct(running, jnp.float32)]
+        scratch = []
+    count = len(blocks) * SIDE * rows
     return pl.pallas_call(
-        functools.partial(second_product, rows, core, starts),
+        functools.partial(second_product, rows, starts, ending),
         in_specs=[INSIDE] * len(inputs),
         out_specs=[INSIDE] * len(outs),
         out_shape=outs,
-        scratch_shapes=[
-            pltpu.VMEM((TURNS, 2 * cols, SIDE * rows), jnp.bfloat16),
-            pltpu.VMEM((cols, width), jnp.float32),
-        ],
+        scratch_shapes=scratch + [pltpu.VMEM((len(blocks), 2 * cols, SIDE * rows), jnp.bfloat16)],
         compiler_params=pltpu.CompilerParams(vmem_limit_bytes=LIMIT),
         cost_estimate=pl.CostEstimate(
-            flops=2 * TURNS * SIDE * rows * width * 8 * cols,
-            bytes_accessed=2 * TURNS * SIDE * rows * width,
+            flops=2 * count * width * 8 * cols,
+            bytes_accessed=2 * count * width,
             transcendentals=0,
         ),
     )(*inputs)
@@ -345,7 +318,7 @@
 
 
 def middle(*refs):
-    noisy_ref, rhs_ref, image_ref, rest_ref, known_ref, copies_ref = refs[NEAR:]
+    noisy_ref, rhs_ref, image_ref, rest_ref, known_ref, packed_ref = refs[NEAR:]
     rhs = rhs_ref[...]
     rows = rhs.shape[1]
     total = refs[0][...]
@@ -362,9 +335,7 @@
     lanes = spread_lanes((row_sum(rhs * rest), row_sum(rest * rest)), known_ref.shape)
     high = rest.astype(jnp.bfloat16)
     low = (rest - high.astype(jnp.float32)).astype(jnp.bfloat16)
-    packed = jnp.concatenate([high, low, lanes], axis=1)
-    for k in range(copies_ref.shape[0]):
-        copies_ref[k] = packed
+    packed_ref[...] = jnp.concatenate([high, low, lanes], axis=1)
 
 
 def closing(*refs):
@@ -440,21 +411,33 @@
     across = partner(third, CORE_MASK)
     half_c, total = first_call([third], total)
     half_d, *parts = first_call([across], total, True)
-    skip = SIDE * rows
-    own_pieces = [(half_a, 0), (pair_a, 0), (pair_b, 0), (half_c, 0)]
-    other_pieces = [(half_b, 0), (pair_a, skip), (pair_b, skip), (half_d, 0)]
-
-    image, rest, known, copies = small_call(
+
+    wide_shape = ((cols, 2 * rows + LANES), jnp.bfloat16)
+    image, rest, known, packed = small_call(
         middle,
-        [field_shape, field_shape, lanes_shape, ((CHIPS, cols, 2 * rows + LANES), jnp.bfloat16)],
+        [field_shape, field_shape, lanes_shape, wide_shape],
         *exchange(parts, NEAR_MASKS),
         noisy,
         rhs,
     )
-    copies = share(copies)
-    other = partner(copies, CORE_MASK)
-    half_total = run_second(0, own_pieces, copies, rows)[0]
-    parts = run_second(1, other_pieces, other, rows, half_total, copies)
+    side = [packed]
+    for k in range(1, SIDE):
+        side.append(partner(packed, reach(SIDE_MASKS, k), reach(LINE_MASKS, k)))
+    own = run_bundle(side, [])
+    across = partner(own, CORE_MASK)
+    first, second = [partner(own, *line_masks(turn)) for turn in (1, 2)]
+    skip = SIDE * rows
+    total = run_second([own], [(half_a, 0)], None, rows)[0]
+    total = run_second([across], [(half_b, 0)], total, rows)[0]
+    first, second, total = lax.optimization_barrier((first, second, total))
+    third = partner(second, *line_masks(1))
+    across = [partner(item, CORE_MASK) for item in (first, second)]
+    total = run_second([first, second], [(pair_a, 0), (pair_b, 0)], total, rows)[0]
+    total = run_second(across, [(pair_a, skip), (pair_b, skip)], total, rows)[0]
+    third, total = lax.optimization_barrier((third, total))
+    across = partner(third, CORE_MASK)
+    total = run_second([third], [(half_c, 0)], total, rows)[0]
+    parts = run_second([across], [(half_d, 0)], total, rows, True)
     field, residual, direction, image_dir, norm_next, curve = small_call(
         closing,
         [field_shape] * 4 + [lanes_shape, ((DEVICES, cols), jnp.float32)],

time: 104 us -> 104 us (level)
  blocking collectives: 34.9 us -> 16.4 us
  starting transfers between devices: 26.3 us -> 36.8 us
  waiting for transfers between devices: 13 us -> 20.7 us
    all_to_all x1 -> x0, blocking collectives: 20.5 us -> none  [share(): return lax.all_to_all(copies, 'pts', 0, 0, axis_index_groups=chip_groups())]
    ppermute x20 -> x29, starting transfers between devices: 26.3 us -> 36.8 us  [partner(): return lax.ppermute(value, 'pts', pairs)]
    ppermute x20 -> x29, waiting for transfers between devices: 13 us -> 20.7 us  [partner(): return lax.ppermute(value, 'pts', pairs)]
    all_to_all x1, blocking collectives: 14.4 us -> 16.4 us  [per_device(): lax.all_to_all(curve[:, None, :], 'pts', 0, 0).reshape(DEVICES, cols)]
    pallas_call x2 -> x6, Pallas kernels: 6.7 us -> 7.1 us  [run_second(): pl.pallas_call(functools.partial(second_product, rows, starts, ending), i...]
  transfers between devices with their start and end apart: 20 -> 29, of which waited for: 9 -> 15; matrix products, arithmetic and copies ran while one was open for 0% -> 0% of each run, Pallas kernels for 21% -> 23%
where the time goes in v5:
time: 104 us
  starting transfers between devices  36.8 us (35%)
  Pallas kernels  29 us (28%)
  waiting for transfers between devices  20.7 us (20%)
  blocking collectives  16.4 us (16%)
    ppermute x29, starting transfers between devices, partner(): return lax.ppermute(value, 'pts', pairs)  36.8 us
    ppermute x29, waiting for transfers between devices, partner(): return lax.ppermute(value, 'pts', pairs)  20.7 us
    pallas_call x6, Pallas kernels, run_first(): pl.pallas_call(functools.partial(first_product, scale_of(feats), rows, le...  19 us
    all_to_all x1, blocking collectives, per_device(): lax.all_to_all(curve[:, None, :], 'pts', 0, 0).reshape(DEVICES, cols)  16.4 us
    pallas_call x6, Pallas kernels, run_second(): pl.pallas_call(functools.partial(second_product, rows, starts, ending), i...  7.1 us
  transfers between devices with their start and end apart: 29, of which 15 were waited for; matrix products, arithmetic and copies ran while one was open for 0% of the time, Pallas kernels for 23%

profile of v5, /device:TPU:1, one launch (start us, length us, event | category | flops | bytes accessed | tf_op | source)
XLA Modules:
  0.0 103.6 jit_solution(8702360030044339097)
XLA Ops:
  0.6 3.6 %collective-permute-start.3 = (bf16[384,128]{1,0:T(8,128)(2,1)}, bf16[384,128]{1,0:T(8,128)(2,1)S(1)}, u32[]{:S(2)}, u32[]{:S(2)}) collective-permute-start(bf16[384,128]{1,0:T(8,128)(2,1)} %points_ref.1), channel_id=1, source_target_pairs={{0,10},{1,11},{2,8},{3,9},{4,14},{5,15},{6,12},{7,13},{8,2},{9,3},... | collective-permute-start | bytes 294920 | tf_op jit(solution)/shard_map/ppermute | solution.py:46
  4.2 1.0 shard_map.50
  5.2 2.6 %collective-permute-start.2 = (bf16[512,128]{1,0:T(8,128)(2,1)S(1)}, bf16[512,128]{1,0:T(8,128)(2,1)S(1)}, u32[]{:S(2)}, u32[]{:S(2)}) collective-permute-start(bf16[512,128]{1,0:T(8,128)(2,1)S(1)} %get-tuple-element.49.refs_0_), channel_id=1, source_target_pairs={{0,30},{1,97},{2,28},{3,99},{4,26},{5,101},{6,24},{7,103},{8,22},{... | collective-permute-start | bytes 393224 | tf_op jit(solution)/shard_map/ppermute | solution.py:46
  7.8 0.5 collective-permute-start.1
  8.3 0.3 collective-permute-start
  8.5 0.2 collective-permute-start.5
  8.7 0.1 collective-permute-start.4
  8.8 3.7 %collective-permute-done.5.refs_6_.refs_3_ = bf16[384,128]{1,0:T(8,128)(2,1)S(1)} collective-permute-done((bf16[384,128]{1,0:T(8,128)(2,1)}, bf16[384,128]{1,0:T(8,128)(2,1)S(1)}, u32[]{:S(2)}, u32[]{:S(2)}) %collective-permute-start.5) | collective-permute-done | bytes 98336 | tf_op jit(solution)/shard_map/ppermute | solution.py:46
  12.5 0.2 collective-permute-done.4.refs_5_.refs_2_
  12.7 0.0 collective-permute-done.2.refs_3_
  12.7 0.7 collective-permute-done.1.refs_2_
  13.4 4.3 %collective-permute-start.8 = (bf16[4,512,128]{2,1,0:T(8,128)(2,1)S(1)}, bf16[4,512,128]{2,1,0:T(8,128)(2,1)S(1)}, u32[]{:S(2)}, u32[]{:S(2)}) collective-permute-start(bf16[4,512,128]{2,1,0:T(8,128)(2,1)S(1)} %shard_map.51.refs_0_), channel_id=1, source_target_pairs={{0,1},{1,0},{2,3},{3,2},{4,5},{5,4},{6,7},{7,6},{8,9},{9,8},{10,11... | collective-permute-start | bytes 1572872 | tf_op jit(solution)/shard_map/ppermute | solution.py:46
  17.7 1.9 %collective-permute-start.7 = (bf16[4,512,128]{2,1,0:T(8,128)(2,1)S(1)}, bf16[4,512,128]{2,1,0:T(8,128)(2,1)S(1)}, u32[]{:S(2)}, u32[]{:S(2)}) collective-permute-start(bf16[4,512,128]{2,1,0:T(8,128)(2,1)S(1)} %shard_map.51.refs_0_), channel_id=1, source_target_pairs={{0,96},{1,25},{2,98},{3,27},{4,100},{5,29},{6,102},{7,31},{8,104},... | collective-permute-start | bytes 1572872 | tf_op jit(solution)/shard_map/ppermute | solution.py:46
  19.6 1.7 %collective-permute-start.6 = (bf16[4,512,128]{2,1,0:T(8,128)(2,1)S(1)}, bf16[4,512,128]{2,1,0:T(8,128)(2,1)S(1)}, u32[]{:S(2)}, u32[]{:S(2)}) collective-permute-start(bf16[4,512,128]{2,1,0:T(8,128)(2,1)S(1)} %shard_map.51.refs_0_), channel_id=1, source_target_pairs={{0,32},{1,7},{2,34},{3,5},{4,36},{5,3},{6,38},{7,1},{8,40},{9,15},... | collective-permute-start | bytes 1572872 | tf_op jit(solution)/shard_map/ppermute | solution.py:46
  21.3 0.4 shard_map.52
  21.7 2.4 %shard_map.53 = (bf16[1536,1536]{1,0:T(8,128)(2,1)S(1)}, f32[32,1664]{1,0:T(8,128)S(1)}) custom-call(bf16[4,512,128]{2,1,0:T(8,128)(2,1)S(1)} %shard_map.51.refs_0_, bf16[128,1536]{1,0:T(8,128)(2,1)S(1)} %get-tuple-element.50.refs_1_.refs_2_, f32[8,1536]{1,0:T(8,128)S(1)} %get-tuple-element.51.refs_2_.refs_3_), custom_call_target="tpu_custom_call" | custom-call | flops 1207959552 | bytes 4718592 | tf_op jit(solution)/shard_map/pallas_call | solution.py:178
  24.1 2.4 %shard_map.54 = (bf16[1536,1536]{1,0:T(8,128)(2,1)S(1)}, f32[32,1664]{1,0:T(8,128)S(1)}) custom-call(bf16[4,512,128]{2,1,0:T(8,128)(2,1)S(1)} %collective-permute-done.8.refs_0_, bf16[128,1536]{1,0:T(8,128)(2,1)S(1)} %get-tuple-element.50.refs_1_.refs_2_, f32[8,1536]{1,0:T(8,128)S(1)} %get-tuple-element.51.refs_2_.refs_3_, ...), custom_call_target="tpu_custom_call" | custom-call | flops 1207959552 | bytes 4718592 | tf_op jit(solution)/shard_map/pallas_call | solution.py:178
  26.5 0.8 collective-permute-done.7.refs_0_
  27.3 1.6 %collective-permute-done.6.refs_0_ = bf16[4,512,128]{2,1,0:T(8,128)(2,1)S(1)} collective-permute-done((bf16[4,512,128]{2,1,0:T(8,128)(2,1)S(1)}, bf16[4,512,128]{2,1,0:T(8,128)(2,1)S(1)}, u32[]{:S(2)}, u32[]{:S(2)}) %collective-permute-start.6) | collective-permute-done | bytes 524320 | tf_op jit(solution)/shard_map/ppermute | solution.py:46
  28.9 0.9 collective-permute-start.11
  29.8 0.0 collective-permute-start.10
  29.8 1.6 %collective-permute-start.9 = (bf16[4,512,128]{2,1,0:T(8,128)(2,1)S(1)}, bf16[4,512,128]{2,1,0:T(8,128)(2,1)S(1)}, u32[]{:S(2)}, u32[]{:S(2)}) collective-permute-start(bf16[4,512,128]{2,1,0:T(8,128)(2,1)S(1)} %collective-permute-done.7.refs_0_), channel_id=1, source_target_pairs={{0,32},{1,7},{2,34},{3,5},{4,36},{5,3},{6,38},{7,1},{8,40},{9,15},... | collective-permute-start | bytes 1572872 | tf_op jit(solution)/shard_map/ppermute | solution.py:46
  31.4 4.8 %shard_map.55 = (bf16[3072,1536]{1,0:T(8,128)(2,1)S(1)}, f32[32,1664]{1,0:T(8,128)S(1)}) custom-call(bf16[4,512,128]{2,1,0:T(8,128)(2,1)S(1)} %collective-permute-done.6.refs_0_, bf16[4,512,128]{2,1,0:T(8,128)(2,1)S(1)} %collective-permute-done.11.refs_1_, bf16[128,1536]{1,0:T(8,128)(2,1)S(1)} %get-tuple-element.50.refs_1_.refs_2_, ...), custom_call_target="tpu_custom_call" | custom-call | flops 2415919104 | bytes 9437184 | tf_op jit(solution)/shard_map/pallas_call | solution.py:178
  36.2 0.0 collective-permute-done.10.refs_1_
  36.2 4.8 %shard_map.56 = (bf16[3072,1536]{1,0:T(8,128)(2,1)S(1)}, f32[32,1664]{1,0:T(8,128)S(1)}) custom-call(bf16[4,512,128]{2,1,0:T(8,128)(2,1)S(1)} %collective-permute-done.7.refs_0_, bf16[4,512,128]{2,1,0:T(8,128)(2,1)S(1)} %collective-permute-done.10.refs_1_, bf16[128,1536]{1,0:T(8,128)(2,1)S(1)} %get-tuple-element.50.refs_1_.refs_2_, ...), custom_call_target="tpu_custom_call" | custom-call | flops 2415919104 | bytes 9437184 | tf_op jit(solution)/shard_map/pallas_call | solution.py:178
  41.0 0.0 collective-permute-done.9.refs_0_
  41.0 0.3 collective-permute-start.12
  41.3 2.4 %shard_map.57 = (bf16[1536,1536]{1,0:T(8,128)(2,1)S(1)}, f32[32,1664]{1,0:T(8,128)S(1)}) custom-call(bf16[4,512,128]{2,1,0:T(8,128)(2,1)S(1)} %collective-permute-done.9.refs_0_, bf16[128,1536]{1,0:T(8,128)(2,1)S(1)} %get-tuple-element.50.refs_1_.refs_2_, f32[8,1536]{1,0:T(8,128)S(1)} %get-tuple-element.51.refs_2_.refs_3_, ...), custom_call_target="tpu_custom_call" | custom-call | flops 1207959552 | bytes 4718592 | tf_op jit(solution)/shard_map/pallas_call | solution.py:178
  43.7 0.0 collective-permute-done.12.refs_0_
  43.7 2.4 %shard_map.58 = (bf16[1536,1536]{1,0:T(8,128)(2,1)S(1)}, f32[32,512]{1,0:T(8,128)S(1)}, f32[32,512]{1,0:T(8,128)S(1)}, f32[32,512]{1,0:T(8,128)S(1)}, f32[32,512]{1,0:T(8,128)S(1)}) custom-call(bf16[4,512,128]{2,1,0:T(8,128)(2,1)S(1)} %collective-permute-done.12.refs_0_, bf16[128,1536]{1,0:T(8,128)(2,1)S(1)} %get-tuple-element.50.refs_1_.refs_2_, ...), custom_call_target="tpu_custom_call" | custom-call | flops 1207959552 | bytes 4718592 | tf_op jit(solution)/shard_map/pallas_call | solution.py:178
  46.1 0.9 collective-permute-start.13
  47.0 1.8 %collective-permute-start.14 = (f32[32,512]{1,0:T(8,128)S(1)}, f32[32,512]{1,0:T(8,128)S(1)}, u32[]{:S(2)}, u32[]{:S(2)}) collective-permute-start(f32[32,512]{1,0:T(8,128)S(1)} %get-tuple-element.64), channel_id=1, source_target_pairs={{0,2},{1,3},{2,0},{3,1},{4,6},{5,7},{6,4},{7,5},{8,10},{9,11},{10,... | collective-permute-start | bytes 196616 | tf_op jit(solution)/shard_map/ppermute | solution.py:46
  48.8 1.4 %collective-permute-done.13.refs_1_ = f32[32,512]{1,0:T(8,128)S(1)} collective-permute-done((f32[32,512]{1,0:T(8,128)S(1)}, f32[32,512]{1,0:T(8,128)S(1)}, u32[]{:S(2)}, u32[]{:S(2)}) %collective-permute-start.13) | collective-permute-done | bytes 65568 | tf_op jit(solution)/shard_map/ppermute | solution.py:46
  50.2 2.3 %collective-permute-done.14.refs_2_ = f32[32,512]{1,0:T(8,128)S(1)} collective-permute-done((f32[32,512]{1,0:T(8,128)S(1)}, f32[32,512]{1,0:T(8,128)S(1)}, u32[]{:S(2)}, u32[]{:S(2)}) %collective-permute-start.14) | collective-permute-done | bytes 65568 | tf_op jit(solution)/shard_map/ppermute | solution.py:46
  52.5 0.2 shard_map.59
  52.7 1.7 %collective-permute-start.18 = (bf16[32,896]{1,0:T(8,128)(2,1)S(1)}, bf16[32,896]{1,0:T(8,128)(2,1)S(1)}, u32[]{:S(2)}, u32[]{:S(2)}) collective-permute-start(bf16[32,896]{1,0:T(8,128)(2,1)S(1)} %get-tuple-element.68.refs_0_), channel_id=1, source_target_pairs={{0,30},{1,97},{2,28},{3,99},{4,26},{5,101},{6,24},{7,103},{8,22},{... | collective-permute-start | bytes 172040 | tf_op jit(solution)/shard_map/ppermute | solution.py:46
  54.4 0.5 collective-permute-start.17
  54.9 1.1 %collective-permute-start.16 = (bf16[32,896]{1,0:T(8,128)(2,1)S(1)}, bf16[32,896]{1,0:T(8,128)(2,1)S(1)}, u32[]{:S(2)}, u32[]{:S(2)}) collective-permute-start(bf16[32,896]{1,0:T(8,128)(2,1)S(1)} %get-tuple-element.68.refs_0_), channel_id=1, source_target_pairs={{0,6},{1,33},{2,4},{3,35},{4,2},{5,37},{6,0},{7,39},{8,14},{9,41},... | collective-permute-start | bytes 172040 | tf_op jit(solution)/shard_map/ppermute | solution.py:46
  56.0 1.0 collective-permute-done.18.refs_3_
  57.0 1.9 %collective-permute-done.17.refs_2_ = bf16[32,896]{1,0:T(8,128)(2,1)S(1)} collective-permute-done((bf16[32,896]{1,0:T(8,128)(2,1)S(1)}, bf16[32,896]{1,0:T(8,128)(2,1)S(1)}, u32[]{:S(2)}, u32[]{:S(2)}) %collective-permute-start.17) | collective-permute-done | bytes 57376 | tf_op jit(solution)/shard_map/ppermute | solution.py:46
  58.9 5.5 %collective-permute-start.21 = (bf16[4,32,896]{2,1,0:T(8,128)(2,1)S(1)}, bf16[4,32,896]{2,1,0:T(8,128)(2,1)S(1)}, u32[]{:S(2)}, u32[]{:S(2)}) collective-permute-start(bf16[4,32,896]{2,1,0:T(8,128)(2,1)S(1)} %shard_map.60.refs_0_), channel_id=1, source_target_pairs={{0,1},{1,0},{2,3},{3,2},{4,5},{5,4},{6,7},{7,6},{8,9},{9,8},{10,11... | collective-permute-start | bytes 688136 | tf_op jit(solution)/shard_map/ppermute | solution.py:46
  64.4 1.9 %collective-permute-start.20 = (bf16[4,32,896]{2,1,0:T(8,128)(2,1)S(1)}, bf16[4,32,896]{2,1,0:T(8,128)(2,1)S(1)}, u32[]{:S(2)}, u32[]{:S(2)}) collective-permute-start(bf16[4,32,896]{2,1,0:T(8,128)(2,1)S(1)} %shard_map.60.refs_0_), channel_id=1, source_target_pairs={{0,96},{1,25},{2,98},{3,27},{4,100},{5,29},{6,102},{7,31},{8,104},... | collective-permute-start | bytes 688136 | tf_op jit(solution)/shard_map/ppermute | solution.py:46
  66.3 1.1 %collective-permute-start.19 = (bf16[4,32,896]{2,1,0:T(8,128)(2,1)S(1)}, bf16[4,32,896]{2,1,0:T(8,128)(2,1)S(1)}, u32[]{:S(2)}, u32[]{:S(2)}) collective-permute-start(bf16[4,32,896]{2,1,0:T(8,128)(2,1)S(1)} %shard_map.60.refs_0_), channel_id=1, source_target_pairs={{0,32},{1,7},{2,34},{3,5},{4,36},{5,3},{6,38},{7,1},{8,40},{9,15},... | collective-permute-start | bytes 688136 | tf_op jit(solution)/shard_map/ppermute | solution.py:46
  67.4 0.9 shard_map.61.refs_2_
  68.3 0.9 shard_map.62.refs_4_
  69.3 1.5 %collective-permute-done.20.refs_1_ = bf16[4,32,896]{2,1,0:T(8,128)(2,1)S(1)} collective-permute-done((bf16[4,32,896]{2,1,0:T(8,128)(2,1)S(1)}, bf16[4,32,896]{2,1,0:T(8,128)(2,1)S(1)}, u32[]{:S(2)}, u32[]{:S(2)}) %collective-permute-start.20) | collective-permute-done | bytes 229408 | tf_op jit(solution)/shard_map/ppermute | solution.py:46
  70.8 1.6 %collective-permute-done.19.refs_0_ = bf16[4,32,896]{2,1,0:T(8,128)(2,1)S(1)} collective-permute-done((bf16[4,32,896]{2,1,0:T(8,128)(2,1)S(1)}, bf16[4,32,896]{2,1,0:T(8,128)(2,1)S(1)}, u32[]{:S(2)}, u32[]{:S(2)}) %collective-permute-start.19) | collective-permute-done | bytes 229408 | tf_op jit(solution)/shard_map/ppermute | solution.py:46
  72.4 0.5 collective-permute-start.24
  72.9 1.1 %collective-permute-start.22 = (bf16[4,32,896]{2,1,0:T(8,128)(2,1)S(1)}, bf16[4,32,896]{2,1,0:T(8,128)(2,1)S(1)}, u32[]{:S(2)}, u32[]{:S(2)}) collective-permute-start(bf16[4,32,896]{2,1,0:T(8,128)(2,1)S(1)} %collective-permute-done.20.refs_1_), channel_id=1, source_target_pairs={{0,32},{1,7},{2,34},{3,5},{4,36},{5,3},{6,38},{7,1},{8,40},{9,15},... | collective-permute-start | bytes 688136 | tf_op jit(solution)/shard_map/ppermute | solution.py:46
  74.0 1.7 %shard_map.63.refs_4_ = f32[32,1664]{1,0:T(8,128)S(1)} custom-call(bf16[4,32,896]{2,1,0:T(8,128)(2,1)S(1)} %collective-permute-done.19.refs_0_, bf16[4,32,896]{2,1,0:T(8,128)(2,1)S(1)} %collective-permute-done.20.refs_1_, bf16[3072,1536]{1,0:T(8,128)(2,1)S(1)} %get-tuple-element.73.refs_2_, bf16[3072,1536]{1,0:T(8,128)(2,1)S(1)} %get-tuple-element.74.refs_3_, ...), custom_call_target="tpu_custom_call" | custom-call | flops 2415919104 | bytes 9437184 | tf_op jit(solution)/shard_map/pallas_call | solution.py:207
  75.7 0.0 collective-permute-done.23.refs_0_
  75.8 1.7 %shard_map.64.refs_2_ = f32[32,1664]{1,0:T(8,128)S(1)} custom-call(bf16[4,32,896]{2,1,0:T(8,128)(2,1)S(1)} %collective-permute-done.23.refs_0_, bf16[4,32,896]{2,1,0:T(8,128)(2,1)S(1)} %collective-permute-done.24.refs_1_, bf16[3072,1536]{1,0:T(8,128)(2,1)S(1)} %get-tuple-element.73.refs_2_, bf16[3072,1536]{1,0:T(8,128)(2,1)S(1)} %get-tuple-element.74.refs_3_, ...), custom_call_target="tpu_custom_call" | custom-call | flops 2415919104 | bytes 9437184 | tf_op jit(solution)/shard_map/pallas_call | solution.py:207
  77.5 1.5 %collective-permute-done.22.refs_0_ = bf16[4,32,896]{2,1,0:T(8,128)(2,1)S(1)} collective-permute-done((bf16[4,32,896]{2,1,0:T(8,128)(2,1)S(1)}, bf16[4,32,896]{2,1,0:T(8,128)(2,1)S(1)}, u32[]{:S(2)}, u32[]{:S(2)}) %collective-permute-start.22) | collective-permute-done | bytes 229408 | tf_op jit(solution)/shard_map/ppermute | solution.py:46
  79.0 0.9 shard_map.65.refs_2_
  79.9 0.6 collective-permute-done.25.refs_0_
  80.5 0.9 shard_map.66
  81.4 0.0 collective-permute-start.26
  81.4 0.1 collective-permute-start.27
  81.5 2.6 %collective-permute-start.28 = (f32[32,512]{1,0:T(8,128)S(1)}, f32[32,512]{1,0:T(8,128)S(1)}, u32[]{:S(2)}, u32[]{:S(2)}) collective-permute-start(f32[32,512]{1,0:T(8,128)S(1)} %get-tuple-element.83), channel_id=1, source_target_pairs={{0,8},{1,9},{2,10},{3,11},{4,12},{5,13},{6,14},{7,15},{8,0},{9,1},... | collective-permute-start | bytes 196616 | tf_op jit(solution)/shard_map/ppermute | solution.py:46
  84.0 1.8 %collective-permute-done.26.refs_1_ = f32[32,512]{1,0:T(8,128)S(1)} collective-permute-done((f32[32,512]{1,0:T(8,128)S(1)}, f32[32,512]{1,0:T(8,128)S(1)}, u32[]{:S(2)}, u32[]{:S(2)}) %collective-permute-start.26) | collective-permute-done | bytes 65568 | tf_op jit(solution)/shard_map/ppermute | solution.py:46
  85.8 0.1 collective-permute-done.28.refs_3_
  86.0 0.4 shard_map.67
  86.4 16.4 %all_to_all.5 = f32[128,1,32]{2,1,0:T(1,128)S(1)} all-to-all(f32[128,1,32]{2,1,0:T(1,128)S(1)} %bitcast.8), channel_id=1, replica_groups=mesh['pts'=128] {'pts'}, dimensions={0} | all-to-all | bytes 32768 | tf_op jit(solution)/shard_map/all_to_all | solution.py:451
  102.8 0.8 shard_map.68
  (14 shorter events, 0.1 us)
Async XLA Ops:
  0.6 8.1 %collective-permute-start.3 = (bf16[384,128]{1,0:T(8,128)(2,1)}, bf16[384,128]{1,0:T(8,128)(2,1)S(1)}, u32[]{:S(2)}, u32[]{:S(2)}) collective-permute-start(bf16[384,128]{1,0:T(8,128)(2,1)} %points_ref.1), channel_id=1, source_target_pairs={{0,10},{1,11},{2,8},{3,9},{4,14},{5,15},{6,12},{7,13},{8,2},{9,3},... | collective-permute-start | bytes 294920 | tf_op jit(solution)/shard_map/ppermute | solution.py:46
  5.2 7.5 %collective-permute-start.2 = (bf16[512,128]{1,0:T(8,128)(2,1)S(1)}, bf16[512,128]{1,0:T(8,128)(2,1)S(1)}, u32[]{:S(2)}, u32[]{:S(2)}) collective-permute-start(bf16[512,128]{1,0:T(8,128)(2,1)S(1)} %get-tuple-element.49.refs_0_), channel_id=1, source_target_pairs={{0,30},{1,97},{2,28},{3,99},{4,26},{5,101},{6,24},{7,103},{8,22},{... | collective-permute-start | bytes 393224 | tf_op jit(solution)/shard_map/ppermute | solution.py:46
  7.8 5.6 %collective-permute-start.1 = (bf16[512,128]{1,0:T(8,128)(2,1)S(1)}, bf16[512,128]{1,0:T(8,128)(2,1)S(1)}, u32[]{:S(2)}, u32[]{:S(2)}) collective-permute-start(bf16[512,128]{1,0:T(8,128)(2,1)S(1)} %get-tuple-element.49.refs_0_), channel_id=1, source_target_pairs={{0,24},{1,65},{2,26},{3,67},{4,28},{5,69},{6,30},{7,71},{8,16},{9,... | collective-permute-start | bytes 393224 | tf_op jit(solution)/shard_map/ppermute | solution.py:46
  8.3 5.1 %collective-permute-start = (bf16[512,128]{1,0:T(8,128)(2,1)S(1)}, bf16[512,128]{1,0:T(8,128)(2,1)S(1)}, u32[]{:S(2)}, u32[]{:S(2)}) collective-permute-start(bf16[512,128]{1,0:T(8,128)(2,1)S(1)} %get-tuple-element.49.refs_0_), channel_id=1, source_target_pairs={{0,6},{1,33},{2,4},{3,35},{4,2},{5,37},{6,0},{7,39},{8,14},{9,41},... | collective-permute-start | bytes 393224 | tf_op jit(solution)/shard_map/ppermute | solution.py:46
  8.5 4.0 %collective-permute-start.5 = (bf16[384,128]{1,0:T(8,128)(2,1)}, bf16[384,128]{1,0:T(8,128)(2,1)S(1)}, u32[]{:S(2)}, u32[]{:S(2)}) collective-permute-start(bf16[384,128]{1,0:T(8,128)(2,1)} %points_ref.1), channel_id=1, source_target_pairs={{0,8},{1,9},{2,10},{3,11},{4,12},{5,13},{6,14},{7,15},{8,0},{9,1},... | collective-permute-start | bytes 294920 | tf_op jit(solution)/shard_map/ppermute | solution.py:46
  8.7 4.0 %collective-permute-start.4 = (bf16[384,128]{1,0:T(8,128)(2,1)}, bf16[384,128]{1,0:T(8,128)(2,1)S(1)}, u32[]{:S(2)}, u32[]{:S(2)}) collective-permute-start(bf16[384,128]{1,0:T(8,128)(2,1)} %points_ref.1), channel_id=1, source_target_pairs={{0,2},{1,3},{2,0},{3,1},{4,6},{5,7},{6,4},{7,5},{8,10},{9,11},{10,... | collective-permute-start | bytes 294920 | tf_op jit(solution)/shard_map/ppermute | solution.py:46
  13.4 10.7 %collective-permute-start.8 = (bf16[4,512,128]{2,1,0:T(8,128)(2,1)S(1)}, bf16[4,512,128]{2,1,0:T(8,128)(2,1)S(1)}, u32[]{:S(2)}, u32[]{:S(2)}) collective-permute-start(bf16[4,512,128]{2,1,0:T(8,128)(2,1)S(1)} %shard_map.51.refs_0_), channel_id=1, source_target_pairs={{0,1},{1,0},{2,3},{3,2},{4,5},{5,4},{6,7},{7,6},{8,9},{9,8},{10,11... | collective-permute-start | bytes 1572872 | tf_op jit(solution)/shard_map/ppermute | solution.py:46
  17.7 9.5 %collective-permute-start.7 = (bf16[4,512,128]{2,1,0:T(8,128)(2,1)S(1)}, bf16[4,512,128]{2,1,0:T(8,128)(2,1)S(1)}, u32[]{:S(2)}, u32[]{:S(2)}) collective-permute-start(bf16[4,512,128]{2,1,0:T(8,128)(2,1)S(1)} %shard_map.51.refs_0_), channel_id=1, source_target_pairs={{0,96},{1,25},{2,98},{3,27},{4,100},{5,29},{6,102},{7,31},{8,104},... | collective-permute-start | bytes 1572872 | tf_op jit(solution)/shard_map/ppermute | solution.py:46
  19.6 9.2 %collective-permute-start.6 = (bf16[4,512,128]{2,1,0:T(8,128)(2,1)S(1)}, bf16[4,512,128]{2,1,0:T(8,128)(2,1)S(1)}, u32[]{:S(2)}, u32[]{:S(2)}) collective-permute-start(bf16[4,512,128]{2,1,0:T(8,128)(2,1)S(1)} %shard_map.51.refs_0_), channel_id=1, source_target_pairs={{0,32},{1,7},{2,34},{3,5},{4,36},{5,3},{6,38},{7,1},{8,40},{9,15},... | collective-permute-start | bytes 1572872 | tf_op jit(solution)/shard_map/ppermute | solution.py:46
  28.9 2.5 %collective-permute-start.11 = (bf16[4,512,128]{2,1,0:T(8,128)(2,1)S(1)}, bf16[4,512,128]{2,1,0:T(8,128)(2,1)S(1)}, u32[]{:S(2)}, u32[]{:S(2)}) collective-permute-start(bf16[4,512,128]{2,1,0:T(8,128)(2,1)S(1)} %collective-permute-done.6.refs_0_), channel_id=1, source_target_pairs={{0,1},{1,0},{2,3},{3,2},{4,5},{5,4},{6,7},{7,6},{8,9},{9,8},{10,11... | collective-permute-start | bytes 1572872 | tf_op jit(solution)/shard_map/ppermute | solution.py:46
  29.8 6.4 %collective-permute-start.10 = (bf16[4,512,128]{2,1,0:T(8,128)(2,1)S(1)}, bf16[4,512,128]{2,1,0:T(8,128)(2,1)S(1)}, u32[]{:S(2)}, u32[]{:S(2)}) collective-permute-start(bf16[4,512,128]{2,1,0:T(8,128)(2,1)S(1)} %collective-permute-done.7.refs_0_), channel_id=1, source_target_pairs={{0,1},{1,0},{2,3},{3,2},{4,5},{5,4},{6,7},{7,6},{8,9},{9,8},{10,11... | collective-permute-start | bytes 1572872 | tf_op jit(solution)/shard_map/ppermute | solution.py:46
  29.8 11.2 %collective-permute-start.9 = (bf16[4,512,128]{2,1,0:T(8,128)(2,1)S(1)}, bf16[4,512,128]{2,1,0:T(8,128)(2,1)S(1)}, u32[]{:S(2)}, u32[]{:S(2)}) collective-permute-start(bf16[4,512,128]{2,1,0:T(8,128)(2,1)S(1)} %collective-permute-done.7.refs_0_), channel_id=1, source_target_pairs={{0,32},{1,7},{2,34},{3,5},{4,36},{5,3},{6,38},{7,1},{8,40},{9,15},... | collective-permute-start | bytes 1572872 | tf_op jit(solution)/shard_map/ppermute | solution.py:46
  41.0 2.7 %collective-permute-start.12 = (bf16[4,512,128]{2,1,0:T(8,128)(2,1)S(1)}, bf16[4,512,128]{2,1,0:T(8,128)(2,1)S(1)}, u32[]{:S(2)}, u32[]{:S(2)}) collective-permute-start(bf16[4,512,128]{2,1,0:T(8,128)(2,1)S(1)} %collective-permute-done.9.refs_0_), channel_id=1, source_target_pairs={{0,1},{1,0},{2,3},{3,2},{4,5},{5,4},{6,7},{7,6},{8,9},{9,8},{10,11... | collective-permute-start | bytes 1572872 | tf_op jit(solution)/shard_map/ppermute | solution.py:46
  46.1 4.1 %collective-permute-start.13 = (f32[32,512]{1,0:T(8,128)S(1)}, f32[32,512]{1,0:T(8,128)S(1)}, u32[]{:S(2)}, u32[]{:S(2)}) collective-permute-start(f32[32,512]{1,0:T(8,128)S(1)} %get-tuple-element.63), channel_id=1, source_target_pairs={{0,10},{1,11},{2,8},{3,9},{4,14},{5,15},{6,12},{7,13},{8,2},{9,3},... | collective-permute-start | bytes 196616 | tf_op jit(solution)/shard_map/ppermute | solution.py:46
  47.0 5.4 %collective-permute-start.14 = (f32[32,512]{1,0:T(8,128)S(1)}, f32[32,512]{1,0:T(8,128)S(1)}, u32[]{:S(2)}, u32[]{:S(2)}) collective-permute-start(f32[32,512]{1,0:T(8,128)S(1)} %get-tuple-element.64), channel_id=1, source_target_pairs={{0,2},{1,3},{2,0},{3,1},{4,6},{5,7},{6,4},{7,5},{8,10},{9,11},{10,... | collective-permute-start | bytes 196616 | tf_op jit(solution)/shard_map/ppermute | solution.py:46
  48.8 3.7 %collective-permute-start.15 = (f32[32,512]{1,0:T(8,128)S(1)}, f32[32,512]{1,0:T(8,128)S(1)}, u32[]{:S(2)}, u32[]{:S(2)}) collective-permute-start(f32[32,512]{1,0:T(8,128)S(1)} %get-tuple-element.65), channel_id=1, source_target_pairs={{0,8},{1,9},{2,10},{3,11},{4,12},{5,13},{6,14},{7,15},{8,0},{9,1},... | collective-permute-start | bytes 196616 | tf_op jit(solution)/shard_map/ppermute | solution.py:46
  52.7 4.3 %collective-permute-start.18 = (bf16[32,896]{1,0:T(8,128)(2,1)S(1)}, bf16[32,896]{1,0:T(8,128)(2,1)S(1)}, u32[]{:S(2)}, u32[]{:S(2)}) collective-permute-start(bf16[32,896]{1,0:T(8,128)(2,1)S(1)} %get-tuple-element.68.refs_0_), channel_id=1, source_target_pairs={{0,30},{1,97},{2,28},{3,99},{4,26},{5,101},{6,24},{7,103},{8,22},{... | collective-permute-start | bytes 172040 | tf_op jit(solution)/shard_map/ppermute | solution.py:46
  54.4 4.5 %collective-permute-start.17 = (bf16[32,896]{1,0:T(8,128)(2,1)S(1)}, bf16[32,896]{1,0:T(8,128)(2,1)S(1)}, u32[]{:S(2)}, u32[]{:S(2)}) collective-permute-start(bf16[32,896]{1,0:T(8,128)(2,1)S(1)} %get-tuple-element.68.refs_0_), channel_id=1, source_target_pairs={{0,24},{1,65},{2,26},{3,67},{4,28},{5,69},{6,30},{7,71},{8,16},{9,... | collective-permute-start | bytes 172040 | tf_op jit(solution)/shard_map/ppermute | solution.py:46
  54.9 4.0 %collective-permute-start.16 = (bf16[32,896]{1,0:T(8,128)(2,1)S(1)}, bf16[32,896]{1,0:T(8,128)(2,1)S(1)}, u32[]{:S(2)}, u32[]{:S(2)}) collective-permute-start(bf16[32,896]{1,0:T(8,128)(2,1)S(1)} %get-tuple-element.68.refs_0_), channel_id=1, source_target_pairs={{0,6},{1,33},{2,4},{3,35},{4,2},{5,37},{6,0},{7,39},{8,14},{9,41},... | collective-permute-start | bytes 172040 | tf_op jit(solution)/shard_map/ppermute | solution.py:46
  58.9 9.4 %collective-permute-start.21 = (bf16[4,32,896]{2,1,0:T(8,128)(2,1)S(1)}, bf16[4,32,896]{2,1,0:T(8,128)(2,1)S(1)}, u32[]{:S(2)}, u32[]{:S(2)}) collective-permute-start(bf16[4,32,896]{2,1,0:T(8,128)(2,1)S(1)} %shard_map.60.refs_0_), channel_id=1, source_target_pairs={{0,1},{1,0},{2,3},{3,2},{4,5},{5,4},{6,7},{7,6},{8,9},{9,8},{10,11... | collective-permute-start | bytes 688136 | tf_op jit(solution)/shard_map/ppermute | solution.py:46
  64.4 6.4 %collective-permute-start.20 = (bf16[4,32,896]{2,1,0:T(8,128)(2,1)S(1)}, bf16[4,32,896]{2,1,0:T(8,128)(2,1)S(1)}, u32[]{:S(2)}, u32[]{:S(2)}) collective-permute-start(bf16[4,32,896]{2,1,0:T(8,128)(2,1)S(1)} %shard_map.60.refs_0_), channel_id=1, source_target_pairs={{0,96},{1,25},{2,98},{3,27},{4,100},{5,29},{6,102},{7,31},{8,104},... | collective-permute-start | bytes 688136 | tf_op jit(solution)/shard_map/ppermute | solution.py:46
  66.3 6.1 %collective-permute-start.19 = (bf16[4,32,896]{2,1,0:T(8,128)(2,1)S(1)}, bf16[4,32,896]{2,1,0:T(8,128)(2,1)S(1)}, u32[]{:S(2)}, u32[]{:S(2)}) collective-permute-start(bf16[4,32,896]{2,1,0:T(8,128)(2,1)S(1)} %shard_map.60.refs_0_), channel_id=1, source_target_pairs={{0,32},{1,7},{2,34},{3,5},{4,36},{5,3},{6,38},{7,1},{8,40},{9,15},... | collective-permute-start | bytes 688136 | tf_op jit(solution)/shard_map/ppermute | solution.py:46
  72.4 3.4 %collective-permute-start.23 = (bf16[4,32,896]{2,1,0:T(8,128)(2,1)S(1)}, bf16[4,32,896]{2,1,0:T(8,128)(2,1)S(1)}, u32[]{:S(2)}, u32[]{:S(2)}) collective-permute-start(bf16[4,32,896]{2,1,0:T(8,128)(2,1)S(1)} %collective-permute-done.19.refs_0_), channel_id=1, source_target_pairs={{0,1},{1,0},{2,3},{3,2},{4,5},{5,4},{6,7},{7,6},{8,9},{9,8},{10,11... | collective-permute-start | bytes 688136 | tf_op jit(solution)/shard_map/ppermute | solution.py:46
  72.4 3.4 %collective-permute-start.24 = (bf16[4,32,896]{2,1,0:T(8,128)(2,1)S(1)}, bf16[4,32,896]{2,1,0:T(8,128)(2,1)S(1)}, u32[]{:S(2)}, u32[]{:S(2)}) collective-permute-start(bf16[4,32,896]{2,1,0:T(8,128)(2,1)S(1)} %collective-permute-done.20.refs_1_), channel_id=1, source_target_pairs={{0,1},{1,0},{2,3},{3,2},{4,5},{5,4},{6,7},{7,6},{8,9},{9,8},{10,11... | collective-permute-start | bytes 688136 | tf_op jit(solution)/shard_map/ppermute | solution.py:46
  72.9 6.1 %collective-permute-start.22 = (bf16[4,32,896]{2,1,0:T(8,128)(2,1)S(1)}, bf16[4,32,896]{2,1,0:T(8,128)(2,1)S(1)}, u32[]{:S(2)}, u32[]{:S(2)}) collective-permute-start(bf16[4,32,896]{2,1,0:T(8,128)(2,1)S(1)} %collective-permute-done.20.refs_1_), channel_id=1, source_target_pairs={{0,32},{1,7},{2,34},{3,5},{4,36},{5,3},{6,38},{7,1},{8,40},{9,15},... | collective-permute-start | bytes 688136 | tf_op jit(solution)/shard_map/ppermute | solution.py:46
  79.0 1.5 %collective-permute-start.25 = (bf16[4,32,896]{2,1,0:T(8,128)(2,1)S(1)}, bf16[4,32,896]{2,1,0:T(8,128)(2,1)S(1)}, u32[]{:S(2)}, u32[]{:S(2)}) collective-permute-start(bf16[4,32,896]{2,1,0:T(8,128)(2,1)S(1)} %collective-permute-done.22.refs_0_), channel_id=1, source_target_pairs={{0,1},{1,0},{2,3},{3,2},{4,5},{5,4},{6,7},{7,6},{8,9},{9,8},{10,11... | collective-permute-start | bytes 688136 | tf_op jit(solution)/shard_map/ppermute | solution.py:46
  81.4 4.5 %collective-permute-start.26 = (f32[32,512]{1,0:T(8,128)S(1)}, f32[32,512]{1,0:T(8,128)S(1)}, u32[]{:S(2)}, u32[]{:S(2)}) collective-permute-start(f32[32,512]{1,0:T(8,128)S(1)} %get-tuple-element.81), channel_id=1, source_target_pairs={{0,10},{1,11},{2,8},{3,9},{4,14},{5,15},{6,12},{7,13},{8,2},{9,3},... | collective-permute-start | bytes 196616 | tf_op jit(solution)/shard_map/ppermute | solution.py:46
  81.4 4.5 %collective-permute-start.27 = (f32[32,512]{1,0:T(8,128)S(1)}, f32[32,512]{1,0:T(8,128)S(1)}, u32[]{:S(2)}, u32[]{:S(2)}) collective-permute-start(f32[32,512]{1,0:T(8,128)S(1)} %get-tuple-element.82), channel_id=1, source_target_pairs={{0,2},{1,3},{2,0},{3,1},{4,6},{5,7},{6,4},{7,5},{8,10},{9,11},{10,... | collective-permute-start | bytes 196616 | tf_op jit(solution)/shard_map/ppermute | solution.py:46
  81.5 4.5 %collective-permute-start.28 = (f32[32,512]{1,0:T(8,128)S(1)}, f32[32,512]{1,0:T(8,128)S(1)}, u32[]{:S(2)}, u32[]{:S(2)}) collective-permute-start(f32[32,512]{1,0:T(8,128)S(1)} %get-tuple-element.83), channel_id=1, source_target_pairs={{0,8},{1,9},{2,10},{3,11},{4,12},{5,13},{6,14},{7,15},{8,0},{9,1},... | collective-permute-start | bytes 196616 | tf_op jit(solution)/shard_map/ppermute | solution.py:46

commit v6 on v4

--- a/solution.py
+++ b/solution.py
@@ -25,6 +25,7 @@
 CHUNK = 512
 UNIT = 256
 SPLITS = 3
+SUMS = 3
 LIMIT = 6 * 1024 * 1024
 SMALL = 8 * 1024 * 1024
 INSIDE = pl.BlockSpec(memory_space=pltpu.VMEM)
@@ -166,8 +167,11 @@
             odd_slot = SIDE * side + ODD_LINES[n]
             slot = jnp.bitwise_xor(place, jnp.where(odd == core, even_slot, odd_slot))
             part = pl.ds(side * rows, rows)
-            vec_ref[n, :cols, part] = blocks_ref[slot, :, pl.ds(0, rows)]
-            vec_ref[n, cols:, part] = blocks_ref[slot, :, pl.ds(rows, rows)]
+            block = blocks_ref[slot].astype(jnp.float32)
+            value = block[:, :rows] + collect_lanes(block[:, rows:], SUMS)[-1]
+            high = value.astype(jnp.bfloat16)
+            vec_ref[n, :cols, part] = high
+            vec_ref[n, cols:, part] = (value - high.astype(jnp.float32)).astype(jnp.bfloat16)
     for c in range(total_ref.shape[1] // CHUNK):
         part = pl.ds(c * CHUNK, CHUNK)
         value = jnp.zeros((2 * cols, CHUNK), jnp.float32)
@@ -184,8 +188,8 @@
         other_ref = refs[TURNS + 2]
         lanes = jnp.zeros((total_ref.shape[0], LANES), jnp.float32)
         for k in range(CHIPS):
-            lanes += blocks_ref[k, :, 2 * rows :].astype(jnp.float32)
-            lanes += other_ref[k, :, 2 * rows :].astype(jnp.float32)
+            lanes += blocks_ref[k, :, rows:].astype(jnp.float32)
+            lanes += other_ref[k, :, rows:].astype(jnp.float32)
         for k, ref in enumerate(refs[TURNS + 3 : TURNS + 3 + NEAR]):
             ref[:, :rows] = total_ref[:, pl.ds(k * rows, rows)]
             ref[:, rows:] = lanes
@@ -359,10 +363,9 @@
     rest_ref[...] = rest
     lane = lax.broadcasted_iota(jnp.int32, known_ref.shape, 1)
     known_ref[...] = jnp.where(lane == 0, norm, shift)
-    lanes = spread_lanes((row_sum(rhs * rest), row_sum(rest * rest)), known_ref.shape)
-    high = rest.astype(jnp.bfloat16)
-    low = (rest - high.astype(jnp.float32)).astype(jnp.bfloat16)
-    packed = jnp.concatenate([high, low, lanes], axis=1)
+    mean = row_sum(rest) * (1.0 / rows)
+    lanes = spread_lanes((row_sum(rhs * rest), row_sum(rest * rest), mean), known_ref.shape)
+    packed = jnp.concatenate([(rest - mean).astype(jnp.bfloat16), lanes], axis=1)
     for k in range(copies_ref.shape[0]):
         copies_ref[k] = packed
 
@@ -446,7 +449,7 @@
 
     image, rest, known, copies = small_call(
         middle,
-        [field_shape, field_shape, lanes_shape, ((CHIPS, cols, 2 * rows + LANES), jnp.bfloat16)],
+        [field_shape, field_shape, lanes_shape, ((CHIPS, cols, rows + LANES), jnp.bfloat16)],
         *exchange(parts, NEAR_MASKS),
         noisy,
         rhs,

time: 104 us -> 99.7 us (0.959)
  blocking collectives: 34.9 us -> 30.4 us
    all_to_all x1, blocking collectives: 20.5 us -> 15.9 us  [share(): return lax.all_to_all(copies, 'pts', 0, 0, axis_index_groups=chip_groups())]
  transfers between devices with their start and end apart: 20 -> 20, of which waited for: 9 -> 9; matrix products, arithmetic and copies ran while one was open for 0% -> 0% of each run, Pallas kernels for 21% -> 22%
where the time goes in v6:
time: 99.7 us; the launch traced here: 99.5 us
  blocking collectives  30.4 us (30%)
  Pallas kernels  28.9 us (29%)
  starting transfers between devices  26.5 us (27%)
  waiting for transfers between devices  13 us (13%)
    ppermute x20, starting transfers between devices, partner(): return lax.ppermute(value, 'pts', pairs)  26.5 us
    pallas_call x6, Pallas kernels, run_first(): pl.pallas_call(functools.partial(first_product, scale_of(feats), rows, le...  19 us
    all_to_all x1, blocking collectives, share(): return lax.all_to_all(copies, 'pts', 0, 0, axis_index_groups=chip_groups())  15.9 us
    all_to_all x1, blocking collectives, per_device(): lax.all_to_all(curve[:, None, :], 'pts', 0, 0).reshape(DEVICES, cols)  14.5 us
    ppermute x20, waiting for transfers between devices, partner(): return lax.ppermute(value, 'pts', pairs)  13 us
    pallas_call x2, Pallas kernels, run_second(): pl.pallas_call(functools.partial(second_product, rows, core, starts), in_...  6.97 us
  transfers between devices with their start and end apart: 20, of which 9 were waited for; matrix products, arithmetic and copies ran while one was open for 0% of the time, Pallas kernels for 22%

profile of v6, /device:TPU:1, one launch (start us, length us, event | category | flops | bytes accessed | tf_op | source)
XLA Modules:
  0.0 99.5 jit_solution(5899105886640592583)
XLA Ops:
  0.6 3.6 %collective-permute-start.3 = (bf16[384,128]{1,0:T(8,128)(2,1)}, bf16[384,128]{1,0:T(8,128)(2,1)S(1)}, u32[]{:S(2)}, u32[]{:S(2)}) collective-permute-start(bf16[384,128]{1,0:T(8,128)(2,1)} %points_ref.1), channel_id=1, source_target_pairs={{0,10},{1,11},{2,8},{3,9},{4,14},{5,15},{6,12},{7,13},{8,2},{9,3},... | collective-permute-start | bytes 294920 | tf_op jit(solution)/shard_map/ppermute | solution.py:66
  4.2 1.0 %shard_map.50 = (bf16[512,128]{1,0:T(8,128)(2,1)S(1)}, f32[32,384]{1,0:T(8,128)S(1)}, f32[32,384]{1,0:T(8,128)S(1)}, f32[1,384]{1,0:T(1,128)S(1)}) custom-call(bf16[384,128]{1,0:T(8,128)(2,1)} %points_ref.1, f32[32,384]{1,0:T(8,128)} %bitcast.9, f32[384]{0:T(512)} %noise_ref.1), custom_call_target="tpu_custom_call" | custom-call | tf_op jit(solution)/shard_map/pallas_call | solution.py:310
  5.2 2.6 %collective-permute-start.2 = (bf16[512,128]{1,0:T(8,128)(2,1)S(1)}, bf16[512,128]{1,0:T(8,128)(2,1)S(1)}, u32[]{:S(2)}, u32[]{:S(2)}) collective-permute-start(bf16[512,128]{1,0:T(8,128)(2,1)S(1)} %get-tuple-element.44.refs_0_), channel_id=1, source_target_pairs={{0,30},{1,97},{2,28},{3,99},{4,26},{5,101},{6,24},{7,103},{8,22},{... | collective-permute-start | bytes 393224 | tf_op jit(solution)/shard_map/ppermute | solution.py:66
  7.8 0.5 collective-permute-start.1
  8.3 0.3 collective-permute-start
  8.5 0.2 collective-permute-start.5
  8.7 0.0 collective-permute-done.3.refs_4_.refs_1_
  8.7 0.1 collective-permute-start.4
  8.8 3.7 %collective-permute-done.5.refs_6_.refs_3_ = bf16[384,128]{1,0:T(8,128)(2,1)S(1)} collective-permute-done((bf16[384,128]{1,0:T(8,128)(2,1)}, bf16[384,128]{1,0:T(8,128)(2,1)S(1)}, u32[]{:S(2)}, u32[]{:S(2)}) %collective-permute-start.5) | collective-permute-done | bytes 98336 | tf_op jit(solution)/shard_map/ppermute | solution.py:66
  12.5 0.2 collective-permute-done.4.refs_5_.refs_2_
  12.7 0.0 collective-permute-done.2.refs_3_
  12.7 0.7 collective-permute-done.1.refs_2_
  13.4 0.0 collective-permute-done.refs_1_
  13.4 4.3 %collective-permute-start.6 = (bf16[4,512,128]{2,1,0:T(8,128)(2,1)S(1)}, bf16[4,512,128]{2,1,0:T(8,128)(2,1)S(1)}, u32[]{:S(2)}, u32[]{:S(2)}) collective-permute-start(bf16[4,512,128]{2,1,0:T(8,128)(2,1)S(1)} %shard_map.51.refs_0_), channel_id=1, source_target_pairs={{0,1},{1,0},{2,3},{3,2},{4,5},{5,4},{6,7},{7,6},{8,9},{9,8},{10,11... | collective-permute-start | bytes 1572872 | tf_op jit(solution)/shard_map/ppermute | solution.py:66
  17.7 1.9 %collective-permute-start.8 = (bf16[4,512,128]{2,1,0:T(8,128)(2,1)S(1)}, bf16[4,512,128]{2,1,0:T(8,128)(2,1)S(1)}, u32[]{:S(2)}, u32[]{:S(2)}) collective-permute-start(bf16[4,512,128]{2,1,0:T(8,128)(2,1)S(1)} %shard_map.51.refs_0_), channel_id=1, source_target_pairs={{0,96},{1,25},{2,98},{3,27},{4,100},{5,29},{6,102},{7,31},{8,104},... | collective-permute-start | bytes 1572872 | tf_op jit(solution)/shard_map/ppermute | solution.py:66
  19.6 1.7 %collective-permute-start.7 = (bf16[4,512,128]{2,1,0:T(8,128)(2,1)S(1)}, bf16[4,512,128]{2,1,0:T(8,128)(2,1)S(1)}, u32[]{:S(2)}, u32[]{:S(2)}) collective-permute-start(bf16[4,512,128]{2,1,0:T(8,128)(2,1)S(1)} %shard_map.51.refs_0_), channel_id=1, source_target_pairs={{0,32},{1,7},{2,34},{3,5},{4,36},{5,3},{6,38},{7,1},{8,40},{9,15},... | collective-permute-start | bytes 1572872 | tf_op jit(solution)/shard_map/ppermute | solution.py:66
  21.3 0.4 shard_map.52
  21.7 2.4 %shard_map.53 = (bf16[1536,1536]{1,0:T(8,128)(2,1)S(1)}, f32[32,1664]{1,0:T(8,128)S(1)}) custom-call(bf16[4,512,128]{2,1,0:T(8,128)(2,1)S(1)} %shard_map.51.refs_0_, bf16[128,1536]{1,0:T(8,128)(2,1)S(1)} %get-tuple-element.45.refs_1_.refs_2_, f32[8,1536]{1,0:T(8,128)S(1)} %get-tuple-element.46.refs_2_.refs_3_), custom_call_target="tpu_custom_call" | custom-call | flops 1207959552 | bytes 4718592 | tf_op jit(solution)/shard_map/pallas_call | solution.py:210
  24.1 0.0 collective-permute-done.6.refs_0_
  24.1 2.4 %shard_map.54 = (bf16[1536,1536]{1,0:T(8,128)(2,1)S(1)}, f32[32,1664]{1,0:T(8,128)S(1)}) custom-call(bf16[4,512,128]{2,1,0:T(8,128)(2,1)S(1)} %collective-permute-done.6.refs_0_, bf16[128,1536]{1,0:T(8,128)(2,1)S(1)} %get-tuple-element.45.refs_1_.refs_2_, f32[8,1536]{1,0:T(8,128)S(1)} %get-tuple-element.46.refs_2_.refs_3_, ...), custom_call_target="tpu_custom_call" | custom-call | flops 1207959552 | bytes 4718592 | tf_op jit(solution)/shard_map/pallas_call | solution.py:210
  26.4 0.8 collective-permute-done.8.refs_0_
  27.3 1.6 %collective-permute-done.7.refs_0_ = bf16[4,512,128]{2,1,0:T(8,128)(2,1)S(1)} collective-permute-done((bf16[4,512,128]{2,1,0:T(8,128)(2,1)S(1)}, bf16[4,512,128]{2,1,0:T(8,128)(2,1)S(1)}, u32[]{:S(2)}, u32[]{:S(2)}) %collective-permute-start.7) | collective-permute-done | bytes 524320 | tf_op jit(solution)/shard_map/ppermute | solution.py:66
  28.9 0.9 collective-permute-start.9
  29.8 0.0 collective-permute-start.10
  29.8 1.6 %collective-permute-start.11 = (bf16[4,512,128]{2,1,0:T(8,128)(2,1)S(1)}, bf16[4,512,128]{2,1,0:T(8,128)(2,1)S(1)}, u32[]{:S(2)}, u32[]{:S(2)}) collective-permute-start(bf16[4,512,128]{2,1,0:T(8,128)(2,1)S(1)} %collective-permute-done.8.refs_0_), channel_id=1, source_target_pairs={{0,32},{1,7},{2,34},{3,5},{4,36},{5,3},{6,38},{7,1},{8,40},{9,15},... | collective-permute-start | bytes 1572872 | tf_op jit(solution)/shard_map/ppermute | solution.py:66
  31.4 0.0 collective-permute-done.9.refs_1_
  31.4 4.8 %shard_map.55 = (bf16[3072,1536]{1,0:T(8,128)(2,1)S(1)}, f32[32,1664]{1,0:T(8,128)S(1)}) custom-call(bf16[4,512,128]{2,1,0:T(8,128)(2,1)S(1)} %collective-permute-done.7.refs_0_, bf16[4,512,128]{2,1,0:T(8,128)(2,1)S(1)} %collective-permute-done.9.refs_1_, bf16[128,1536]{1,0:T(8,128)(2,1)S(1)} %get-tuple-element.45.refs_1_.refs_2_, ...), custom_call_target="tpu_custom_call" | custom-call | flops 2415919104 | bytes 9437184 | tf_op jit(solution)/shard_map/pallas_call | solution.py:210
  36.2 0.0 collective-permute-done.10.refs_1_
  36.2 4.8 %shard_map.56 = (bf16[3072,1536]{1,0:T(8,128)(2,1)S(1)}, f32[32,1664]{1,0:T(8,128)S(1)}) custom-call(bf16[4,512,128]{2,1,0:T(8,128)(2,1)S(1)} %collective-permute-done.8.refs_0_, bf16[4,512,128]{2,1,0:T(8,128)(2,1)S(1)} %collective-permute-done.10.refs_1_, bf16[128,1536]{1,0:T(8,128)(2,1)S(1)} %get-tuple-element.45.refs_1_.refs_2_, ...), custom_call_target="tpu_custom_call" | custom-call | flops 2415919104 | bytes 9437184 | tf_op jit(solution)/shard_map/pallas_call | solution.py:210
  41.0 0.0 collective-permute-done.11.refs_0_
  41.0 0.3 collective-permute-start.12
  41.3 2.4 %shard_map.57 = (bf16[1536,1536]{1,0:T(8,128)(2,1)S(1)}, f32[32,1664]{1,0:T(8,128)S(1)}) custom-call(bf16[4,512,128]{2,1,0:T(8,128)(2,1)S(1)} %collective-permute-done.11.refs_0_, bf16[128,1536]{1,0:T(8,128)(2,1)S(1)} %get-tuple-element.45.refs_1_.refs_2_, f32[8,1536]{1,0:T(8,128)S(1)} %get-tuple-element.46.refs_2_.refs_3_, ...), custom_call_target="tpu_custom_call" | custom-call | flops 1207959552 | bytes 4718592 | tf_op jit(solution)/shard_map/pallas_call | solution.py:210
  43.7 0.0 collective-permute-done.12.refs_0_
  43.7 2.4 %shard_map.58 = (bf16[1536,1536]{1,0:T(8,128)(2,1)S(1)}, f32[32,512]{1,0:T(8,128)S(1)}, f32[32,512]{1,0:T(8,128)S(1)}, f32[32,512]{1,0:T(8,128)S(1)}, f32[32,512]{1,0:T(8,128)S(1)}) custom-call(bf16[4,512,128]{2,1,0:T(8,128)(2,1)S(1)} %collective-permute-done.12.refs_0_, bf16[128,1536]{1,0:T(8,128)(2,1)S(1)} %get-tuple-element.45.refs_1_.refs_2_, ...), custom_call_target="tpu_custom_call" | custom-call | flops 1207959552 | bytes 4718592 | tf_op jit(solution)/shard_map/pallas_call | solution.py:210
  46.1 0.9 collective-permute-start.13
  47.0 1.8 %collective-permute-start.14 = (f32[32,512]{1,0:T(8,128)S(1)}, f32[32,512]{1,0:T(8,128)S(1)}, u32[]{:S(2)}, u32[]{:S(2)}) collective-permute-start(f32[32,512]{1,0:T(8,128)S(1)} %get-tuple-element.63), channel_id=1, source_target_pairs={{0,2},{1,3},{2,0},{3,1},{4,6},{5,7},{6,4},{7,5},{8,10},{9,11},{10,... | collective-permute-start | bytes 196616 | tf_op jit(solution)/shard_map/ppermute | solution.py:66
  48.8 0.0 collective-permute-start.15
  48.8 1.4 %collective-permute-done.13.refs_1_ = f32[32,512]{1,0:T(8,128)S(1)} collective-permute-done((f32[32,512]{1,0:T(8,128)S(1)}, f32[32,512]{1,0:T(8,128)S(1)}, u32[]{:S(2)}, u32[]{:S(2)}) %collective-permute-start.13) | collective-permute-done | bytes 65568 | tf_op jit(solution)/shard_map/ppermute | solution.py:66
  50.2 2.3 %collective-permute-done.14.refs_2_ = f32[32,512]{1,0:T(8,128)S(1)} collective-permute-done((f32[32,512]{1,0:T(8,128)S(1)}, f32[32,512]{1,0:T(8,128)S(1)}, u32[]{:S(2)}, u32[]{:S(2)}) %collective-permute-start.14) | collective-permute-done | bytes 65568 | tf_op jit(solution)/shard_map/ppermute | solution.py:66
  52.5 0.0 collective-permute-done.15.refs_3_
  52.5 0.2 shard_map.59
  52.7 15.9 %all_to_all.10.refs_4_.refs_6_ = bf16[16,32,512]{2,1,0:T(8,128)(2,1)S(1)} all-to-all(bf16[16,32,512]{2,1,0:T(8,128)(2,1)S(1)} %get-tuple-element.67), channel_id=1, replica_groups={{0,6,24,30,32,38,56,62,64,70,88,94,96,102,120,126},{1,7,25,31,33,39,57,..., dimensions={0} | all-to-all | bytes 1048576 | tf_op jit(solution)/shard_map/all_to_all | solution.py:78
  68.6 3.2 %collective-permute-start.16 = (bf16[16,32,512]{2,1,0:T(8,128)(2,1)S(1)}, bf16[16,32,512]{2,1,0:T(8,128)(2,1)S(1)}, u32[]{:S(2)}, u32[]{:S(2)}) collective-permute-start(bf16[16,32,512]{2,1,0:T(8,128)(2,1)S(1)} %all_to_all.10.refs_4_.refs_6_), channel_id=1, source_target_pairs={{0,1},{1,0},{2,3},{3,2},{4,5},{5,4},{6,7},{7,6},{8,9},{9,8},{10,11... | collective-permute-start | bytes 1572872 | tf_op jit(solution)/shard_map/ppermute | solution.py:66
  71.8 3.5 %shard_map.60.refs_5_ = f32[32,1536]{1,0:T(8,128)S(1)} custom-call(bf16[1536,1536]{1,0:T(8,128)(2,1)S(1)} %get-tuple-element.68.refs_0_, bf16[3072,1536]{1,0:T(8,128)(2,1)S(1)} %get-tuple-element.52.refs_1_, bf16[3072,1536]{1,0:T(8,128)(2,1)S(1)} %get-tuple-element.55.refs_2_, bf16[1536,1536]{1,0:T(8,128)(2,1)S(1)} %get-tuple-element.69.refs_3_, ...), custom_call_target="tpu_custom_call" | custom-call | flops 4831838208 | bytes 18874368 | tf_op jit(solution)/shard_map/pallas_call | solution.py:235
  75.3 0.0 collective-permute-done.16.refs_4_
  75.3 3.5 %shard_map.61 = (f32[32,512]{1,0:T(8,128)S(1)}, f32[32,512]{1,0:T(8,128)S(1)}, f32[32,512]{1,0:T(8,128)S(1)}, f32[32,512]{1,0:T(8,128)S(1)}) custom-call(bf16[1536,1536]{1,0:T(8,128)(2,1)S(1)} %get-tuple-element.48.refs_0_, bf16[3072,1536]{1,0:T(8,128)(2,1)S(1)} %get-tuple-element.52.refs_1_, bf16[3072,1536]{1,0:T(8,128)(2,1)S(1)} %get-tuple-element.55.refs_2_, ...), custom_call_target="tpu_custom_call" | custom-call | flops 4831838208 | bytes 18874368 | tf_op jit(solution)/shard_map/pallas_call | solution.py:235
  78.8 0.0 collective-permute-start.17
  78.8 0.1 collective-permute-start.18
  78.9 2.5 %collective-permute-start.19 = (f32[32,512]{1,0:T(8,128)S(1)}, f32[32,512]{1,0:T(8,128)S(1)}, u32[]{:S(2)}, u32[]{:S(2)}) collective-permute-start(f32[32,512]{1,0:T(8,128)S(1)} %get-tuple-element.73), channel_id=1, source_target_pairs={{0,8},{1,9},{2,10},{3,11},{4,12},{5,13},{6,14},{7,15},{8,0},{9,1},... | collective-permute-start | bytes 196616 | tf_op jit(solution)/shard_map/ppermute | solution.py:66
  81.5 2.0 %collective-permute-done.17.refs_1_ = f32[32,512]{1,0:T(8,128)S(1)} collective-permute-done((f32[32,512]{1,0:T(8,128)S(1)}, f32[32,512]{1,0:T(8,128)S(1)}, u32[]{:S(2)}, u32[]{:S(2)}) %collective-permute-start.17) | collective-permute-done | bytes 65568 | tf_op jit(solution)/shard_map/ppermute | solution.py:66
  83.5 0.3 collective-permute-done.18.refs_2_
  83.8 0.0 collective-permute-done.19.refs_3_
  83.8 0.4 shard_map.62
  84.2 14.5 %all_to_all.11 = f32[128,1,32]{2,1,0:T(1,128)S(1)} all-to-all(f32[128,1,32]{2,1,0:T(1,128)S(1)} %bitcast.8), channel_id=1, replica_groups=mesh['pts'=128] {'pts'}, dimensions={0} | all-to-all | bytes 32768 | tf_op jit(solution)/shard_map/all_to_all | solution.py:471
  98.7 0.8 shard_map.63
  (1 shorter events, 0.0 us)
Async XLA Ops:
  0.6 8.1 %collective-permute-start.3 = (bf16[384,128]{1,0:T(8,128)(2,1)}, bf16[384,128]{1,0:T(8,128)(2,1)S(1)}, u32[]{:S(2)}, u32[]{:S(2)}) collective-permute-start(bf16[384,128]{1,0:T(8,128)(2,1)} %points_ref.1), channel_id=1, source_target_pairs={{0,10},{1,11},{2,8},{3,9},{4,14},{5,15},{6,12},{7,13},{8,2},{9,3},... | collective-permute-start | bytes 294920 | tf_op jit(solution)/shard_map/ppermute | solution.py:66
  5.2 7.5 %collective-permute-start.2 = (bf16[512,128]{1,0:T(8,128)(2,1)S(1)}, bf16[512,128]{1,0:T(8,128)(2,1)S(1)}, u32[]{:S(2)}, u32[]{:S(2)}) collective-permute-start(bf16[512,128]{1,0:T(8,128)(2,1)S(1)} %get-tuple-element.44.refs_0_), channel_id=1, source_target_pairs={{0,30},{1,97},{2,28},{3,99},{4,26},{5,101},{6,24},{7,103},{8,22},{... | collective-permute-start | bytes 393224 | tf_op jit(solution)/shard_map/ppermute | solution.py:66
  7.8 5.6 %collective-permute-start.1 = (bf16[512,128]{1,0:T(8,128)(2,1)S(1)}, bf16[512,128]{1,0:T(8,128)(2,1)S(1)}, u32[]{:S(2)}, u32[]{:S(2)}) collective-permute-start(bf16[512,128]{1,0:T(8,128)(2,1)S(1)} %get-tuple-element.44.refs_0_), channel_id=1, source_target_pairs={{0,24},{1,65},{2,26},{3,67},{4,28},{5,69},{6,30},{7,71},{8,16},{9,... | collective-permute-start | bytes 393224 | tf_op jit(solution)/shard_map/ppermute | solution.py:66
  8.3 5.1 %collective-permute-start = (bf16[512,128]{1,0:T(8,128)(2,1)S(1)}, bf16[512,128]{1,0:T(8,128)(2,1)S(1)}, u32[]{:S(2)}, u32[]{:S(2)}) collective-permute-start(bf16[512,128]{1,0:T(8,128)(2,1)S(1)} %get-tuple-element.44.refs_0_), channel_id=1, source_target_pairs={{0,6},{1,33},{2,4},{3,35},{4,2},{5,37},{6,0},{7,39},{8,14},{9,41},... | collective-permute-start | bytes 393224 | tf_op jit(solution)/shard_map/ppermute | solution.py:66
  8.5 4.0 %collective-permute-start.5 = (bf16[384,128]{1,0:T(8,128)(2,1)}, bf16[384,128]{1,0:T(8,128)(2,1)S(1)}, u32[]{:S(2)}, u32[]{:S(2)}) collective-permute-start(bf16[384,128]{1,0:T(8,128)(2,1)} %points_ref.1), channel_id=1, source_target_pairs={{0,8},{1,9},{2,10},{3,11},{4,12},{5,13},{6,14},{7,15},{8,0},{9,1},... | collective-permute-start | bytes 294920 | tf_op jit(solution)/shard_map/ppermute | solution.py:66
  8.7 4.0 %collective-permute-start.4 = (bf16[384,128]{1,0:T(8,128)(2,1)}, bf16[384,128]{1,0:T(8,128)(2,1)S(1)}, u32[]{:S(2)}, u32[]{:S(2)}) collective-permute-start(bf16[384,128]{1,0:T(8,128)(2,1)} %points_ref.1), channel_id=1, source_target_pairs={{0,2},{1,3},{2,0},{3,1},{4,6},{5,7},{6,4},{7,5},{8,10},{9,11},{10,... | collective-permute-start | bytes 294920 | tf_op jit(solution)/shard_map/ppermute | solution.py:66
  13.4 10.7 %collective-permute-start.6 = (bf16[4,512,128]{2,1,0:T(8,128)(2,1)S(1)}, bf16[4,512,128]{2,1,0:T(8,128)(2,1)S(1)}, u32[]{:S(2)}, u32[]{:S(2)}) collective-permute-start(bf16[4,512,128]{2,1,0:T(8,128)(2,1)S(1)} %shard_map.51.refs_0_), channel_id=1, source_target_pairs={{0,1},{1,0},{2,3},{3,2},{4,5},{5,4},{6,7},{7,6},{8,9},{9,8},{10,11... | collective-permute-start | bytes 1572872 | tf_op jit(solution)/shard_map/ppermute | solution.py:66
  17.7 9.5 %collective-permute-start.8 = (bf16[4,512,128]{2,1,0:T(8,128)(2,1)S(1)}, bf16[4,512,128]{2,1,0:T(8,128)(2,1)S(1)}, u32[]{:S(2)}, u32[]{:S(2)}) collective-permute-start(bf16[4,512,128]{2,1,0:T(8,128)(2,1)S(1)} %shard_map.51.refs_0_), channel_id=1, source_target_pairs={{0,96},{1,25},{2,98},{3,27},{4,100},{5,29},{6,102},{7,31},{8,104},... | collective-permute-start | bytes 1572872 | tf_op jit(solution)/shard_map/ppermute | solution.py:66
  19.6 9.2 %collective-permute-start.7 = (bf16[4,512,128]{2,1,0:T(8,128)(2,1)S(1)}, bf16[4,512,128]{2,1,0:T(8,128)(2,1)S(1)}, u32[]{:S(2)}, u32[]{:S(2)}) collective-permute-start(bf16[4,512,128]{2,1,0:T(8,128)(2,1)S(1)} %shard_map.51.refs_0_), channel_id=1, source_target_pairs={{0,32},{1,7},{2,34},{3,5},{4,36},{5,3},{6,38},{7,1},{8,40},{9,15},... | collective-permute-start | bytes 1572872 | tf_op jit(solution)/shard_map/ppermute | solution.py:66
  28.9 2.5 %collective-permute-start.9 = (bf16[4,512,128]{2,1,0:T(8,128)(2,1)S(1)}, bf16[4,512,128]{2,1,0:T(8,128)(2,1)S(1)}, u32[]{:S(2)}, u32[]{:S(2)}) collective-permute-start(bf16[4,512,128]{2,1,0:T(8,128)(2,1)S(1)} %collective-permute-done.7.refs_0_), channel_id=1, source_target_pairs={{0,1},{1,0},{2,3},{3,2},{4,5},{5,4},{6,7},{7,6},{8,9},{9,8},{10,11... | collective-permute-start | bytes 1572872 | tf_op jit(solution)/shard_map/ppermute | solution.py:66
  29.8 6.4 %collective-permute-start.10 = (bf16[4,512,128]{2,1,0:T(8,128)(2,1)S(1)}, bf16[4,512,128]{2,1,0:T(8,128)(2,1)S(1)}, u32[]{:S(2)}, u32[]{:S(2)}) collective-permute-start(bf16[4,512,128]{2,1,0:T(8,128)(2,1)S(1)} %collective-permute-done.8.refs_0_), channel_id=1, source_target_pairs={{0,1},{1,0},{2,3},{3,2},{4,5},{5,4},{6,7},{7,6},{8,9},{9,8},{10,11... | collective-permute-start | bytes 1572872 | tf_op jit(solution)/shard_map/ppermute | solution.py:66
  29.8 11.2 %collective-permute-start.11 = (bf16[4,512,128]{2,1,0:T(8,128)(2,1)S(1)}, bf16[4,512,128]{2,1,0:T(8,128)(2,1)S(1)}, u32[]{:S(2)}, u32[]{:S(2)}) collective-permute-start(bf16[4,512,128]{2,1,0:T(8,128)(2,1)S(1)} %collective-permute-done.8.refs_0_), channel_id=1, source_target_pairs={{0,32},{1,7},{2,34},{3,5},{4,36},{5,3},{6,38},{7,1},{8,40},{9,15},... | collective-permute-start | bytes 1572872 | tf_op jit(solution)/shard_map/ppermute | solution.py:66
  41.0 2.7 %collective-permute-start.12 = (bf16[4,512,128]{2,1,0:T(8,128)(2,1)S(1)}, bf16[4,512,128]{2,1,0:T(8,128)(2,1)S(1)}, u32[]{:S(2)}, u32[]{:S(2)}) collective-permute-start(bf16[4,512,128]{2,1,0:T(8,128)(2,1)S(1)} %collective-permute-done.11.refs_0_), channel_id=1, source_target_pairs={{0,1},{1,0},{2,3},{3,2},{4,5},{5,4},{6,7},{7,6},{8,9},{9,8},{10,11... | collective-permute-start | bytes 1572872 | tf_op jit(solution)/shard_map/ppermute | solution.py:66
  46.1 4.1 %collective-permute-start.13 = (f32[32,512]{1,0:T(8,128)S(1)}, f32[32,512]{1,0:T(8,128)S(1)}, u32[]{:S(2)}, u32[]{:S(2)}) collective-permute-start(f32[32,512]{1,0:T(8,128)S(1)} %get-tuple-element.62), channel_id=1, source_target_pairs={{0,10},{1,11},{2,8},{3,9},{4,14},{5,15},{6,12},{7,13},{8,2},{9,3},... | collective-permute-start | bytes 196616 | tf_op jit(solution)/shard_map/ppermute | solution.py:66
  47.0 5.4 %collective-permute-start.14 = (f32[32,512]{1,0:T(8,128)S(1)}, f32[32,512]{1,0:T(8,128)S(1)}, u32[]{:S(2)}, u32[]{:S(2)}) collective-permute-start(f32[32,512]{1,0:T(8,128)S(1)} %get-tuple-element.63), channel_id=1, source_target_pairs={{0,2},{1,3},{2,0},{3,1},{4,6},{5,7},{6,4},{7,5},{8,10},{9,11},{10,... | collective-permute-start | bytes 196616 | tf_op jit(solution)/shard_map/ppermute | solution.py:66
  48.8 3.7 %collective-permute-start.15 = (f32[32,512]{1,0:T(8,128)S(1)}, f32[32,512]{1,0:T(8,128)S(1)}, u32[]{:S(2)}, u32[]{:S(2)}) collective-permute-start(f32[32,512]{1,0:T(8,128)S(1)} %get-tuple-element.64), channel_id=1, source_target_pairs={{0,8},{1,9},{2,10},{3,11},{4,12},{5,13},{6,14},{7,15},{8,0},{9,1},... | collective-permute-start | bytes 196616 | tf_op jit(solution)/shard_map/ppermute | solution.py:66
  68.6 6.6 %collective-permute-start.16 = (bf16[16,32,512]{2,1,0:T(8,128)(2,1)S(1)}, bf16[16,32,512]{2,1,0:T(8,128)(2,1)S(1)}, u32[]{:S(2)}, u32[]{:S(2)}) collective-permute-start(bf16[16,32,512]{2,1,0:T(8,128)(2,1)S(1)} %all_to_all.10.refs_4_.refs_6_), channel_id=1, source_target_pairs={{0,1},{1,0},{2,3},{3,2},{4,5},{5,4},{6,7},{7,6},{8,9},{9,8},{10,11... | collective-permute-start | bytes 1572872 | tf_op jit(solution)/shard_map/ppermute | solution.py:66
  78.8 4.7 %collective-permute-start.17 = (f32[32,512]{1,0:T(8,128)S(1)}, f32[32,512]{1,0:T(8,128)S(1)}, u32[]{:S(2)}, u32[]{:S(2)}) collective-permute-start(f32[32,512]{1,0:T(8,128)S(1)} %get-tuple-element.71), channel_id=1, source_target_pairs={{0,10},{1,11},{2,8},{3,9},{4,14},{5,15},{6,12},{7,13},{8,2},{9,3},... | collective-permute-start | bytes 196616 | tf_op jit(solution)/shard_map/ppermute | solution.py:66
  78.8 5.0 %collective-permute-start.18 = (f32[32,512]{1,0:T(8,128)S(1)}, f32[32,512]{1,0:T(8,128)S(1)}, u32[]{:S(2)}, u32[]{:S(2)}) collective-permute-start(f32[32,512]{1,0:T(8,128)S(1)} %get-tuple-element.72), channel_id=1, source_target_pairs={{0,2},{1,3},{2,0},{3,1},{4,6},{5,7},{6,4},{7,5},{8,10},{9,11},{10,... | collective-permute-start | bytes 196616 | tf_op jit(solution)/shard_map/ppermute | solution.py:66
  78.9 4.9 %collective-permute-start.19 = (f32[32,512]{1,0:T(8,128)S(1)}, f32[32,512]{1,0:T(8,128)S(1)}, u32[]{:S(2)}, u32[]{:S(2)}) collective-permute-start(f32[32,512]{1,0:T(8,128)S(1)} %get-tuple-element.73), channel_id=1, source_target_pairs={{0,8},{1,9},{2,10},{3,11},{4,12},{5,13},{6,14},{7,15},{8,0},{9,1},... | collective-permute-start | bytes 196616 | tf_op jit(solution)/shard_map/ppermute | solution.py:66

commit v7 on v6

--- a/solution.py
+++ b/solution.py
@@ -19,8 +19,8 @@
 ODD_LINES = (0, 1, 2, 3)
 TURNS = 4
 CHIPS = SIDE * TURNS
-PAIR = 2
-UNROLL = 2
+PAIR = 1
+UNROLL = 4
 LANES = 128
 CHUNK = 512
 UNIT = 256
@@ -418,15 +418,15 @@
     for k in range(1, SIDE):
         side.append(partner(packed, reach(SIDE_MASKS, k), reach(LINE_MASKS, k)))
     near = exchange([points] * NEAR, NEAR_MASKS)
-    own = run_bundle(side, near[1:])
-    own_across = partner(own, CORE_MASK)
-    first, second = [partner(own, *line_masks(turn)) for turn in (1, 2)]
     near, half = small_call(
         functools.partial(prepare, scale_of(feats)),
         [((feats, NEAR * rows), points.dtype), ((8, NEAR * rows), jnp.float32)],
         packed,
         *near[1:],
     )
+    own = run_bundle(side, [half])
+    own_across = partner(own, CORE_MASK)
+    first, second = [partner(own, *line_masks(turn)) for turn in (1, 2)]
 
     def first_call(far, last, ending=False):
         return run_first(far, near, half, last, rows, cols, ending)

time: 99.7 us -> 101 us (1.013)
  Pallas kernels: 28.9 us -> 30.6 us
  waiting for transfers between devices: 13 us -> 11.9 us
    pallas_call x6, Pallas kernels: 19 us -> 20.8 us  [run_first(): pl.pallas_call(functools.partial(first_product, scale_of(feats), rows, le...]
    ppermute x20, waiting for transfers between devices: 13 us -> 11.9 us  [partner(): return lax.ppermute(value, 'pts', pairs)]
  transfers between devices with their start and end apart: 20 -> 20, of which waited for: 9 -> 10; matrix products, arithmetic and copies ran while one was open for 0% -> 0% of each run, Pallas kernels for 22% -> 23%
where the time goes in v7:
time: 101 us
  blocking collectives  30.7 us (30%)
  Pallas kernels  30.6 us (30%)
  starting transfers between devices  27.2 us (27%)
  waiting for transfers between devices  11.9 us (12%)
    ppermute x20, starting transfers between devices, partner(): return lax.ppermute(value, 'pts', pairs)  27.2 us
    pallas_call x6, Pallas kernels, run_first(): pl.pallas_call(functools.partial(first_product, scale_of(feats), rows, le...  20.8 us
    all_to_all x1, blocking collectives, share(): return lax.all_to_all(copies, 'pts', 0, 0, axis_index_groups=chip_groups())  16.2 us
    all_to_all x1, blocking collectives, per_device(): lax.all_to_all(curve[:, None, :], 'pts', 0, 0).reshape(DEVICES, cols)  14.5 us
    ppermute x20, waiting for transfers between devices, partner(): return lax.ppermute(value, 'pts', pairs)  11.9 us
    pallas_call x2, Pallas kernels, run_second(): pl.pallas_call(functools.partial(second_product, rows, core, starts), in_...  6.97 us
  transfers between devices with their start and end apart: 20, of which 10 were waited for; matrix products, arithmetic and copies ran while one was open for 0% of the time, Pallas kernels for 23%

profile of v7, /device:TPU:1, one launch (start us, length us, event | category | flops | bytes accessed | tf_op | source)
XLA Modules:
  0.0 101.1 jit_solution(6168588786058151797)
XLA Ops:
  0.6 3.6 %collective-permute-start.3 = (bf16[384,128]{1,0:T(8,128)(2,1)}, bf16[384,128]{1,0:T(8,128)(2,1)S(1)}, u32[]{:S(2)}, u32[]{:S(2)}) collective-permute-start(bf16[384,128]{1,0:T(8,128)(2,1)} %points_ref.1), channel_id=1, source_target_pairs={{0,10},{1,11},{2,8},{3,9},{4,14},{5,15},{6,12},{7,13},{8,2},{9,3},... | collective-permute-start | bytes 294920 | tf_op jit(solution)/shard_map/ppermute | solution.py:66
  4.2 1.0 shard_map.50
  5.2 2.6 %collective-permute-start.2 = (bf16[512,128]{1,0:T(8,128)(2,1)S(1)}, bf16[512,128]{1,0:T(8,128)(2,1)S(1)}, u32[]{:S(2)}, u32[]{:S(2)}) collective-permute-start(bf16[512,128]{1,0:T(8,128)(2,1)S(1)} %get-tuple-element.44.refs_0_), channel_id=1, source_target_pairs={{0,30},{1,97},{2,28},{3,99},{4,26},{5,101},{6,24},{7,103},{8,22},{... | collective-permute-start | bytes 393224 | tf_op jit(solution)/shard_map/ppermute | solution.py:66
  7.8 0.5 collective-permute-start.1
  8.3 0.3 collective-permute-start
  8.5 0.2 collective-permute-start.5
  8.7 0.0 collective-permute-done.3.refs_1_
  8.7 0.1 collective-permute-start.4
  8.8 3.7 %collective-permute-done.5.refs_3_ = bf16[384,128]{1,0:T(8,128)(2,1)S(1)} collective-permute-done((bf16[384,128]{1,0:T(8,128)(2,1)}, bf16[384,128]{1,0:T(8,128)(2,1)S(1)}, u32[]{:S(2)}, u32[]{:S(2)}) %collective-permute-start.5) | collective-permute-done | bytes 98336 | tf_op jit(solution)/shard_map/ppermute | solution.py:66
  12.5 0.2 collective-permute-done.4.refs_2_
  12.7 0.4 shard_map.51
  13.1 0.0 collective-permute-done.2.refs_3_
  13.1 0.3 collective-permute-done.1.refs_2_
  13.4 0.0 collective-permute-done.refs_1_
  13.4 4.3 %collective-permute-start.6 = (bf16[4,512,128]{2,1,0:T(8,128)(2,1)S(1)}, bf16[4,512,128]{2,1,0:T(8,128)(2,1)S(1)}, u32[]{:S(2)}, u32[]{:S(2)}) collective-permute-start(bf16[4,512,128]{2,1,0:T(8,128)(2,1)S(1)} %shard_map.52.refs_0_), channel_id=1, source_target_pairs={{0,1},{1,0},{2,3},{3,2},{4,5},{5,4},{6,7},{7,6},{8,9},{9,8},{10,11... | collective-permute-start | bytes 1572872 | tf_op jit(solution)/shard_map/ppermute | solution.py:66
  17.7 1.9 %collective-permute-start.8 = (bf16[4,512,128]{2,1,0:T(8,128)(2,1)S(1)}, bf16[4,512,128]{2,1,0:T(8,128)(2,1)S(1)}, u32[]{:S(2)}, u32[]{:S(2)}) collective-permute-start(bf16[4,512,128]{2,1,0:T(8,128)(2,1)S(1)} %shard_map.52.refs_0_), channel_id=1, source_target_pairs={{0,96},{1,25},{2,98},{3,27},{4,100},{5,29},{6,102},{7,31},{8,104},... | collective-permute-start | bytes 1572872 | tf_op jit(solution)/shard_map/ppermute | solution.py:66
  19.6 2.1 %collective-permute-start.7 = (bf16[4,512,128]{2,1,0:T(8,128)(2,1)S(1)}, bf16[4,512,128]{2,1,0:T(8,128)(2,1)S(1)}, u32[]{:S(2)}, u32[]{:S(2)}) collective-permute-start(bf16[4,512,128]{2,1,0:T(8,128)(2,1)S(1)} %shard_map.52.refs_0_), channel_id=1, source_target_pairs={{0,32},{1,7},{2,34},{3,5},{4,36},{5,3},{6,38},{7,1},{8,40},{9,15},... | collective-permute-start | bytes 1572872 | tf_op jit(solution)/shard_map/ppermute | solution.py:66
  21.7 2.5 %shard_map.53 = (bf16[1536,1536]{1,0:T(8,128)(2,1)S(1)}, f32[32,1664]{1,0:T(8,128)S(1)}) custom-call(bf16[4,512,128]{2,1,0:T(8,128)(2,1)S(1)} %shard_map.52.refs_0_, bf16[128,1536]{1,0:T(8,128)(2,1)S(1)} %get-tuple-element.46.refs_1_.refs_2_, f32[8,1536]{1,0:T(8,128)S(1)} %get-tuple-element.45.refs_4_.refs_2_.refs_3_), custom_call_target="tpu_custom_call" | custom-call | flops 1207959552 | bytes 4718592 | tf_op jit(solution)/shard_map/pallas_call | solution.py:210
  24.3 0.0 collective-permute-done.6.refs_0_
  24.3 2.6 %shard_map.54 = (bf16[1536,1536]{1,0:T(8,128)(2,1)S(1)}, f32[32,1664]{1,0:T(8,128)S(1)}) custom-call(bf16[4,512,128]{2,1,0:T(8,128)(2,1)S(1)} %collective-permute-done.6.refs_0_, bf16[128,1536]{1,0:T(8,128)(2,1)S(1)} %get-tuple-element.46.refs_1_.refs_2_, f32[8,1536]{1,0:T(8,128)S(1)} %get-tuple-element.45.refs_4_.refs_2_.refs_3_, ...), custom_call_target="tpu_custom_call" | custom-call | flops 1207959552 | bytes 4718592 | tf_op jit(solution)/shard_map/pallas_call | solution.py:210
  26.9 0.4 collective-permute-done.8.refs_0_
  27.3 1.6 %collective-permute-done.7.refs_0_ = bf16[4,512,128]{2,1,0:T(8,128)(2,1)S(1)} collective-permute-done((bf16[4,512,128]{2,1,0:T(8,128)(2,1)S(1)}, bf16[4,512,128]{2,1,0:T(8,128)(2,1)S(1)}, u32[]{:S(2)}, u32[]{:S(2)}) %collective-permute-start.7) | collective-permute-done | bytes 524320 | tf_op jit(solution)/shard_map/ppermute | solution.py:66
  28.9 0.9 collective-permute-start.9
  29.8 0.0 collective-permute-start.10
  29.8 2.0 %collective-permute-start.11 = (bf16[4,512,128]{2,1,0:T(8,128)(2,1)S(1)}, bf16[4,512,128]{2,1,0:T(8,128)(2,1)S(1)}, u32[]{:S(2)}, u32[]{:S(2)}) collective-permute-start(bf16[4,512,128]{2,1,0:T(8,128)(2,1)S(1)} %collective-permute-done.8.refs_0_), channel_id=1, source_target_pairs={{0,32},{1,7},{2,34},{3,5},{4,36},{5,3},{6,38},{7,1},{8,40},{9,15},... | collective-permute-start | bytes 1572872 | tf_op jit(solution)/shard_map/ppermute | solution.py:66
  31.8 0.0 collective-permute-done.9.refs_1_
  31.8 5.2 %shard_map.55 = (bf16[3072,1536]{1,0:T(8,128)(2,1)S(1)}, f32[32,1664]{1,0:T(8,128)S(1)}) custom-call(bf16[4,512,128]{2,1,0:T(8,128)(2,1)S(1)} %collective-permute-done.7.refs_0_, bf16[4,512,128]{2,1,0:T(8,128)(2,1)S(1)} %collective-permute-done.9.refs_1_, bf16[128,1536]{1,0:T(8,128)(2,1)S(1)} %get-tuple-element.46.refs_1_.refs_2_, ...), custom_call_target="tpu_custom_call" | custom-call | flops 2415919104 | bytes 9437184 | tf_op jit(solution)/shard_map/pallas_call | solution.py:210
  37.0 0.0 collective-permute-done.10.refs_1_
  37.0 5.2 %shard_map.56 = (bf16[3072,1536]{1,0:T(8,128)(2,1)S(1)}, f32[32,1664]{1,0:T(8,128)S(1)}) custom-call(bf16[4,512,128]{2,1,0:T(8,128)(2,1)S(1)} %collective-permute-done.8.refs_0_, bf16[4,512,128]{2,1,0:T(8,128)(2,1)S(1)} %collective-permute-done.10.refs_1_, bf16[128,1536]{1,0:T(8,128)(2,1)S(1)} %get-tuple-element.46.refs_1_.refs_2_, ...), custom_call_target="tpu_custom_call" | custom-call | flops 2415919104 | bytes 9437184 | tf_op jit(solution)/shard_map/pallas_call | solution.py:210
  42.3 0.0 collective-permute-done.11.refs_0_
  42.3 0.0 collective-permute-start.12
  42.3 2.6 %shard_map.57 = (bf16[1536,1536]{1,0:T(8,128)(2,1)S(1)}, f32[32,1664]{1,0:T(8,128)S(1)}) custom-call(bf16[4,512,128]{2,1,0:T(8,128)(2,1)S(1)} %collective-permute-done.11.refs_0_, bf16[128,1536]{1,0:T(8,128)(2,1)S(1)} %get-tuple-element.46.refs_1_.refs_2_, f32[8,1536]{1,0:T(8,128)S(1)} %get-tuple-element.45.refs_4_.refs_2_.refs_3_, ...), custom_call_target="tpu_custom_call" | custom-call | flops 1207959552 | bytes 4718592 | tf_op jit(solution)/shard_map/pallas_call | solution.py:210
  44.9 0.0 collective-permute-done.12.refs_0_
  44.9 2.6 %shard_map.58 = (bf16[1536,1536]{1,0:T(8,128)(2,1)S(1)}, f32[32,512]{1,0:T(8,128)S(1)}, f32[32,512]{1,0:T(8,128)S(1)}, f32[32,512]{1,0:T(8,128)S(1)}, f32[32,512]{1,0:T(8,128)S(1)}) custom-call(bf16[4,512,128]{2,1,0:T(8,128)(2,1)S(1)} %collective-permute-done.12.refs_0_, bf16[128,1536]{1,0:T(8,128)(2,1)S(1)} %get-tuple-element.46.refs_1_.refs_2_, ...), custom_call_target="tpu_custom_call" | custom-call | flops 1207959552 | bytes 4718592 | tf_op jit(solution)/shard_map/pallas_call | solution.py:210
  47.5 1.1 %collective-permute-start.13 = (f32[32,512]{1,0:T(8,128)S(1)}, f32[32,512]{1,0:T(8,128)S(1)}, u32[]{:S(2)}, u32[]{:S(2)}) collective-permute-start(f32[32,512]{1,0:T(8,128)S(1)} %get-tuple-element.62), channel_id=1, source_target_pairs={{0,10},{1,11},{2,8},{3,9},{4,14},{5,15},{6,12},{7,13},{8,2},{9,3},... | collective-permute-start | bytes 196616 | tf_op jit(solution)/shard_map/ppermute | solution.py:66
  48.6 1.8 %collective-permute-start.14 = (f32[32,512]{1,0:T(8,128)S(1)}, f32[32,512]{1,0:T(8,128)S(1)}, u32[]{:S(2)}, u32[]{:S(2)}) collective-permute-start(f32[32,512]{1,0:T(8,128)S(1)} %get-tuple-element.63), channel_id=1, source_target_pairs={{0,2},{1,3},{2,0},{3,1},{4,6},{5,7},{6,4},{7,5},{8,10},{9,11},{10,... | collective-permute-start | bytes 196616 | tf_op jit(solution)/shard_map/ppermute | solution.py:66
  50.4 0.0 collective-permute-start.15
  50.4 1.1 %collective-permute-done.13.refs_1_ = f32[32,512]{1,0:T(8,128)S(1)} collective-permute-done((f32[32,512]{1,0:T(8,128)S(1)}, f32[32,512]{1,0:T(8,128)S(1)}, u32[]{:S(2)}, u32[]{:S(2)}) %collective-permute-start.13) | collective-permute-done | bytes 65568 | tf_op jit(solution)/shard_map/ppermute | solution.py:66
  51.5 2.1 %collective-permute-done.14.refs_2_ = f32[32,512]{1,0:T(8,128)S(1)} collective-permute-done((f32[32,512]{1,0:T(8,128)S(1)}, f32[32,512]{1,0:T(8,128)S(1)}, u32[]{:S(2)}, u32[]{:S(2)}) %collective-permute-start.14) | collective-permute-done | bytes 65568 | tf_op jit(solution)/shard_map/ppermute | solution.py:66
  53.6 0.2 collective-permute-done.15.refs_3_
  53.8 0.2 shard_map.59
  54.1 16.2 %all_to_all.10.refs_4_.refs_6_ = bf16[16,32,512]{2,1,0:T(8,128)(2,1)S(1)} all-to-all(bf16[16,32,512]{2,1,0:T(8,128)(2,1)S(1)} %get-tuple-element.67), channel_id=1, replica_groups={{0,6,24,30,32,38,56,62,64,70,88,94,96,102,120,126},{1,7,25,31,33,39,57,..., dimensions={0} | all-to-all | bytes 1048576 | tf_op jit(solution)/shard_map/all_to_all | solution.py:78
  70.3 3.1 %collective-permute-start.16 = (bf16[16,32,512]{2,1,0:T(8,128)(2,1)S(1)}, bf16[16,32,512]{2,1,0:T(8,128)(2,1)S(1)}, u32[]{:S(2)}, u32[]{:S(2)}) collective-permute-start(bf16[16,32,512]{2,1,0:T(8,128)(2,1)S(1)} %all_to_all.10.refs_4_.refs_6_), channel_id=1, source_target_pairs={{0,1},{1,0},{2,3},{3,2},{4,5},{5,4},{6,7},{7,6},{8,9},{9,8},{10,11... | collective-permute-start | bytes 1572872 | tf_op jit(solution)/shard_map/ppermute | solution.py:66
  73.4 3.5 %shard_map.60.refs_5_ = f32[32,1536]{1,0:T(8,128)S(1)} custom-call(bf16[1536,1536]{1,0:T(8,128)(2,1)S(1)} %get-tuple-element.68.refs_0_, bf16[3072,1536]{1,0:T(8,128)(2,1)S(1)} %get-tuple-element.52.refs_1_, bf16[3072,1536]{1,0:T(8,128)(2,1)S(1)} %get-tuple-element.55.refs_2_, bf16[1536,1536]{1,0:T(8,128)(2,1)S(1)} %get-tuple-element.69.refs_3_, ...), custom_call_target="tpu_custom_call" | custom-call | flops 4831838208 | bytes 18874368 | tf_op jit(solution)/shard_map/pallas_call | solution.py:235
  76.9 0.0 collective-permute-done.16.refs_4_
  76.9 3.5 %shard_map.61 = (f32[32,512]{1,0:T(8,128)S(1)}, f32[32,512]{1,0:T(8,128)S(1)}, f32[32,512]{1,0:T(8,128)S(1)}, f32[32,512]{1,0:T(8,128)S(1)}) custom-call(bf16[1536,1536]{1,0:T(8,128)(2,1)S(1)} %get-tuple-element.48.refs_0_, bf16[3072,1536]{1,0:T(8,128)(2,1)S(1)} %get-tuple-element.52.refs_1_, bf16[3072,1536]{1,0:T(8,128)(2,1)S(1)} %get-tuple-element.55.refs_2_, ...), custom_call_target="tpu_custom_call" | custom-call | flops 4831838208 | bytes 18874368 | tf_op jit(solution)/shard_map/pallas_call | solution.py:235
  80.4 0.0 collective-permute-start.17
  80.4 0.1 collective-permute-start.18
  80.5 2.5 %collective-permute-start.19 = (f32[32,512]{1,0:T(8,128)S(1)}, f32[32,512]{1,0:T(8,128)S(1)}, u32[]{:S(2)}, u32[]{:S(2)}) collective-permute-start(f32[32,512]{1,0:T(8,128)S(1)} %get-tuple-element.73), channel_id=1, source_target_pairs={{0,8},{1,9},{2,10},{3,11},{4,12},{5,13},{6,14},{7,15},{8,0},{9,1},... | collective-permute-start | bytes 196616 | tf_op jit(solution)/shard_map/ppermute | solution.py:66
  83.1 2.0 %collective-permute-done.17.refs_1_ = f32[32,512]{1,0:T(8,128)S(1)} collective-permute-done((f32[32,512]{1,0:T(8,128)S(1)}, f32[32,512]{1,0:T(8,128)S(1)}, u32[]{:S(2)}, u32[]{:S(2)}) %collective-permute-start.17) | collective-permute-done | bytes 65568 | tf_op jit(solution)/shard_map/ppermute | solution.py:66
  85.1 0.3 collective-permute-done.18.refs_2_
  85.4 0.0 collective-permute-done.19.refs_3_
  85.4 0.4 shard_map.62
  85.9 14.5 %all_to_all.11 = f32[128,1,32]{2,1,0:T(1,128)S(1)} all-to-all(f32[128,1,32]{2,1,0:T(1,128)S(1)} %bitcast.8), channel_id=1, replica_groups=mesh['pts'=128] {'pts'}, dimensions={0} | all-to-all | bytes 32768 | tf_op jit(solution)/shard_map/all_to_all | solution.py:471
  100.3 0.8 shard_map.63
  (1 shorter events, 0.0 us)
Async XLA Ops:
  0.6 8.1 %collective-permute-start.3 = (bf16[384,128]{1,0:T(8,128)(2,1)}, bf16[384,128]{1,0:T(8,128)(2,1)S(1)}, u32[]{:S(2)}, u32[]{:S(2)}) collective-permute-start(bf16[384,128]{1,0:T(8,128)(2,1)} %points_ref.1), channel_id=1, source_target_pairs={{0,10},{1,11},{2,8},{3,9},{4,14},{5,15},{6,12},{7,13},{8,2},{9,3},... | collective-permute-start | bytes 294920 | tf_op jit(solution)/shard_map/ppermute | solution.py:66
  5.2 7.9 %collective-permute-start.2 = (bf16[512,128]{1,0:T(8,128)(2,1)S(1)}, bf16[512,128]{1,0:T(8,128)(2,1)S(1)}, u32[]{:S(2)}, u32[]{:S(2)}) collective-permute-start(bf16[512,128]{1,0:T(8,128)(2,1)S(1)} %get-tuple-element.44.refs_0_), channel_id=1, source_target_pairs={{0,30},{1,97},{2,28},{3,99},{4,26},{5,101},{6,24},{7,103},{8,22},{... | collective-permute-start | bytes 393224 | tf_op jit(solution)/shard_map/ppermute | solution.py:66
  7.8 5.6 %collective-permute-start.1 = (bf16[512,128]{1,0:T(8,128)(2,1)S(1)}, bf16[512,128]{1,0:T(8,128)(2,1)S(1)}, u32[]{:S(2)}, u32[]{:S(2)}) collective-permute-start(bf16[512,128]{1,0:T(8,128)(2,1)S(1)} %get-tuple-element.44.refs_0_), channel_id=1, source_target_pairs={{0,24},{1,65},{2,26},{3,67},{4,28},{5,69},{6,30},{7,71},{8,16},{9,... | collective-permute-start | bytes 393224 | tf_op jit(solution)/shard_map/ppermute | solution.py:66
  8.3 5.1 %collective-permute-start = (bf16[512,128]{1,0:T(8,128)(2,1)S(1)}, bf16[512,128]{1,0:T(8,128)(2,1)S(1)}, u32[]{:S(2)}, u32[]{:S(2)}) collective-permute-start(bf16[512,128]{1,0:T(8,128)(2,1)S(1)} %get-tuple-element.44.refs_0_), channel_id=1, source_target_pairs={{0,6},{1,33},{2,4},{3,35},{4,2},{5,37},{6,0},{7,39},{8,14},{9,41},... | collective-permute-start | bytes 393224 | tf_op jit(solution)/shard_map/ppermute | solution.py:66
  8.5 4.0 %collective-permute-start.5 = (bf16[384,128]{1,0:T(8,128)(2,1)}, bf16[384,128]{1,0:T(8,128)(2,1)S(1)}, u32[]{:S(2)}, u32[]{:S(2)}) collective-permute-start(bf16[384,128]{1,0:T(8,128)(2,1)} %points_ref.1), channel_id=1, source_target_pairs={{0,8},{1,9},{2,10},{3,11},{4,12},{5,13},{6,14},{7,15},{8,0},{9,1},... | collective-permute-start | bytes 294920 | tf_op jit(solution)/shard_map/ppermute | solution.py:66
  8.7 4.0 %collective-permute-start.4 = (bf16[384,128]{1,0:T(8,128)(2,1)}, bf16[384,128]{1,0:T(8,128)(2,1)S(1)}, u32[]{:S(2)}, u32[]{:S(2)}) collective-permute-start(bf16[384,128]{1,0:T(8,128)(2,1)} %points_ref.1), channel_id=1, source_target_pairs={{0,2},{1,3},{2,0},{3,1},{4,6},{5,7},{6,4},{7,5},{8,10},{9,11},{10,... | collective-permute-start | bytes 294920 | tf_op jit(solution)/shard_map/ppermute | solution.py:66
  13.4 10.9 %collective-permute-start.6 = (bf16[4,512,128]{2,1,0:T(8,128)(2,1)S(1)}, bf16[4,512,128]{2,1,0:T(8,128)(2,1)S(1)}, u32[]{:S(2)}, u32[]{:S(2)}) collective-permute-start(bf16[4,512,128]{2,1,0:T(8,128)(2,1)S(1)} %shard_map.52.refs_0_), channel_id=1, source_target_pairs={{0,1},{1,0},{2,3},{3,2},{4,5},{5,4},{6,7},{7,6},{8,9},{9,8},{10,11... | collective-permute-start | bytes 1572872 | tf_op jit(solution)/shard_map/ppermute | solution.py:66
  17.7 9.5 %collective-permute-start.8 = (bf16[4,512,128]{2,1,0:T(8,128)(2,1)S(1)}, bf16[4,512,128]{2,1,0:T(8,128)(2,1)S(1)}, u32[]{:S(2)}, u32[]{:S(2)}) collective-permute-start(bf16[4,512,128]{2,1,0:T(8,128)(2,1)S(1)} %shard_map.52.refs_0_), channel_id=1, source_target_pairs={{0,96},{1,25},{2,98},{3,27},{4,100},{5,29},{6,102},{7,31},{8,104},... | collective-permute-start | bytes 1572872 | tf_op jit(solution)/shard_map/ppermute | solution.py:66
  19.6 9.2 %collective-permute-start.7 = (bf16[4,512,128]{2,1,0:T(8,128)(2,1)S(1)}, bf16[4,512,128]{2,1,0:T(8,128)(2,1)S(1)}, u32[]{:S(2)}, u32[]{:S(2)}) collective-permute-start(bf16[4,512,128]{2,1,0:T(8,128)(2,1)S(1)} %shard_map.52.refs_0_), channel_id=1, source_target_pairs={{0,32},{1,7},{2,34},{3,5},{4,36},{5,3},{6,38},{7,1},{8,40},{9,15},... | collective-permute-start | bytes 1572872 | tf_op jit(solution)/shard_map/ppermute | solution.py:66
  28.9 2.9 %collective-permute-start.9 = (bf16[4,512,128]{2,1,0:T(8,128)(2,1)S(1)}, bf16[4,512,128]{2,1,0:T(8,128)(2,1)S(1)}, u32[]{:S(2)}, u32[]{:S(2)}) collective-permute-start(bf16[4,512,128]{2,1,0:T(8,128)(2,1)S(1)} %collective-permute-done.7.refs_0_), channel_id=1, source_target_pairs={{0,1},{1,0},{2,3},{3,2},{4,5},{5,4},{6,7},{7,6},{8,9},{9,8},{10,11... | collective-permute-start | bytes 1572872 | tf_op jit(solution)/shard_map/ppermute | solution.py:66
  29.8 7.3 %collective-permute-start.10 = (bf16[4,512,128]{2,1,0:T(8,128)(2,1)S(1)}, bf16[4,512,128]{2,1,0:T(8,128)(2,1)S(1)}, u32[]{:S(2)}, u32[]{:S(2)}) collective-permute-start(bf16[4,512,128]{2,1,0:T(8,128)(2,1)S(1)} %collective-permute-done.8.refs_0_), channel_id=1, source_target_pairs={{0,1},{1,0},{2,3},{3,2},{4,5},{5,4},{6,7},{7,6},{8,9},{9,8},{10,11... | collective-permute-start | bytes 1572872 | tf_op jit(solution)/shard_map/ppermute | solution.py:66
  29.8 12.5 %collective-permute-start.11 = (bf16[4,512,128]{2,1,0:T(8,128)(2,1)S(1)}, bf16[4,512,128]{2,1,0:T(8,128)(2,1)S(1)}, u32[]{:S(2)}, u32[]{:S(2)}) collective-permute-start(bf16[4,512,128]{2,1,0:T(8,128)(2,1)S(1)} %collective-permute-done.8.refs_0_), channel_id=1, source_target_pairs={{0,32},{1,7},{2,34},{3,5},{4,36},{5,3},{6,38},{7,1},{8,40},{9,15},... | collective-permute-start | bytes 1572872 | tf_op jit(solution)/shard_map/ppermute | solution.py:66
  42.3 2.6 %collective-permute-start.12 = (bf16[4,512,128]{2,1,0:T(8,128)(2,1)S(1)}, bf16[4,512,128]{2,1,0:T(8,128)(2,1)S(1)}, u32[]{:S(2)}, u32[]{:S(2)}) collective-permute-start(bf16[4,512,128]{2,1,0:T(8,128)(2,1)S(1)} %collective-permute-done.11.refs_0_), channel_id=1, source_target_pairs={{0,1},{1,0},{2,3},{3,2},{4,5},{5,4},{6,7},{7,6},{8,9},{9,8},{10,11... | collective-permute-start | bytes 1572872 | tf_op jit(solution)/shard_map/ppermute | solution.py:66
  47.5 4.0 %collective-permute-start.13 = (f32[32,512]{1,0:T(8,128)S(1)}, f32[32,512]{1,0:T(8,128)S(1)}, u32[]{:S(2)}, u32[]{:S(2)}) collective-permute-start(f32[32,512]{1,0:T(8,128)S(1)} %get-tuple-element.62), channel_id=1, source_target_pairs={{0,10},{1,11},{2,8},{3,9},{4,14},{5,15},{6,12},{7,13},{8,2},{9,3},... | collective-permute-start | bytes 196616 | tf_op jit(solution)/shard_map/ppermute | solution.py:66
  48.6 5.0 %collective-permute-start.14 = (f32[32,512]{1,0:T(8,128)S(1)}, f32[32,512]{1,0:T(8,128)S(1)}, u32[]{:S(2)}, u32[]{:S(2)}) collective-permute-start(f32[32,512]{1,0:T(8,128)S(1)} %get-tuple-element.63), channel_id=1, source_target_pairs={{0,2},{1,3},{2,0},{3,1},{4,6},{5,7},{6,4},{7,5},{8,10},{9,11},{10,... | collective-permute-start | bytes 196616 | tf_op jit(solution)/shard_map/ppermute | solution.py:66
  50.4 3.4 %collective-permute-start.15 = (f32[32,512]{1,0:T(8,128)S(1)}, f32[32,512]{1,0:T(8,128)S(1)}, u32[]{:S(2)}, u32[]{:S(2)}) collective-permute-start(f32[32,512]{1,0:T(8,128)S(1)} %get-tuple-element.64), channel_id=1, source_target_pairs={{0,8},{1,9},{2,10},{3,11},{4,12},{5,13},{6,14},{7,15},{8,0},{9,1},... | collective-permute-start | bytes 196616 | tf_op jit(solution)/shard_map/ppermute | solution.py:66
  70.3 6.6 %collective-permute-start.16 = (bf16[16,32,512]{2,1,0:T(8,128)(2,1)S(1)}, bf16[16,32,512]{2,1,0:T(8,128)(2,1)S(1)}, u32[]{:S(2)}, u32[]{:S(2)}) collective-permute-start(bf16[16,32,512]{2,1,0:T(8,128)(2,1)S(1)} %all_to_all.10.refs_4_.refs_6_), channel_id=1, source_target_pairs={{0,1},{1,0},{2,3},{3,2},{4,5},{5,4},{6,7},{7,6},{8,9},{9,8},{10,11... | collective-permute-start | bytes 1572872 | tf_op jit(solution)/shard_map/ppermute | solution.py:66
  80.4 4.7 %collective-permute-start.17 = (f32[32,512]{1,0:T(8,128)S(1)}, f32[32,512]{1,0:T(8,128)S(1)}, u32[]{:S(2)}, u32[]{:S(2)}) collective-permute-start(f32[32,512]{1,0:T(8,128)S(1)} %get-tuple-element.71), channel_id=1, source_target_pairs={{0,10},{1,11},{2,8},{3,9},{4,14},{5,15},{6,12},{7,13},{8,2},{9,3},... | collective-permute-start | bytes 196616 | tf_op jit(solution)/shard_map/ppermute | solution.py:66
  80.4 5.0 %collective-permute-start.18 = (f32[32,512]{1,0:T(8,128)S(1)}, f32[32,512]{1,0:T(8,128)S(1)}, u32[]{:S(2)}, u32[]{:S(2)}) collective-permute-start(f32[32,512]{1,0:T(8,128)S(1)} %get-tuple-element.72), channel_id=1, source_target_pairs={{0,2},{1,3},{2,0},{3,1},{4,6},{5,7},{6,4},{7,5},{8,10},{9,11},{10,... | collective-permute-start | bytes 196616 | tf_op jit(solution)/shard_map/ppermute | solution.py:66
  80.5 4.9 %collective-permute-start.19 = (f32[32,512]{1,0:T(8,128)S(1)}, f32[32,512]{1,0:T(8,128)S(1)}, u32[]{:S(2)}, u32[]{:S(2)}) collective-permute-start(f32[32,512]{1,0:T(8,128)S(1)} %get-tuple-element.73), channel_id=1, source_target_pairs={{0,8},{1,9},{2,10},{3,11},{4,12},{5,13},{6,14},{7,15},{8,0},{9,1},... | collective-permute-start | bytes 196616 | tf_op jit(solution)/shard_map/ppermute | solution.py:66

commit v8 on v6

--- a/solution.py
+++ b/solution.py
@@ -19,8 +19,6 @@
 ODD_LINES = (0, 1, 2, 3)
 TURNS = 4
 CHIPS = SIDE * TURNS
-PAIR = 2
-UNROLL = 2
 LANES = 128
 CHUNK = 512
 UNIT = 256
@@ -102,55 +100,64 @@
 def first_product(scale, rows, count, opening, ending, *refs):
     far_refs = refs[:count]
     near_ref, half_ref = refs[count : count + 2]
-    kern_ref, sum_ref, far_ref = refs[count + 2 + (0 if opening else 1) :][:1] + refs[-2:]
+    kern_ref = refs[count + 2 + (0 if opening else 1)]
+    sum_ref, far_ref, vec_ref = refs[-3:]
     sum_ref[...] = jnp.zeros_like(sum_ref) if opening else refs[count + 2][...]
     cols = sum_ref.shape[0]
-    width = near_ref.shape[1]
-    chunks = width // UNIT
-    tall = rows + cols * (rows // near_ref.shape[0])
+    feats, width = near_ref.shape
+    tall = rows + cols * (rows // feats)
     for k, ref in enumerate(far_refs):
-        far_ref[pl.ds(k * SIDE, SIDE)] = ref[...]
         for j in range(SIDE):
+            at = (k * SIDE + j) * rows
+            far_ref[pl.ds(at, rows), :] = ref[j, :rows, :]
+            for n in range(rows // feats):
+                part = pl.ds(at + n * feats, feats)
+                vec_ref[:, part] = ref[j, pl.ds(rows + n * cols, cols), :]
             sum_ref[:, width:] += ref[j, pl.ds(tall, cols), :].astype(jnp.float32)
 
-    @pl.loop(0, far_ref.shape[0] // (PAIR * UNROLL))
+    bundle_rows = SIDE * rows
+
+    @pl.loop(0, count)
     def _(step):
-        units, far, vec, far_half, here = [], [], [], [], []
-        for u in range(UNROLL):
-            first = PAIR * (UNROLL * step + u)
-            block = jnp.concatenate([far_ref[first + k, :rows, :] for k in range(PAIR)], axis=0)
-            pieces = [
-                far_ref[first + k, pl.ds(at, cols), :]
-                for k in range(PAIR)
-                for at in range(rows, tall, cols)
-            ]
+        far, vec, far_half, here, units = [], [], [], [], []
+        for r in range(bundle_rows // UNIT):
+            at = pl.ds(pl.multiple_of(step * bundle_rows + r * UNIT, UNIT), UNIT)
+            block = far_ref[at, :]
             block_f = block.astype(jnp.float32)
             far.append(block)
-            vec.append(jnp.concatenate(pieces, axis=1))
+            vec.append(vec_ref[:, at])
             far_half.append(jnp.sum(block_f * block_f, axis=1, keepdims=True) * (-0.5 * scale))
-            here.append(pl.ds(pl.multiple_of(first * rows, PAIR * rows), PAIR * rows))
-            units += [(u, pl.ds(c * UNIT, UNIT)) for c in range(chunks)]
-        cross, tile = {}, {}
-        for c in range(len(units) + 2):
-            if c < len(units):
-                u, part = units[c]
-                cross[c] = jnp.dot(far[u], near_ref[:, part], preferred_element_type=jnp.float32)
-            if 0 <= c - 1 < len(units):
-                u, part = units[c - 1]
-                tile[c - 1] = jnp.exp2(
-                    cross.pop(c - 1) * scale + far_half[u] + half_ref[0:1, part]
+            here.append(at)
+        for c in range(width // UNIT):
+            units += [(r, c) for r in range(len(far))]
+        cross, tile, image = {}, {}, {}
+        for n in range(len(units) + 2):
+            if n < len(units):
+                r, c = units[n]
+                near = near_ref[:, pl.ds(c * UNIT, UNIT)]
+                cross[n] = jnp.dot(far[r], near, preferred_element_type=jnp.float32)
+            if 0 <= n - 1 < len(units):
+                r, c = units[n - 1]
+                part = pl.ds(c * UNIT, UNIT)
+                tile[n - 1] = jnp.exp2(
+                    cross.pop(n - 1) * scale + far_half[r] + half_ref[0:1, part]
                 ).astype(jnp.bfloat16)
-                kern_ref[here[u], part] = tile[c - 1]
-            if 0 <= c - 2 < len(units):
-                u, part = units[c - 2]
-                sum_ref[:, part] += jnp.dot(
-                    vec[u], tile.pop(c - 2), preferred_element_type=jnp.float32
-                )
+                kern_ref[here[r], part] = tile[n - 1]
+            if 0 <= n - 2 < len(units):
+                r, c = units[n - 2]
+                value = jnp.dot(vec[r], tile.pop(n - 2), preferred_element_type=jnp.float32)
+                image[c] = value if r == 0 else image[c] + value
+                if r == len(far) - 1:
+                    sum_ref[:, pl.ds(c * UNIT, UNIT)] += image.pop(c)
 
     if ending:
-        for k, ref in enumerate(refs[-2 - NEAR : -2]):
-            ref[:, :rows] = sum_ref[:, pl.ds(k * rows, rows)]
-            ref[:, rows:] = sum_ref[:, width:]
+        write_parts(rows, width, sum_ref, refs[-3 - NEAR : -3])
+
+
+def write_parts(rows, width, sum_ref, outs):
+    for k, ref in enumerate(outs):
+        ref[:, :rows] = sum_ref[:, pl.ds(k * rows, rows)]
+        ref[:, rows:] = sum_ref[:, width:]
 
 
 def second_product(rows, core, starts, *refs):
@@ -212,7 +219,8 @@
         in_specs=[INSIDE] * len(inputs),
         out_specs=[INSIDE] * (1 + len(outs)),
         out_shape=[pltpu.VMEM((count, width), jnp.bfloat16)] + outs,
-        scratch_shapes=scratch + [pltpu.VMEM((len(far) * SIDE,) + far[0].shape[1:], jnp.bfloat16)],
+        scratch_shapes=scratch
+        + [pltpu.VMEM((count, feats), jnp.bfloat16), pltpu.VMEM((cols, count), jnp.bfloat16)],
         compiler_params=pltpu.CompilerParams(vmem_limit_bytes=LIMIT),
         cost_estimate=pl.CostEstimate(
             flops=4 * count * width * feats,

time: 99.7 us -> 101 us (1.013)
  Pallas kernels: 28.9 us -> 31.2 us
    pallas_call x6, Pallas kernels: 19 us -> 21.3 us  [run_first(): pl.pallas_call(functools.partial(first_product, scale_of(feats), rows, le...]
  transfers between devices with their start and end apart: 20 -> 20, of which waited for: 9 -> 9; matrix products, arithmetic and copies ran while one was open for 0% -> 0% of each run, Pallas kernels for 22% -> 23%
where the time goes in v8:
time: 101 us
  Pallas kernels  31.2 us (31%)
  blocking collectives  30.4 us (30%)
  starting transfers between devices  26.5 us (26%)
  waiting for transfers between devices  12.5 us (12%)
    ppermute x20, starting transfers between devices, partner(): return lax.ppermute(value, 'pts', pairs)  26.5 us
    pallas_call x6, Pallas kernels, run_first(): pl.pallas_call(functools.partial(first_product, scale_of(feats), rows, le...  21.3 us
    all_to_all x1, blocking collectives, share(): return lax.all_to_all(copies, 'pts', 0, 0, axis_index_groups=chip_groups())  15.9 us
    all_to_all x1, blocking collectives, per_device(): lax.all_to_all(curve[:, None, :], 'pts', 0, 0).reshape(DEVICES, cols)  14.5 us
    ppermute x20, waiting for transfers between devices, partner(): return lax.ppermute(value, 'pts', pairs)  12.5 us
    pallas_call x2, Pallas kernels, run_second(): pl.pallas_call(functools.partial(second_product, rows, core, starts), in_...  6.97 us
  transfers between devices with their start and end apart: 20, of which 9 were waited for; matrix products, arithmetic and copies ran while one was open for 0% of the time, Pallas kernels for 23%

profile of v8, /device:TPU:1, one launch (start us, length us, event | category | flops | bytes accessed | tf_op | source)
XLA Modules:
  0.0 101.3 jit_solution(6433581234045270479)
XLA Ops:
  0.6 3.6 %collective-permute-start.3 = (bf16[384,128]{1,0:T(8,128)(2,1)}, bf16[384,128]{1,0:T(8,128)(2,1)S(1)}, u32[]{:S(2)}, u32[]{:S(2)}) collective-permute-start(bf16[384,128]{1,0:T(8,128)(2,1)} %points_ref.1), channel_id=1, source_target_pairs={{0,10},{1,11},{2,8},{3,9},{4,14},{5,15},{6,12},{7,13},{8,2},{9,3},... | collective-permute-start | bytes 294920 | tf_op jit(solution)/shard_map/ppermute | solution.py:64
  4.2 1.0 shard_map.50
  5.2 2.6 %collective-permute-start.2 = (bf16[512,128]{1,0:T(8,128)(2,1)S(1)}, bf16[512,128]{1,0:T(8,128)(2,1)S(1)}, u32[]{:S(2)}, u32[]{:S(2)}) collective-permute-start(bf16[512,128]{1,0:T(8,128)(2,1)S(1)} %get-tuple-element.44.refs_0_), channel_id=1, source_target_pairs={{0,30},{1,97},{2,28},{3,99},{4,26},{5,101},{6,24},{7,103},{8,22},{... | collective-permute-start | bytes 393224 | tf_op jit(solution)/shard_map/ppermute | solution.py:64
  7.8 0.5 collective-permute-start.1
  8.3 0.3 collective-permute-start
  8.5 0.2 collective-permute-start.5
  8.7 0.0 collective-permute-done.3.refs_4_.refs_1_
  8.7 0.1 collective-permute-start.4
  8.8 3.7 %collective-permute-done.5.refs_6_.refs_3_ = bf16[384,128]{1,0:T(8,128)(2,1)S(1)} collective-permute-done((bf16[384,128]{1,0:T(8,128)(2,1)}, bf16[384,128]{1,0:T(8,128)(2,1)S(1)}, u32[]{:S(2)}, u32[]{:S(2)}) %collective-permute-start.5) | collective-permute-done | bytes 98336 | tf_op jit(solution)/shard_map/ppermute | solution.py:64
  12.5 0.2 collective-permute-done.4.refs_5_.refs_2_
  12.7 0.0 collective-permute-done.2.refs_3_
  12.7 0.7 collective-permute-done.1.refs_2_
  13.4 0.0 collective-permute-done.refs_1_
  13.4 4.3 %collective-permute-start.6 = (bf16[4,512,128]{2,1,0:T(8,128)(2,1)S(1)}, bf16[4,512,128]{2,1,0:T(8,128)(2,1)S(1)}, u32[]{:S(2)}, u32[]{:S(2)}) collective-permute-start(bf16[4,512,128]{2,1,0:T(8,128)(2,1)S(1)} %shard_map.51.refs_0_), channel_id=1, source_target_pairs={{0,1},{1,0},{2,3},{3,2},{4,5},{5,4},{6,7},{7,6},{8,9},{9,8},{10,11... | collective-permute-start | bytes 1572872 | tf_op jit(solution)/shard_map/ppermute | solution.py:64
  17.7 1.9 %collective-permute-start.8 = (bf16[4,512,128]{2,1,0:T(8,128)(2,1)S(1)}, bf16[4,512,128]{2,1,0:T(8,128)(2,1)S(1)}, u32[]{:S(2)}, u32[]{:S(2)}) collective-permute-start(bf16[4,512,128]{2,1,0:T(8,128)(2,1)S(1)} %shard_map.51.refs_0_), channel_id=1, source_target_pairs={{0,96},{1,25},{2,98},{3,27},{4,100},{5,29},{6,102},{7,31},{8,104},... | collective-permute-start | bytes 1572872 | tf_op jit(solution)/shard_map/ppermute | solution.py:64
  19.6 1.7 %collective-permute-start.7 = (bf16[4,512,128]{2,1,0:T(8,128)(2,1)S(1)}, bf16[4,512,128]{2,1,0:T(8,128)(2,1)S(1)}, u32[]{:S(2)}, u32[]{:S(2)}) collective-permute-start(bf16[4,512,128]{2,1,0:T(8,128)(2,1)S(1)} %shard_map.51.refs_0_), channel_id=1, source_target_pairs={{0,32},{1,7},{2,34},{3,5},{4,36},{5,3},{6,38},{7,1},{8,40},{9,15},... | collective-permute-start | bytes 1572872 | tf_op jit(solution)/shard_map/ppermute | solution.py:64
  21.3 0.4 shard_map.52
  21.7 2.6 %shard_map.53 = (bf16[1536,1536]{1,0:T(8,128)(2,1)S(1)}, f32[32,1664]{1,0:T(8,128)S(1)}) custom-call(bf16[4,512,128]{2,1,0:T(8,128)(2,1)S(1)} %shard_map.51.refs_0_, bf16[128,1536]{1,0:T(8,128)(2,1)S(1)} %get-tuple-element.45.refs_1_.refs_2_, f32[8,1536]{1,0:T(8,128)S(1)} %get-tuple-element.46.refs_2_.refs_3_), custom_call_target="tpu_custom_call" | custom-call | flops 1207959552 | bytes 4718592 | tf_op jit(solution)/shard_map/pallas_call | solution.py:217
  24.3 0.0 collective-permute-done.6.refs_0_
  24.3 2.6 %shard_map.54 = (bf16[1536,1536]{1,0:T(8,128)(2,1)S(1)}, f32[32,1664]{1,0:T(8,128)S(1)}) custom-call(bf16[4,512,128]{2,1,0:T(8,128)(2,1)S(1)} %collective-permute-done.6.refs_0_, bf16[128,1536]{1,0:T(8,128)(2,1)S(1)} %get-tuple-element.45.refs_1_.refs_2_, f32[8,1536]{1,0:T(8,128)S(1)} %get-tuple-element.46.refs_2_.refs_3_, ...), custom_call_target="tpu_custom_call" | custom-call | flops 1207959552 | bytes 4718592 | tf_op jit(solution)/shard_map/pallas_call | solution.py:217
  27.0 0.3 collective-permute-done.8.refs_0_
  27.3 1.6 %collective-permute-done.7.refs_0_ = bf16[4,512,128]{2,1,0:T(8,128)(2,1)S(1)} collective-permute-done((bf16[4,512,128]{2,1,0:T(8,128)(2,1)S(1)}, bf16[4,512,128]{2,1,0:T(8,128)(2,1)S(1)}, u32[]{:S(2)}, u32[]{:S(2)}) %collective-permute-start.7) | collective-permute-done | bytes 524320 | tf_op jit(solution)/shard_map/ppermute | solution.py:64
  28.9 0.9 collective-permute-start.9
  29.8 0.0 collective-permute-start.10
  29.8 1.6 %collective-permute-start.11 = (bf16[4,512,128]{2,1,0:T(8,128)(2,1)S(1)}, bf16[4,512,128]{2,1,0:T(8,128)(2,1)S(1)}, u32[]{:S(2)}, u32[]{:S(2)}) collective-permute-start(bf16[4,512,128]{2,1,0:T(8,128)(2,1)S(1)} %collective-permute-done.8.refs_0_), channel_id=1, source_target_pairs={{0,32},{1,7},{2,34},{3,5},{4,36},{5,3},{6,38},{7,1},{8,40},{9,15},... | collective-permute-start | bytes 1572872 | tf_op jit(solution)/shard_map/ppermute | solution.py:64
  31.4 0.0 collective-permute-done.9.refs_1_
  31.4 5.4 %shard_map.55 = (bf16[3072,1536]{1,0:T(8,128)(2,1)S(1)}, f32[32,1664]{1,0:T(8,128)S(1)}) custom-call(bf16[4,512,128]{2,1,0:T(8,128)(2,1)S(1)} %collective-permute-done.7.refs_0_, bf16[4,512,128]{2,1,0:T(8,128)(2,1)S(1)} %collective-permute-done.9.refs_1_, bf16[128,1536]{1,0:T(8,128)(2,1)S(1)} %get-tuple-element.45.refs_1_.refs_2_, ...), custom_call_target="tpu_custom_call" | custom-call | flops 2415919104 | bytes 9437184 | tf_op jit(solution)/shard_map/pallas_call | solution.py:217
  36.8 0.0 collective-permute-done.10.refs_1_
  36.9 5.4 %shard_map.56 = (bf16[3072,1536]{1,0:T(8,128)(2,1)S(1)}, f32[32,1664]{1,0:T(8,128)S(1)}) custom-call(bf16[4,512,128]{2,1,0:T(8,128)(2,1)S(1)} %collective-permute-done.8.refs_0_, bf16[4,512,128]{2,1,0:T(8,128)(2,1)S(1)} %collective-permute-done.10.refs_1_, bf16[128,1536]{1,0:T(8,128)(2,1)S(1)} %get-tuple-element.45.refs_1_.refs_2_, ...), custom_call_target="tpu_custom_call" | custom-call | flops 2415919104 | bytes 9437184 | tf_op jit(solution)/shard_map/pallas_call | solution.py:217
  42.3 0.0 collective-permute-done.11.refs_0_
  42.3 0.4 collective-permute-start.12
  42.7 2.6 %shard_map.57 = (bf16[1536,1536]{1,0:T(8,128)(2,1)S(1)}, f32[32,1664]{1,0:T(8,128)S(1)}) custom-call(bf16[4,512,128]{2,1,0:T(8,128)(2,1)S(1)} %collective-permute-done.11.refs_0_, bf16[128,1536]{1,0:T(8,128)(2,1)S(1)} %get-tuple-element.45.refs_1_.refs_2_, f32[8,1536]{1,0:T(8,128)S(1)} %get-tuple-element.46.refs_2_.refs_3_, ...), custom_call_target="tpu_custom_call" | custom-call | flops 1207959552 | bytes 4718592 | tf_op jit(solution)/shard_map/pallas_call | solution.py:217
  45.3 0.0 collective-permute-done.12.refs_0_
  45.3 2.6 %shard_map.58 = (bf16[1536,1536]{1,0:T(8,128)(2,1)S(1)}, f32[32,512]{1,0:T(8,128)S(1)}, f32[32,512]{1,0:T(8,128)S(1)}, f32[32,512]{1,0:T(8,128)S(1)}, f32[32,512]{1,0:T(8,128)S(1)}) custom-call(bf16[4,512,128]{2,1,0:T(8,128)(2,1)S(1)} %collective-permute-done.12.refs_0_, bf16[128,1536]{1,0:T(8,128)(2,1)S(1)} %get-tuple-element.45.refs_1_.refs_2_, ...), custom_call_target="tpu_custom_call" | custom-call | flops 1207959552 | bytes 4718592 | tf_op jit(solution)/shard_map/pallas_call | solution.py:217
  47.9 0.9 collective-permute-start.13
  48.8 1.8 %collective-permute-start.14 = (f32[32,512]{1,0:T(8,128)S(1)}, f32[32,512]{1,0:T(8,128)S(1)}, u32[]{:S(2)}, u32[]{:S(2)}) collective-permute-start(f32[32,512]{1,0:T(8,128)S(1)} %get-tuple-element.63), channel_id=1, source_target_pairs={{0,2},{1,3},{2,0},{3,1},{4,6},{5,7},{6,4},{7,5},{8,10},{9,11},{10,... | collective-permute-start | bytes 196616 | tf_op jit(solution)/shard_map/ppermute | solution.py:64
  50.6 0.0 collective-permute-start.15
  50.6 1.7 %collective-permute-done.13.refs_1_ = f32[32,512]{1,0:T(8,128)S(1)} collective-permute-done((f32[32,512]{1,0:T(8,128)S(1)}, f32[32,512]{1,0:T(8,128)S(1)}, u32[]{:S(2)}, u32[]{:S(2)}) %collective-permute-start.13) | collective-permute-done | bytes 65568 | tf_op jit(solution)/shard_map/ppermute | solution.py:64
  52.3 2.0 %collective-permute-done.14.refs_2_ = f32[32,512]{1,0:T(8,128)S(1)} collective-permute-done((f32[32,512]{1,0:T(8,128)S(1)}, f32[32,512]{1,0:T(8,128)S(1)}, u32[]{:S(2)}, u32[]{:S(2)}) %collective-permute-start.14) | collective-permute-done | bytes 65568 | tf_op jit(solution)/shard_map/ppermute | solution.py:64
  54.2 0.0 collective-permute-done.15.refs_3_
  54.2 0.2 shard_map.59
  54.5 15.9 %all_to_all.10.refs_4_.refs_6_ = bf16[16,32,512]{2,1,0:T(8,128)(2,1)S(1)} all-to-all(bf16[16,32,512]{2,1,0:T(8,128)(2,1)S(1)} %get-tuple-element.67), channel_id=1, replica_groups={{0,6,24,30,32,38,56,62,64,70,88,94,96,102,120,126},{1,7,25,31,33,39,57,..., dimensions={0} | all-to-all | bytes 1048576 | tf_op jit(solution)/shard_map/all_to_all | solution.py:76
  70.4 3.2 %collective-permute-start.16 = (bf16[16,32,512]{2,1,0:T(8,128)(2,1)S(1)}, bf16[16,32,512]{2,1,0:T(8,128)(2,1)S(1)}, u32[]{:S(2)}, u32[]{:S(2)}) collective-permute-start(bf16[16,32,512]{2,1,0:T(8,128)(2,1)S(1)} %all_to_all.10.refs_4_.refs_6_), channel_id=1, source_target_pairs={{0,1},{1,0},{2,3},{3,2},{4,5},{5,4},{6,7},{7,6},{8,9},{9,8},{10,11... | collective-permute-start | bytes 1572872 | tf_op jit(solution)/shard_map/ppermute | solution.py:64
  73.6 3.5 %shard_map.60.refs_5_ = f32[32,1536]{1,0:T(8,128)S(1)} custom-call(bf16[1536,1536]{1,0:T(8,128)(2,1)S(1)} %get-tuple-element.68.refs_0_, bf16[3072,1536]{1,0:T(8,128)(2,1)S(1)} %get-tuple-element.52.refs_1_, bf16[3072,1536]{1,0:T(8,128)(2,1)S(1)} %get-tuple-element.55.refs_2_, bf16[1536,1536]{1,0:T(8,128)(2,1)S(1)} %get-tuple-element.69.refs_3_, ...), custom_call_target="tpu_custom_call" | custom-call | flops 4831838208 | bytes 18874368 | tf_op jit(solution)/shard_map/pallas_call | solution.py:243
  77.0 0.0 collective-permute-done.16.refs_4_
  77.0 3.5 %shard_map.61 = (f32[32,512]{1,0:T(8,128)S(1)}, f32[32,512]{1,0:T(8,128)S(1)}, f32[32,512]{1,0:T(8,128)S(1)}, f32[32,512]{1,0:T(8,128)S(1)}) custom-call(bf16[1536,1536]{1,0:T(8,128)(2,1)S(1)} %get-tuple-element.48.refs_0_, bf16[3072,1536]{1,0:T(8,128)(2,1)S(1)} %get-tuple-element.52.refs_1_, bf16[3072,1536]{1,0:T(8,128)(2,1)S(1)} %get-tuple-element.55.refs_2_, ...), custom_call_target="tpu_custom_call" | custom-call | flops 4831838208 | bytes 18874368 | tf_op jit(solution)/shard_map/pallas_call | solution.py:243
  80.5 0.0 collective-permute-start.17
  80.6 0.1 collective-permute-start.18
  80.7 2.5 %collective-permute-start.19 = (f32[32,512]{1,0:T(8,128)S(1)}, f32[32,512]{1,0:T(8,128)S(1)}, u32[]{:S(2)}, u32[]{:S(2)}) collective-permute-start(f32[32,512]{1,0:T(8,128)S(1)} %get-tuple-element.73), channel_id=1, source_target_pairs={{0,8},{1,9},{2,10},{3,11},{4,12},{5,13},{6,14},{7,15},{8,0},{9,1},... | collective-permute-start | bytes 196616 | tf_op jit(solution)/shard_map/ppermute | solution.py:64
  83.2 2.0 %collective-permute-done.17.refs_1_ = f32[32,512]{1,0:T(8,128)S(1)} collective-permute-done((f32[32,512]{1,0:T(8,128)S(1)}, f32[32,512]{1,0:T(8,128)S(1)}, u32[]{:S(2)}, u32[]{:S(2)}) %collective-permute-start.17) | collective-permute-done | bytes 65568 | tf_op jit(solution)/shard_map/ppermute | solution.py:64
  85.2 0.3 collective-permute-done.18.refs_2_
  85.6 0.0 collective-permute-done.19.refs_3_
  85.6 0.4 shard_map.62
  86.0 14.5 %all_to_all.11 = f32[128,1,32]{2,1,0:T(1,128)S(1)} all-to-all(f32[128,1,32]{2,1,0:T(1,128)S(1)} %bitcast.8), channel_id=1, replica_groups=mesh['pts'=128] {'pts'}, dimensions={0} | all-to-all | bytes 32768 | tf_op jit(solution)/shard_map/all_to_all | solution.py:479
  100.5 0.8 shard_map.63
  (1 shorter events, 0.0 us)
Async XLA Ops:
  0.6 8.1 %collective-permute-start.3 = (bf16[384,128]{1,0:T(8,128)(2,1)}, bf16[384,128]{1,0:T(8,128)(2,1)S(1)}, u32[]{:S(2)}, u32[]{:S(2)}) collective-permute-start(bf16[384,128]{1,0:T(8,128)(2,1)} %points_ref.1), channel_id=1, source_target_pairs={{0,10},{1,11},{2,8},{3,9},{4,14},{5,15},{6,12},{7,13},{8,2},{9,3},... | collective-permute-start | bytes 294920 | tf_op jit(solution)/shard_map/ppermute | solution.py:64
  5.2 7.5 %collective-permute-start.2 = (bf16[512,128]{1,0:T(8,128)(2,1)S(1)}, bf16[512,128]{1,0:T(8,128)(2,1)S(1)}, u32[]{:S(2)}, u32[]{:S(2)}) collective-permute-start(bf16[512,128]{1,0:T(8,128)(2,1)S(1)} %get-tuple-element.44.refs_0_), channel_id=1, source_target_pairs={{0,30},{1,97},{2,28},{3,99},{4,26},{5,101},{6,24},{7,103},{8,22},{... | collective-permute-start | bytes 393224 | tf_op jit(solution)/shard_map/ppermute | solution.py:64
  7.8 5.6 %collective-permute-start.1 = (bf16[512,128]{1,0:T(8,128)(2,1)S(1)}, bf16[512,128]{1,0:T(8,128)(2,1)S(1)}, u32[]{:S(2)}, u32[]{:S(2)}) collective-permute-start(bf16[512,128]{1,0:T(8,128)(2,1)S(1)} %get-tuple-element.44.refs_0_), channel_id=1, source_target_pairs={{0,24},{1,65},{2,26},{3,67},{4,28},{5,69},{6,30},{7,71},{8,16},{9,... | collective-permute-start | bytes 393224 | tf_op jit(solution)/shard_map/ppermute | solution.py:64
  8.3 5.1 %collective-permute-start = (bf16[512,128]{1,0:T(8,128)(2,1)S(1)}, bf16[512,128]{1,0:T(8,128)(2,1)S(1)}, u32[]{:S(2)}, u32[]{:S(2)}) collective-permute-start(bf16[512,128]{1,0:T(8,128)(2,1)S(1)} %get-tuple-element.44.refs_0_), channel_id=1, source_target_pairs={{0,6},{1,33},{2,4},{3,35},{4,2},{5,37},{6,0},{7,39},{8,14},{9,41},... | collective-permute-start | bytes 393224 | tf_op jit(solution)/shard_map/ppermute | solution.py:64
  8.5 4.0 %collective-permute-start.5 = (bf16[384,128]{1,0:T(8,128)(2,1)}, bf16[384,128]{1,0:T(8,128)(2,1)S(1)}, u32[]{:S(2)}, u32[]{:S(2)}) collective-permute-start(bf16[384,128]{1,0:T(8,128)(2,1)} %points_ref.1), channel_id=1, source_target_pairs={{0,8},{1,9},{2,10},{3,11},{4,12},{5,13},{6,14},{7,15},{8,0},{9,1},... | collective-permute-start | bytes 294920 | tf_op jit(solution)/shard_map/ppermute | solution.py:64
  8.7 4.0 %collective-permute-start.4 = (bf16[384,128]{1,0:T(8,128)(2,1)}, bf16[384,128]{1,0:T(8,128)(2,1)S(1)}, u32[]{:S(2)}, u32[]{:S(2)}) collective-permute-start(bf16[384,128]{1,0:T(8,128)(2,1)} %points_ref.1), channel_id=1, source_target_pairs={{0,2},{1,3},{2,0},{3,1},{4,6},{5,7},{6,4},{7,5},{8,10},{9,11},{10,... | collective-permute-start | bytes 294920 | tf_op jit(solution)/shard_map/ppermute | solution.py:64
  13.4 10.9 %collective-permute-start.6 = (bf16[4,512,128]{2,1,0:T(8,128)(2,1)S(1)}, bf16[4,512,128]{2,1,0:T(8,128)(2,1)S(1)}, u32[]{:S(2)}, u32[]{:S(2)}) collective-permute-start(bf16[4,512,128]{2,1,0:T(8,128)(2,1)S(1)} %shard_map.51.refs_0_), channel_id=1, source_target_pairs={{0,1},{1,0},{2,3},{3,2},{4,5},{5,4},{6,7},{7,6},{8,9},{9,8},{10,11... | collective-permute-start | bytes 1572872 | tf_op jit(solution)/shard_map/ppermute | solution.py:64
  17.7 9.5 %collective-permute-start.8 = (bf16[4,512,128]{2,1,0:T(8,128)(2,1)S(1)}, bf16[4,512,128]{2,1,0:T(8,128)(2,1)S(1)}, u32[]{:S(2)}, u32[]{:S(2)}) collective-permute-start(bf16[4,512,128]{2,1,0:T(8,128)(2,1)S(1)} %shard_map.51.refs_0_), channel_id=1, source_target_pairs={{0,96},{1,25},{2,98},{3,27},{4,100},{5,29},{6,102},{7,31},{8,104},... | collective-permute-start | bytes 1572872 | tf_op jit(solution)/shard_map/ppermute | solution.py:64
  19.6 9.2 %collective-permute-start.7 = (bf16[4,512,128]{2,1,0:T(8,128)(2,1)S(1)}, bf16[4,512,128]{2,1,0:T(8,128)(2,1)S(1)}, u32[]{:S(2)}, u32[]{:S(2)}) collective-permute-start(bf16[4,512,128]{2,1,0:T(8,128)(2,1)S(1)} %shard_map.51.refs_0_), channel_id=1, source_target_pairs={{0,32},{1,7},{2,34},{3,5},{4,36},{5,3},{6,38},{7,1},{8,40},{9,15},... | collective-permute-start | bytes 1572872 | tf_op jit(solution)/shard_map/ppermute | solution.py:64
  28.9 2.5 %collective-permute-start.9 = (bf16[4,512,128]{2,1,0:T(8,128)(2,1)S(1)}, bf16[4,512,128]{2,1,0:T(8,128)(2,1)S(1)}, u32[]{:S(2)}, u32[]{:S(2)}) collective-permute-start(bf16[4,512,128]{2,1,0:T(8,128)(2,1)S(1)} %collective-permute-done.7.refs_0_), channel_id=1, source_target_pairs={{0,1},{1,0},{2,3},{3,2},{4,5},{5,4},{6,7},{7,6},{8,9},{9,8},{10,11... | collective-permute-start | bytes 1572872 | tf_op jit(solution)/shard_map/ppermute | solution.py:64
  29.8 7.1 %collective-permute-start.10 = (bf16[4,512,128]{2,1,0:T(8,128)(2,1)S(1)}, bf16[4,512,128]{2,1,0:T(8,128)(2,1)S(1)}, u32[]{:S(2)}, u32[]{:S(2)}) collective-permute-start(bf16[4,512,128]{2,1,0:T(8,128)(2,1)S(1)} %collective-permute-done.8.refs_0_), channel_id=1, source_target_pairs={{0,1},{1,0},{2,3},{3,2},{4,5},{5,4},{6,7},{7,6},{8,9},{9,8},{10,11... | collective-permute-start | bytes 1572872 | tf_op jit(solution)/shard_map/ppermute | solution.py:64
  29.8 12.5 %collective-permute-start.11 = (bf16[4,512,128]{2,1,0:T(8,128)(2,1)S(1)}, bf16[4,512,128]{2,1,0:T(8,128)(2,1)S(1)}, u32[]{:S(2)}, u32[]{:S(2)}) collective-permute-start(bf16[4,512,128]{2,1,0:T(8,128)(2,1)S(1)} %collective-permute-done.8.refs_0_), channel_id=1, source_target_pairs={{0,32},{1,7},{2,34},{3,5},{4,36},{5,3},{6,38},{7,1},{8,40},{9,15},... | collective-permute-start | bytes 1572872 | tf_op jit(solution)/shard_map/ppermute | solution.py:64
  42.3 3.0 %collective-permute-start.12 = (bf16[4,512,128]{2,1,0:T(8,128)(2,1)S(1)}, bf16[4,512,128]{2,1,0:T(8,128)(2,1)S(1)}, u32[]{:S(2)}, u32[]{:S(2)}) collective-permute-start(bf16[4,512,128]{2,1,0:T(8,128)(2,1)S(1)} %collective-permute-done.11.refs_0_), channel_id=1, source_target_pairs={{0,1},{1,0},{2,3},{3,2},{4,5},{5,4},{6,7},{7,6},{8,9},{9,8},{10,11... | collective-permute-start | bytes 1572872 | tf_op jit(solution)/shard_map/ppermute | solution.py:64
  47.9 4.4 %collective-permute-start.13 = (f32[32,512]{1,0:T(8,128)S(1)}, f32[32,512]{1,0:T(8,128)S(1)}, u32[]{:S(2)}, u32[]{:S(2)}) collective-permute-start(f32[32,512]{1,0:T(8,128)S(1)} %get-tuple-element.62), channel_id=1, source_target_pairs={{0,10},{1,11},{2,8},{3,9},{4,14},{5,15},{6,12},{7,13},{8,2},{9,3},... | collective-permute-start | bytes 196616 | tf_op jit(solution)/shard_map/ppermute | solution.py:64
  48.8 5.5 %collective-permute-start.14 = (f32[32,512]{1,0:T(8,128)S(1)}, f32[32,512]{1,0:T(8,128)S(1)}, u32[]{:S(2)}, u32[]{:S(2)}) collective-permute-start(f32[32,512]{1,0:T(8,128)S(1)} %get-tuple-element.63), channel_id=1, source_target_pairs={{0,2},{1,3},{2,0},{3,1},{4,6},{5,7},{6,4},{7,5},{8,10},{9,11},{10,... | collective-permute-start | bytes 196616 | tf_op jit(solution)/shard_map/ppermute | solution.py:64
  50.6 3.7 %collective-permute-start.15 = (f32[32,512]{1,0:T(8,128)S(1)}, f32[32,512]{1,0:T(8,128)S(1)}, u32[]{:S(2)}, u32[]{:S(2)}) collective-permute-start(f32[32,512]{1,0:T(8,128)S(1)} %get-tuple-element.64), channel_id=1, source_target_pairs={{0,8},{1,9},{2,10},{3,11},{4,12},{5,13},{6,14},{7,15},{8,0},{9,1},... | collective-permute-start | bytes 196616 | tf_op jit(solution)/shard_map/ppermute | solution.py:64
  70.4 6.6 %collective-permute-start.16 = (bf16[16,32,512]{2,1,0:T(8,128)(2,1)S(1)}, bf16[16,32,512]{2,1,0:T(8,128)(2,1)S(1)}, u32[]{:S(2)}, u32[]{:S(2)}) collective-permute-start(bf16[16,32,512]{2,1,0:T(8,128)(2,1)S(1)} %all_to_all.10.refs_4_.refs_6_), channel_id=1, source_target_pairs={{0,1},{1,0},{2,3},{3,2},{4,5},{5,4},{6,7},{7,6},{8,9},{9,8},{10,11... | collective-permute-start | bytes 1572872 | tf_op jit(solution)/shard_map/ppermute | solution.py:64
  80.5 4.7 %collective-permute-start.17 = (f32[32,512]{1,0:T(8,128)S(1)}, f32[32,512]{1,0:T(8,128)S(1)}, u32[]{:S(2)}, u32[]{:S(2)}) collective-permute-start(f32[32,512]{1,0:T(8,128)S(1)} %get-tuple-element.71), channel_id=1, source_target_pairs={{0,10},{1,11},{2,8},{3,9},{4,14},{5,15},{6,12},{7,13},{8,2},{9,3},... | collective-permute-start | bytes 196616 | tf_op jit(solution)/shard_map/ppermute | solution.py:64
  80.6 5.0 %collective-permute-start.18 = (f32[32,512]{1,0:T(8,128)S(1)}, f32[32,512]{1,0:T(8,128)S(1)}, u32[]{:S(2)}, u32[]{:S(2)}) collective-permute-start(f32[32,512]{1,0:T(8,128)S(1)} %get-tuple-element.72), channel_id=1, source_target_pairs={{0,2},{1,3},{2,0},{3,1},{4,6},{5,7},{6,4},{7,5},{8,10},{9,11},{10,... | collective-permute-start | bytes 196616 | tf_op jit(solution)/shard_map/ppermute | solution.py:64
  80.7 4.9 %collective-permute-start.19 = (f32[32,512]{1,0:T(8,128)S(1)}, f32[32,512]{1,0:T(8,128)S(1)}, u32[]{:S(2)}, u32[]{:S(2)}) collective-permute-start(f32[32,512]{1,0:T(8,128)S(1)} %get-tuple-element.73), channel_id=1, source_target_pairs={{0,8},{1,9},{2,10},{3,11},{4,12},{5,13},{6,14},{7,15},{8,0},{9,1},... | collective-permute-start | bytes 196616 | tf_op jit(solution)/shard_map/ppermute | solution.py:64

commit v9 on v6

--- a/solution.py
+++ b/solution.py
@@ -22,7 +22,7 @@
 PAIR = 2
 UNROLL = 2
 LANES = 128
-CHUNK = 512
+CHUNK = 256
 UNIT = 256
 SPLITS = 3
 SUMS = 3
@@ -41,6 +41,10 @@
         if (k >> bit) & 1:
             mask ^= step
     return mask
+
+
+def core_groups():
+    return [[k for k in range(DEVICES) if k % 2 == odd] for odd in range(2)]
 
 
 def chip_groups():
@@ -395,12 +399,12 @@
     direction_ref[...] = direction
     image_dir_ref[...] = image_dir
     norm_ref[...] = jnp.broadcast_to(norm_next, norm_ref.shape)
-    curve_ref[...] = jnp.broadcast_to(curve_two, norm_ref.shape).T
-
-
-def finish(curve_ref, norm_ref, field_ref, residual_ref, direction_ref, image_dir_ref, *outs):
+    curve_ref[...] = jnp.broadcast_to(curve_two, norm_ref.shape).T[: curve_ref.shape[0]]
+
+
+def finish(curve_ref, other_ref, norm_ref, field_ref, residual_ref, direction_ref, image_dir_ref, *outs):
     cols = curve_ref.shape[1]
-    curve = jnp.sum(curve_ref[...], axis=0, keepdims=True)
+    curve = jnp.sum(curve_ref[...] + other_ref[...], axis=0, keepdims=True)
     curve = jnp.concatenate([curve, jnp.ones((1, LANES - cols), jnp.float32)], axis=1)
     curve = jnp.broadcast_to(curve, (LANES, LANES)).T[:cols, 0:1]
     alpha = norm_ref[:, 0:1] / curve
@@ -460,7 +464,7 @@
     parts = run_second(1, other_pieces, other, rows, half_total, copies)
     field, residual, direction, image_dir, norm_next, curve = small_call(
         closing,
-        [field_shape] * 4 + [lanes_shape, ((DEVICES, cols), jnp.float32)],
+        [field_shape] * 4 + [lanes_shape, ((DEVICES // 2, cols), jnp.float32)],
         *exchange(parts, NEAR_MASKS),
         noise,
         rhs,
@@ -468,9 +472,10 @@
         rest,
         known,
     )
-    curve = lax.all_to_all(curve[:, None, :], "pts", 0, 0).reshape(DEVICES, cols)
+    curve = lax.all_to_all(curve[:, None, :], "pts", 0, 0, axis_index_groups=core_groups())
+    curves = [item.reshape(DEVICES // 2, cols) for item in (curve, partner(curve, CORE_MASK))]
     field, residual = small_call(
-        finish, [field_shape] * 2, curve, norm_next, field, residual, direction, image_dir
+        finish, [field_shape] * 2, *curves, norm_next, field, residual, direction, image_dir
     )
     return (field.T, residual.T)
 

time: 99.7 us -> 102 us (1.023)
  starting transfers between devices: 26.5 us -> 29.1 us
    ppermute x20 -> x21, starting transfers between devices: 26.5 us -> 29.1 us  [partner(): return lax.ppermute(value, 'pts', pairs)]
    ppermute x20 -> x21, waiting for transfers between devices: 13 us -> 13.8 us  [partner(): return lax.ppermute(value, 'pts', pairs)]
  transfers between devices with their start and end apart: 20 -> 21, of which waited for: 9 -> 10; matrix products, arithmetic and copies ran while one was open for 0% -> 0% of each run, Pallas kernels for 22% -> 21%
where the time goes in v9:
time: 102 us
  blocking collectives  29.4 us (29%)
  starting transfers between devices  29.1 us (29%)
  Pallas kernels  28.8 us (28%)
  waiting for transfers between devices  13.8 us (14%)
    ppermute x21, starting transfers between devices, partner(): return lax.ppermute(value, 'pts', pairs)  29.1 us
    pallas_call x6, Pallas kernels, run_first(): pl.pallas_call(functools.partial(first_product, scale_of(feats), rows, le...  19 us
    all_to_all x1, blocking collectives, share(): return lax.all_to_all(copies, 'pts', 0, 0, axis_index_groups=chip_groups())  15.9 us
    ppermute x21, waiting for transfers between devices, partner(): return lax.ppermute(value, 'pts', pairs)  13.8 us
    all_to_all x1, blocking collectives, per_device(): lax.all_to_all(curve[:, None, :], 'pts', 0, 0, axis_index_groups=core_gro...  13.5 us
    pallas_call x2, Pallas kernels, run_second(): pl.pallas_call(functools.partial(second_product, rows, core, starts), in_...  6.97 us
  transfers between devices with their start and end apart: 21, of which 10 were waited for; matrix products, arithmetic and copies ran while one was open for 0% of the time, Pallas kernels for 21%

profile of v9, /device:TPU:1, one launch (start us, length us, event | category | flops | bytes accessed | tf_op | source)
XLA Modules:
  0.0 102.0 jit_solution(3943219879515669994)
XLA Ops:
  0.6 3.6 %collective-permute-start.3 = (bf16[384,128]{1,0:T(8,128)(2,1)}, bf16[384,128]{1,0:T(8,128)(2,1)S(1)}, u32[]{:S(2)}, u32[]{:S(2)}) collective-permute-start(bf16[384,128]{1,0:T(8,128)(2,1)} %points_ref.1), channel_id=1, source_target_pairs={{0,10},{1,11},{2,8},{3,9},{4,14},{5,15},{6,12},{7,13},{8,2},{9,3},... | collective-permute-start | bytes 294920 | tf_op jit(solution)/shard_map/ppermute | solution.py:70
  4.2 1.0 shard_map.50
  5.2 2.6 %collective-permute-start.2 = (bf16[512,128]{1,0:T(8,128)(2,1)S(1)}, bf16[512,128]{1,0:T(8,128)(2,1)S(1)}, u32[]{:S(2)}, u32[]{:S(2)}) collective-permute-start(bf16[512,128]{1,0:T(8,128)(2,1)S(1)} %get-tuple-element.44.refs_0_), channel_id=1, source_target_pairs={{0,30},{1,97},{2,28},{3,99},{4,26},{5,101},{6,24},{7,103},{8,22},{... | collective-permute-start | bytes 393224 | tf_op jit(solution)/shard_map/ppermute | solution.py:70
  7.8 0.5 collective-permute-start.1
  8.3 0.3 collective-permute-start
  8.5 0.2 collective-permute-start.5
  8.7 0.0 collective-permute-done.3.refs_4_.refs_1_
  8.7 0.1 collective-permute-start.4
  8.8 3.7 %collective-permute-done.5.refs_6_.refs_3_ = bf16[384,128]{1,0:T(8,128)(2,1)S(1)} collective-permute-done((bf16[384,128]{1,0:T(8,128)(2,1)}, bf16[384,128]{1,0:T(8,128)(2,1)S(1)}, u32[]{:S(2)}, u32[]{:S(2)}) %collective-permute-start.5) | collective-permute-done | bytes 98336 | tf_op jit(solution)/shard_map/ppermute | solution.py:70
  12.5 0.2 collective-permute-done.4.refs_5_.refs_2_
  12.7 0.0 collective-permute-done.2.refs_3_
  12.7 0.7 collective-permute-done.1.refs_2_
  13.4 0.0 collective-permute-done.refs_1_
  13.4 4.3 %collective-permute-start.6 = (bf16[4,512,128]{2,1,0:T(8,128)(2,1)S(1)}, bf16[4,512,128]{2,1,0:T(8,128)(2,1)S(1)}, u32[]{:S(2)}, u32[]{:S(2)}) collective-permute-start(bf16[4,512,128]{2,1,0:T(8,128)(2,1)S(1)} %shard_map.51.refs_0_), channel_id=1, source_target_pairs={{0,1},{1,0},{2,3},{3,2},{4,5},{5,4},{6,7},{7,6},{8,9},{9,8},{10,11... | collective-permute-start | bytes 1572872 | tf_op jit(solution)/shard_map/ppermute | solution.py:70
  17.7 1.9 %collective-permute-start.8 = (bf16[4,512,128]{2,1,0:T(8,128)(2,1)S(1)}, bf16[4,512,128]{2,1,0:T(8,128)(2,1)S(1)}, u32[]{:S(2)}, u32[]{:S(2)}) collective-permute-start(bf16[4,512,128]{2,1,0:T(8,128)(2,1)S(1)} %shard_map.51.refs_0_), channel_id=1, source_target_pairs={{0,96},{1,25},{2,98},{3,27},{4,100},{5,29},{6,102},{7,31},{8,104},... | collective-permute-start | bytes 1572872 | tf_op jit(solution)/shard_map/ppermute | solution.py:70
  19.6 1.7 %collective-permute-start.7 = (bf16[4,512,128]{2,1,0:T(8,128)(2,1)S(1)}, bf16[4,512,128]{2,1,0:T(8,128)(2,1)S(1)}, u32[]{:S(2)}, u32[]{:S(2)}) collective-permute-start(bf16[4,512,128]{2,1,0:T(8,128)(2,1)S(1)} %shard_map.51.refs_0_), channel_id=1, source_target_pairs={{0,32},{1,7},{2,34},{3,5},{4,36},{5,3},{6,38},{7,1},{8,40},{9,15},... | collective-permute-start | bytes 1572872 | tf_op jit(solution)/shard_map/ppermute | solution.py:70
  21.3 0.4 shard_map.52
  21.7 2.4 %shard_map.53 = (bf16[1536,1536]{1,0:T(8,128)(2,1)S(1)}, f32[32,1664]{1,0:T(8,128)S(1)}) custom-call(bf16[4,512,128]{2,1,0:T(8,128)(2,1)S(1)} %shard_map.51.refs_0_, bf16[128,1536]{1,0:T(8,128)(2,1)S(1)} %get-tuple-element.45.refs_1_.refs_2_, f32[8,1536]{1,0:T(8,128)S(1)} %get-tuple-element.46.refs_2_.refs_3_), custom_call_target="tpu_custom_call" | custom-call | flops 1207959552 | bytes 4718592 | tf_op jit(solution)/shard_map/pallas_call | solution.py:214
  24.1 0.0 collective-permute-done.6.refs_0_
  24.1 2.4 %shard_map.54 = (bf16[1536,1536]{1,0:T(8,128)(2,1)S(1)}, f32[32,1664]{1,0:T(8,128)S(1)}) custom-call(bf16[4,512,128]{2,1,0:T(8,128)(2,1)S(1)} %collective-permute-done.6.refs_0_, bf16[128,1536]{1,0:T(8,128)(2,1)S(1)} %get-tuple-element.45.refs_1_.refs_2_, f32[8,1536]{1,0:T(8,128)S(1)} %get-tuple-element.46.refs_2_.refs_3_, ...), custom_call_target="tpu_custom_call" | custom-call | flops 1207959552 | bytes 4718592 | tf_op jit(solution)/shard_map/pallas_call | solution.py:214
  26.4 0.8 collective-permute-done.8.refs_0_
  27.3 1.6 %collective-permute-done.7.refs_0_ = bf16[4,512,128]{2,1,0:T(8,128)(2,1)S(1)} collective-permute-done((bf16[4,512,128]{2,1,0:T(8,128)(2,1)S(1)}, bf16[4,512,128]{2,1,0:T(8,128)(2,1)S(1)}, u32[]{:S(2)}, u32[]{:S(2)}) %collective-permute-start.7) | collective-permute-done | bytes 524320 | tf_op jit(solution)/shard_map/ppermute | solution.py:70
  28.9 0.9 collective-permute-start.9
  29.8 0.0 collective-permute-start.10
  29.8 1.6 %collective-permute-start.11 = (bf16[4,512,128]{2,1,0:T(8,128)(2,1)S(1)}, bf16[4,512,128]{2,1,0:T(8,128)(2,1)S(1)}, u32[]{:S(2)}, u32[]{:S(2)}) collective-permute-start(bf16[4,512,128]{2,1,0:T(8,128)(2,1)S(1)} %collective-permute-done.8.refs_0_), channel_id=1, source_target_pairs={{0,32},{1,7},{2,34},{3,5},{4,36},{5,3},{6,38},{7,1},{8,40},{9,15},... | collective-permute-start | bytes 1572872 | tf_op jit(solution)/shard_map/ppermute | solution.py:70
  31.4 0.0 collective-permute-done.9.refs_1_
  31.4 4.8 %shard_map.55 = (bf16[3072,1536]{1,0:T(8,128)(2,1)S(1)}, f32[32,1664]{1,0:T(8,128)S(1)}) custom-call(bf16[4,512,128]{2,1,0:T(8,128)(2,1)S(1)} %collective-permute-done.7.refs_0_, bf16[4,512,128]{2,1,0:T(8,128)(2,1)S(1)} %collective-permute-done.9.refs_1_, bf16[128,1536]{1,0:T(8,128)(2,1)S(1)} %get-tuple-element.45.refs_1_.refs_2_, ...), custom_call_target="tpu_custom_call" | custom-call | flops 2415919104 | bytes 9437184 | tf_op jit(solution)/shard_map/pallas_call | solution.py:214
  36.2 0.0 collective-permute-done.10.refs_1_
  36.2 4.8 %shard_map.56 = (bf16[3072,1536]{1,0:T(8,128)(2,1)S(1)}, f32[32,1664]{1,0:T(8,128)S(1)}) custom-call(bf16[4,512,128]{2,1,0:T(8,128)(2,1)S(1)} %collective-permute-done.8.refs_0_, bf16[4,512,128]{2,1,0:T(8,128)(2,1)S(1)} %collective-permute-done.10.refs_1_, bf16[128,1536]{1,0:T(8,128)(2,1)S(1)} %get-tuple-element.45.refs_1_.refs_2_, ...), custom_call_target="tpu_custom_call" | custom-call | flops 2415919104 | bytes 9437184 | tf_op jit(solution)/shard_map/pallas_call | solution.py:214
  41.0 0.0 collective-permute-done.11.refs_0_
  41.0 0.3 collective-permute-start.12
  41.3 2.4 %shard_map.57 = (bf16[1536,1536]{1,0:T(8,128)(2,1)S(1)}, f32[32,1664]{1,0:T(8,128)S(1)}) custom-call(bf16[4,512,128]{2,1,0:T(8,128)(2,1)S(1)} %collective-permute-done.11.refs_0_, bf16[128,1536]{1,0:T(8,128)(2,1)S(1)} %get-tuple-element.45.refs_1_.refs_2_, f32[8,1536]{1,0:T(8,128)S(1)} %get-tuple-element.46.refs_2_.refs_3_, ...), custom_call_target="tpu_custom_call" | custom-call | flops 1207959552 | bytes 4718592 | tf_op jit(solution)/shard_map/pallas_call | solution.py:214
  43.7 0.0 collective-permute-done.12.refs_0_
  43.7 2.4 %shard_map.58 = (bf16[1536,1536]{1,0:T(8,128)(2,1)S(1)}, f32[32,512]{1,0:T(8,128)S(1)}, f32[32,512]{1,0:T(8,128)S(1)}, f32[32,512]{1,0:T(8,128)S(1)}, f32[32,512]{1,0:T(8,128)S(1)}) custom-call(bf16[4,512,128]{2,1,0:T(8,128)(2,1)S(1)} %collective-permute-done.12.refs_0_, bf16[128,1536]{1,0:T(8,128)(2,1)S(1)} %get-tuple-element.45.refs_1_.refs_2_, ...), custom_call_target="tpu_custom_call" | custom-call | flops 1207959552 | bytes 4718592 | tf_op jit(solution)/shard_map/pallas_call | solution.py:214
  46.1 0.9 collective-permute-start.13
  47.0 1.8 %collective-permute-start.14 = (f32[32,512]{1,0:T(8,128)S(1)}, f32[32,512]{1,0:T(8,128)S(1)}, u32[]{:S(2)}, u32[]{:S(2)}) collective-permute-start(f32[32,512]{1,0:T(8,128)S(1)} %get-tuple-element.63), channel_id=1, source_target_pairs={{0,2},{1,3},{2,0},{3,1},{4,6},{5,7},{6,4},{7,5},{8,10},{9,11},{10,... | collective-permute-start | bytes 196616 | tf_op jit(solution)/shard_map/ppermute | solution.py:70
  48.8 0.0 collective-permute-start.15
  48.8 1.4 %collective-permute-done.13.refs_1_ = f32[32,512]{1,0:T(8,128)S(1)} collective-permute-done((f32[32,512]{1,0:T(8,128)S(1)}, f32[32,512]{1,0:T(8,128)S(1)}, u32[]{:S(2)}, u32[]{:S(2)}) %collective-permute-start.13) | collective-permute-done | bytes 65568 | tf_op jit(solution)/shard_map/ppermute | solution.py:70
  50.2 2.3 %collective-permute-done.14.refs_2_ = f32[32,512]{1,0:T(8,128)S(1)} collective-permute-done((f32[32,512]{1,0:T(8,128)S(1)}, f32[32,512]{1,0:T(8,128)S(1)}, u32[]{:S(2)}, u32[]{:S(2)}) %collective-permute-start.14) | collective-permute-done | bytes 65568 | tf_op jit(solution)/shard_map/ppermute | solution.py:70
  52.5 0.0 collective-permute-done.15.refs_3_
  52.5 0.2 shard_map.59
  52.7 15.9 %all_to_all.10.refs_4_.refs_6_ = bf16[16,32,512]{2,1,0:T(8,128)(2,1)S(1)} all-to-all(bf16[16,32,512]{2,1,0:T(8,128)(2,1)S(1)} %get-tuple-element.67), channel_id=1, replica_groups={{0,6,24,30,32,38,56,62,64,70,88,94,96,102,120,126},{1,7,25,31,33,39,57,..., dimensions={0} | all-to-all | bytes 1048576 | tf_op jit(solution)/shard_map/all_to_all | solution.py:82
  68.6 3.2 %collective-permute-start.16 = (bf16[16,32,512]{2,1,0:T(8,128)(2,1)S(1)}, bf16[16,32,512]{2,1,0:T(8,128)(2,1)S(1)}, u32[]{:S(2)}, u32[]{:S(2)}) collective-permute-start(bf16[16,32,512]{2,1,0:T(8,128)(2,1)S(1)} %all_to_all.10.refs_4_.refs_6_), channel_id=1, source_target_pairs={{0,1},{1,0},{2,3},{3,2},{4,5},{5,4},{6,7},{7,6},{8,9},{9,8},{10,11... | collective-permute-start | bytes 1572872 | tf_op jit(solution)/shard_map/ppermute | solution.py:70
  71.8 3.5 %shard_map.60.refs_5_ = f32[32,1536]{1,0:T(8,128)S(1)} custom-call(bf16[1536,1536]{1,0:T(8,128)(2,1)S(1)} %get-tuple-element.68.refs_0_, bf16[3072,1536]{1,0:T(8,128)(2,1)S(1)} %get-tuple-element.52.refs_1_, bf16[3072,1536]{1,0:T(8,128)(2,1)S(1)} %get-tuple-element.55.refs_2_, bf16[1536,1536]{1,0:T(8,128)(2,1)S(1)} %get-tuple-element.69.refs_3_, ...), custom_call_target="tpu_custom_call" | custom-call | flops 4831838208 | bytes 18874368 | tf_op jit(solution)/shard_map/pallas_call | solution.py:239
  75.3 0.0 collective-permute-done.16.refs_4_
  75.3 3.5 %shard_map.61 = (f32[32,512]{1,0:T(8,128)S(1)}, f32[32,512]{1,0:T(8,128)S(1)}, f32[32,512]{1,0:T(8,128)S(1)}, f32[32,512]{1,0:T(8,128)S(1)}) custom-call(bf16[1536,1536]{1,0:T(8,128)(2,1)S(1)} %get-tuple-element.48.refs_0_, bf16[3072,1536]{1,0:T(8,128)(2,1)S(1)} %get-tuple-element.52.refs_1_, bf16[3072,1536]{1,0:T(8,128)(2,1)S(1)} %get-tuple-element.55.refs_2_, ...), custom_call_target="tpu_custom_call" | custom-call | flops 4831838208 | bytes 18874368 | tf_op jit(solution)/shard_map/pallas_call | solution.py:239
  78.8 0.0 collective-permute-start.17
  78.8 0.1 collective-permute-start.18
  78.9 2.5 %collective-permute-start.19 = (f32[32,512]{1,0:T(8,128)S(1)}, f32[32,512]{1,0:T(8,128)S(1)}, u32[]{:S(2)}, u32[]{:S(2)}) collective-permute-start(f32[32,512]{1,0:T(8,128)S(1)} %get-tuple-element.73), channel_id=1, source_target_pairs={{0,8},{1,9},{2,10},{3,11},{4,12},{5,13},{6,14},{7,15},{8,0},{9,1},... | collective-permute-start | bytes 196616 | tf_op jit(solution)/shard_map/ppermute | solution.py:70
  81.5 2.0 %collective-permute-done.17.refs_1_ = f32[32,512]{1,0:T(8,128)S(1)} collective-permute-done((f32[32,512]{1,0:T(8,128)S(1)}, f32[32,512]{1,0:T(8,128)S(1)}, u32[]{:S(2)}, u32[]{:S(2)}) %collective-permute-start.17) | collective-permute-done | bytes 65568 | tf_op jit(solution)/shard_map/ppermute | solution.py:70
  83.5 0.3 collective-permute-done.18.refs_2_
  83.8 0.0 collective-permute-done.19.refs_3_
  83.8 0.4 shard_map.62
  84.2 13.5 %all_to_all.11 = f32[64,1,32]{2,1,0:T(1,128)S(1)} all-to-all(f32[64,1,32]{2,1,0:T(1,128)S(1)} %bitcast.12), channel_id=1, replica_groups={{0,2,4,6,8,10,12,14,16,18,20,22,24,26,28,30,32,34,36,38,40,42,44,46,48,..., dimensions={0} | all-to-all | bytes 16384 | tf_op jit(solution)/shard_map/all_to_all | solution.py:475
  97.7 2.6 %collective-permute-start.20 = (f32[64,1,32]{2,0,1:T(8,128)S(1)}, f32[64,1,32]{2,0,1:T(8,128)S(1)}, u32[]{:S(2)}, u32[]{:S(2)}) collective-permute-start(f32[64,1,32]{2,0,1:T(8,128)S(1)} %bitcast.9), channel_id=1, source_target_pairs={{0,1},{1,0},{2,3},{3,2},{4,5},{5,4},{6,7},{7,6},{8,9},{9,8},{10,11... | collective-permute-start | bytes 24584 | tf_op jit(solution)/shard_map/ppermute | solution.py:70
  100.3 0.9 collective-permute-done.20
  101.1 0.8 shard_map.63
  (1 shorter events, 0.0 us)
Async XLA Ops:
  0.6 8.1 %collective-permute-start.3 = (bf16[384,128]{1,0:T(8,128)(2,1)}, bf16[384,128]{1,0:T(8,128)(2,1)S(1)}, u32[]{:S(2)}, u32[]{:S(2)}) collective-permute-start(bf16[384,128]{1,0:T(8,128)(2,1)} %points_ref.1), channel_id=1, source_target_pairs={{0,10},{1,11},{2,8},{3,9},{4,14},{5,15},{6,12},{7,13},{8,2},{9,3},... | collective-permute-start | bytes 294920 | tf_op jit(solution)/shard_map/ppermute | solution.py:70
  5.2 7.5 %collective-permute-start.2 = (bf16[512,128]{1,0:T(8,128)(2,1)S(1)}, bf16[512,128]{1,0:T(8,128)(2,1)S(1)}, u32[]{:S(2)}, u32[]{:S(2)}) collective-permute-start(bf16[512,128]{1,0:T(8,128)(2,1)S(1)} %get-tuple-element.44.refs_0_), channel_id=1, source_target_pairs={{0,30},{1,97},{2,28},{3,99},{4,26},{5,101},{6,24},{7,103},{8,22},{... | collective-permute-start | bytes 393224 | tf_op jit(solution)/shard_map/ppermute | solution.py:70
  7.8 5.6 %collective-permute-start.1 = (bf16[512,128]{1,0:T(8,128)(2,1)S(1)}, bf16[512,128]{1,0:T(8,128)(2,1)S(1)}, u32[]{:S(2)}, u32[]{:S(2)}) collective-permute-start(bf16[512,128]{1,0:T(8,128)(2,1)S(1)} %get-tuple-element.44.refs_0_), channel_id=1, source_target_pairs={{0,24},{1,65},{2,26},{3,67},{4,28},{5,69},{6,30},{7,71},{8,16},{9,... | collective-permute-start | bytes 393224 | tf_op jit(solution)/shard_map/ppermute | solution.py:70
  8.3 5.1 %collective-permute-start = (bf16[512,128]{1,0:T(8,128)(2,1)S(1)}, bf16[512,128]{1,0:T(8,128)(2,1)S(1)}, u32[]{:S(2)}, u32[]{:S(2)}) collective-permute-start(bf16[512,128]{1,0:T(8,128)(2,1)S(1)} %get-tuple-element.44.refs_0_), channel_id=1, source_target_pairs={{0,6},{1,33},{2,4},{3,35},{4,2},{5,37},{6,0},{7,39},{8,14},{9,41},... | collective-permute-start | bytes 393224 | tf_op jit(solution)/shard_map/ppermute | solution.py:70
  8.5 4.0 %collective-permute-start.5 = (bf16[384,128]{1,0:T(8,128)(2,1)}, bf16[384,128]{1,0:T(8,128)(2,1)S(1)}, u32[]{:S(2)}, u32[]{:S(2)}) collective-permute-start(bf16[384,128]{1,0:T(8,128)(2,1)} %points_ref.1), channel_id=1, source_target_pairs={{0,8},{1,9},{2,10},{3,11},{4,12},{5,13},{6,14},{7,15},{8,0},{9,1},... | collective-permute-start | bytes 294920 | tf_op jit(solution)/shard_map/ppermute | solution.py:70
  8.7 4.0 %collective-permute-start.4 = (bf16[384,128]{1,0:T(8,128)(2,1)}, bf16[384,128]{1,0:T(8,128)(2,1)S(1)}, u32[]{:S(2)}, u32[]{:S(2)}) collective-permute-start(bf16[384,128]{1,0:T(8,128)(2,1)} %points_ref.1), channel_id=1, source_target_pairs={{0,2},{1,3},{2,0},{3,1},{4,6},{5,7},{6,4},{7,5},{8,10},{9,11},{10,... | collective-permute-start | bytes 294920 | tf_op jit(solution)/shard_map/ppermute | solution.py:70
  13.4 10.7 %collective-permute-start.6 = (bf16[4,512,128]{2,1,0:T(8,128)(2,1)S(1)}, bf16[4,512,128]{2,1,0:T(8,128)(2,1)S(1)}, u32[]{:S(2)}, u32[]{:S(2)}) collective-permute-start(bf16[4,512,128]{2,1,0:T(8,128)(2,1)S(1)} %shard_map.51.refs_0_), channel_id=1, source_target_pairs={{0,1},{1,0},{2,3},{3,2},{4,5},{5,4},{6,7},{7,6},{8,9},{9,8},{10,11... | collective-permute-start | bytes 1572872 | tf_op jit(solution)/shard_map/ppermute | solution.py:70
  17.7 9.5 %collective-permute-start.8 = (bf16[4,512,128]{2,1,0:T(8,128)(2,1)S(1)}, bf16[4,512,128]{2,1,0:T(8,128)(2,1)S(1)}, u32[]{:S(2)}, u32[]{:S(2)}) collective-permute-start(bf16[4,512,128]{2,1,0:T(8,128)(2,1)S(1)} %shard_map.51.refs_0_), channel_id=1, source_target_pairs={{0,96},{1,25},{2,98},{3,27},{4,100},{5,29},{6,102},{7,31},{8,104},... | collective-permute-start | bytes 1572872 | tf_op jit(solution)/shard_map/ppermute | solution.py:70
  19.6 9.2 %collective-permute-start.7 = (bf16[4,512,128]{2,1,0:T(8,128)(2,1)S(1)}, bf16[4,512,128]{2,1,0:T(8,128)(2,1)S(1)}, u32[]{:S(2)}, u32[]{:S(2)}) collective-permute-start(bf16[4,512,128]{2,1,0:T(8,128)(2,1)S(1)} %shard_map.51.refs_0_), channel_id=1, source_target_pairs={{0,32},{1,7},{2,34},{3,5},{4,36},{5,3},{6,38},{7,1},{8,40},{9,15},... | collective-permute-start | bytes 1572872 | tf_op jit(solution)/shard_map/ppermute | solution.py:70
  28.9 2.5 %collective-permute-start.9 = (bf16[4,512,128]{2,1,0:T(8,128)(2,1)S(1)}, bf16[4,512,128]{2,1,0:T(8,128)(2,1)S(1)}, u32[]{:S(2)}, u32[]{:S(2)}) collective-permute-start(bf16[4,512,128]{2,1,0:T(8,128)(2,1)S(1)} %collective-permute-done.7.refs_0_), channel_id=1, source_target_pairs={{0,1},{1,0},{2,3},{3,2},{4,5},{5,4},{6,7},{7,6},{8,9},{9,8},{10,11... | collective-permute-start | bytes 1572872 | tf_op jit(solution)/shard_map/ppermute | solution.py:70
  29.8 6.4 %collective-permute-start.10 = (bf16[4,512,128]{2,1,0:T(8,128)(2,1)S(1)}, bf16[4,512,128]{2,1,0:T(8,128)(2,1)S(1)}, u32[]{:S(2)}, u32[]{:S(2)}) collective-permute-start(bf16[4,512,128]{2,1,0:T(8,128)(2,1)S(1)} %collective-permute-done.8.refs_0_), channel_id=1, source_target_pairs={{0,1},{1,0},{2,3},{3,2},{4,5},{5,4},{6,7},{7,6},{8,9},{9,8},{10,11... | collective-permute-start | bytes 1572872 | tf_op jit(solution)/shard_map/ppermute | solution.py:70
  29.8 11.2 %collective-permute-start.11 = (bf16[4,512,128]{2,1,0:T(8,128)(2,1)S(1)}, bf16[4,512,128]{2,1,0:T(8,128)(2,1)S(1)}, u32[]{:S(2)}, u32[]{:S(2)}) collective-permute-start(bf16[4,512,128]{2,1,0:T(8,128)(2,1)S(1)} %collective-permute-done.8.refs_0_), channel_id=1, source_target_pairs={{0,32},{1,7},{2,34},{3,5},{4,36},{5,3},{6,38},{7,1},{8,40},{9,15},... | collective-permute-start | bytes 1572872 | tf_op jit(solution)/shard_map/ppermute | solution.py:70
  41.0 2.7 %collective-permute-start.12 = (bf16[4,512,128]{2,1,0:T(8,128)(2,1)S(1)}, bf16[4,512,128]{2,1,0:T(8,128)(2,1)S(1)}, u32[]{:S(2)}, u32[]{:S(2)}) collective-permute-start(bf16[4,512,128]{2,1,0:T(8,128)(2,1)S(1)} %collective-permute-done.11.refs_0_), channel_id=1, source_target_pairs={{0,1},{1,0},{2,3},{3,2},{4,5},{5,4},{6,7},{7,6},{8,9},{9,8},{10,11... | collective-permute-start | bytes 1572872 | tf_op jit(solution)/shard_map/ppermute | solution.py:70
  46.1 4.1 %collective-permute-start.13 = (f32[32,512]{1,0:T(8,128)S(1)}, f32[32,512]{1,0:T(8,128)S(1)}, u32[]{:S(2)}, u32[]{:S(2)}) collective-permute-start(f32[32,512]{1,0:T(8,128)S(1)} %get-tuple-element.62), channel_id=1, source_target_pairs={{0,10},{1,11},{2,8},{3,9},{4,14},{5,15},{6,12},{7,13},{8,2},{9,3},... | collective-permute-start | bytes 196616 | tf_op jit(solution)/shard_map/ppermute | solution.py:70
  47.0 5.4 %collective-permute-start.14 = (f32[32,512]{1,0:T(8,128)S(1)}, f32[32,512]{1,0:T(8,128)S(1)}, u32[]{:S(2)}, u32[]{:S(2)}) collective-permute-start(f32[32,512]{1,0:T(8,128)S(1)} %get-tuple-element.63), channel_id=1, source_target_pairs={{0,2},{1,3},{2,0},{3,1},{4,6},{5,7},{6,4},{7,5},{8,10},{9,11},{10,... | collective-permute-start | bytes 196616 | tf_op jit(solution)/shard_map/ppermute | solution.py:70
  48.8 3.7 %collective-permute-start.15 = (f32[32,512]{1,0:T(8,128)S(1)}, f32[32,512]{1,0:T(8,128)S(1)}, u32[]{:S(2)}, u32[]{:S(2)}) collective-permute-start(f32[32,512]{1,0:T(8,128)S(1)} %get-tuple-element.64), channel_id=1, source_target_pairs={{0,8},{1,9},{2,10},{3,11},{4,12},{5,13},{6,14},{7,15},{8,0},{9,1},... | collective-permute-start | bytes 196616 | tf_op jit(solution)/shard_map/ppermute | solution.py:70
  68.6 6.6 %collective-permute-start.16 = (bf16[16,32,512]{2,1,0:T(8,128)(2,1)S(1)}, bf16[16,32,512]{2,1,0:T(8,128)(2,1)S(1)}, u32[]{:S(2)}, u32[]{:S(2)}) collective-permute-start(bf16[16,32,512]{2,1,0:T(8,128)(2,1)S(1)} %all_to_all.10.refs_4_.refs_6_), channel_id=1, source_target_pairs={{0,1},{1,0},{2,3},{3,2},{4,5},{5,4},{6,7},{7,6},{8,9},{9,8},{10,11... | collective-permute-start | bytes 1572872 | tf_op jit(solution)/shard_map/ppermute | solution.py:70
  78.8 4.7 %collective-permute-start.17 = (f32[32,512]{1,0:T(8,128)S(1)}, f32[32,512]{1,0:T(8,128)S(1)}, u32[]{:S(2)}, u32[]{:S(2)}) collective-permute-start(f32[32,512]{1,0:T(8,128)S(1)} %get-tuple-element.71), channel_id=1, source_target_pairs={{0,10},{1,11},{2,8},{3,9},{4,14},{5,15},{6,12},{7,13},{8,2},{9,3},... | collective-permute-start | bytes 196616 | tf_op jit(solution)/shard_map/ppermute | solution.py:70
  78.8 5.0 %collective-permute-start.18 = (f32[32,512]{1,0:T(8,128)S(1)}, f32[32,512]{1,0:T(8,128)S(1)}, u32[]{:S(2)}, u32[]{:S(2)}) collective-permute-start(f32[32,512]{1,0:T(8,128)S(1)} %get-tuple-element.72), channel_id=1, source_target_pairs={{0,2},{1,3},{2,0},{3,1},{4,6},{5,7},{6,4},{7,5},{8,10},{9,11},{10,... | collective-permute-start | bytes 196616 | tf_op jit(solution)/shard_map/ppermute | solution.py:70
  78.9 4.9 %collective-permute-start.19 = (f32[32,512]{1,0:T(8,128)S(1)}, f32[32,512]{1,0:T(8,128)S(1)}, u32[]{:S(2)}, u32[]{:S(2)}) collective-permute-start(f32[32,512]{1,0:T(8,128)S(1)} %get-tuple-element.73), channel_id=1, source_target_pairs={{0,8},{1,9},{2,10},{3,11},{4,12},{5,13},{6,14},{7,15},{8,0},{9,1},... | collective-permute-start | bytes 196616 | tf_op jit(solution)/shard_map/ppermute | solution.py:70
  97.7 3.4 %collective-permute-start.20 = (f32[64,1,32]{2,0,1:T(8,128)S(1)}, f32[64,1,32]{2,0,1:T(8,128)S(1)}, u32[]{:S(2)}, u32[]{:S(2)}) collective-permute-start(f32[64,1,32]{2,0,1:T(8,128)S(1)} %bitcast.9), channel_id=1, source_target_pairs={{0,1},{1,0},{2,3},{3,2},{4,5},{5,4},{6,7},{7,6},{8,9},{9,8},{10,11... | collective-permute-start | bytes 24584 | tf_op jit(solution)/shard_map/ppermute | solution.py:70

commit v10 on v6

--- a/solution.py
+++ b/solution.py
@@ -20,7 +20,6 @@
 TURNS = 4
 CHIPS = SIDE * TURNS
 PAIR = 2
-UNROLL = 2
 LANES = 128
 CHUNK = 512
 UNIT = 256
@@ -102,53 +101,45 @@
 def first_product(scale, rows, count, opening, ending, *refs):
     far_refs = refs[:count]
     near_ref, half_ref = refs[count : count + 2]
-    kern_ref, sum_ref, far_ref = refs[count + 2 + (0 if opening else 1) :][:1] + refs[-2:]
+    kern_ref = refs[count + 2 + (0 if opening else 1)]
+    sum_ref = refs[-1]
     sum_ref[...] = jnp.zeros_like(sum_ref) if opening else refs[count + 2][...]
     cols = sum_ref.shape[0]
     width = near_ref.shape[1]
-    chunks = width // UNIT
     tall = rows + cols * (rows // near_ref.shape[0])
+    units, far, vec, far_half, here = [], [], [], [], []
     for k, ref in enumerate(far_refs):
-        far_ref[pl.ds(k * SIDE, SIDE)] = ref[...]
         for j in range(SIDE):
             sum_ref[:, width:] += ref[j, pl.ds(tall, cols), :].astype(jnp.float32)
-
-    @pl.loop(0, far_ref.shape[0] // (PAIR * UNROLL))
-    def _(step):
-        units, far, vec, far_half, here = [], [], [], [], []
-        for u in range(UNROLL):
-            first = PAIR * (UNROLL * step + u)
-            block = jnp.concatenate([far_ref[first + k, :rows, :] for k in range(PAIR)], axis=0)
-            pieces = [
-                far_ref[first + k, pl.ds(at, cols), :]
-                for k in range(PAIR)
-                for at in range(rows, tall, cols)
-            ]
+        for first in range(0, SIDE, PAIR):
+            blocks = range(first, first + PAIR)
+            block = jnp.concatenate([ref[j, :rows, :] for j in blocks], axis=0)
+            pieces = [ref[j, pl.ds(at, cols), :] for j in blocks for at in range(rows, tall, cols)]
             block_f = block.astype(jnp.float32)
+            units += [(len(far), pl.ds(at, UNIT)) for at in range(0, width, UNIT)]
             far.append(block)
             vec.append(jnp.concatenate(pieces, axis=1))
             far_half.append(jnp.sum(block_f * block_f, axis=1, keepdims=True) * (-0.5 * scale))
-            here.append(pl.ds(pl.multiple_of(first * rows, PAIR * rows), PAIR * rows))
-            units += [(u, pl.ds(c * UNIT, UNIT)) for c in range(chunks)]
-        cross, tile = {}, {}
-        for c in range(len(units) + 2):
-            if c < len(units):
-                u, part = units[c]
-                cross[c] = jnp.dot(far[u], near_ref[:, part], preferred_element_type=jnp.float32)
-            if 0 <= c - 1 < len(units):
-                u, part = units[c - 1]
-                tile[c - 1] = jnp.exp2(
-                    cross.pop(c - 1) * scale + far_half[u] + half_ref[0:1, part]
-                ).astype(jnp.bfloat16)
-                kern_ref[here[u], part] = tile[c - 1]
-            if 0 <= c - 2 < len(units):
-                u, part = units[c - 2]
-                sum_ref[:, part] += jnp.dot(
-                    vec[u], tile.pop(c - 2), preferred_element_type=jnp.float32
-                )
+            here.append(pl.ds((k * SIDE + first) * rows, PAIR * rows))
+    cross, tile = {}, {}
+    for c in range(len(units) + 2):
+        if c < len(units):
+            u, part = units[c]
+            cross[c] = jnp.dot(far[u], near_ref[:, part], preferred_element_type=jnp.float32)
+        if 0 <= c - 1 < len(units):
+            u, part = units[c - 1]
+            tile[c - 1] = jnp.exp2(
+                cross.pop(c - 1) * scale + far_half[u] + half_ref[0:1, part]
+            ).astype(jnp.bfloat16)
+            kern_ref[here[u], part] = tile[c - 1]
+        if 0 <= c - 2 < len(units):
+            u, part = units[c - 2]
+            sum_ref[:, part] += jnp.dot(
+                vec[u], tile.pop(c - 2), preferred_element_type=jnp.float32
+            )
 
     if ending:
-        for k, ref in enumerate(refs[-2 - NEAR : -2]):
+        for k, ref in enumerate(refs[-1 - NEAR : -1]):
             ref[:, :rows] = sum_ref[:, pl.ds(k * rows, rows)]
             ref[:, rows:] = sum_ref[:, width:]
 
@@ -212,7 +203,7 @@
         in_specs=[INSIDE] * len(inputs),
         out_specs=[INSIDE] * (1 + len(outs)),
         out_shape=[pltpu.VMEM((count, width), jnp.bfloat16)] + outs,
-        scratch_shapes=scratch + [pltpu.VMEM((len(far) * SIDE,) + far[0].shape[1:], jnp.bfloat16)],
+        scratch_shapes=scratch,
         compiler_params=pltpu.CompilerParams(vmem_limit_bytes=LIMIT),
         cost_estimate=pl.CostEstimate(
             flops=4 * count * width * feats,

time: 99.7 us -> 99.4 us (level)
  transfers between devices with their start and end apart: 20 -> 20, of which waited for: 9 -> 9; matrix products, arithmetic and copies ran while one was open for 0% -> 0% of each run, Pallas kernels for 22% -> 21%
where the time goes in v10:
time: 99.4 us; the launch traced here: 99.2 us
  blocking collectives  30.4 us (31%)
  Pallas kernels  28.4 us (29%)
  starting transfers between devices  26.7 us (27%)
  waiting for transfers between devices  13 us (13%)
    ppermute x20, starting transfers between devices, partner(): return lax.ppermute(value, 'pts', pairs)  26.7 us
    pallas_call x6, Pallas kernels, run_first(): pl.pallas_call(functools.partial(first_product, scale_of(feats), rows, le...  18.5 us
    all_to_all x1, blocking collectives, share(): return lax.all_to_all(copies, 'pts', 0, 0, axis_index_groups=chip_groups())  15.9 us
    all_to_all x1, blocking collectives, per_device(): lax.all_to_all(curve[:, None, :], 'pts', 0, 0).reshape(DEVICES, cols)  14.5 us
    ppermute x20, waiting for transfers between devices, partner(): return lax.ppermute(value, 'pts', pairs)  13 us
    pallas_call x2, Pallas kernels, run_second(): pl.pallas_call(functools.partial(second_product, rows, core, starts), in_...  6.97 us
  transfers between devices with their start and end apart: 20, of which 9 were waited for; matrix products, arithmetic and copies ran while one was open for 0% of the time, Pallas kernels for 21%

profile of v10, /device:TPU:1, one launch (start us, length us, event | category | flops | bytes accessed | tf_op | source)
XLA Modules:
  0.0 99.2 jit_solution(2723765315125280008)
XLA Ops:
  0.6 3.6 %collective-permute-start.3 = (bf16[384,128]{1,0:T(8,128)(2,1)}, bf16[384,128]{1,0:T(8,128)(2,1)S(1)}, u32[]{:S(2)}, u32[]{:S(2)}) collective-permute-start(bf16[384,128]{1,0:T(8,128)(2,1)} %points_ref.1), channel_id=1, source_target_pairs={{0,10},{1,11},{2,8},{3,9},{4,14},{5,15},{6,12},{7,13},{8,2},{9,3},... | collective-permute-start | bytes 294920 | tf_op jit(solution)/shard_map/ppermute | solution.py:65
  4.2 1.0 %shard_map.50 = (bf16[512,128]{1,0:T(8,128)(2,1)S(1)}, f32[32,384]{1,0:T(8,128)S(1)}, f32[32,384]{1,0:T(8,128)S(1)}, f32[1,384]{1,0:T(1,128)S(1)}) custom-call(bf16[384,128]{1,0:T(8,128)(2,1)} %points_ref.1, f32[32,384]{1,0:T(8,128)} %bitcast.9, f32[384]{0:T(512)} %noise_ref.1), custom_call_target="tpu_custom_call" | custom-call | tf_op jit(solution)/shard_map/pallas_call | solution.py:301
  5.2 2.6 %collective-permute-start.2 = (bf16[512,128]{1,0:T(8,128)(2,1)S(1)}, bf16[512,128]{1,0:T(8,128)(2,1)S(1)}, u32[]{:S(2)}, u32[]{:S(2)}) collective-permute-start(bf16[512,128]{1,0:T(8,128)(2,1)S(1)} %get-tuple-element.44.refs_0_), channel_id=1, source_target_pairs={{0,30},{1,97},{2,28},{3,99},{4,26},{5,101},{6,24},{7,103},{8,22},{... | collective-permute-start | bytes 393224 | tf_op jit(solution)/shard_map/ppermute | solution.py:65
  7.8 0.5 collective-permute-start.1
  8.3 0.3 collective-permute-start
  8.5 0.2 collective-permute-start.5
  8.7 0.0 collective-permute-done.3.refs_4_.refs_1_
  8.7 0.1 collective-permute-start.4
  8.8 3.7 %collective-permute-done.5.refs_6_.refs_3_ = bf16[384,128]{1,0:T(8,128)(2,1)S(1)} collective-permute-done((bf16[384,128]{1,0:T(8,128)(2,1)}, bf16[384,128]{1,0:T(8,128)(2,1)S(1)}, u32[]{:S(2)}, u32[]{:S(2)}) %collective-permute-start.5) | collective-permute-done | bytes 98336 | tf_op jit(solution)/shard_map/ppermute | solution.py:65
  12.5 0.2 collective-permute-done.4.refs_5_.refs_2_
  12.7 0.0 collective-permute-done.2.refs_3_
  12.7 0.7 collective-permute-done.1.refs_2_
  13.4 0.0 collective-permute-done.refs_1_
  13.4 4.3 %collective-permute-start.6 = (bf16[4,512,128]{2,1,0:T(8,128)(2,1)S(1)}, bf16[4,512,128]{2,1,0:T(8,128)(2,1)S(1)}, u32[]{:S(2)}, u32[]{:S(2)}) collective-permute-start(bf16[4,512,128]{2,1,0:T(8,128)(2,1)S(1)} %shard_map.51.refs_0_), channel_id=1, source_target_pairs={{0,1},{1,0},{2,3},{3,2},{4,5},{5,4},{6,7},{7,6},{8,9},{9,8},{10,11... | collective-permute-start | bytes 1572872 | tf_op jit(solution)/shard_map/ppermute | solution.py:65
  17.7 1.9 %collective-permute-start.8 = (bf16[4,512,128]{2,1,0:T(8,128)(2,1)S(1)}, bf16[4,512,128]{2,1,0:T(8,128)(2,1)S(1)}, u32[]{:S(2)}, u32[]{:S(2)}) collective-permute-start(bf16[4,512,128]{2,1,0:T(8,128)(2,1)S(1)} %shard_map.51.refs_0_), channel_id=1, source_target_pairs={{0,96},{1,25},{2,98},{3,27},{4,100},{5,29},{6,102},{7,31},{8,104},... | collective-permute-start | bytes 1572872 | tf_op jit(solution)/shard_map/ppermute | solution.py:65
  19.6 1.7 %collective-permute-start.7 = (bf16[4,512,128]{2,1,0:T(8,128)(2,1)S(1)}, bf16[4,512,128]{2,1,0:T(8,128)(2,1)S(1)}, u32[]{:S(2)}, u32[]{:S(2)}) collective-permute-start(bf16[4,512,128]{2,1,0:T(8,128)(2,1)S(1)} %shard_map.51.refs_0_), channel_id=1, source_target_pairs={{0,32},{1,7},{2,34},{3,5},{4,36},{5,3},{6,38},{7,1},{8,40},{9,15},... | collective-permute-start | bytes 1572872 | tf_op jit(solution)/shard_map/ppermute | solution.py:65
  21.3 0.4 shard_map.52
  21.7 2.4 %shard_map.53 = (bf16[1536,1536]{1,0:T(8,128)(2,1)S(1)}, f32[32,1664]{1,0:T(8,128)S(1)}) custom-call(bf16[4,512,128]{2,1,0:T(8,128)(2,1)S(1)} %shard_map.51.refs_0_, bf16[128,1536]{1,0:T(8,128)(2,1)S(1)} %get-tuple-element.45.refs_1_.refs_2_, f32[8,1536]{1,0:T(8,128)S(1)} %get-tuple-element.46.refs_2_.refs_3_), custom_call_target="tpu_custom_call" | custom-call | flops 1207959552 | bytes 4718592 | tf_op jit(solution)/shard_map/pallas_call | solution.py:201
  24.1 0.0 collective-permute-done.6.refs_0_
  24.1 2.4 %shard_map.54 = (bf16[1536,1536]{1,0:T(8,128)(2,1)S(1)}, f32[32,1664]{1,0:T(8,128)S(1)}) custom-call(bf16[4,512,128]{2,1,0:T(8,128)(2,1)S(1)} %collective-permute-done.6.refs_0_, bf16[128,1536]{1,0:T(8,128)(2,1)S(1)} %get-tuple-element.45.refs_1_.refs_2_, f32[8,1536]{1,0:T(8,128)S(1)} %get-tuple-element.46.refs_2_.refs_3_, ...), custom_call_target="tpu_custom_call" | custom-call | flops 1207959552 | bytes 4718592 | tf_op jit(solution)/shard_map/pallas_call | solution.py:201
  26.5 0.8 collective-permute-done.8.refs_0_
  27.3 1.6 %collective-permute-done.7.refs_0_ = bf16[4,512,128]{2,1,0:T(8,128)(2,1)S(1)} collective-permute-done((bf16[4,512,128]{2,1,0:T(8,128)(2,1)S(1)}, bf16[4,512,128]{2,1,0:T(8,128)(2,1)S(1)}, u32[]{:S(2)}, u32[]{:S(2)}) %collective-permute-start.7) | collective-permute-done | bytes 524320 | tf_op jit(solution)/shard_map/ppermute | solution.py:65
  28.9 0.9 collective-permute-start.9
  29.8 0.0 collective-permute-start.10
  29.8 1.6 %collective-permute-start.11 = (bf16[4,512,128]{2,1,0:T(8,128)(2,1)S(1)}, bf16[4,512,128]{2,1,0:T(8,128)(2,1)S(1)}, u32[]{:S(2)}, u32[]{:S(2)}) collective-permute-start(bf16[4,512,128]{2,1,0:T(8,128)(2,1)S(1)} %collective-permute-done.8.refs_0_), channel_id=1, source_target_pairs={{0,32},{1,7},{2,34},{3,5},{4,36},{5,3},{6,38},{7,1},{8,40},{9,15},... | collective-permute-start | bytes 1572872 | tf_op jit(solution)/shard_map/ppermute | solution.py:65
  31.4 0.0 collective-permute-done.9.refs_1_
  31.4 4.5 %shard_map.55 = (bf16[3072,1536]{1,0:T(8,128)(2,1)S(1)}, f32[32,1664]{1,0:T(8,128)S(1)}) custom-call(bf16[4,512,128]{2,1,0:T(8,128)(2,1)S(1)} %collective-permute-done.7.refs_0_, bf16[4,512,128]{2,1,0:T(8,128)(2,1)S(1)} %collective-permute-done.9.refs_1_, bf16[128,1536]{1,0:T(8,128)(2,1)S(1)} %get-tuple-element.45.refs_1_.refs_2_, ...), custom_call_target="tpu_custom_call" | custom-call | flops 2415919104 | bytes 9437184 | tf_op jit(solution)/shard_map/pallas_call | solution.py:201
  35.9 0.0 collective-permute-done.10.refs_1_
  35.9 4.5 %shard_map.56 = (bf16[3072,1536]{1,0:T(8,128)(2,1)S(1)}, f32[32,1664]{1,0:T(8,128)S(1)}) custom-call(bf16[4,512,128]{2,1,0:T(8,128)(2,1)S(1)} %collective-permute-done.8.refs_0_, bf16[4,512,128]{2,1,0:T(8,128)(2,1)S(1)} %collective-permute-done.10.refs_1_, bf16[128,1536]{1,0:T(8,128)(2,1)S(1)} %get-tuple-element.45.refs_1_.refs_2_, ...), custom_call_target="tpu_custom_call" | custom-call | flops 2415919104 | bytes 9437184 | tf_op jit(solution)/shard_map/pallas_call | solution.py:201
  40.5 0.0 collective-permute-done.11.refs_0_
  40.5 0.6 collective-permute-start.12
  41.0 2.4 %shard_map.57 = (bf16[1536,1536]{1,0:T(8,128)(2,1)S(1)}, f32[32,1664]{1,0:T(8,128)S(1)}) custom-call(bf16[4,512,128]{2,1,0:T(8,128)(2,1)S(1)} %collective-permute-done.11.refs_0_, bf16[128,1536]{1,0:T(8,128)(2,1)S(1)} %get-tuple-element.45.refs_1_.refs_2_, f32[8,1536]{1,0:T(8,128)S(1)} %get-tuple-element.46.refs_2_.refs_3_, ...), custom_call_target="tpu_custom_call" | custom-call | flops 1207959552 | bytes 4718592 | tf_op jit(solution)/shard_map/pallas_call | solution.py:201
  43.4 0.0 collective-permute-done.12.refs_0_
  43.4 2.4 %shard_map.58 = (bf16[1536,1536]{1,0:T(8,128)(2,1)S(1)}, f32[32,512]{1,0:T(8,128)S(1)}, f32[32,512]{1,0:T(8,128)S(1)}, f32[32,512]{1,0:T(8,128)S(1)}, f32[32,512]{1,0:T(8,128)S(1)}) custom-call(bf16[4,512,128]{2,1,0:T(8,128)(2,1)S(1)} %collective-permute-done.12.refs_0_, bf16[128,1536]{1,0:T(8,128)(2,1)S(1)} %get-tuple-element.45.refs_1_.refs_2_, ...), custom_call_target="tpu_custom_call" | custom-call | flops 1207959552 | bytes 4718592 | tf_op jit(solution)/shard_map/pallas_call | solution.py:201
  45.8 0.9 collective-permute-start.13
  46.7 1.8 %collective-permute-start.14 = (f32[32,512]{1,0:T(8,128)S(1)}, f32[32,512]{1,0:T(8,128)S(1)}, u32[]{:S(2)}, u32[]{:S(2)}) collective-permute-start(f32[32,512]{1,0:T(8,128)S(1)} %get-tuple-element.63), channel_id=1, source_target_pairs={{0,2},{1,3},{2,0},{3,1},{4,6},{5,7},{6,4},{7,5},{8,10},{9,11},{10,... | collective-permute-start | bytes 196616 | tf_op jit(solution)/shard_map/ppermute | solution.py:65
  48.5 0.0 collective-permute-start.15
  48.5 1.4 %collective-permute-done.13.refs_1_ = f32[32,512]{1,0:T(8,128)S(1)} collective-permute-done((f32[32,512]{1,0:T(8,128)S(1)}, f32[32,512]{1,0:T(8,128)S(1)}, u32[]{:S(2)}, u32[]{:S(2)}) %collective-permute-start.13) | collective-permute-done | bytes 65568 | tf_op jit(solution)/shard_map/ppermute | solution.py:65
  49.9 2.3 %collective-permute-done.14.refs_2_ = f32[32,512]{1,0:T(8,128)S(1)} collective-permute-done((f32[32,512]{1,0:T(8,128)S(1)}, f32[32,512]{1,0:T(8,128)S(1)}, u32[]{:S(2)}, u32[]{:S(2)}) %collective-permute-start.14) | collective-permute-done | bytes 65568 | tf_op jit(solution)/shard_map/ppermute | solution.py:65
  52.2 0.0 collective-permute-done.15.refs_3_
  52.2 0.2 shard_map.59
  52.4 15.9 %all_to_all.10.refs_4_.refs_6_ = bf16[16,32,512]{2,1,0:T(8,128)(2,1)S(1)} all-to-all(bf16[16,32,512]{2,1,0:T(8,128)(2,1)S(1)} %get-tuple-element.67), channel_id=1, replica_groups={{0,6,24,30,32,38,56,62,64,70,88,94,96,102,120,126},{1,7,25,31,33,39,57,..., dimensions={0} | all-to-all | bytes 1048576 | tf_op jit(solution)/shard_map/all_to_all | solution.py:77
  68.3 3.2 %collective-permute-start.16 = (bf16[16,32,512]{2,1,0:T(8,128)(2,1)S(1)}, bf16[16,32,512]{2,1,0:T(8,128)(2,1)S(1)}, u32[]{:S(2)}, u32[]{:S(2)}) collective-permute-start(bf16[16,32,512]{2,1,0:T(8,128)(2,1)S(1)} %all_to_all.10.refs_4_.refs_6_), channel_id=1, source_target_pairs={{0,1},{1,0},{2,3},{3,2},{4,5},{5,4},{6,7},{7,6},{8,9},{9,8},{10,11... | collective-permute-start | bytes 1572872 | tf_op jit(solution)/shard_map/ppermute | solution.py:65
  71.5 3.5 %shard_map.60.refs_5_ = f32[32,1536]{1,0:T(8,128)S(1)} custom-call(bf16[1536,1536]{1,0:T(8,128)(2,1)S(1)} %get-tuple-element.68.refs_0_, bf16[3072,1536]{1,0:T(8,128)(2,1)S(1)} %get-tuple-element.52.refs_1_, bf16[3072,1536]{1,0:T(8,128)(2,1)S(1)} %get-tuple-element.55.refs_2_, bf16[1536,1536]{1,0:T(8,128)(2,1)S(1)} %get-tuple-element.69.refs_3_, ...), custom_call_target="tpu_custom_call" | custom-call | flops 4831838208 | bytes 18874368 | tf_op jit(solution)/shard_map/pallas_call | solution.py:226
  75.0 0.0 collective-permute-done.16.refs_4_
  75.0 3.5 %shard_map.61 = (f32[32,512]{1,0:T(8,128)S(1)}, f32[32,512]{1,0:T(8,128)S(1)}, f32[32,512]{1,0:T(8,128)S(1)}, f32[32,512]{1,0:T(8,128)S(1)}) custom-call(bf16[1536,1536]{1,0:T(8,128)(2,1)S(1)} %get-tuple-element.48.refs_0_, bf16[3072,1536]{1,0:T(8,128)(2,1)S(1)} %get-tuple-element.52.refs_1_, bf16[3072,1536]{1,0:T(8,128)(2,1)S(1)} %get-tuple-element.55.refs_2_, ...), custom_call_target="tpu_custom_call" | custom-call | flops 4831838208 | bytes 18874368 | tf_op jit(solution)/shard_map/pallas_call | solution.py:226
  78.5 0.0 collective-permute-start.17
  78.5 0.1 collective-permute-start.18
  78.6 2.5 %collective-permute-start.19 = (f32[32,512]{1,0:T(8,128)S(1)}, f32[32,512]{1,0:T(8,128)S(1)}, u32[]{:S(2)}, u32[]{:S(2)}) collective-permute-start(f32[32,512]{1,0:T(8,128)S(1)} %get-tuple-element.73), channel_id=1, source_target_pairs={{0,8},{1,9},{2,10},{3,11},{4,12},{5,13},{6,14},{7,15},{8,0},{9,1},... | collective-permute-start | bytes 196616 | tf_op jit(solution)/shard_map/ppermute | solution.py:65
  81.2 2.0 %collective-permute-done.17.refs_1_ = f32[32,512]{1,0:T(8,128)S(1)} collective-permute-done((f32[32,512]{1,0:T(8,128)S(1)}, f32[32,512]{1,0:T(8,128)S(1)}, u32[]{:S(2)}, u32[]{:S(2)}) %collective-permute-start.17) | collective-permute-done | bytes 65568 | tf_op jit(solution)/shard_map/ppermute | solution.py:65
  83.2 0.3 collective-permute-done.18.refs_2_
  83.5 0.0 collective-permute-done.19.refs_3_
  83.5 0.4 shard_map.62
  84.0 14.5 %all_to_all.11 = f32[128,1,32]{2,1,0:T(1,128)S(1)} all-to-all(f32[128,1,32]{2,1,0:T(1,128)S(1)} %bitcast.8), channel_id=1, replica_groups=mesh['pts'=128] {'pts'}, dimensions={0} | all-to-all | bytes 32768 | tf_op jit(solution)/shard_map/all_to_all | solution.py:462
  98.4 0.8 shard_map.63
  (1 shorter events, 0.0 us)
Async XLA Ops:
  0.6 8.1 %collective-permute-start.3 = (bf16[384,128]{1,0:T(8,128)(2,1)}, bf16[384,128]{1,0:T(8,128)(2,1)S(1)}, u32[]{:S(2)}, u32[]{:S(2)}) collective-permute-start(bf16[384,128]{1,0:T(8,128)(2,1)} %points_ref.1), channel_id=1, source_target_pairs={{0,10},{1,11},{2,8},{3,9},{4,14},{5,15},{6,12},{7,13},{8,2},{9,3},... | collective-permute-start | bytes 294920 | tf_op jit(solution)/shard_map/ppermute | solution.py:65
  5.2 7.5 %collective-permute-start.2 = (bf16[512,128]{1,0:T(8,128)(2,1)S(1)}, bf16[512,128]{1,0:T(8,128)(2,1)S(1)}, u32[]{:S(2)}, u32[]{:S(2)}) collective-permute-start(bf16[512,128]{1,0:T(8,128)(2,1)S(1)} %get-tuple-element.44.refs_0_), channel_id=1, source_target_pairs={{0,30},{1,97},{2,28},{3,99},{4,26},{5,101},{6,24},{7,103},{8,22},{... | collective-permute-start | bytes 393224 | tf_op jit(solution)/shard_map/ppermute | solution.py:65
  7.8 5.6 %collective-permute-start.1 = (bf16[512,128]{1,0:T(8,128)(2,1)S(1)}, bf16[512,128]{1,0:T(8,128)(2,1)S(1)}, u32[]{:S(2)}, u32[]{:S(2)}) collective-permute-start(bf16[512,128]{1,0:T(8,128)(2,1)S(1)} %get-tuple-element.44.refs_0_), channel_id=1, source_target_pairs={{0,24},{1,65},{2,26},{3,67},{4,28},{5,69},{6,30},{7,71},{8,16},{9,... | collective-permute-start | bytes 393224 | tf_op jit(solution)/shard_map/ppermute | solution.py:65
  8.3 5.1 %collective-permute-start = (bf16[512,128]{1,0:T(8,128)(2,1)S(1)}, bf16[512,128]{1,0:T(8,128)(2,1)S(1)}, u32[]{:S(2)}, u32[]{:S(2)}) collective-permute-start(bf16[512,128]{1,0:T(8,128)(2,1)S(1)} %get-tuple-element.44.refs_0_), channel_id=1, source_target_pairs={{0,6},{1,33},{2,4},{3,35},{4,2},{5,37},{6,0},{7,39},{8,14},{9,41},... | collective-permute-start | bytes 393224 | tf_op jit(solution)/shard_map/ppermute | solution.py:65
  8.5 4.0 %collective-permute-start.5 = (bf16[384,128]{1,0:T(8,128)(2,1)}, bf16[384,128]{1,0:T(8,128)(2,1)S(1)}, u32[]{:S(2)}, u32[]{:S(2)}) collective-permute-start(bf16[384,128]{1,0:T(8,128)(2,1)} %points_ref.1), channel_id=1, source_target_pairs={{0,8},{1,9},{2,10},{3,11},{4,12},{5,13},{6,14},{7,15},{8,0},{9,1},... | collective-permute-start | bytes 294920 | tf_op jit(solution)/shard_map/ppermute | solution.py:65
  8.7 4.0 %collective-permute-start.4 = (bf16[384,128]{1,0:T(8,128)(2,1)}, bf16[384,128]{1,0:T(8,128)(2,1)S(1)}, u32[]{:S(2)}, u32[]{:S(2)}) collective-permute-start(bf16[384,128]{1,0:T(8,128)(2,1)} %points_ref.1), channel_id=1, source_target_pairs={{0,2},{1,3},{2,0},{3,1},{4,6},{5,7},{6,4},{7,5},{8,10},{9,11},{10,... | collective-permute-start | bytes 294920 | tf_op jit(solution)/shard_map/ppermute | solution.py:65
  13.4 10.7 %collective-permute-start.6 = (bf16[4,512,128]{2,1,0:T(8,128)(2,1)S(1)}, bf16[4,512,128]{2,1,0:T(8,128)(2,1)S(1)}, u32[]{:S(2)}, u32[]{:S(2)}) collective-permute-start(bf16[4,512,128]{2,1,0:T(8,128)(2,1)S(1)} %shard_map.51.refs_0_), channel_id=1, source_target_pairs={{0,1},{1,0},{2,3},{3,2},{4,5},{5,4},{6,7},{7,6},{8,9},{9,8},{10,11... | collective-permute-start | bytes 1572872 | tf_op jit(solution)/shard_map/ppermute | solution.py:65
  17.7 9.5 %collective-permute-start.8 = (bf16[4,512,128]{2,1,0:T(8,128)(2,1)S(1)}, bf16[4,512,128]{2,1,0:T(8,128)(2,1)S(1)}, u32[]{:S(2)}, u32[]{:S(2)}) collective-permute-start(bf16[4,512,128]{2,1,0:T(8,128)(2,1)S(1)} %shard_map.51.refs_0_), channel_id=1, source_target_pairs={{0,96},{1,25},{2,98},{3,27},{4,100},{5,29},{6,102},{7,31},{8,104},... | collective-permute-start | bytes 1572872 | tf_op jit(solution)/shard_map/ppermute | solution.py:65
  19.6 9.2 %collective-permute-start.7 = (bf16[4,512,128]{2,1,0:T(8,128)(2,1)S(1)}, bf16[4,512,128]{2,1,0:T(8,128)(2,1)S(1)}, u32[]{:S(2)}, u32[]{:S(2)}) collective-permute-start(bf16[4,512,128]{2,1,0:T(8,128)(2,1)S(1)} %shard_map.51.refs_0_), channel_id=1, source_target_pairs={{0,32},{1,7},{2,34},{3,5},{4,36},{5,3},{6,38},{7,1},{8,40},{9,15},... | collective-permute-start | bytes 1572872 | tf_op jit(solution)/shard_map/ppermute | solution.py:65
  28.9 2.5 %collective-permute-start.9 = (bf16[4,512,128]{2,1,0:T(8,128)(2,1)S(1)}, bf16[4,512,128]{2,1,0:T(8,128)(2,1)S(1)}, u32[]{:S(2)}, u32[]{:S(2)}) collective-permute-start(bf16[4,512,128]{2,1,0:T(8,128)(2,1)S(1)} %collective-permute-done.7.refs_0_), channel_id=1, source_target_pairs={{0,1},{1,0},{2,3},{3,2},{4,5},{5,4},{6,7},{7,6},{8,9},{9,8},{10,11... | collective-permute-start | bytes 1572872 | tf_op jit(solution)/shard_map/ppermute | solution.py:65
  29.8 6.2 %collective-permute-start.10 = (bf16[4,512,128]{2,1,0:T(8,128)(2,1)S(1)}, bf16[4,512,128]{2,1,0:T(8,128)(2,1)S(1)}, u32[]{:S(2)}, u32[]{:S(2)}) collective-permute-start(bf16[4,512,128]{2,1,0:T(8,128)(2,1)S(1)} %collective-permute-done.8.refs_0_), channel_id=1, source_target_pairs={{0,1},{1,0},{2,3},{3,2},{4,5},{5,4},{6,7},{7,6},{8,9},{9,8},{10,11... | collective-permute-start | bytes 1572872 | tf_op jit(solution)/shard_map/ppermute | solution.py:65
  29.8 10.7 %collective-permute-start.11 = (bf16[4,512,128]{2,1,0:T(8,128)(2,1)S(1)}, bf16[4,512,128]{2,1,0:T(8,128)(2,1)S(1)}, u32[]{:S(2)}, u32[]{:S(2)}) collective-permute-start(bf16[4,512,128]{2,1,0:T(8,128)(2,1)S(1)} %collective-permute-done.8.refs_0_), channel_id=1, source_target_pairs={{0,32},{1,7},{2,34},{3,5},{4,36},{5,3},{6,38},{7,1},{8,40},{9,15},... | collective-permute-start | bytes 1572872 | tf_op jit(solution)/shard_map/ppermute | solution.py:65
  40.5 2.9 %collective-permute-start.12 = (bf16[4,512,128]{2,1,0:T(8,128)(2,1)S(1)}, bf16[4,512,128]{2,1,0:T(8,128)(2,1)S(1)}, u32[]{:S(2)}, u32[]{:S(2)}) collective-permute-start(bf16[4,512,128]{2,1,0:T(8,128)(2,1)S(1)} %collective-permute-done.11.refs_0_), channel_id=1, source_target_pairs={{0,1},{1,0},{2,3},{3,2},{4,5},{5,4},{6,7},{7,6},{8,9},{9,8},{10,11... | collective-permute-start | bytes 1572872 | tf_op jit(solution)/shard_map/ppermute | solution.py:65
  45.8 4.1 %collective-permute-start.13 = (f32[32,512]{1,0:T(8,128)S(1)}, f32[32,512]{1,0:T(8,128)S(1)}, u32[]{:S(2)}, u32[]{:S(2)}) collective-permute-start(f32[32,512]{1,0:T(8,128)S(1)} %get-tuple-element.62), channel_id=1, source_target_pairs={{0,10},{1,11},{2,8},{3,9},{4,14},{5,15},{6,12},{7,13},{8,2},{9,3},... | collective-permute-start | bytes 196616 | tf_op jit(solution)/shard_map/ppermute | solution.py:65
  46.7 5.5 %collective-permute-start.14 = (f32[32,512]{1,0:T(8,128)S(1)}, f32[32,512]{1,0:T(8,128)S(1)}, u32[]{:S(2)}, u32[]{:S(2)}) collective-permute-start(f32[32,512]{1,0:T(8,128)S(1)} %get-tuple-element.63), channel_id=1, source_target_pairs={{0,2},{1,3},{2,0},{3,1},{4,6},{5,7},{6,4},{7,5},{8,10},{9,11},{10,... | collective-permute-start | bytes 196616 | tf_op jit(solution)/shard_map/ppermute | solution.py:65
  48.5 3.7 %collective-permute-start.15 = (f32[32,512]{1,0:T(8,128)S(1)}, f32[32,512]{1,0:T(8,128)S(1)}, u32[]{:S(2)}, u32[]{:S(2)}) collective-permute-start(f32[32,512]{1,0:T(8,128)S(1)} %get-tuple-element.64), channel_id=1, source_target_pairs={{0,8},{1,9},{2,10},{3,11},{4,12},{5,13},{6,14},{7,15},{8,0},{9,1},... | collective-permute-start | bytes 196616 | tf_op jit(solution)/shard_map/ppermute | solution.py:65
  68.3 6.6 %collective-permute-start.16 = (bf16[16,32,512]{2,1,0:T(8,128)(2,1)S(1)}, bf16[16,32,512]{2,1,0:T(8,128)(2,1)S(1)}, u32[]{:S(2)}, u32[]{:S(2)}) collective-permute-start(bf16[16,32,512]{2,1,0:T(8,128)(2,1)S(1)} %all_to_all.10.refs_4_.refs_6_), channel_id=1, source_target_pairs={{0,1},{1,0},{2,3},{3,2},{4,5},{5,4},{6,7},{7,6},{8,9},{9,8},{10,11... | collective-permute-start | bytes 1572872 | tf_op jit(solution)/shard_map/ppermute | solution.py:65
  78.5 4.7 %collective-permute-start.17 = (f32[32,512]{1,0:T(8,128)S(1)}, f32[32,512]{1,0:T(8,128)S(1)}, u32[]{:S(2)}, u32[]{:S(2)}) collective-permute-start(f32[32,512]{1,0:T(8,128)S(1)} %get-tuple-element.71), channel_id=1, source_target_pairs={{0,10},{1,11},{2,8},{3,9},{4,14},{5,15},{6,12},{7,13},{8,2},{9,3},... | collective-permute-start | bytes 196616 | tf_op jit(solution)/shard_map/ppermute | solution.py:65
  78.5 5.0 %collective-permute-start.18 = (f32[32,512]{1,0:T(8,128)S(1)}, f32[32,512]{1,0:T(8,128)S(1)}, u32[]{:S(2)}, u32[]{:S(2)}) collective-permute-start(f32[32,512]{1,0:T(8,128)S(1)} %get-tuple-element.72), channel_id=1, source_target_pairs={{0,2},{1,3},{2,0},{3,1},{4,6},{5,7},{6,4},{7,5},{8,10},{9,11},{10,... | collective-permute-start | bytes 196616 | tf_op jit(solution)/shard_map/ppermute | solution.py:65
  78.6 4.9 %collective-permute-start.19 = (f32[32,512]{1,0:T(8,128)S(1)}, f32[32,512]{1,0:T(8,128)S(1)}, u32[]{:S(2)}, u32[]{:S(2)}) collective-permute-start(f32[32,512]{1,0:T(8,128)S(1)} %get-tuple-element.73), channel_id=1, source_target_pairs={{0,8},{1,9},{2,10},{3,11},{4,12},{5,13},{6,14},{7,15},{8,0},{9,1},... | collective-permute-start | bytes 196616 | tf_op jit(solution)/shard_map/ppermute | solution.py:65

commit v11 on v10

--- a/solution.py
+++ b/solution.py
@@ -409,7 +409,7 @@
     for k in range(1, SIDE):
         side.append(partner(packed, reach(SIDE_MASKS, k), reach(LINE_MASKS, k)))
     near = exchange([points] * NEAR, NEAR_MASKS)
-    own = run_bundle(side, near[1:])
+    own = run_bundle(side, near[1:2])
     own_across = partner(own, CORE_MASK)
     first, second = [partner(own, *line_masks(turn)) for turn in (1, 2)]
     near, half = small_call(

time: 99.4 us -> 101 us (1.016)
  starting transfers between devices: 26.7 us -> 28.2 us
    ppermute x20, starting transfers between devices: 26.7 us -> 28.2 us  [partner(): return lax.ppermute(value, 'pts', pairs)]
  transfers between devices with their start and end apart: 20 -> 20, of which waited for: 9 -> 7; matrix products, arithmetic and copies ran while one was open for 0% -> 0% of each run, Pallas kernels for 21% -> 20%
where the time goes in v11:
time: 101 us
  blocking collectives  31 us (31%)
  Pallas kernels  28.4 us (28%)
  starting transfers between devices  28.2 us (28%)
  waiting for transfers between devices  12.7 us (13%)
    ppermute x20, starting transfers between devices, partner(): return lax.ppermute(value, 'pts', pairs)  28.2 us
    pallas_call x6, Pallas kernels, run_first(): pl.pallas_call(functools.partial(first_product, scale_of(feats), rows, le...  18.5 us
    all_to_all x1, blocking collectives, share(): return lax.all_to_all(copies, 'pts', 0, 0, axis_index_groups=chip_groups())  16.5 us
    all_to_all x1, blocking collectives, per_device(): lax.all_to_all(curve[:, None, :], 'pts', 0, 0).reshape(DEVICES, cols)  14.5 us
    ppermute x20, waiting for transfers between devices, partner(): return lax.ppermute(value, 'pts', pairs)  12.7 us
    pallas_call x2, Pallas kernels, run_second(): pl.pallas_call(functools.partial(second_product, rows, core, starts), in_...  6.97 us
  transfers between devices with their start and end apart: 20, of which 7 were waited for; matrix products, arithmetic and copies ran while one was open for 0% of the time, Pallas kernels for 20%

profile of v11, /device:TPU:1, one launch (start us, length us, event | category | flops | bytes accessed | tf_op | source)
XLA Modules:
  0.0 101.0 jit_solution(7985276751660945524)
XLA Ops:
  0.6 1.0 shard_map.50
  1.6 3.4 %collective-permute-start.2 = (bf16[512,128]{1,0:T(8,128)(2,1)S(1)}, bf16[512,128]{1,0:T(8,128)(2,1)S(1)}, u32[]{:S(2)}, u32[]{:S(2)}) collective-permute-start(bf16[512,128]{1,0:T(8,128)(2,1)S(1)} %get-tuple-element.44.refs_0_), channel_id=1, source_target_pairs={{0,30},{1,97},{2,28},{3,99},{4,26},{5,101},{6,24},{7,103},{8,22},{... | collective-permute-start | bytes 393224 | tf_op jit(solution)/shard_map/ppermute | solution.py:65
  5.0 0.5 collective-permute-start.1
  5.5 0.1 collective-permute-start
  5.7 2.8 %collective-permute-start.3 = (bf16[384,128]{1,0:T(8,128)(2,1)}, bf16[384,128]{1,0:T(8,128)(2,1)S(1)}, u32[]{:S(2)}, u32[]{:S(2)}) collective-permute-start(bf16[384,128]{1,0:T(8,128)(2,1)} %points_ref.1), channel_id=1, source_target_pairs={{0,10},{1,11},{2,8},{3,9},{4,14},{5,15},{6,12},{7,13},{8,2},{9,3},... | collective-permute-start | bytes 294920 | tf_op jit(solution)/shard_map/ppermute | solution.py:65
  8.4 2.5 %collective-permute-done.3.refs_4_.refs_1_ = bf16[384,128]{1,0:T(8,128)(2,1)S(1)} collective-permute-done((bf16[384,128]{1,0:T(8,128)(2,1)}, bf16[384,128]{1,0:T(8,128)(2,1)S(1)}, u32[]{:S(2)}, u32[]{:S(2)}) %collective-permute-start.3) | collective-permute-done | bytes 98336 | tf_op jit(solution)/shard_map/ppermute | solution.py:65
  10.9 0.0 collective-permute-done.2.refs_3_
  10.9 0.0 collective-permute-done.1.refs_2_
  10.9 0.0 collective-permute-done.refs_1_
  11.0 5.2 %collective-permute-start.4 = (bf16[4,512,128]{2,1,0:T(8,128)(2,1)S(1)}, bf16[4,512,128]{2,1,0:T(8,128)(2,1)S(1)}, u32[]{:S(2)}, u32[]{:S(2)}) collective-permute-start(bf16[4,512,128]{2,1,0:T(8,128)(2,1)S(1)} %shard_map.51.refs_0_), channel_id=1, source_target_pairs={{0,1},{1,0},{2,3},{3,2},{4,5},{5,4},{6,7},{7,6},{8,9},{9,8},{10,11... | collective-permute-start | bytes 1572872 | tf_op jit(solution)/shard_map/ppermute | solution.py:65
  16.2 2.7 %collective-permute-start.8 = (bf16[4,512,128]{2,1,0:T(8,128)(2,1)S(1)}, bf16[4,512,128]{2,1,0:T(8,128)(2,1)S(1)}, u32[]{:S(2)}, u32[]{:S(2)}) collective-permute-start(bf16[4,512,128]{2,1,0:T(8,128)(2,1)S(1)} %shard_map.51.refs_0_), channel_id=1, source_target_pairs={{0,96},{1,25},{2,98},{3,27},{4,100},{5,29},{6,102},{7,31},{8,104},... | collective-permute-start | bytes 1572872 | tf_op jit(solution)/shard_map/ppermute | solution.py:65
  18.9 2.5 %collective-permute-start.7 = (bf16[4,512,128]{2,1,0:T(8,128)(2,1)S(1)}, bf16[4,512,128]{2,1,0:T(8,128)(2,1)S(1)}, u32[]{:S(2)}, u32[]{:S(2)}) collective-permute-start(bf16[4,512,128]{2,1,0:T(8,128)(2,1)S(1)} %shard_map.51.refs_0_), channel_id=1, source_target_pairs={{0,32},{1,7},{2,34},{3,5},{4,36},{5,3},{6,38},{7,1},{8,40},{9,15},... | collective-permute-start | bytes 1572872 | tf_op jit(solution)/shard_map/ppermute | solution.py:65
  21.5 0.0 collective-permute-start.6
  21.5 0.0 collective-permute-start.5
  21.5 4.0 %collective-permute-done.6.refs_3_ = bf16[384,128]{1,0:T(8,128)(2,1)S(1)} collective-permute-done((bf16[384,128]{1,0:T(8,128)(2,1)}, bf16[384,128]{1,0:T(8,128)(2,1)S(1)}, u32[]{:S(2)}, u32[]{:S(2)}) %collective-permute-start.6) | collective-permute-done | bytes 98336 | tf_op jit(solution)/shard_map/ppermute | solution.py:65
  25.4 0.0 collective-permute-done.5.refs_2_
  25.4 0.4 shard_map.52
  25.8 2.4 %shard_map.53 = (bf16[1536,1536]{1,0:T(8,128)(2,1)S(1)}, f32[32,1664]{1,0:T(8,128)S(1)}) custom-call(bf16[4,512,128]{2,1,0:T(8,128)(2,1)S(1)} %shard_map.51.refs_0_, bf16[128,1536]{1,0:T(8,128)(2,1)S(1)} %get-tuple-element.45.refs_1_.refs_2_, f32[8,1536]{1,0:T(8,128)S(1)} %get-tuple-element.46.refs_2_.refs_3_), custom_call_target="tpu_custom_call" | custom-call | flops 1207959552 | bytes 4718592 | tf_op jit(solution)/shard_map/pallas_call | solution.py:201
  28.2 0.0 collective-permute-done.4.refs_0_
  28.2 2.4 %shard_map.54 = (bf16[1536,1536]{1,0:T(8,128)(2,1)S(1)}, f32[32,1664]{1,0:T(8,128)S(1)}) custom-call(bf16[4,512,128]{2,1,0:T(8,128)(2,1)S(1)} %collective-permute-done.4.refs_0_, bf16[128,1536]{1,0:T(8,128)(2,1)S(1)} %get-tuple-element.45.refs_1_.refs_2_, f32[8,1536]{1,0:T(8,128)S(1)} %get-tuple-element.46.refs_2_.refs_3_, ...), custom_call_target="tpu_custom_call" | custom-call | flops 1207959552 | bytes 4718592 | tf_op jit(solution)/shard_map/pallas_call | solution.py:201
  30.6 0.0 collective-permute-done.8.refs_0_
  30.6 0.0 collective-permute-done.7.refs_0_
  30.6 0.1 collective-permute-start.9
  30.7 0.5 collective-permute-start.10
  31.2 1.2 %collective-permute-start.11 = (bf16[4,512,128]{2,1,0:T(8,128)(2,1)S(1)}, bf16[4,512,128]{2,1,0:T(8,128)(2,1)S(1)}, u32[]{:S(2)}, u32[]{:S(2)}) collective-permute-start(bf16[4,512,128]{2,1,0:T(8,128)(2,1)S(1)} %collective-permute-done.8.refs_0_), channel_id=1, source_target_pairs={{0,32},{1,7},{2,34},{3,5},{4,36},{5,3},{6,38},{7,1},{8,40},{9,15},... | collective-permute-start | bytes 1572872 | tf_op jit(solution)/shard_map/ppermute | solution.py:65
  32.4 0.2 collective-permute-done.9.refs_1_
  32.6 4.5 %shard_map.55 = (bf16[3072,1536]{1,0:T(8,128)(2,1)S(1)}, f32[32,1664]{1,0:T(8,128)S(1)}) custom-call(bf16[4,512,128]{2,1,0:T(8,128)(2,1)S(1)} %collective-permute-done.7.refs_0_, bf16[4,512,128]{2,1,0:T(8,128)(2,1)S(1)} %collective-permute-done.9.refs_1_, bf16[128,1536]{1,0:T(8,128)(2,1)S(1)} %get-tuple-element.45.refs_1_.refs_2_, ...), custom_call_target="tpu_custom_call" | custom-call | flops 2415919104 | bytes 9437184 | tf_op jit(solution)/shard_map/pallas_call | solution.py:201
  37.1 0.0 collective-permute-done.10.refs_1_
  37.1 4.5 %shard_map.56 = (bf16[3072,1536]{1,0:T(8,128)(2,1)S(1)}, f32[32,1664]{1,0:T(8,128)S(1)}) custom-call(bf16[4,512,128]{2,1,0:T(8,128)(2,1)S(1)} %collective-permute-done.8.refs_0_, bf16[4,512,128]{2,1,0:T(8,128)(2,1)S(1)} %collective-permute-done.10.refs_1_, bf16[128,1536]{1,0:T(8,128)(2,1)S(1)} %get-tuple-element.45.refs_1_.refs_2_, ...), custom_call_target="tpu_custom_call" | custom-call | flops 2415919104 | bytes 9437184 | tf_op jit(solution)/shard_map/pallas_call | solution.py:201
  41.7 0.0 collective-permute-done.11.refs_0_
  41.7 0.5 collective-permute-start.12
  42.2 2.4 %shard_map.57 = (bf16[1536,1536]{1,0:T(8,128)(2,1)S(1)}, f32[32,1664]{1,0:T(8,128)S(1)}) custom-call(bf16[4,512,128]{2,1,0:T(8,128)(2,1)S(1)} %collective-permute-done.11.refs_0_, bf16[128,1536]{1,0:T(8,128)(2,1)S(1)} %get-tuple-element.45.refs_1_.refs_2_, f32[8,1536]{1,0:T(8,128)S(1)} %get-tuple-element.46.refs_2_.refs_3_, ...), custom_call_target="tpu_custom_call" | custom-call | flops 1207959552 | bytes 4718592 | tf_op jit(solution)/shard_map/pallas_call | solution.py:201
  44.5 0.0 collective-permute-done.12.refs_0_
  44.5 2.4 %shard_map.58 = (bf16[1536,1536]{1,0:T(8,128)(2,1)S(1)}, f32[32,512]{1,0:T(8,128)S(1)}, f32[32,512]{1,0:T(8,128)S(1)}, f32[32,512]{1,0:T(8,128)S(1)}, f32[32,512]{1,0:T(8,128)S(1)}) custom-call(bf16[4,512,128]{2,1,0:T(8,128)(2,1)S(1)} %collective-permute-done.12.refs_0_, bf16[128,1536]{1,0:T(8,128)(2,1)S(1)} %get-tuple-element.45.refs_1_.refs_2_, ...), custom_call_target="tpu_custom_call" | custom-call | flops 1207959552 | bytes 4718592 | tf_op jit(solution)/shard_map/pallas_call | solution.py:201
  46.9 1.2 %collective-permute-start.13 = (f32[32,512]{1,0:T(8,128)S(1)}, f32[32,512]{1,0:T(8,128)S(1)}, u32[]{:S(2)}, u32[]{:S(2)}) collective-permute-start(f32[32,512]{1,0:T(8,128)S(1)} %get-tuple-element.62), channel_id=1, source_target_pairs={{0,10},{1,11},{2,8},{3,9},{4,14},{5,15},{6,12},{7,13},{8,2},{9,3},... | collective-permute-start | bytes 196616 | tf_op jit(solution)/shard_map/ppermute | solution.py:65
  48.1 1.4 %collective-permute-start.14 = (f32[32,512]{1,0:T(8,128)S(1)}, f32[32,512]{1,0:T(8,128)S(1)}, u32[]{:S(2)}, u32[]{:S(2)}) collective-permute-start(f32[32,512]{1,0:T(8,128)S(1)} %get-tuple-element.63), channel_id=1, source_target_pairs={{0,2},{1,3},{2,0},{3,1},{4,6},{5,7},{6,4},{7,5},{8,10},{9,11},{10,... | collective-permute-start | bytes 196616 | tf_op jit(solution)/shard_map/ppermute | solution.py:65
  49.5 0.1 collective-permute-start.15
  49.6 1.4 %collective-permute-done.13.refs_1_ = f32[32,512]{1,0:T(8,128)S(1)} collective-permute-done((f32[32,512]{1,0:T(8,128)S(1)}, f32[32,512]{1,0:T(8,128)S(1)}, u32[]{:S(2)}, u32[]{:S(2)}) %collective-permute-start.13) | collective-permute-done | bytes 65568 | tf_op jit(solution)/shard_map/ppermute | solution.py:65
  51.0 2.2 %collective-permute-done.14.refs_2_ = f32[32,512]{1,0:T(8,128)S(1)} collective-permute-done((f32[32,512]{1,0:T(8,128)S(1)}, f32[32,512]{1,0:T(8,128)S(1)}, u32[]{:S(2)}, u32[]{:S(2)}) %collective-permute-start.14) | collective-permute-done | bytes 65568 | tf_op jit(solution)/shard_map/ppermute | solution.py:65
  53.2 0.0 collective-permute-done.15.refs_3_
  53.2 0.2 shard_map.59
  53.5 16.5 %all_to_all.10.refs_4_.refs_6_ = bf16[16,32,512]{2,1,0:T(8,128)(2,1)S(1)} all-to-all(bf16[16,32,512]{2,1,0:T(8,128)(2,1)S(1)} %get-tuple-element.67), channel_id=1, replica_groups={{0,6,24,30,32,38,56,62,64,70,88,94,96,102,120,126},{1,7,25,31,33,39,57,..., dimensions={0} | all-to-all | bytes 1048576 | tf_op jit(solution)/shard_map/all_to_all | solution.py:77
  70.0 3.3 %collective-permute-start.16 = (bf16[16,32,512]{2,1,0:T(8,128)(2,1)S(1)}, bf16[16,32,512]{2,1,0:T(8,128)(2,1)S(1)}, u32[]{:S(2)}, u32[]{:S(2)}) collective-permute-start(bf16[16,32,512]{2,1,0:T(8,128)(2,1)S(1)} %all_to_all.10.refs_4_.refs_6_), channel_id=1, source_target_pairs={{0,1},{1,0},{2,3},{3,2},{4,5},{5,4},{6,7},{7,6},{8,9},{9,8},{10,11... | collective-permute-start | bytes 1572872 | tf_op jit(solution)/shard_map/ppermute | solution.py:65
  73.3 3.5 %shard_map.60.refs_5_ = f32[32,1536]{1,0:T(8,128)S(1)} custom-call(bf16[1536,1536]{1,0:T(8,128)(2,1)S(1)} %get-tuple-element.68.refs_0_, bf16[3072,1536]{1,0:T(8,128)(2,1)S(1)} %get-tuple-element.52.refs_1_, bf16[3072,1536]{1,0:T(8,128)(2,1)S(1)} %get-tuple-element.55.refs_2_, bf16[1536,1536]{1,0:T(8,128)(2,1)S(1)} %get-tuple-element.69.refs_3_, ...), custom_call_target="tpu_custom_call" | custom-call | flops 4831838208 | bytes 18874368 | tf_op jit(solution)/shard_map/pallas_call | solution.py:226
  76.8 0.0 collective-permute-done.16.refs_4_
  76.8 3.5 %shard_map.61 = (f32[32,512]{1,0:T(8,128)S(1)}, f32[32,512]{1,0:T(8,128)S(1)}, f32[32,512]{1,0:T(8,128)S(1)}, f32[32,512]{1,0:T(8,128)S(1)}) custom-call(bf16[1536,1536]{1,0:T(8,128)(2,1)S(1)} %get-tuple-element.48.refs_0_, bf16[3072,1536]{1,0:T(8,128)(2,1)S(1)} %get-tuple-element.52.refs_1_, bf16[3072,1536]{1,0:T(8,128)(2,1)S(1)} %get-tuple-element.55.refs_2_, ...), custom_call_target="tpu_custom_call" | custom-call | flops 4831838208 | bytes 18874368 | tf_op jit(solution)/shard_map/pallas_call | solution.py:226
  80.3 0.0 collective-permute-start.17
  80.3 0.1 collective-permute-start.18
  80.4 2.5 %collective-permute-start.19 = (f32[32,512]{1,0:T(8,128)S(1)}, f32[32,512]{1,0:T(8,128)S(1)}, u32[]{:S(2)}, u32[]{:S(2)}) collective-permute-start(f32[32,512]{1,0:T(8,128)S(1)} %get-tuple-element.73), channel_id=1, source_target_pairs={{0,8},{1,9},{2,10},{3,11},{4,12},{5,13},{6,14},{7,15},{8,0},{9,1},... | collective-permute-start | bytes 196616 | tf_op jit(solution)/shard_map/ppermute | solution.py:65
  83.0 2.0 %collective-permute-done.17.refs_1_ = f32[32,512]{1,0:T(8,128)S(1)} collective-permute-done((f32[32,512]{1,0:T(8,128)S(1)}, f32[32,512]{1,0:T(8,128)S(1)}, u32[]{:S(2)}, u32[]{:S(2)}) %collective-permute-start.17) | collective-permute-done | bytes 65568 | tf_op jit(solution)/shard_map/ppermute | solution.py:65
  85.0 0.3 collective-permute-done.18.refs_2_
  85.3 0.0 collective-permute-done.19.refs_3_
  85.3 0.4 shard_map.62
  85.7 14.5 %all_to_all.11 = f32[128,1,32]{2,1,0:T(1,128)S(1)} all-to-all(f32[128,1,32]{2,1,0:T(1,128)S(1)} %bitcast.8), channel_id=1, replica_groups=mesh['pts'=128] {'pts'}, dimensions={0} | all-to-all | bytes 32768 | tf_op jit(solution)/shard_map/all_to_all | solution.py:462
  100.2 0.8 shard_map.63
  (1 shorter events, 0.0 us)
Async XLA Ops:
  1.6 9.3 %collective-permute-start.2 = (bf16[512,128]{1,0:T(8,128)(2,1)S(1)}, bf16[512,128]{1,0:T(8,128)(2,1)S(1)}, u32[]{:S(2)}, u32[]{:S(2)}) collective-permute-start(bf16[512,128]{1,0:T(8,128)(2,1)S(1)} %get-tuple-element.44.refs_0_), channel_id=1, source_target_pairs={{0,30},{1,97},{2,28},{3,99},{4,26},{5,101},{6,24},{7,103},{8,22},{... | collective-permute-start | bytes 393224 | tf_op jit(solution)/shard_map/ppermute | solution.py:65
  5.0 5.9 %collective-permute-start.1 = (bf16[512,128]{1,0:T(8,128)(2,1)S(1)}, bf16[512,128]{1,0:T(8,128)(2,1)S(1)}, u32[]{:S(2)}, u32[]{:S(2)}) collective-permute-start(bf16[512,128]{1,0:T(8,128)(2,1)S(1)} %get-tuple-element.44.refs_0_), channel_id=1, source_target_pairs={{0,24},{1,65},{2,26},{3,67},{4,28},{5,69},{6,30},{7,71},{8,16},{9,... | collective-permute-start | bytes 393224 | tf_op jit(solution)/shard_map/ppermute | solution.py:65
  5.5 5.4 %collective-permute-start = (bf16[512,128]{1,0:T(8,128)(2,1)S(1)}, bf16[512,128]{1,0:T(8,128)(2,1)S(1)}, u32[]{:S(2)}, u32[]{:S(2)}) collective-permute-start(bf16[512,128]{1,0:T(8,128)(2,1)S(1)} %get-tuple-element.44.refs_0_), channel_id=1, source_target_pairs={{0,6},{1,33},{2,4},{3,35},{4,2},{5,37},{6,0},{7,39},{8,14},{9,41},... | collective-permute-start | bytes 393224 | tf_op jit(solution)/shard_map/ppermute | solution.py:65
  5.7 5.3 %collective-permute-start.3 = (bf16[384,128]{1,0:T(8,128)(2,1)}, bf16[384,128]{1,0:T(8,128)(2,1)S(1)}, u32[]{:S(2)}, u32[]{:S(2)}) collective-permute-start(bf16[384,128]{1,0:T(8,128)(2,1)} %points_ref.1), channel_id=1, source_target_pairs={{0,10},{1,11},{2,8},{3,9},{4,14},{5,15},{6,12},{7,13},{8,2},{9,3},... | collective-permute-start | bytes 294920 | tf_op jit(solution)/shard_map/ppermute | solution.py:65
  11.0 17.2 %collective-permute-start.4 = (bf16[4,512,128]{2,1,0:T(8,128)(2,1)S(1)}, bf16[4,512,128]{2,1,0:T(8,128)(2,1)S(1)}, u32[]{:S(2)}, u32[]{:S(2)}) collective-permute-start(bf16[4,512,128]{2,1,0:T(8,128)(2,1)S(1)} %shard_map.51.refs_0_), channel_id=1, source_target_pairs={{0,1},{1,0},{2,3},{3,2},{4,5},{5,4},{6,7},{7,6},{8,9},{9,8},{10,11... | collective-permute-start | bytes 1572872 | tf_op jit(solution)/shard_map/ppermute | solution.py:65
  16.2 14.4 %collective-permute-start.8 = (bf16[4,512,128]{2,1,0:T(8,128)(2,1)S(1)}, bf16[4,512,128]{2,1,0:T(8,128)(2,1)S(1)}, u32[]{:S(2)}, u32[]{:S(2)}) collective-permute-start(bf16[4,512,128]{2,1,0:T(8,128)(2,1)S(1)} %shard_map.51.refs_0_), channel_id=1, source_target_pairs={{0,96},{1,25},{2,98},{3,27},{4,100},{5,29},{6,102},{7,31},{8,104},... | collective-permute-start | bytes 1572872 | tf_op jit(solution)/shard_map/ppermute | solution.py:65
  18.9 11.7 %collective-permute-start.7 = (bf16[4,512,128]{2,1,0:T(8,128)(2,1)S(1)}, bf16[4,512,128]{2,1,0:T(8,128)(2,1)S(1)}, u32[]{:S(2)}, u32[]{:S(2)}) collective-permute-start(bf16[4,512,128]{2,1,0:T(8,128)(2,1)S(1)} %shard_map.51.refs_0_), channel_id=1, source_target_pairs={{0,32},{1,7},{2,34},{3,5},{4,36},{5,3},{6,38},{7,1},{8,40},{9,15},... | collective-permute-start | bytes 1572872 | tf_op jit(solution)/shard_map/ppermute | solution.py:65
  21.5 4.0 %collective-permute-start.6 = (bf16[384,128]{1,0:T(8,128)(2,1)}, bf16[384,128]{1,0:T(8,128)(2,1)S(1)}, u32[]{:S(2)}, u32[]{:S(2)}) collective-permute-start(bf16[384,128]{1,0:T(8,128)(2,1)} %points_ref.1), channel_id=1, source_target_pairs={{0,8},{1,9},{2,10},{3,11},{4,12},{5,13},{6,14},{7,15},{8,0},{9,1},... | collective-permute-start | bytes 294920 | tf_op jit(solution)/shard_map/ppermute | solution.py:65
  21.5 4.0 %collective-permute-start.5 = (bf16[384,128]{1,0:T(8,128)(2,1)}, bf16[384,128]{1,0:T(8,128)(2,1)S(1)}, u32[]{:S(2)}, u32[]{:S(2)}) collective-permute-start(bf16[384,128]{1,0:T(8,128)(2,1)} %points_ref.1), channel_id=1, source_target_pairs={{0,2},{1,3},{2,0},{3,1},{4,6},{5,7},{6,4},{7,5},{8,10},{9,11},{10,... | collective-permute-start | bytes 294920 | tf_op jit(solution)/shard_map/ppermute | solution.py:65
  30.6 2.0 %collective-permute-start.9 = (bf16[4,512,128]{2,1,0:T(8,128)(2,1)S(1)}, bf16[4,512,128]{2,1,0:T(8,128)(2,1)S(1)}, u32[]{:S(2)}, u32[]{:S(2)}) collective-permute-start(bf16[4,512,128]{2,1,0:T(8,128)(2,1)S(1)} %collective-permute-done.7.refs_0_), channel_id=1, source_target_pairs={{0,1},{1,0},{2,3},{3,2},{4,5},{5,4},{6,7},{7,6},{8,9},{9,8},{10,11... | collective-permute-start | bytes 1572872 | tf_op jit(solution)/shard_map/ppermute | solution.py:65
  30.7 6.4 %collective-permute-start.10 = (bf16[4,512,128]{2,1,0:T(8,128)(2,1)S(1)}, bf16[4,512,128]{2,1,0:T(8,128)(2,1)S(1)}, u32[]{:S(2)}, u32[]{:S(2)}) collective-permute-start(bf16[4,512,128]{2,1,0:T(8,128)(2,1)S(1)} %collective-permute-done.8.refs_0_), channel_id=1, source_target_pairs={{0,1},{1,0},{2,3},{3,2},{4,5},{5,4},{6,7},{7,6},{8,9},{9,8},{10,11... | collective-permute-start | bytes 1572872 | tf_op jit(solution)/shard_map/ppermute | solution.py:65
  31.2 10.5 %collective-permute-start.11 = (bf16[4,512,128]{2,1,0:T(8,128)(2,1)S(1)}, bf16[4,512,128]{2,1,0:T(8,128)(2,1)S(1)}, u32[]{:S(2)}, u32[]{:S(2)}) collective-permute-start(bf16[4,512,128]{2,1,0:T(8,128)(2,1)S(1)} %collective-permute-done.8.refs_0_), channel_id=1, source_target_pairs={{0,32},{1,7},{2,34},{3,5},{4,36},{5,3},{6,38},{7,1},{8,40},{9,15},... | collective-permute-start | bytes 1572872 | tf_op jit(solution)/shard_map/ppermute | solution.py:65
  41.7 2.9 %collective-permute-start.12 = (bf16[4,512,128]{2,1,0:T(8,128)(2,1)S(1)}, bf16[4,512,128]{2,1,0:T(8,128)(2,1)S(1)}, u32[]{:S(2)}, u32[]{:S(2)}) collective-permute-start(bf16[4,512,128]{2,1,0:T(8,128)(2,1)S(1)} %collective-permute-done.11.refs_0_), channel_id=1, source_target_pairs={{0,1},{1,0},{2,3},{3,2},{4,5},{5,4},{6,7},{7,6},{8,9},{9,8},{10,11... | collective-permute-start | bytes 1572872 | tf_op jit(solution)/shard_map/ppermute | solution.py:65
  46.9 4.1 %collective-permute-start.13 = (f32[32,512]{1,0:T(8,128)S(1)}, f32[32,512]{1,0:T(8,128)S(1)}, u32[]{:S(2)}, u32[]{:S(2)}) collective-permute-start(f32[32,512]{1,0:T(8,128)S(1)} %get-tuple-element.62), channel_id=1, source_target_pairs={{0,10},{1,11},{2,8},{3,9},{4,14},{5,15},{6,12},{7,13},{8,2},{9,3},... | collective-permute-start | bytes 196616 | tf_op jit(solution)/shard_map/ppermute | solution.py:65
  48.1 5.1 %collective-permute-start.14 = (f32[32,512]{1,0:T(8,128)S(1)}, f32[32,512]{1,0:T(8,128)S(1)}, u32[]{:S(2)}, u32[]{:S(2)}) collective-permute-start(f32[32,512]{1,0:T(8,128)S(1)} %get-tuple-element.63), channel_id=1, source_target_pairs={{0,2},{1,3},{2,0},{3,1},{4,6},{5,7},{6,4},{7,5},{8,10},{9,11},{10,... | collective-permute-start | bytes 196616 | tf_op jit(solution)/shard_map/ppermute | solution.py:65
  49.5 3.7 %collective-permute-start.15 = (f32[32,512]{1,0:T(8,128)S(1)}, f32[32,512]{1,0:T(8,128)S(1)}, u32[]{:S(2)}, u32[]{:S(2)}) collective-permute-start(f32[32,512]{1,0:T(8,128)S(1)} %get-tuple-element.64), channel_id=1, source_target_pairs={{0,8},{1,9},{2,10},{3,11},{4,12},{5,13},{6,14},{7,15},{8,0},{9,1},... | collective-permute-start | bytes 196616 | tf_op jit(solution)/shard_map/ppermute | solution.py:65
  70.0 6.8 %collective-permute-start.16 = (bf16[16,32,512]{2,1,0:T(8,128)(2,1)S(1)}, bf16[16,32,512]{2,1,0:T(8,128)(2,1)S(1)}, u32[]{:S(2)}, u32[]{:S(2)}) collective-permute-start(bf16[16,32,512]{2,1,0:T(8,128)(2,1)S(1)} %all_to_all.10.refs_4_.refs_6_), channel_id=1, source_target_pairs={{0,1},{1,0},{2,3},{3,2},{4,5},{5,4},{6,7},{7,6},{8,9},{9,8},{10,11... | collective-permute-start | bytes 1572872 | tf_op jit(solution)/shard_map/ppermute | solution.py:65
  80.3 4.7 %collective-permute-start.17 = (f32[32,512]{1,0:T(8,128)S(1)}, f32[32,512]{1,0:T(8,128)S(1)}, u32[]{:S(2)}, u32[]{:S(2)}) collective-permute-start(f32[32,512]{1,0:T(8,128)S(1)} %get-tuple-element.71), channel_id=1, source_target_pairs={{0,10},{1,11},{2,8},{3,9},{4,14},{5,15},{6,12},{7,13},{8,2},{9,3},... | collective-permute-start | bytes 196616 | tf_op jit(solution)/shard_map/ppermute | solution.py:65
  80.3 5.0 %collective-permute-start.18 = (f32[32,512]{1,0:T(8,128)S(1)}, f32[32,512]{1,0:T(8,128)S(1)}, u32[]{:S(2)}, u32[]{:S(2)}) collective-permute-start(f32[32,512]{1,0:T(8,128)S(1)} %get-tuple-element.72), channel_id=1, source_target_pairs={{0,2},{1,3},{2,0},{3,1},{4,6},{5,7},{6,4},{7,5},{8,10},{9,11},{10,... | collective-permute-start | bytes 196616 | tf_op jit(solution)/shard_map/ppermute | solution.py:65
  80.4 4.9 %collective-permute-start.19 = (f32[32,512]{1,0:T(8,128)S(1)}, f32[32,512]{1,0:T(8,128)S(1)}, u32[]{:S(2)}, u32[]{:S(2)}) collective-permute-start(f32[32,512]{1,0:T(8,128)S(1)} %get-tuple-element.73), channel_id=1, source_target_pairs={{0,8},{1,9},{2,10},{3,11},{4,12},{5,13},{6,14},{7,15},{8,0},{9,1},... | collective-permute-start | bytes 196616 | tf_op jit(solution)/shard_map/ppermute | solution.py:65
